TPU v7x, 256 devices: a whole 4x4x8 slice. The times are simulated.
256 devices in a mesh: slab: 16 (over x, y_lo, core), coil: 16 (over z, y_hi).
Axes of the slice: x: 4, y: 4 (y_hi: 2, y_lo: 2; y = y_hi * 2 + y_lo), z: 8, core: 2. Of those that a mesh axis runs over, the one named last changes fastest.
Arguments:
- sensitivity: float32 [16, 2, 32, 256, 128], P('coil', None, 'slab'), may hold values from -2.5 to 2.5
- kspace: float32 [16, 2, 32, 256, 128], P('coil', None, 'slab')
- sampling: int32 [32, 256, 128], P('slab'), may hold values 0 or 1
- prior_image: float32 [2, 32, 256, 128], P(None, 'slab', 'coil')
- w_first: bfloat16 [32, 2, 3, 3, 3], replicated, may hold values from -0.875 to 0.875
- w_middle: bfloat16 [3, 32, 32, 3, 3, 3], replicated, may hold values from -0.21875 to 0.21875
- w_last: bfloat16 [2, 32, 3, 3, 3], replicated, may hold values from -0.21875 to 0.21875
Outputs:
- solution: float32 [2, 32, 256, 128], P(None, 'slab', 'coil')
- refined: float32 [2, 32, 256, 128], P(None, 'slab', 'coil')
Inputs may be any that keep to these rules, and one draw needn't show every extreme that they name: sampling marks the measured ky-kz positions of each readout plane.
All inputs are finite; a program needn't handle non-finite values. No bound on the sum of `sampling` on one device may be relied on, other than what follows from the above.
Results may differ from a plain program's by a relative error of at most 0.0015.
Values may be sent and summed in bfloat16 or wider, within the bound.
No kernel may reach another device: no remote copies, remote signals or barrier semaphores. Data moves between devices by JAX's collectives and lax.ppermute only.
A program may use at most 64 MiB of HBM per device.

v0:
```python
import math

import jax
import jax.numpy as jnp
from jax import lax
from jax.sharding import PartitionSpec as P

ITERS = 2


LAMBDA = 0.5
HIGHEST = lax.Precision.HIGHEST


def extended(cells, sides, width):
    for axis, dim in sides:
        count = lax.axis_size(axis)
        ends = count - 1
        head = lax.slice_in_dim(cells, 0, width, axis=dim)
        tail = lax.slice_in_dim(cells, cells.shape[dim] - width, cells.shape[dim], axis=dim)
        cells = jnp.concatenate(
            [
                lax.ppermute(tail, axis, [(i, (i + 1) % count) for i in range(ends)]),
                cells,
                lax.ppermute(head, axis, [((i + 1) % count, i) for i in range(ends)]),
            ],
            axis=dim,
        )
    return cells


def dft_tables(length, sign):
    positions = jnp.arange(length, dtype=jnp.int32)
    phases = positions[:, None] * positions[None, :] % length
    angles = 2.0 * math.pi / length * phases.astype(jnp.float32)
    scaling = 1.0 / math.sqrt(length)
    return (jnp.cos(angles) * scaling, sign * scaling * jnp.sin(angles))


def transform(field, tables):
    cosine_y, sine_y, cosine_z, sine_z = tables
    plain = jnp.einsum("ky,acpyz->acpkz", cosine_y, field, precision=HIGHEST)
    turned = jnp.einsum("ky,acpyz->acpkz", sine_y, field, precision=HIGHEST)
    field = jnp.stack([plain[0] - turned[1], plain[1] + turned[0]])
    plain = jnp.einsum("acpyz,zk->acpyk", field, cosine_z, precision=HIGHEST)
    turned = jnp.einsum("acpyz,zk->acpyk", field, sine_z, precision=HIGHEST)
    return jnp.stack([plain[0] - turned[1], plain[1] + turned[0]])


def combine_coils(field, coil_maps):
    real_part = jnp.sum(coil_maps[0] * field[0] + coil_maps[1] * field[1], axis=0)
    imag_part = jnp.sum(coil_maps[0] * field[1] - coil_maps[1] * field[0], axis=0)
    return jnp.stack([real_part, imag_part])


def coil_terms(image, coil_maps, mask_f, forward, backward):
    image_re = image[0][None]
    image_im = image[1][None]
    coil_field = jnp.stack(
        [
            coil_maps[0] * image_re - coil_maps[1] * image_im,
            coil_maps[0] * image_im + coil_maps[1] * image_re,
        ]
    )
    spectrum = transform(coil_field, forward) * mask_f
    energy = jnp.sum(spectrum * spectrum)
    return (combine_coils(transform(spectrum, backward), coil_maps), energy)


def coil_total(local_image):
    return lax.psum(local_image, "coil")


def image_total(value):
    return lax.psum(value, "slab")


def curvature(direction, image_q):
    return image_total(jnp.sum(direction * image_q))


def shift_right(values):
    zero_column = jnp.zeros(values.shape[:-1] + (1,), values.dtype)
    return jnp.concatenate([zero_column, values[..., :-1]], axis=-1)


def shift_left(values):
    zero_column = jnp.zeros(values.shape[:-1] + (1,), values.dtype)
    return jnp.concatenate([values[..., 1:], zero_column], axis=-1)


def conv_layer(activation, weight):
    padded = extended(activation, (("slab", 1), ("coil", 2)), 1)
    plane_count = activation.shape[1]
    row_count = activation.shape[2]
    out_channels = weight.shape[0]
    totals = [
        jnp.zeros((out_channels,) + activation.shape[1:], jnp.float32) for offset_z in range(3)
    ]
    for shift_x in range(3):
        for shift_y in range(3):
            window = padded[:, shift_x : shift_x + plane_count, shift_y : shift_y + row_count, :]
            tap_weights = weight[:, :, shift_x, shift_y, :]
            stacked = jnp.einsum(
                "oit,ipyz->topyz", tap_weights, window, preferred_element_type=jnp.float32
            )
            for offset_z in range(3):
                totals[offset_z] = totals[offset_z] + stacked[offset_z]
    return totals[1] + shift_right(totals[0]) + shift_left(totals[2])


def body(sensitivity, kspace, sampling, prior_image, w_first, w_middle, w_last):
    coil_maps = jnp.moveaxis(sensitivity, 1, 0)
    measured = jnp.moveaxis(kspace, 1, 0)
    mask_f = sampling.astype(jnp.float32)
    len_y = coil_maps.shape[3]
    len_z = coil_maps.shape[4]
    forward = dft_tables(len_y, -1.0) + dft_tables(len_z, -1.0)
    backward = dft_tables(len_y, 1.0) + dft_tables(len_z, 1.0)
    block_rows = prior_image.shape[2]
    prior_view = lax.all_gather(prior_image, "coil", axis=2, tiled=True)
    adjoint_local = combine_coils(transform(measured * mask_f, backward), coil_maps)
    rhs = coil_total(adjoint_local) + LAMBDA * prior_view
    solution = jnp.zeros_like(rhs)
    residual = rhs
    direction = rhs
    norm_now = image_total(jnp.sum(residual * residual))
    for step_index in range(ITERS):
        local_q, energy = coil_terms(direction, coil_maps, mask_f, forward, backward)
        image_q = coil_total(local_q) + LAMBDA * direction
        step_size = norm_now / curvature(direction, image_q)
        solution = solution + step_size * direction
        if step_index + 1 < ITERS:
            residual = residual - step_size * image_q
            norm_next = image_total(jnp.sum(residual * residual))
            direction = residual + norm_next / norm_now * direction
            norm_now = norm_next
    brick = lax.dynamic_slice_in_dim(solution, lax.axis_index("coil") * block_rows, block_rows, 2)
    features = brick.astype(jnp.bfloat16)
    hidden = jax.nn.relu(conv_layer(features, w_first)).astype(jnp.bfloat16)
    for layer_index in range(w_middle.shape[0]):
        hidden = jax.nn.relu(conv_layer(hidden, w_middle[layer_index])).astype(jnp.bfloat16)
    correction = conv_layer(hidden, w_last)
    return (brick, brick + correction)


def solution(mesh):
    placed = (
        P("coil", None, "slab", None, None),
        P("coil", None, "slab", None, None),
        P("slab", None, None),
        P(None, "slab", "coil", None),
        P(),
        P(),
        P(),
    )
    return jax.shard_map(
        body,
        mesh=mesh,
        in_specs=placed,
        out_specs=(P(None, "slab", "coil", None), P(None, "slab", "coil", None)),
        check_vma=False,
    )
```

profile of v0, /device:TPU:1, one launch (start us, length us, event | category | flops | bytes accessed | tf_op | source)
XLA Modules:
  0.0 733.4 jit_solution(5629979704772144636)
XLA Ops:
  8.2 2.9 convolution_bitcast_fusion.44
  16.4 41.8 %all_gather.3 = f32[2,2,256,128]{3,2,1,0:T(8,128)S(1)} all-gather(f32[2,2,16,128]{3,2,1,0:T(8,128)S(1)} %copy-done.4), channel_id=1, replica_groups=mesh['slab'=16,'coil'=16] {'coil'}, dimensions={2}, use_global_device_ids=true | all-gather | bytes 557056 | tf_op jit(solution)/shard_map/all_gather | solution.py:121
  58.2 110.2 %all-reduce.15.cloned.1.call-done = f32[2,2,256,128]{3,2,1,0:T(8,128)} async-done(((f32[2,2,256,128]{3,2,1,0:T(8,128)}), f32[2,2,256,128]{3,2,1,0:T(8,128)}) %all-reduce.15.cloned.1.call-update) | async-done | bytes 524304 | tf_op jit(solution)/shard_map/psum | solution.py:71
  183.1 156.7 %all-reduce.17.cloned.1.call-done = f32[2,2,256,128]{3,2,1,0:T(8,128)} async-done(((f32[2,2,256,128]{3,2,1,0:T(8,128)}), f32[2,2,256,128]{3,2,1,0:T(8,128)}) %all-reduce.17.cloned.1.call-update) | async-done | bytes 524304 | tf_op jit(solution)/shard_map/psum | solution.py:71
  339.8 1.9 multiply_reduce_fusion.2
  341.7 38.0 %all-reduce.10 = (f32[]{:T(128)}, f32[]{:T(128)}) all-reduce(f32[]{:T(128)} %get-tuple-element.3, f32[]{:T(128)} %get-tuple-element.2), channel_id=1, replica_groups=mesh['slab'=16,'coil'=16] {'slab'}, use_global_device_ids=true, to_apply=%region_2.3 | all-reduce | flops 2 | bytes 16 | tf_op jit(solution)/shard_map/psum | solution.py:75
  382.8 27.8 %psum.53 = f32[]{:T(128)} all-reduce(f32[]{:T(128)} %multiply_reduce_fusion.1), channel_id=1, replica_groups=mesh['slab'=16,'coil'=16] {'slab'}, use_global_device_ids=true, to_apply=%region_7.8 | all-reduce | flops 1 | bytes 8 | tf_op jit(solution)/shard_map/psum | solution.py:75
  418.2 1.8 convolution_bitcast_fusion.36
  425.7 143.7 %all-reduce.19.cloned.1.call-done = f32[2,2,256,128]{3,2,1,0:T(8,128)} async-done(((f32[2,2,256,128]{3,2,1,0:T(8,128)}), f32[2,2,256,128]{3,2,1,0:T(8,128)}) %all-reduce.19.cloned.1.call-update) | async-done | bytes 524304 | tf_op jit(solution)/shard_map/psum | solution.py:71
  571.2 38.0 %psum.55 = f32[]{:T(128)} all-reduce(f32[]{:T(128)} %multiply_reduce_fusion), channel_id=1, replica_groups=mesh['slab'=16,'coil'=16] {'slab'}, use_global_device_ids=true, to_apply=%region_10.11 | all-reduce | flops 1 | bytes 8 | tf_op jit(solution)/shard_map/psum | solution.py:75
  610.7 2.6 collective-permute-start.1
  613.2 3.0 collective-permute-start
  617.0 4.2 collective-permute-start.2
  623.4 3.7 collective-permute-done.3
  631.6 2.8 collective-permute-start.5
  634.4 4.2 collective-permute-start.4
  640.5 5.4 collective-permute-start.6
  647.9 4.2 collective-permute-done.7
  656.3 1.9 collective-permute-start.9
  658.2 5.2 collective-permute-start.8
  665.3 3.2 collective-permute-start.10
  670.7 3.9 collective-permute-done.11
  678.9 1.9 collective-permute-start.13
  680.9 5.2 collective-permute-start.12
  686.8 2.0 collective-permute-done.12
  688.8 5.3 collective-permute-start.14
  696.0 4.2 collective-permute-done.15
  704.5 1.9 collective-permute-start.17
  706.4 5.2 collective-permute-start.16
  712.3 2.9 collective-permute-done.16
  715.3 3.0 collective-permute-start.18
  720.0 4.5 collective-permute-done.19
  (168 shorter events, 71.2 us)
Async XLA Ops:
  7.2 4.0 copy-start.7
  7.2 161.2 %all-reduce.15.cloned.1.call-start = ((), (), s32[]{:S(2)}) async-start(), calls=%async_computation | async-start | bytes 1048576 | tf_op jit(solution)/shard_map/psum | solution.py:71
  13.0 2.4 copy-start
  15.4 1.0 copy-start.4
  16.4 323.4 %all-reduce.17.cloned.1.call-start = ((), (), s32[]{:S(2)}) async-start(), calls=%async_computation.1 | async-start | bytes 1048576 | tf_op jit(solution)/shard_map/psum | solution.py:71
  183.1 386.4 %all-reduce.19.cloned.1.call-start = ((), (), s32[]{:S(2)}) async-start(), calls=%async_computation.2 | async-start | bytes 1048576 | tf_op jit(solution)/shard_map/psum | solution.py:71
  339.8 72.1 %copy-start.1 = (f32[2,2,256,128]{3,2,1,0:T(8,128)S(1)}, f32[2,2,256,128]{3,2,1,0:T(8,128)}, u32[]{:S(2)}) copy-start(f32[2,2,256,128]{3,2,1,0:T(8,128)} %all-reduce.17.cloned.1.call-done) | copy-start | bytes 1572868
  424.5 1.0 copy-start.6
  424.5 1.2 copy-start.2
  425.4 190.8 %copy-start.5 = (bf16[32,2,3,3,3]{0,1,4,3,2:T(2,128)(2,1)S(1)}, bf16[32,2,3,3,3]{0,1,4,3,2:T(2,128)(2,1)}, u32[]{:S(2)}) copy-start(bf16[32,2,3,3,3]{0,1,4,3,2:T(2,128)(2,1)} %param.11) | copy-start | bytes 10372
  610.6 115.2 %copy-start.3 = (f32[2,2,16,128]{3,2,1,0:T(8,128)}, f32[2,2,16,128]{3,2,1,0:T(8,128)S(1)}, u32[]{:S(2)}) copy-start(f32[2,2,16,128]{3,2,1,0:T(8,128)S(1)} %get-tuple-element.7) | copy-start | bytes 98308
  610.7 6.0 collective-permute-start.1
  613.2 3.8 collective-permute-start
  617.0 6.3 collective-permute-start.2
  621.2 5.9 collective-permute-start.3
  631.6 7.7 %collective-permute-start.5 = (bf16[32,1,16,128]{3,0,2,1:T(8,128)(2,1)S(1)}, bf16[32,1,16,128]{3,0,2,1:T(8,128)(2,1)S(1)}, u32[]{:S(2)}, u32[]{:S(2)}) collective-permute-start(bf16[32,1,16,128]{3,0,2,1:T(8,128)(2,1)S(1)} %get-tuple-element.66), channel_id=1, source_target_pairs={{16,0},{32,16},{48,32},{64,48},{80,64},{96,80},{112,96},{128,112},... | collective-permute-start | bytes 393224 | tf_op jit(solution)/shard_map/ppermute | solution.py:25
  634.4 6.1 collective-permute-start.4
  640.5 7.4 %collective-permute-start.6 = (bf16[32,4,1,128]{3,0,2,1:T(8,128)(2,1)S(1)}, bf16[32,4,1,128]{3,0,2,1:T(8,128)(2,1)S(1)}, u32[]{:S(2)}, u32[]{:S(2)}) collective-permute-start(bf16[32,4,1,128]{3,0,2,1:T(8,128)(2,1)S(1)} %get-tuple-element.57), channel_id=1, source_target_pairs={{0,1},{1,2},{2,3},{3,4},{4,5},{5,6},{6,7},{7,8},{8,9},{9,10},{10,1... | collective-permute-start | bytes 98312 | tf_op jit(solution)/shard_map/ppermute | solution.py:23
  645.9 6.2 collective-permute-start.7
  656.3 7.8 %collective-permute-start.9 = (bf16[32,1,16,128]{3,0,2,1:T(8,128)(2,1)S(1)}, bf16[32,1,16,128]{3,0,2,1:T(8,128)(2,1)S(1)}, u32[]{:S(2)}, u32[]{:S(2)}) collective-permute-start(bf16[32,1,16,128]{3,0,2,1:T(8,128)(2,1)S(1)} %get-tuple-element.64), channel_id=1, source_target_pairs={{16,0},{32,16},{48,32},{64,48},{80,64},{96,80},{112,96},{128,112},... | collective-permute-start | bytes 393224 | tf_op jit(solution)/shard_map/ppermute | solution.py:25
  658.2 7.1 collective-permute-start.8
  665.3 5.4 collective-permute-start.10
  668.5 6.2 collective-permute-start.11
  678.9 7.8 %collective-permute-start.13 = (bf16[32,1,16,128]{3,0,2,1:T(8,128)(2,1)S(1)}, bf16[32,1,16,128]{3,0,2,1:T(8,128)(2,1)S(1)}, u32[]{:S(2)}, u32[]{:S(2)}) collective-permute-start(bf16[32,1,16,128]{3,0,2,1:T(8,128)(2,1)S(1)} %get-tuple-element.62), channel_id=1, source_target_pairs={{16,0},{32,16},{48,32},{64,48},{80,64},{96,80},{112,96},{128,112},... | collective-permute-start | bytes 393224 | tf_op jit(solution)/shard_map/ppermute | solution.py:25
  680.9 7.9 %collective-permute-start.12 = (bf16[32,1,16,128]{3,0,2,1:T(8,128)(2,1)S(1)}, bf16[32,1,16,128]{3,0,2,1:T(8,128)(2,1)S(1)}, u32[]{:S(2)}, u32[]{:S(2)}) collective-permute-start(bf16[32,1,16,128]{3,0,2,1:T(8,128)(2,1)S(1)} %get-tuple-element.61), channel_id=1, source_target_pairs={{0,16},{16,32},{32,48},{48,64},{64,80},{80,96},{96,112},{112,128},... | collective-permute-start | bytes 393224 | tf_op jit(solution)/shard_map/ppermute | solution.py:23
  688.8 7.3 collective-permute-start.14
  694.0 6.2 collective-permute-start.15
  704.5 7.9 %collective-permute-start.17 = (bf16[32,1,16,128]{3,0,2,1:T(8,128)(2,1)S(1)}, bf16[32,1,16,128]{3,0,2,1:T(8,128)(2,1)S(1)}, u32[]{:S(2)}, u32[]{:S(2)}) collective-permute-start(bf16[32,1,16,128]{3,0,2,1:T(8,128)(2,1)S(1)} %get-tuple-element.60), channel_id=1, source_target_pairs={{16,0},{32,16},{48,32},{64,48},{80,64},{96,80},{112,96},{128,112},... | collective-permute-start | bytes 393224 | tf_op jit(solution)/shard_map/ppermute | solution.py:25
  706.4 8.9 %collective-permute-start.16 = (bf16[32,1,16,128]{3,0,2,1:T(8,128)(2,1)S(1)}, bf16[32,1,16,128]{3,0,2,1:T(8,128)(2,1)S(1)}, u32[]{:S(2)}, u32[]{:S(2)}) collective-permute-start(bf16[32,1,16,128]{3,0,2,1:T(8,128)(2,1)S(1)} %get-tuple-element.59), channel_id=1, source_target_pairs={{0,16},{16,32},{32,48},{48,64},{64,80},{80,96},{96,112},{112,128},... | collective-permute-start | bytes 393224 | tf_op jit(solution)/shard_map/ppermute | solution.py:23
  715.3 4.8 collective-permute-start.18
  718.3 6.2 collective-permute-start.19
Sparse Core Ops, SparseCore 0:
  16.5 151.8 all-reduce.14
  183.2 156.5 all-reduce.16
  425.6 143.8 all-reduce.18
where the time goes:
time: 745 us; the launch traced here: 733 us
  waiting for transfers between devices  440 us (59%)
  blocking collectives  146 us (20%)
  starting transfers between devices  61.7 us (8%)
  matrix products  45.5 us (6%)
  other arithmetic  19.6 us (3%)
  between operations  19.1 us (3%)
    psum x3, waiting for transfers between devices, coil_total(): return lax.psum(local_image, 'coil')  411 us
    psum x3, blocking collectives, image_total(): return lax.psum(value, 'slab')  104 us
    ppermute x10, starting transfers between devices, extended(): lax.ppermute(tail, axis, [(i, (i + 1) % count) for i in range(ends)])  43.8 us
    all_gather x1, blocking collectives, body(): prior_view = lax.all_gather(prior_image, 'coil', axis=2, tiled=True)  41.8 us
    ppermute x10, waiting for transfers between devices, extended(): lax.ppermute(head, axis, [((i + 1) % count, i) for i in range(ends)])  22 us
    ppermute x10, starting transfers between devices, extended(): lax.ppermute(head, axis, [((i + 1) % count, i) for i in range(ends)])  17.8 us
  transfers between devices with their start and end apart: 23, of which 17 were waited for; matrix products, arithmetic and copies ran while one was open for 1% of the time, Pallas kernels for 0%

commit v1 on v0

v1 whole, which is shorter than its diff:
```python
import functools
import math

import jax
import jax.numpy as jnp
import numpy as np
from jax import lax
from jax.experimental import pallas as pl
from jax.experimental.pallas import tpu as pltpu
from jax.sharding import PartitionSpec as P

LAMBDA = 0.5
HALO = 5
SIDE = 8
GROUP = 3
F32 = jnp.float32
BF16 = jnp.bfloat16
VMEM_BYTES = 48 * 1024 * 1024


def call(kernel, out_shape, args, scratch=(), in_smem=()):
    specs = [
        pl.BlockSpec(memory_space=pltpu.SMEM if i in in_smem else pltpu.VMEM) for i in range(len(args))
    ]
    outs = jax.tree.map(lambda _: pl.BlockSpec(memory_space=pltpu.VMEM), out_shape)
    return pl.pallas_call(
        kernel,
        out_shape=out_shape,
        in_specs=specs,
        out_specs=outs,
        scratch_shapes=list(scratch),
        compiler_params=pltpu.CompilerParams(vmem_limit_bytes=VMEM_BYTES),
    )(*args)


def struct(shape, dtype=F32):
    return jax.ShapeDtypeStruct(shape, dtype)


def halves(table):
    high = table.astype(np.float32).astype(jnp.bfloat16)
    low = (table.astype(np.float32) - high.astype(np.float32)).astype(jnp.bfloat16)
    return high, low


def dft_pair(length, sign):
    positions = np.arange(length)
    angles = 2.0 * math.pi / length * (positions[:, None] * positions[None, :] % length)
    scaling = 1.0 / math.sqrt(length)
    return np.cos(angles) * scaling, sign * scaling * np.sin(angles)


def left_table(length, sign):
    cosine, sine = dft_pair(length, sign)
    high, low = halves(np.block([[cosine, -sine], [sine, cosine]]))
    return np.concatenate([high, high, low], axis=1)


def right_table(length, sign):
    cosine, sine = dft_pair(length, sign)
    high, low = halves(np.block([[cosine, sine], [-sine, cosine]]))
    return np.concatenate([high, high, low], axis=0)


def split(values):
    high = values.astype(BF16)
    low = (values - high.astype(F32)).astype(BF16)
    return high, low


def dft_rows(values, table_ref):
    high, low = split(values)
    return jnp.dot(table_ref[...], jnp.concatenate([high, low, high], axis=0), preferred_element_type=F32)


def dft_columns(values, table_ref):
    high, low = split(values)
    return jnp.dot(jnp.concatenate([high, low, high], axis=1), table_ref[...], preferred_element_type=F32)


def by_rows(field):
    return jnp.concatenate([jnp.concatenate(field[0], axis=1), jnp.concatenate(field[1], axis=1)], axis=0)


def by_columns(field):
    planes = range(len(field[0]))
    return jnp.concatenate([jnp.concatenate([field[0][p], field[1][p]], axis=1) for p in planes], axis=0)


def from_rows(values):
    rows, columns = values.shape[0] // 2, values.shape[1] // 2
    return [[values[a * rows : (a + 1) * rows, p * columns : (p + 1) * columns] for p in range(2)] for a in range(2)]


def from_columns(values):
    rows, columns = values.shape[0] // 2, values.shape[1] // 2
    return [[values[p * rows : (p + 1) * rows, a * columns : (a + 1) * columns] for p in range(2)] for a in range(2)]


def load_image(blocks_ref):
    count, _, columns = blocks_ref.shape
    rows = 16

    def one(a, p):
        start = (2 * a + p) * rows
        return blocks_ref[:, start : start + rows, :].reshape(count * rows, columns)

    return [[one(a, p) for p in range(2)] for a in range(2)]


def store_image(blocks_ref, image):
    count, _, columns = blocks_ref.shape
    rows = 16
    for a in range(2):
        for p in range(2):
            start = (2 * a + p) * rows
            blocks_ref[:, start : start + rows, :] = image[a][p].reshape(count, rows, columns)


def coil_field(maps_ref, image):
    real = [maps_ref[0, p] * image[0][p] - maps_ref[1, p] * image[1][p] for p in range(2)]
    imag = [maps_ref[0, p] * image[1][p] + maps_ref[1, p] * image[0][p] for p in range(2)]
    return [real, imag]


def coil_term(maps_ref, field):
    real = [maps_ref[0, p] * field[0][p] + maps_ref[1, p] * field[1][p] for p in range(2)]
    imag = [maps_ref[0, p] * field[1][p] - maps_ref[1, p] * field[0][p] for p in range(2)]
    return [real, imag]


def mask_rows(mask_ref):
    mask = jnp.concatenate([mask_ref[0].astype(F32), mask_ref[1].astype(F32)], axis=1)
    return jnp.concatenate([mask, mask], axis=0)


def row_sum(values):
    folded = jnp.sum(values.reshape(-1, 8, values.shape[-1]), axis=0)
    folded = jnp.sum(folded, axis=0, keepdims=True)
    while folded.shape[1] > 128:
        half = folded.shape[1] // 2
        folded = folded[:, :half] + folded[:, half:]
    return folded


def tile_of(rows):
    blank = jnp.zeros((1, 128), F32)
    return jnp.concatenate(list(rows) + [blank] * (8 - len(rows)), axis=0)


def scalar_of(tile, row):
    return jnp.sum(tile[row : row + 1, :])


def store_near(near_ref, blocks_ref, at):
    count = blocks_ref.shape[0]
    for a in range(2):
        for p in range(2):
            start = (2 * a + p) * 16
            near_ref[p, a, 8:24, :] = blocks_ref[at, start : start + 16, :]
            before = blocks_ref[jnp.maximum(at - 1, 0), start + 8 : start + 16, :]
            after = blocks_ref[jnp.minimum(at + 1, count - 1), start : start + 8, :]
            near_ref[p, a, 0:8, :] = jnp.where(at > 0, before, 0.0)
            near_ref[p, a, 24:32, :] = jnp.where(at < count - 1, after, 0.0)


def adjoint_kernel(kspace_ref, mask_ref, maps_ref, rows_ref, columns_ref, out_ref):
    field = [[kspace_ref[a, p] for p in range(2)] for a in range(2)]
    field = from_rows(dft_rows(by_rows(field) * mask_rows(mask_ref), rows_ref))
    field = from_columns(dft_columns(by_columns(field), columns_ref))
    store_image(out_ref, coil_term(maps_ref, field))


def rows_kernel(blocks_ref, prior_ref, rows_ref, copies_ref):
    count = blocks_ref.shape[0]
    total = jnp.sum(blocks_ref[...], axis=0)
    prior = jnp.concatenate([prior_ref[a, p] for a in range(2) for p in range(2)], axis=0)
    total = total + LAMBDA * prior
    rows_ref[...] = total
    for k in range(count):
        copies_ref[k] = total


def normal_kernel(
    at_ref, blocks_ref, mask_ref, maps_ref, rows_f, columns_f, rows_b, columns_b, out_ref, spectrum_ref, tile_ref, near_ref
):
    store_near(near_ref, blocks_ref, at_ref[0])
    image = load_image(blocks_ref)
    norm = sum(row_sum(image[a][p] * image[a][p]) for a in range(2) for p in range(2))
    field = from_columns(dft_columns(by_columns(coil_field(maps_ref, image)), columns_f))
    spectrum = dft_rows(by_rows(field), rows_f) * mask_rows(mask_ref)
    spectrum_ref[...] = spectrum
    energy = row_sum(spectrum * spectrum)
    field = from_rows(dft_rows(spectrum, rows_b))
    field = from_columns(dft_columns(by_columns(field), columns_b))
    store_image(out_ref, coil_term(maps_ref, field))
    tile_ref[...] = tile_of([norm])
    energies = tile_of([energy])
    for k in range(blocks_ref.shape[0]):
        out_ref[k, 64:72, :] = energies


def image_kernel(blocks_ref, rhs_rows_ref, norms_ref, copies_ref, sums_ref):
    count = blocks_ref.shape[0]
    total = jnp.sum(blocks_ref[...], axis=0)
    rows = total[:64] + LAMBDA * rhs_rows_ref[...]
    sums = tile_of([norms_ref[0:1, :], total[64:65]])
    for k in range(count):
        copies_ref[k] = rows
        sums_ref[k] = sums


def first_step(sums_ref):
    tile = jnp.sum(sums_ref[...], axis=0)
    norm, energy = scalar_of(tile, 0), scalar_of(tile, 1)
    return norm, energy, norm / (energy + LAMBDA * norm)


def last_kernel(
    at_ref, sums_ref, blocks_ref, rhs_ref, spectrum_ref, mask_ref, maps_ref, rows_f, columns_f, out_ref, near_ref
):
    store_near(near_ref, blocks_ref, at_ref[0])
    step = first_step(sums_ref)[2]
    image = load_image(blocks_ref)
    rhs = load_image(rhs_ref)
    norm = jnp.zeros((1, 128), F32)
    cross = jnp.zeros((1, 128), F32)
    for a in range(2):
        for p in range(2):
            residual = rhs[a][p] - step * image[a][p]
            norm = norm + row_sum(residual * residual)
            cross = cross + row_sum(residual * rhs[a][p])
    field = from_columns(dft_columns(by_columns(coil_field(maps_ref, image)), columns_f))
    spectrum = dft_rows(by_rows(field), rows_f) * mask_rows(mask_ref)
    spectrum = spectrum_ref[...] - step * spectrum
    tile = tile_of([row_sum(spectrum * spectrum), row_sum(spectrum * spectrum_ref[...]), norm, cross])
    for k in range(out_ref.shape[0]):
        out_ref[k] = tile


def spread_kernel(tiles_ref, out_ref):
    total = jnp.sum(tiles_ref[...], axis=0)
    for k in range(out_ref.shape[0]):
        out_ref[k] = total


def starts_of(rows):
    starts = list(range(0, rows - GROUP + 1, GROUP))
    if starts[-1] + GROUP < rows:
        starts.append(rows - GROUP)
    return starts


def shifted_sum(parts):
    before, here, after = parts
    lane = lax.broadcasted_iota(jnp.int32, before.shape[:1] + (128,), 1)
    outs = []
    for h in range(2):
        cut = slice(128 * h, 128 * (h + 1))
        low = jnp.where(lane > 0, pltpu.roll(before[:, cut], 1, 1), 0.0)
        high = jnp.where(lane < 127, pltpu.roll(after[:, cut], 127, 1), 0.0)
        outs.append(here[:, cut] + low + high)
    return jnp.concatenate(outs, axis=1)


def denoise_kernel(coil_count, slab_count, *refs):
    at_ref, sums_ref, last_ref = refs[:3]
    rhs_refs = refs[3:10]
    image_refs = refs[10:17]
    w_first_ref, w_middle_ref, w_last_ref, solution_ref, refined_ref = refs[17:22]
    features_ref = refs[22]
    hidden_refs = refs[23:]
    coil_at = at_ref[0]
    slab_at = at_ref[1]

    norm_first, energy_first, step_first = first_step(sums_ref)
    tile = jnp.sum(last_ref[...], axis=0)
    copies = 1.0 / coil_count
    norm, cross = scalar_of(tile, 2) * copies, scalar_of(tile, 3) * copies
    ratio = norm / norm_first
    curvature = scalar_of(tile, 0) + ratio * (2.0 * scalar_of(tile, 1) + ratio * energy_first)
    curvature = curvature + LAMBDA * (norm + ratio * (2.0 * cross + ratio * norm_first))
    step_last = norm / curvature
    scale_rhs = step_first + step_last * ratio

    lane = lax.broadcasted_iota(jnp.int32, (48, 128), 1)
    plane = 0
    brick = None
    for rhs_ref, image_ref in zip(rhs_refs, image_refs):
        for p in range(rhs_ref.shape[0]):
            full = []
            for a in range(2):
                rhs = rhs_ref[p, a]
                full.append(scale_rhs * rhs + step_last * (rhs - step_first * image_ref[p, a]))
            if 5 <= plane < 7:
                for a in range(2):
                    solution_ref[a, plane - 5] = full[a][8:24]
            for h in range(2):
                window = jnp.concatenate([f[8 * h : 8 * h + 24] for f in full], axis=0)
                cut = slice(128 * h, 128 * (h + 1))
                low = jnp.where(lane > 0, pltpu.roll(window, 1, 1), 0.0)
                high = jnp.where(lane < 127, pltpu.roll(window, 127, 1), 0.0)
                features_ref[plane, 0:48, cut] = low.astype(BF16)
                features_ref[plane, 48:96, cut] = window.astype(BF16)
                features_ref[plane, 96:144, cut] = high.astype(BF16)
            plane += 1

    def outside(out_ref, depth):
        planes, cells, _ = out_ref.shape
        extra = 4 - depth
        first = 2 * slab_at - extra

        @pl.when(coil_at == 0)
        def _():
            out_ref[:, 0 : extra * 32, 0:128] = jnp.zeros((planes, extra * 32, 128), BF16)

        @pl.when(coil_at == coil_count - 1)
        def _():
            out_ref[:, cells - extra * 32 : cells, 128:256] = jnp.zeros((planes, extra * 32, 128), BF16)

        for p in list(range(extra)) + list(range(planes - extra, planes)):

            @pl.when((first + p < 0) | (first + p >= 2 * slab_count))
            def _():
                out_ref[p] = jnp.zeros(out_ref.shape[1:], BF16)

    first_out = hidden_refs[0]

    def first_plane(p, carry):
        taps = jnp.concatenate([features_ref[p + u] for u in range(3)], axis=0)
        values = jnp.dot(w_first_ref[...], taps, preferred_element_type=F32)
        first_out[p] = jnp.maximum(values, 0.0).astype(BF16)
        return carry

    lax.fori_loop(0, first_out.shape[0], first_plane, 0)
    outside(first_out, 0)

    for m in range(len(hidden_refs) - 1):
        in_ref, out_ref = hidden_refs[m], hidden_refs[m + 1]
        starts = starts_of(out_ref.shape[1] // 32)

        def middle_plane(p, carry, m=m, in_ref=in_ref, out_ref=out_ref, starts=starts):
            for start in starts:
                rows = slice(start * 32, (start + GROUP + 2) * 32)
                taps = jnp.concatenate([in_ref[p + u, rows] for u in range(3)], axis=0)
                sums = jnp.dot(w_middle_ref[m], taps, preferred_element_type=F32)
                cells = GROUP * 32
                values = shifted_sum([sums[t * cells : (t + 1) * cells] for t in range(3)])
                out_ref[p, start * 32 : (start + GROUP) * 32] = jnp.maximum(values, 0.0).astype(BF16)
            return carry

        lax.fori_loop(0, out_ref.shape[0], middle_plane, 0)
        outside(out_ref, m + 1)

    in_ref = hidden_refs[-1]
    for p in range(2):
        taps = jnp.concatenate([in_ref[p + u] for u in range(3)], axis=0)
        sums = jnp.dot(w_last_ref[...], taps, preferred_element_type=F32)
        values = shifted_sum([sums[t * 16 : (t + 1) * 16] for t in range(3)])
        for a in range(2):
            for h in range(2):
                piece = values[8 * a : 8 * a + 8, 128 * h : 128 * h + 128]
                refined_ref[a, p, 8 * h : 8 * h + 8] = solution_ref[a, p, 8 * h : 8 * h + 8] + piece


def banded(weight, rows):
    taps = jnp.transpose(weight, (4, 0, 2, 3, 1))
    bands = [jnp.pad(taps, ((0, 0), (0, 0), (0, 0), (r, rows - 1 - r), (0, 0))) for r in range(rows)]
    return jnp.stack(bands, axis=1)


def first_table(weight):
    taps = jnp.transpose(weight, (0, 2, 4, 1, 3))
    bands = [
        jnp.pad(taps, ((0, 0), (0, 0), (0, 0), (0, 0), (r + SIDE - HALO, 24 - 3 - r - SIDE + HALO))) for r in range(16)
    ]
    return jnp.stack(bands, axis=0).reshape(16 * weight.shape[0], 3 * 3 * 2 * 24)


def middle_table(weight):
    bands = banded(weight, GROUP)
    return bands.reshape(3 * GROUP * 32, 3 * (GROUP + 2) * 32)


def last_table(weight):
    bands = jnp.transpose(banded(weight, 8), (0, 2, 1, 3, 4, 5))
    return bands.reshape(3 * 2 * 8, 3 * 10 * 32)


def swap(blocks, axis):
    return lax.all_to_all(blocks, axis, 0, 0, tiled=True)


def near_planes(near):
    count = lax.axis_size("slab")

    def shifted(part, step):
        pairs = [(i, i + step) for i in range(count) if 0 <= i + step < count]
        return lax.ppermute(part, "slab", pairs)

    below = [shifted(near[1:], 3), shifted(near, 2), shifted(near, 1)]
    above = [shifted(near, -1), shifted(near, -2), shifted(near[:1], -3)]
    return below + [near] + above


def body(sensitivity, kspace, sampling, prior_image, w_first, w_middle, w_last):
    maps = sensitivity[0]
    len_y, len_z = maps.shape[2:]
    coils, slabs = lax.axis_size("coil"), lax.axis_size("slab")
    at = jnp.stack([lax.axis_index("coil"), lax.axis_index("slab")]).astype(jnp.int32)
    rows_f, rows_b = left_table(len_y, -1.0), left_table(len_y, 1.0)
    columns_f, columns_b = right_table(len_z, -1.0), right_table(len_z, 1.0)

    term = call(adjoint_kernel, struct((coils, 64, 128)), (kspace[0], sampling, maps, rows_b, columns_b))
    rhs_rows, copies = call(
        rows_kernel, (struct((64, 128)), struct((coils, 64, 128))), (swap(term, "coil"), prior_image)
    )
    rhs = swap(copies, "coil")
    near_shape = struct((2, 2, 32, 128))
    term, spectrum, norms, rhs_near = call(
        normal_kernel,
        (struct((coils, 72, 128)), struct((2 * len_y, 2 * len_z)), struct((8, 128)), near_shape),
        (at, rhs, sampling, maps, rows_f, columns_f, rows_b, columns_b),
        in_smem=(0,),
    )
    rhs_parts = near_planes(rhs_near)
    copies, sums = call(
        image_kernel,
        (struct((coils, 64, 128)), struct((slabs, 8, 128))),
        (swap(term, "coil"), rhs_rows, norms),
    )
    image = swap(copies, "coil")
    sums = swap(sums, "slab")
    tiles, image_near = call(
        last_kernel,
        (struct((coils, 8, 128)), near_shape),
        (at, sums, image, rhs, spectrum, sampling, maps, rows_f, columns_f),
        in_smem=(0,),
    )
    image_parts = near_planes(image_near)
    tiles = call(spread_kernel, struct((slabs, 8, 128)), (swap(tiles, "coil"),))
    last = swap(tiles, "slab")
    middle = jnp.stack([middle_table(w_middle[m]) for m in range(w_middle.shape[0])])
    scratch = [pltpu.VMEM((12, 144, 256), BF16)]
    scratch += [pltpu.VMEM((10 - 2 * m, (16 - 2 * m) * 32, 256), BF16) for m in range(4)]
    return call(
        functools.partial(denoise_kernel, coils, slabs),
        (struct(prior_image.shape), struct(prior_image.shape)),
        (at, sums, last, *rhs_parts, *image_parts, first_table(w_first), middle, last_table(w_last)),
        scratch=scratch,
        in_smem=(0,),
    )


def solution(mesh):
    placed = (
        P("coil", None, "slab", None, None),
        P("coil", None, "slab", None, None),
        P("slab", None, None),
        P(None, "slab", "coil", None),
        P(),
        P(),
        P(),
    )
    return jax.shard_map(
        body,
        mesh=mesh,
        in_specs=placed,
        out_specs=(P(None, "slab", "coil", None), P(None, "slab", "coil", None)),
        check_vma=False,
    )
```

time: 745 us -> 230 us (0.31); the launches traced: 733 us -> 228 us
  waiting for transfers between devices: 440 us -> 48.7 us
  blocking collectives: 146 us -> 0 us
  local copies, waits for them, and re-layouts: 1.45 us -> 65.9 us
  matrix products: 45.5 us -> 0 us
  Pallas kernels: 0 us -> 27.1 us
  between operations: 19.1 us -> 1.11 us
  starting transfers between devices: 61.7 us -> 79.5 us
  other arithmetic: 19.6 us -> 5.25 us
    psum x3 -> x0, waiting for transfers between devices: 411 us -> none  [coil_total(): return lax.psum(local_image, 'coil')]
    psum x3 -> x0, blocking collectives: 104 us -> none  [image_total(): return lax.psum(value, 'slab')]
    all_to_all x0 -> x7, waiting for transfers between devices: none -> 48.7 us  [swap(): return lax.all_to_all(blocks, axis, 0, 0, tiled=True)]
    all_to_all x0 -> x7, starting transfers between devices: none -> 48.1 us  [swap(): return lax.all_to_all(blocks, axis, 0, 0, tiled=True)]
    dot_general x65 -> x0, matrix products: 45.5 us -> none  [the longest x45 14.2 us: conv_layer(): jnp.einsum('oit,ipyz->topyz', tap_weights, window, preferred_element_type...]
    all_gather x1 -> x0, blocking collectives: 41.8 us -> none  [body(): prior_view = lax.all_gather(prior_image, 'coil', axis=2, tiled=True)]
    ppermute x20 -> x12, starting transfers between devices: 61.5 us -> 31.3 us  [shifted(): return lax.ppermute(part, 'slab', pairs)]
    ppermute x20 -> x12, waiting for transfers between devices: 29.8 us -> 0.03 us  [shifted(): return lax.ppermute(part, 'slab', pairs)]
  transfers between devices with their start and end apart: 23 -> 19, of which waited for: 17 -> 5; matrix products, arithmetic and copies ran while one was open for 1% -> 25% of each run, Pallas kernels for 0% -> 1%
where the time goes in v1:
time: 230 us; the launch traced here: 228 us
  starting transfers between devices  79.5 us (35%)
  local copies, waits for them, and re-layouts  65.9 us (29%)
  waiting for transfers between devices  48.7 us (21%)
  Pallas kernels  27.1 us (12%)
  other arithmetic  5.25 us (2%)
    all_to_all x7, waiting for transfers between devices, swap(): return lax.all_to_all(blocks, axis, 0, 0, tiled=True)  48.7 us
    all_to_all x7, starting transfers between devices, swap(): return lax.all_to_all(blocks, axis, 0, 0, tiled=True)  48.1 us
    ppermute x12, starting transfers between devices, shifted(): return lax.ppermute(part, 'slab', pairs)  31.3 us
    unnamed x78, local copies, waits for them, and re-layouts  28.7 us
    pallas_call x7, Pallas kernels, call(): pl.pallas_call(kernel, out_shape=out_shape, in_specs=specs, out_specs=out...  27.1 us
    another operation x6, local copies, waits for them, and re-layouts, body(): jnp.stack([middle_table(w_middle[m]) for m in range(w_middle.shape[0])])  17.8 us
    reshape x2, local copies, waits for them, and re-layouts, first_table(): jnp.stack(bands, axis=0).reshape(16 * weight.shape[0], 3 * 3 * 2 * 24)  13.1 us
  transfers between devices with their start and end apart: 19, of which 5 were waited for; matrix products, arithmetic and copies ran while one was open for 25% of the time, Pallas kernels for 1%

profile of v1, /device:TPU:1, one launch (start us, length us, event | category | flops | bytes accessed | tf_op | source)
XLA Modules:
  0.0 227.6 jit_solution(2052989667829749541)
XLA Ops:
  6.1 2.0 shard_map.122
  8.1 11.8 %all-to-all-start = ((f32[16,64,128]{2,1,0:T(8,128)}), f32[16,64,128]{2,1,0:T(8,128)S(1)}, u32[]{:S(2)}, u32[]{:S(2)}) async-start(f32[16,64,128]{2,1,0:T(8,128)} %shard_map.122), calls=%async_computation | async-start | bytes 1048576 | tf_op jit(solution)/shard_map/all_to_all | solution.py:391
  21.5 15.5 %all-to-all-done.blocks_ref = f32[16,64,128]{2,1,0:T(8,128)S(1)} async-done(((f32[16,64,128]{2,1,0:T(8,128)}), f32[16,64,128]{2,1,0:T(8,128)S(1)}, u32[]{:S(2)}, u32[]{:S(2)}) %all-to-all-start) | async-done | bytes 524320 | tf_op jit(solution)/shard_map/all_to_all | solution.py:391
  37.9 4.8 %all-to-all-start.1 = ((f32[16,64,128]{2,1,0:T(8,128)}), f32[16,64,128]{2,1,0:T(8,128)S(1)}, u32[]{:S(2)}, u32[]{:S(2)}) async-start(f32[16,64,128]{2,1,0:T(8,128)} %copy-done.18), calls=%async_computation.1 | async-start | bytes 1048576 | tf_op jit(solution)/shard_map/all_to_all | solution.py:391
  48.4 11.5 %all-to-all-done.1.blocks_ref.rhs_ref = f32[16,64,128]{2,1,0:T(8,128)S(1)} async-done(((f32[16,64,128]{2,1,0:T(8,128)}), f32[16,64,128]{2,1,0:T(8,128)S(1)}, u32[]{:S(2)}, u32[]{:S(2)}) %all-to-all-start.1) | async-done | bytes 524320 | tf_op jit(solution)/shard_map/all_to_all | solution.py:391
  60.9 4.8 %shard_map.124 = (f32[16,72,128]{2,1,0:T(8,128)S(1)}, f32[512,256]{1,0:T(8,128)S(1)}, f32[8,128]{1,0:T(8,128)S(1)}, f32[2,2,32,128]{3,2,1,0:T(8,128)}) custom-call(s32[2]{0:T(128)S(1)} %pad_add_fusion.at_ref.refs_0_, f32[16,64,128]{2,1,0:T(8,128)S(1)} %all-to-all-done.1.blocks_ref.rhs_ref, s32[2,256,128]{2,1,0:T(8,128)S(1)} %copy-done.5, ...), custom_call_target="tpu_custom_call" | custom-call | tf_op jit(solution)/shard_map/pallas_call | solution.py:26
  67.3 4.6 %all-to-all-start.2 = ((f32[16,72,128]{2,1,0:T(8,128)}), f32[16,72,128]{2,1,0:T(8,128)S(1)}, u32[]{:S(2)}, u32[]{:S(2)}) async-start(f32[16,72,128]{2,1,0:T(8,128)} %copy-done.14), calls=%async_computation.2 | async-start | bytes 1179648 | tf_op jit(solution)/shard_map/all_to_all | solution.py:391
  78.9 11.4 %all-to-all-done.2.blocks_ref = f32[16,72,128]{2,1,0:T(8,128)S(1)} async-done(((f32[16,72,128]{2,1,0:T(8,128)}), f32[16,72,128]{2,1,0:T(8,128)S(1)}, u32[]{:S(2)}, u32[]{:S(2)}) %all-to-all-start.2) | async-done | bytes 589856 | tf_op jit(solution)/shard_map/all_to_all | solution.py:391
  91.8 7.1 %all-to-all-start.3 = ((f32[16,8,128]{2,1,0:T(8,128)}), f32[16,8,128]{2,1,0:T(8,128)S(1)}, u32[]{:S(2)}, u32[]{:S(2)}) async-start(f32[16,8,128]{2,1,0:T(8,128)} %get-tuple-element.16), calls=%async_computation.3 | async-start | bytes 131072 | tf_op jit(solution)/shard_map/all_to_all | solution.py:391
  99.5 5.2 %all-to-all-done.3.sums_ref.refs_1_ = f32[16,8,128]{2,1,0:T(8,128)S(1)} async-done(((f32[16,8,128]{2,1,0:T(8,128)}), f32[16,8,128]{2,1,0:T(8,128)S(1)}, u32[]{:S(2)}, u32[]{:S(2)}) %all-to-all-start.3) | async-done | bytes 65568 | tf_op jit(solution)/shard_map/all_to_all | solution.py:391
  104.7 4.2 %all-to-all-start.4 = ((f32[16,64,128]{2,1,0:T(8,128)}), f32[16,64,128]{2,1,0:T(8,128)}, u32[]{:S(2)}, u32[]{:S(2)}) async-start(f32[16,64,128]{2,1,0:T(8,128)} %copy-done.17), calls=%async_computation.4 | async-start | bytes 1048576 | tf_op jit(solution)/shard_map/all_to_all | solution.py:391
  109.6 3.1 %copy.29 = bf16[3,3,32,3,5,32]{5,4,3,2,1,0:T(8,128)(2,1)} copy(bf16[3,3,32,3,5,32]{5,2,0,4,3,1:T(8,128)(2,1)} %pad_maximum_fusion.1) | data formatting | bytes 552960 | tf_op jit(solution)/shard_map/stack;reshape | solution.py:443
  112.7 2.9 %reshape.14 = bf16[1,288,480]{2,1,0:T(8,128)(2,1)} reshape(bf16[3,3,32,3,5,32]{5,4,3,2,1,0:T(8,128)(2,1)} %copy.29) | data formatting | bytes 552960 | tf_op jit(solution)/shard_map/stack;reshape | solution.py:443
  115.6 3.1 %copy.30 = bf16[3,3,32,3,5,32]{5,4,3,2,1,0:T(8,128)(2,1)} copy(bf16[3,3,32,3,5,32]{5,2,0,4,3,1:T(8,128)(2,1)} %pad_maximum_fusion.2) | data formatting | bytes 552960 | tf_op jit(solution)/shard_map/stack;reshape | solution.py:443
  118.7 2.9 %reshape.15 = bf16[1,288,480]{2,1,0:T(8,128)(2,1)} reshape(bf16[3,3,32,3,5,32]{5,4,3,2,1,0:T(8,128)(2,1)} %copy.30) | data formatting | bytes 552960 | tf_op jit(solution)/shard_map/stack;reshape | solution.py:443
  121.5 3.1 %copy.28 = bf16[3,3,32,3,5,32]{5,4,3,2,1,0:T(8,128)(2,1)} copy(bf16[3,3,32,3,5,32]{5,2,0,4,3,1:T(8,128)(2,1)} %pad_maximum_fusion) | data formatting | bytes 552960 | tf_op jit(solution)/shard_map/stack;reshape | solution.py:443
  124.6 2.9 %reshape.13 = bf16[1,288,480]{2,1,0:T(8,128)(2,1)} reshape(bf16[3,3,32,3,5,32]{5,4,3,2,1,0:T(8,128)(2,1)} %copy.28) | data formatting | bytes 552960 | tf_op jit(solution)/shard_map/stack;reshape | solution.py:443
  132.2 2.9 %collective-permute-start.1 = (f32[2,2,32,128]{3,2,1,0:T(8,128)}, f32[2,2,32,128]{3,2,1,0:T(8,128)}, u32[]{:S(2)}, u32[]{:S(2)}) collective-permute-start(f32[2,2,32,128]{3,2,1,0:T(8,128)} %get-tuple-element.20.refs_6_), channel_id=1, source_target_pairs={{0,32},{16,48},{32,64},{48,80},{64,96},{80,112},{96,128},{112,144}... | collective-permute-start | bytes 196616 | tf_op jit(solution)/shard_map/ppermute | solution.py:399
  135.1 2.9 %collective-permute-start.2 = (f32[2,2,32,128]{3,2,1,0:T(8,128)}, f32[2,2,32,128]{3,2,1,0:T(8,128)}, u32[]{:S(2)}, u32[]{:S(2)}) collective-permute-start(f32[2,2,32,128]{3,2,1,0:T(8,128)} %get-tuple-element.20.refs_6_), channel_id=1, source_target_pairs={{0,16},{16,32},{32,48},{48,64},{64,80},{80,96},{96,112},{112,128},... | collective-permute-start | bytes 196616 | tf_op jit(solution)/shard_map/ppermute | solution.py:399
  138.0 2.0 collective-permute-start.3
  141.5 3.8 %collective-permute-start = (f32[1,2,32,128]{3,2,1,0:T(8,128)}, f32[1,2,32,128]{3,2,1,0:T(8,128)S(1)}, u32[]{:S(2)}, u32[]{:S(2)}) collective-permute-start(f32[1,2,32,128]{3,2,1,0:T(8,128)} %get-tuple-element.37), channel_id=1, source_target_pairs={{0,48},{16,64},{32,80},{48,96},{64,112},{80,128},{96,144},{112,160... | collective-permute-start | bytes 98312 | tf_op jit(solution)/shard_map/ppermute | solution.py:399
  150.4 2.5 %shard_map.126 = (f32[16,8,128]{2,1,0:T(8,128)S(1)}, f32[2,2,32,128]{3,2,1,0:T(8,128)S(1)}) custom-call(s32[2]{0:T(128)S(1)} %pad_add_fusion.at_ref.refs_0_, f32[16,8,128]{2,1,0:T(8,128)S(1)} %copy-done.12, f32[16,64,128]{2,1,0:T(8,128)} %all-to-all-done.4.blocks_ref, f32[16,64,128]{2,1,0:T(8,128)S(1)} %all-to-all-done.1.blocks_ref.rhs_ref, ...), custom_call_target="tpu_custom_call" | custom-call | tf_op jit(solution)/shard_map/pallas_call | solution.py:26
  154.1 9.8 %all-to-all-start.5 = ((f32[16,8,128]{2,1,0:T(8,128)}), f32[16,8,128]{2,1,0:T(8,128)S(1)}, u32[]{:S(2)}, u32[]{:S(2)}) async-start(f32[16,8,128]{2,1,0:T(8,128)} %copy-done.22), calls=%async_computation.5 | async-start | bytes 131072 | tf_op jit(solution)/shard_map/all_to_all | solution.py:391
  168.7 5.0 %all-to-all-done.5.tiles_ref = f32[16,8,128]{2,1,0:T(8,128)S(1)} async-done(((f32[16,8,128]{2,1,0:T(8,128)}), f32[16,8,128]{2,1,0:T(8,128)S(1)}, u32[]{:S(2)}, u32[]{:S(2)}) %all-to-all-start.5) | async-done | bytes 65568 | tf_op jit(solution)/shard_map/all_to_all | solution.py:391
  174.4 5.8 %all-to-all-start.6 = ((f32[16,8,128]{2,1,0:T(8,128)}), f32[16,8,128]{2,1,0:T(8,128)S(1)}, u32[]{:S(2)}, u32[]{:S(2)}) async-start(f32[16,8,128]{2,1,0:T(8,128)} %shard_map.127), calls=%async_computation.6 | async-start | bytes 131072 | tf_op jit(solution)/shard_map/all_to_all | solution.py:391
  181.5 4.0 %collective-permute-start.7 = (f32[2,2,32,128]{3,2,1,0:T(8,128)}, f32[2,2,32,128]{3,2,1,0:T(8,128)S(1)}, u32[]{:S(2)}, u32[]{:S(2)}) collective-permute-start(f32[2,2,32,128]{3,2,1,0:T(8,128)} %copy-done.20), channel_id=1, source_target_pairs={{0,32},{16,48},{32,64},{48,80},{64,96},{80,112},{96,128},{112,144}... | collective-permute-start | bytes 196616 | tf_op jit(solution)/shard_map/ppermute | solution.py:399
  185.5 5.0 %collective-permute-start.8 = (f32[2,2,32,128]{3,2,1,0:T(8,128)}, f32[2,2,32,128]{3,2,1,0:T(8,128)S(1)}, u32[]{:S(2)}, u32[]{:S(2)}) collective-permute-start(f32[2,2,32,128]{3,2,1,0:T(8,128)} %copy-done.20), channel_id=1, source_target_pairs={{0,16},{16,32},{32,48},{48,64},{64,80},{80,96},{96,112},{112,128},... | collective-permute-start | bytes 196616 | tf_op jit(solution)/shard_map/ppermute | solution.py:399
  190.5 1.9 collective-permute-start.9
  192.4 3.6 %collective-permute-start.6 = (f32[1,2,32,128]{3,2,1,0:T(8,128)S(1)}, f32[1,2,32,128]{3,2,1,0:T(8,128)S(1)}, u32[]{:S(2)}, u32[]{:S(2)}) collective-permute-start(f32[1,2,32,128]{3,2,1,0:T(8,128)S(1)} %get-tuple-element.35), channel_id=1, source_target_pairs={{0,48},{16,64},{32,80},{48,96},{64,112},{80,128},{96,144},{112,160... | collective-permute-start | bytes 98312 | tf_op jit(solution)/shard_map/ppermute | solution.py:399
  197.5 8.6 %copy.27 = bf16[16,32,3,3,2,24]{5,4,3,2,1,0:T(2,128)(2,1)} copy(bf16[16,32,3,3,2,24]{1,4,3,5,2,0:T(2,128)(2,1)} %bitcast_dynamic-update-slice_fusion) | data formatting | bytes 884736 | tf_op jit(solution)/shard_map/reshape | solution.py:377
  206.1 4.4 %reshape.12.refs_17_ = bf16[512,432]{1,0:T(8,128)(2,1)S(1)} reshape(bf16[16,32,3,3,2,24]{5,4,3,2,1,0:T(2,128)(2,1)} %copy.27) | data formatting | bytes 884736 | tf_op jit(solution)/shard_map/reshape | solution.py:377
  211.1 16.5 %shard_map.128 = (f32[2,2,16,128]{3,2,1,0:T(8,128)}, f32[2,2,16,128]{3,2,1,0:T(8,128)}) custom-call(s32[2]{0:T(128)S(1)} %pad_add_fusion.at_ref.refs_0_, f32[16,8,128]{2,1,0:T(8,128)S(1)} %copy-done.13, f32[16,8,128]{2,1,0:T(8,128)S(1)} %all-to-all-done.6.refs_2_, f32[1,2,32,128]{3,2,1,0:T(8,128)S(1)} %collective-permute-done.refs_3_, ...), custom_call_target="tpu_custom_call" | custom-call | tf_op jit(solution)/shard_map/pallas_call | solution.py:26
  (113 shorter events, 46.9 us)
Async XLA Ops:
  0.6 1.4 copy-start.1
  2.0 1.0 copy-start.2
  6.1 13.9 %copy-start.25 = (bf16[2,32,3,3,3]{1,0,4,3,2:T(2,128)(2,1)S(1)}, bf16[2,32,3,3,3]{1,0,4,3,2:T(2,128)(2,1)}, u32[]{:S(2)}) copy-start(bf16[2,32,3,3,3]{1,0,4,3,2:T(2,128)(2,1)} %param.17) | copy-start | bytes 10372
  6.1 14.0 %copy-start.24 = (bf16[32,2,3,3,3]{0,1,4,3,2:T(2,128)(2,1)S(1)}, bf16[32,2,3,3,3]{0,1,4,3,2:T(2,128)(2,1)}, u32[]{:S(2)}) copy-start(bf16[32,2,3,3,3]{0,1,4,3,2:T(2,128)(2,1)} %param.15) | copy-start | bytes 10372
  6.1 30.9 %copy-start.23 = (f32[2,2,16,128]{3,2,1,0:T(8,128)S(1)}, f32[2,2,16,128]{3,2,1,0:T(8,128)}, u32[]{:S(2)}) copy-start(f32[2,2,16,128]{3,2,1,0:T(8,128)} %prior_ref.1) | copy-start | bytes 98308
  8.1 28.9 %all-to-all-start = ((f32[16,64,128]{2,1,0:T(8,128)}), f32[16,64,128]{2,1,0:T(8,128)S(1)}, u32[]{:S(2)}, u32[]{:S(2)}) async-start(f32[16,64,128]{2,1,0:T(8,128)} %shard_map.122), calls=%async_computation | async-start | bytes 1048576 | tf_op jit(solution)/shard_map/all_to_all | solution.py:391
  19.9 40.0 %copy-start = (bf16[512,1536]{1,0:T(8,128)(2,1)S(1)}, bf16[512,1536]{1,0:T(8,128)(2,1)}, u32[]{:S(2)}) copy-start(bf16[512,1536]{1,0:T(8,128)(2,1)} %constant.20.clone.rows_f) | copy-start | bytes 4718596
  19.9 40.0 %copy-start.3 = (f32[1,2,2,256,128]{4,3,2,1,0:T(8,128)S(1)}, f32[1,2,2,256,128]{4,3,2,1,0:T(8,128)}, u32[]{:S(2)}) copy-start(f32[1,2,2,256,128]{4,3,2,1,0:T(8,128)} %param.11) | copy-start | bytes 1572868
  19.9 40.0 %copy-start.5 = (s32[2,256,128]{2,1,0:T(8,128)S(1)}, s32[2,256,128]{2,1,0:T(8,128)}, u32[]{:S(2)}) copy-start(s32[2,256,128]{2,1,0:T(8,128)} %mask_ref.5) | copy-start | bytes 786436
  19.9 40.0 %copy-start.7 = (bf16[768,256]{1,0:T(8,128)(2,1)S(1)}, bf16[768,256]{1,0:T(8,128)(2,1)}, u32[]{:S(2)}) copy-start(bf16[768,256]{1,0:T(8,128)(2,1)} %constant.21.clone.columns_f) | copy-start | bytes 1179652
  37.9 22.0 %all-to-all-start.1 = ((f32[16,64,128]{2,1,0:T(8,128)}), f32[16,64,128]{2,1,0:T(8,128)S(1)}, u32[]{:S(2)}, u32[]{:S(2)}) async-start(f32[16,64,128]{2,1,0:T(8,128)} %copy-done.18), calls=%async_computation.1 | async-start | bytes 1048576 | tf_op jit(solution)/shard_map/all_to_all | solution.py:391
  67.3 23.0 %all-to-all-start.2 = ((f32[16,72,128]{2,1,0:T(8,128)}), f32[16,72,128]{2,1,0:T(8,128)S(1)}, u32[]{:S(2)}, u32[]{:S(2)}) async-start(f32[16,72,128]{2,1,0:T(8,128)} %copy-done.14), calls=%async_computation.2 | async-start | bytes 1179648 | tf_op jit(solution)/shard_map/all_to_all | solution.py:391
  91.8 13.0 %all-to-all-start.3 = ((f32[16,8,128]{2,1,0:T(8,128)}), f32[16,8,128]{2,1,0:T(8,128)S(1)}, u32[]{:S(2)}, u32[]{:S(2)}) async-start(f32[16,8,128]{2,1,0:T(8,128)} %get-tuple-element.16), calls=%async_computation.3 | async-start | bytes 131072 | tf_op jit(solution)/shard_map/all_to_all | solution.py:391
  104.7 8.0 %copy-start.11 = (f32[16,8,128]{2,1,0:T(8,128)}, f32[16,8,128]{2,1,0:T(8,128)S(1)}, u32[]{:S(2)}) copy-start(f32[16,8,128]{2,1,0:T(8,128)S(1)} %all-to-all-done.3.sums_ref.refs_1_) | copy-start | bytes 196612
  104.7 41.8 %all-to-all-start.4 = ((f32[16,64,128]{2,1,0:T(8,128)}), f32[16,64,128]{2,1,0:T(8,128)}, u32[]{:S(2)}, u32[]{:S(2)}) async-start(f32[16,64,128]{2,1,0:T(8,128)} %copy-done.17), calls=%async_computation.4 | async-start | bytes 1048576 | tf_op jit(solution)/shard_map/all_to_all | solution.py:391
  132.2 47.9 %collective-permute-start.1 = (f32[2,2,32,128]{3,2,1,0:T(8,128)}, f32[2,2,32,128]{3,2,1,0:T(8,128)}, u32[]{:S(2)}, u32[]{:S(2)}) collective-permute-start(f32[2,2,32,128]{3,2,1,0:T(8,128)} %get-tuple-element.20.refs_6_), channel_id=1, source_target_pairs={{0,32},{16,48},{32,64},{48,80},{64,96},{80,112},{96,128},{112,144}... | collective-permute-start | bytes 196616 | tf_op jit(solution)/shard_map/ppermute | solution.py:399
  135.1 46.3 %collective-permute-start.2 = (f32[2,2,32,128]{3,2,1,0:T(8,128)}, f32[2,2,32,128]{3,2,1,0:T(8,128)}, u32[]{:S(2)}, u32[]{:S(2)}) collective-permute-start(f32[2,2,32,128]{3,2,1,0:T(8,128)} %get-tuple-element.20.refs_6_), channel_id=1, source_target_pairs={{0,16},{16,32},{32,48},{48,64},{64,80},{80,96},{96,112},{112,128},... | collective-permute-start | bytes 196616 | tf_op jit(solution)/shard_map/ppermute | solution.py:399
  138.0 47.5 %collective-permute-start.3 = (f32[2,2,32,128]{3,2,1,0:T(8,128)}, f32[2,2,32,128]{3,2,1,0:T(8,128)}, u32[]{:S(2)}, u32[]{:S(2)}) collective-permute-start(f32[2,2,32,128]{3,2,1,0:T(8,128)} %get-tuple-element.20.refs_6_), channel_id=1, source_target_pairs={{16,0},{32,16},{48,32},{64,48},{80,64},{96,80},{112,96},{128,112},... | collective-permute-start | bytes 196616 | tf_op jit(solution)/shard_map/ppermute | solution.py:399
  141.5 23.3 %collective-permute-start = (f32[1,2,32,128]{3,2,1,0:T(8,128)}, f32[1,2,32,128]{3,2,1,0:T(8,128)S(1)}, u32[]{:S(2)}, u32[]{:S(2)}) collective-permute-start(f32[1,2,32,128]{3,2,1,0:T(8,128)} %get-tuple-element.37), channel_id=1, source_target_pairs={{0,48},{16,64},{32,80},{48,96},{64,112},{80,128},{96,144},{112,160... | collective-permute-start | bytes 98312 | tf_op jit(solution)/shard_map/ppermute | solution.py:399
  145.3 20.8 %collective-permute-start.5 = (f32[1,2,32,128]{3,2,1,0:T(8,128)}, f32[1,2,32,128]{3,2,1,0:T(8,128)}, u32[]{:S(2)}, u32[]{:S(2)}) collective-permute-start(f32[1,2,32,128]{3,2,1,0:T(8,128)} %get-tuple-element.36), channel_id=1, source_target_pairs={{48,0},{64,16},{80,32},{96,48},{112,64},{128,80},{144,96},{160,112... | collective-permute-start | bytes 98312 | tf_op jit(solution)/shard_map/ppermute | solution.py:399
  154.1 19.6 %all-to-all-start.5 = ((f32[16,8,128]{2,1,0:T(8,128)}), f32[16,8,128]{2,1,0:T(8,128)S(1)}, u32[]{:S(2)}, u32[]{:S(2)}) async-start(f32[16,8,128]{2,1,0:T(8,128)} %copy-done.22), calls=%async_computation.5 | async-start | bytes 131072 | tf_op jit(solution)/shard_map/all_to_all | solution.py:391
  164.7 25.8 %collective-permute-start.4 = (f32[2,2,32,128]{3,2,1,0:T(8,128)}, f32[2,2,32,128]{3,2,1,0:T(8,128)S(1)}, u32[]{:S(2)}, u32[]{:S(2)}) collective-permute-start(f32[2,2,32,128]{3,2,1,0:T(8,128)} %get-tuple-element.20.refs_6_), channel_id=1, source_target_pairs={{32,0},{48,16},{64,32},{80,48},{96,64},{112,80},{128,96},{144,112}... | collective-permute-start | bytes 196616 | tf_op jit(solution)/shard_map/ppermute | solution.py:399
  166.0 26.4 %collective-permute-start.11 = (f32[1,2,32,128]{3,2,1,0:T(8,128)S(1)}, f32[1,2,32,128]{3,2,1,0:T(8,128)S(1)}, u32[]{:S(2)}, u32[]{:S(2)}) collective-permute-start(f32[1,2,32,128]{3,2,1,0:T(8,128)S(1)} %get-tuple-element.34), channel_id=1, source_target_pairs={{48,0},{64,16},{80,32},{96,48},{112,64},{128,80},{144,96},{160,112... | collective-permute-start | bytes 98312 | tf_op jit(solution)/shard_map/ppermute | solution.py:399
  174.4 36.7 %all-to-all-start.6 = ((f32[16,8,128]{2,1,0:T(8,128)}), f32[16,8,128]{2,1,0:T(8,128)S(1)}, u32[]{:S(2)}, u32[]{:S(2)}) async-start(f32[16,8,128]{2,1,0:T(8,128)} %shard_map.127), calls=%async_computation.6 | async-start | bytes 131072 | tf_op jit(solution)/shard_map/all_to_all | solution.py:391
  180.2 30.8 %collective-permute-start.10 = (f32[2,2,32,128]{3,2,1,0:T(8,128)}, f32[2,2,32,128]{3,2,1,0:T(8,128)S(1)}, u32[]{:S(2)}, u32[]{:S(2)}) collective-permute-start(f32[2,2,32,128]{3,2,1,0:T(8,128)} %copy-done.20), channel_id=1, source_target_pairs={{32,0},{48,16},{64,32},{80,48},{96,64},{112,80},{128,96},{144,112}... | collective-permute-start | bytes 196616 | tf_op jit(solution)/shard_map/ppermute | solution.py:399
  181.5 29.5 %collective-permute-start.7 = (f32[2,2,32,128]{3,2,1,0:T(8,128)}, f32[2,2,32,128]{3,2,1,0:T(8,128)S(1)}, u32[]{:S(2)}, u32[]{:S(2)}) collective-permute-start(f32[2,2,32,128]{3,2,1,0:T(8,128)} %copy-done.20), channel_id=1, source_target_pairs={{0,32},{16,48},{32,64},{48,80},{64,96},{80,112},{96,128},{112,144}... | collective-permute-start | bytes 196616 | tf_op jit(solution)/shard_map/ppermute | solution.py:399
  185.5 25.5 %collective-permute-start.8 = (f32[2,2,32,128]{3,2,1,0:T(8,128)}, f32[2,2,32,128]{3,2,1,0:T(8,128)S(1)}, u32[]{:S(2)}, u32[]{:S(2)}) collective-permute-start(f32[2,2,32,128]{3,2,1,0:T(8,128)} %copy-done.20), channel_id=1, source_target_pairs={{0,16},{16,32},{32,48},{48,64},{64,80},{80,96},{96,112},{112,128},... | collective-permute-start | bytes 196616 | tf_op jit(solution)/shard_map/ppermute | solution.py:399
  190.5 20.5 %collective-permute-start.9 = (f32[2,2,32,128]{3,2,1,0:T(8,128)}, f32[2,2,32,128]{3,2,1,0:T(8,128)S(1)}, u32[]{:S(2)}, u32[]{:S(2)}) collective-permute-start(f32[2,2,32,128]{3,2,1,0:T(8,128)} %copy-done.20), channel_id=1, source_target_pairs={{16,0},{32,16},{48,32},{64,48},{80,64},{96,80},{112,96},{128,112},... | collective-permute-start | bytes 196616 | tf_op jit(solution)/shard_map/ppermute | solution.py:399
  192.4 18.6 %collective-permute-start.6 = (f32[1,2,32,128]{3,2,1,0:T(8,128)S(1)}, f32[1,2,32,128]{3,2,1,0:T(8,128)S(1)}, u32[]{:S(2)}, u32[]{:S(2)}) collective-permute-start(f32[1,2,32,128]{3,2,1,0:T(8,128)S(1)} %get-tuple-element.35), channel_id=1, source_target_pairs={{0,48},{16,64},{32,80},{48,96},{64,112},{80,128},{96,144},{112,160... | collective-permute-start | bytes 98312 | tf_op jit(solution)/shard_map/ppermute | solution.py:399
  206.1 4.5 %copy-start.27 = (bf16[3,8,2,3,10,32]{5,2,0,4,3,1:T(2,128)(2,1)S(1)}, bf16[3,8,2,3,10,32]{5,2,0,4,3,1:T(2,128)(2,1)}, u32[]{:S(2)}) copy-start(bf16[3,8,2,3,10,32]{5,2,0,4,3,1:T(2,128)(2,1)} %constant_dynamic-update-slice_fusion) | copy-start | bytes 276484
  206.1 5.0 %copy-start.13 = (f32[16,8,128]{2,1,0:T(8,128)S(1)}, f32[16,8,128]{2,1,0:T(8,128)}, u32[]{:S(2)}) copy-start(f32[16,8,128]{2,1,0:T(8,128)} %copy-done.11) | copy-start | bytes 196612
  206.1 5.0 %copy-start.21 = (f32[2,2,32,128]{3,2,1,0:T(8,128)S(1)}, f32[2,2,32,128]{3,2,1,0:T(8,128)}, u32[]{:S(2)}) copy-start(f32[2,2,32,128]{3,2,1,0:T(8,128)} %copy-done.20) | copy-start | bytes 196612
  (15 other events, 13.1 us)

commit v2 on v1

--- a/solution.py
+++ b/solution.py
@@ -43,23 +43,22 @@
     return high, low
 
 
-def dft_pair(length, sign):
+def dft_pair(length):
     positions = np.arange(length)
     angles = 2.0 * math.pi / length * (positions[:, None] * positions[None, :] % length)
     scaling = 1.0 / math.sqrt(length)
-    return np.cos(angles) * scaling, sign * scaling * np.sin(angles)
-
-
-def left_table(length, sign):
-    cosine, sine = dft_pair(length, sign)
-    high, low = halves(np.block([[cosine, -sine], [sine, cosine]]))
-    return np.concatenate([high, high, low], axis=1)
-
-
-def right_table(length, sign):
-    cosine, sine = dft_pair(length, sign)
-    high, low = halves(np.block([[cosine, sine], [-sine, cosine]]))
-    return np.concatenate([high, high, low], axis=0)
+    return np.cos(angles) * scaling, scaling * np.sin(angles)
+
+
+def left_table(length):
+    cosine, sine = dft_pair(length)
+    parts = [np.concatenate(halves(part), axis=1) for part in (cosine, sine)]
+    return np.concatenate(parts, axis=0)
+
+
+def right_table(length):
+    cosine, sine = dft_pair(length)
+    return np.concatenate(halves(cosine) + halves(sine), axis=1)
 
 
 def split(values):
@@ -68,28 +67,41 @@
     return high, low
 
 
-def dft_rows(values, table_ref):
+def dft_rows(field, table_ref, sign):
+    values = jnp.concatenate(field[0] + field[1], axis=1)
     high, low = split(values)
-    return jnp.dot(table_ref[...], jnp.concatenate([high, low, high], axis=0), preferred_element_type=F32)
-
-
-def dft_columns(values, table_ref):
+    size = values.shape[0]
+    table_high, table_low = table_ref[:, :size], table_ref[:, size:]
+    table = jnp.concatenate([table_high, table_high, table_low], axis=1)
+    products = jnp.dot(table, jnp.concatenate([high, low, high], axis=0), preferred_element_type=F32)
+    half = values.shape[1] // 2
+    cosine, sine = products[:size], products[size:]
+    real = cosine[:, :half] - sign * sine[:, half:]
+    imag = cosine[:, half:] + sign * sine[:, :half]
+    columns = half // 2
+    return [[part[:, p * columns : (p + 1) * columns] for p in range(2)] for part in (real, imag)]
+
+
+def dft_columns(field, table_ref, sign):
+    values = by_columns(field)
     high, low = split(values)
-    return jnp.dot(jnp.concatenate([high, low, high], axis=1), table_ref[...], preferred_element_type=F32)
-
-
-def by_rows(field):
-    return jnp.concatenate([jnp.concatenate(field[0], axis=1), jnp.concatenate(field[1], axis=1)], axis=0)
+    size = table_ref.shape[0]
+    cosine_high, cosine_low, sine_high, sine_low = [table_ref[:, i * size : (i + 1) * size] for i in range(4)]
+
+    def block(cosine, sine):
+        plus, minus = (sine, -sine) if sign > 0 else (-sine, sine)
+        return jnp.concatenate(
+            [jnp.concatenate([cosine, plus], axis=1), jnp.concatenate([minus, cosine], axis=1)], axis=0
+        )
+
+    table_high = block(cosine_high, sine_high)
+    table = jnp.concatenate([table_high, table_high, block(cosine_low, sine_low)], axis=0)
+    return from_columns(jnp.dot(jnp.concatenate([high, low, high], axis=1), table, preferred_element_type=F32))
 
 
 def by_columns(field):
     planes = range(len(field[0]))
     return jnp.concatenate([jnp.concatenate([field[0][p], field[1][p]], axis=1) for p in planes], axis=0)
-
-
-def from_rows(values):
-    rows, columns = values.shape[0] // 2, values.shape[1] // 2
-    return [[values[a * rows : (a + 1) * rows, p * columns : (p + 1) * columns] for p in range(2)] for a in range(2)]
 
 
 def from_columns(values):
@@ -129,27 +141,24 @@
     return [real, imag]
 
 
-def mask_rows(mask_ref):
-    mask = jnp.concatenate([mask_ref[0].astype(F32), mask_ref[1].astype(F32)], axis=1)
-    return jnp.concatenate([mask, mask], axis=0)
+def masked(field, mask_ref):
+    masks = [mask_ref[p].astype(F32) for p in range(2)]
+    return [[field[a][p] * masks[p] for p in range(2)] for a in range(2)]
+
+
+def inner(first, second):
+    return sum(row_sum(first[a][p] * second[a][p]) for a in range(2) for p in range(2))
 
 
 def row_sum(values):
     folded = jnp.sum(values.reshape(-1, 8, values.shape[-1]), axis=0)
     folded = jnp.sum(folded, axis=0, keepdims=True)
-    while folded.shape[1] > 128:
-        half = folded.shape[1] // 2
-        folded = folded[:, :half] + folded[:, half:]
     return folded
 
 
 def tile_of(rows):
     blank = jnp.zeros((1, 128), F32)
     return jnp.concatenate(list(rows) + [blank] * (8 - len(rows)), axis=0)
-
-
-def scalar_of(tile, row):
-    return jnp.sum(tile[row : row + 1, :])
 
 
 def store_near(near_ref, blocks_ref, at):
@@ -164,10 +173,9 @@
             near_ref[p, a, 24:32, :] = jnp.where(at < count - 1, after, 0.0)
 
 
-def adjoint_kernel(kspace_ref, mask_ref, maps_ref, rows_ref, columns_ref, out_ref):
-    field = [[kspace_ref[a, p] for p in range(2)] for a in range(2)]
-    field = from_rows(dft_rows(by_rows(field) * mask_rows(mask_ref), rows_ref))
-    field = from_columns(dft_columns(by_columns(field), columns_ref))
+def adjoint_kernel(kspace_ref, mask_ref, rows_ref, columns_ref, maps_ref, out_ref):
+    field = masked([[kspace_ref[a, p] for p in range(2)] for a in range(2)], mask_ref)
+    field = dft_columns(dft_rows(field, rows_ref, 1.0), columns_ref, 1.0)
     store_image(out_ref, coil_term(maps_ref, field))
 
 
@@ -182,58 +190,56 @@
 
 
 def normal_kernel(
-    at_ref, blocks_ref, mask_ref, maps_ref, rows_f, columns_f, rows_b, columns_b, out_ref, spectrum_ref, tile_ref, near_ref
+    at_ref, blocks_ref, mask_ref, maps_ref, rows_ref, columns_ref, out_ref, spectrum_ref, tile_ref, near_ref
 ):
     store_near(near_ref, blocks_ref, at_ref[0])
     image = load_image(blocks_ref)
-    norm = sum(row_sum(image[a][p] * image[a][p]) for a in range(2) for p in range(2))
-    field = from_columns(dft_columns(by_columns(coil_field(maps_ref, image)), columns_f))
-    spectrum = dft_rows(by_rows(field), rows_f) * mask_rows(mask_ref)
-    spectrum_ref[...] = spectrum
-    energy = row_sum(spectrum * spectrum)
-    field = from_rows(dft_rows(spectrum, rows_b))
-    field = from_columns(dft_columns(by_columns(field), columns_b))
+    field = dft_columns(coil_field(maps_ref, image), columns_ref, -1.0)
+    spectrum = masked(dft_rows(field, rows_ref, -1.0), mask_ref)
+    for a in range(2):
+        for p in range(2):
+            spectrum_ref[a, p] = spectrum[a][p]
+    field = dft_columns(dft_rows(spectrum, rows_ref, 1.0), columns_ref, 1.0)
     store_image(out_ref, coil_term(maps_ref, field))
-    tile_ref[...] = tile_of([norm])
-    energies = tile_of([energy])
+    tile_ref[...] = tile_of([inner(image, image)])
+    energies = tile_of([inner(spectrum, spectrum)])
     for k in range(blocks_ref.shape[0]):
         out_ref[k, 64:72, :] = energies
 
 
 def image_kernel(blocks_ref, rhs_rows_ref, norms_ref, copies_ref, sums_ref):
-    count = blocks_ref.shape[0]
     total = jnp.sum(blocks_ref[...], axis=0)
     rows = total[:64] + LAMBDA * rhs_rows_ref[...]
-    sums = tile_of([norms_ref[0:1, :], total[64:65]])
-    for k in range(count):
+    for k in range(blocks_ref.shape[0]):
         copies_ref[k] = rows
-        sums_ref[k] = sums
-
-
-def first_step(sums_ref):
-    tile = jnp.sum(sums_ref[...], axis=0)
-    norm, energy = scalar_of(tile, 0), scalar_of(tile, 1)
-    return norm, energy, norm / (energy + LAMBDA * norm)
+    sums_ref[...] = tile_of([norms_ref[0:1, :], total[64:65]])
+
+
+def lane_sum(values):
+    return jnp.sum(values, axis=-1, keepdims=True)
+
+
+def slab_step(norm, energy):
+    curved = energy + LAMBDA * norm
+    return jnp.where(curved > 0.0, norm / jnp.where(curved > 0.0, curved, 1.0), 1.0)
 
 
 def last_kernel(
-    at_ref, sums_ref, blocks_ref, rhs_ref, spectrum_ref, mask_ref, maps_ref, rows_f, columns_f, out_ref, near_ref
+    at_ref, sums_ref, blocks_ref, rhs_ref, spectrum_ref, mask_ref, maps_ref, rows_ref, columns_ref, out_ref, near_ref
 ):
     store_near(near_ref, blocks_ref, at_ref[0])
-    step = first_step(sums_ref)[2]
+    norm, energy = sums_ref[0:1, :], sums_ref[1:2, :]
+    step = slab_step(lane_sum(norm), lane_sum(energy))
     image = load_image(blocks_ref)
     rhs = load_image(rhs_ref)
-    norm = jnp.zeros((1, 128), F32)
-    cross = jnp.zeros((1, 128), F32)
-    for a in range(2):
-        for p in range(2):
-            residual = rhs[a][p] - step * image[a][p]
-            norm = norm + row_sum(residual * residual)
-            cross = cross + row_sum(residual * rhs[a][p])
-    field = from_columns(dft_columns(by_columns(coil_field(maps_ref, image)), columns_f))
-    spectrum = dft_rows(by_rows(field), rows_f) * mask_rows(mask_ref)
-    spectrum = spectrum_ref[...] - step * spectrum
-    tile = tile_of([row_sum(spectrum * spectrum), row_sum(spectrum * spectrum_ref[...]), norm, cross])
+    field = dft_columns(coil_field(maps_ref, image), columns_ref, -1.0)
+    spectrum = masked(dft_rows(field, rows_ref, -1.0), mask_ref)
+    before = [[spectrum_ref[a, p] for p in range(2)] for a in range(2)]
+    residual = [[rhs[a][p] - step * image[a][p] for p in range(2)] for a in range(2)]
+    spectrum = [[before[a][p] - step * spectrum[a][p] for p in range(2)] for a in range(2)]
+    share = 1.0 / out_ref.shape[0]
+    local = [inner(residual, residual), inner(residual, rhs), norm, energy]
+    tile = tile_of([inner(spectrum, spectrum), inner(spectrum, before)] + [share * value for value in local])
     for k in range(out_ref.shape[0]):
         out_ref[k] = tile
 
@@ -242,6 +248,28 @@
     total = jnp.sum(tiles_ref[...], axis=0)
     for k in range(out_ref.shape[0]):
         out_ref[k] = total
+
+
+def final_scales(tiles_ref):
+    curve, curve_cross, norm, cross, norm_first, energy_first = [
+        lane_sum(tiles_ref[:, i, :]) for i in range(6)
+    ]
+
+    def over_slabs(values):
+        return jnp.sum(values, axis=0, keepdims=True)
+
+    all_norm, all_energy = over_slabs(norm_first), over_slabs(energy_first)
+    step_first = all_norm / (all_energy + LAMBDA * all_norm)
+    here = step_first / slab_step(norm_first, energy_first)
+    rest = 1.0 - here
+    curve = over_slabs(here * here * curve + rest * (2.0 * here * curve_cross + rest * energy_first))
+    curve_cross = over_slabs(here * curve_cross + rest * energy_first)
+    norm = over_slabs(here * here * norm + rest * (2.0 * here * cross + rest * norm_first))
+    cross = over_slabs(here * cross + rest * norm_first)
+    ratio = norm / all_norm
+    curvature = curve + ratio * (2.0 * curve_cross + ratio * all_energy)
+    curvature = curvature + LAMBDA * (norm + ratio * (2.0 * cross + ratio * all_norm))
+    return step_first, norm / curvature, ratio
 
 
 def starts_of(rows):
@@ -264,23 +292,16 @@
 
 
 def denoise_kernel(coil_count, slab_count, *refs):
-    at_ref, sums_ref, last_ref = refs[:3]
-    rhs_refs = refs[3:10]
-    image_refs = refs[10:17]
-    w_first_ref, w_middle_ref, w_last_ref, solution_ref, refined_ref = refs[17:22]
-    features_ref = refs[22]
-    hidden_refs = refs[23:]
+    at_ref, last_ref = refs[:2]
+    rhs_refs = refs[2:9]
+    image_refs = refs[9:16]
+    w_first_ref, w_middle_ref, w_last_ref, solution_ref, refined_ref = refs[16:21]
+    features_ref = refs[21]
+    hidden_refs = refs[22:]
     coil_at = at_ref[0]
     slab_at = at_ref[1]
 
-    norm_first, energy_first, step_first = first_step(sums_ref)
-    tile = jnp.sum(last_ref[...], axis=0)
-    copies = 1.0 / coil_count
-    norm, cross = scalar_of(tile, 2) * copies, scalar_of(tile, 3) * copies
-    ratio = norm / norm_first
-    curvature = scalar_of(tile, 0) + ratio * (2.0 * scalar_of(tile, 1) + ratio * energy_first)
-    curvature = curvature + LAMBDA * (norm + ratio * (2.0 * cross + ratio * norm_first))
-    step_last = norm / curvature
+    step_first, step_last, ratio = final_scales(last_ref)
     scale_rhs = step_first + step_last * ratio
 
     lane = lax.broadcasted_iota(jnp.int32, (48, 128), 1)
@@ -328,7 +349,7 @@
 
     def first_plane(p, carry):
         taps = jnp.concatenate([features_ref[p + u] for u in range(3)], axis=0)
-        values = jnp.dot(w_first_ref[...], taps, preferred_element_type=F32)
+        values = jnp.dot(w_first_ref[:, :432], taps, preferred_element_type=F32)
         first_out[p] = jnp.maximum(values, 0.0).astype(BF16)
         return carry
 
@@ -343,7 +364,7 @@
             for start in starts:
                 rows = slice(start * 32, (start + GROUP + 2) * 32)
                 taps = jnp.concatenate([in_ref[p + u, rows] for u in range(3)], axis=0)
-                sums = jnp.dot(w_middle_ref[m], taps, preferred_element_type=F32)
+                sums = jnp.dot(w_middle_ref[m, :, : (GROUP + 2) * 96], taps, preferred_element_type=F32)
                 cells = GROUP * 32
                 values = shifted_sum([sums[t * cells : (t + 1) * cells] for t in range(3)])
                 out_ref[p, start * 32 : (start + GROUP) * 32] = jnp.maximum(values, 0.0).astype(BF16)
@@ -355,36 +376,61 @@
     in_ref = hidden_refs[-1]
     for p in range(2):
         taps = jnp.concatenate([in_ref[p + u] for u in range(3)], axis=0)
-        sums = jnp.dot(w_last_ref[...], taps, preferred_element_type=F32)
-        values = shifted_sum([sums[t * 16 : (t + 1) * 16] for t in range(3)])
-        for a in range(2):
-            for h in range(2):
-                piece = values[8 * a : 8 * a + 8, 128 * h : 128 * h + 128]
+        sums = jnp.dot(w_last_ref[:, :960], taps, preferred_element_type=F32)
+        lane = lax.broadcasted_iota(jnp.int32, (64, 128), 1)
+        for h in range(2):
+            part = sums[:, 128 * h : 128 * (h + 1)]
+            low = jnp.where(lane > 0, pltpu.roll(part, 1, 1), 0.0)
+            high = jnp.where(lane < 127, pltpu.roll(part, 127, 1), 0.0)
+            for a in range(2):
+                rows = []
+                for r in range(8):
+                    at = 8 * r + a
+                    rows.append(low[at : at + 1] + part[at + 2 : at + 3] + high[at + 4 : at + 5])
+                piece = jnp.concatenate(rows, axis=0)
                 refined_ref[a, p, 8 * h : 8 * h + 8] = solution_ref[a, p, 8 * h : 8 * h + 8] + piece
 
 
-def banded(weight, rows):
-    taps = jnp.transpose(weight, (4, 0, 2, 3, 1))
-    bands = [jnp.pad(taps, ((0, 0), (0, 0), (0, 0), (r, rows - 1 - r), (0, 0))) for r in range(rows)]
-    return jnp.stack(bands, axis=1)
-
-
-def first_table(weight):
-    taps = jnp.transpose(weight, (0, 2, 4, 1, 3))
-    bands = [
-        jnp.pad(taps, ((0, 0), (0, 0), (0, 0), (0, 0), (r + SIDE - HALO, 24 - 3 - r - SIDE + HALO))) for r in range(16)
-    ]
-    return jnp.stack(bands, axis=0).reshape(16 * weight.shape[0], 3 * 3 * 2 * 24)
-
-
-def middle_table(weight):
-    bands = banded(weight, GROUP)
-    return bands.reshape(3 * GROUP * 32, 3 * (GROUP + 2) * 32)
-
-
-def last_table(weight):
-    bands = jnp.transpose(banded(weight, 8), (0, 2, 1, 3, 4, 5))
-    return bands.reshape(3 * 2 * 8, 3 * 10 * 32)
+def tables_kernel(first_ref, middle_ref, last_ref, w_first_ref, w_middle_ref, w_last_ref):
+    def spots(size, target, count=512):
+        column = lax.broadcasted_iota(jnp.int32, (size, count), 1)
+        return jnp.where(column == target(lax.broadcasted_iota(jnp.int32, (size, count), 0)), 1.0, 0.0).astype(BF16)
+
+    def first_target(source):
+        channel, u, v, t = source // 27, source // 9 % 3, source // 3 % 3, source % 3
+        return ((u * 3 + t) * 2 + channel) * 24 + SIDE - HALO + v
+
+    base = jnp.dot(first_ref[...], spots(54, first_target), preferred_element_type=F32)
+    for r in range(16):
+        w_first_ref[32 * r : 32 * r + 32] = (pltpu.roll(base, r, 1) if r else base).astype(BF16)
+    for m in range(middle_ref.shape[0]):
+        base = jnp.zeros((96, 512), F32)
+        for u in range(3):
+            for v in range(3):
+                place = spots(32, lambda source: source + (u * (GROUP + 2) + v) * 32)
+                taps = jnp.concatenate([middle_ref[m, u, v, t] for t in range(3)], axis=0)
+                base = base + jnp.dot(taps, place, preferred_element_type=F32)
+        for r in range(GROUP):
+            band = (pltpu.roll(base, 32 * r, 1) if r else base).astype(BF16)
+            for t in range(3):
+                start = (t * GROUP + r) * 32
+                w_middle_ref[m, start : start + 32] = band[32 * t : 32 * t + 32]
+    bands = []
+    for r in range(8):
+        bands.append(pltpu.roll(last_ref[...], 32 * r, 1) if r else last_ref[...])
+    w_last_ref[...] = jnp.concatenate(bands, axis=0).astype(BF16)
+
+
+def tables(w_first, w_middle, w_last):
+    first = w_first.reshape(w_first.shape[0], 54)
+    middle = jnp.transpose(w_middle, (0, 3, 4, 5, 1, 2))
+    last = jnp.pad(jnp.transpose(w_last, (4, 0, 2, 3, 1)), ((0, 0), (0, 0), (0, 0), (0, 7), (0, 0)))
+    last = jnp.pad(last.reshape(6, 960), ((0, 2), (0, 64))).astype(F32)
+    return call(
+        tables_kernel,
+        (struct((512, 512), BF16), struct((3, 96 * GROUP, 512), BF16), struct((64, 1024), BF16)),
+        (first, middle, last),
+    )
 
 
 def swap(blocks, axis):
@@ -408,10 +454,10 @@
     len_y, len_z = maps.shape[2:]
     coils, slabs = lax.axis_size("coil"), lax.axis_size("slab")
     at = jnp.stack([lax.axis_index("coil"), lax.axis_index("slab")]).astype(jnp.int32)
-    rows_f, rows_b = left_table(len_y, -1.0), left_table(len_y, 1.0)
-    columns_f, columns_b = right_table(len_z, -1.0), right_table(len_z, 1.0)
-
-    term = call(adjoint_kernel, struct((coils, 64, 128)), (kspace[0], sampling, maps, rows_b, columns_b))
+    rows, columns = left_table(len_y), right_table(len_z)
+    weights = tables(w_first, w_middle, w_last)
+
+    term = call(adjoint_kernel, struct((coils, 64, 128)), (kspace[0], sampling, rows, columns, maps))
     rhs_rows, copies = call(
         rows_kernel, (struct((64, 128)), struct((coils, 64, 128))), (swap(term, "coil"), prior_image)
     )
@@ -419,34 +465,32 @@
     near_shape = struct((2, 2, 32, 128))
     term, spectrum, norms, rhs_near = call(
         normal_kernel,
-        (struct((coils, 72, 128)), struct((2 * len_y, 2 * len_z)), struct((8, 128)), near_shape),
-        (at, rhs, sampling, maps, rows_f, columns_f, rows_b, columns_b),
+        (struct((coils, 72, 128)), struct((2, 2, len_y, len_z)), struct((8, 128)), near_shape),
+        (at, rhs, sampling, maps, rows, columns),
         in_smem=(0,),
     )
     rhs_parts = near_planes(rhs_near)
     copies, sums = call(
         image_kernel,
-        (struct((coils, 64, 128)), struct((slabs, 8, 128))),
+        (struct((coils, 64, 128)), struct((8, 128))),
         (swap(term, "coil"), rhs_rows, norms),
     )
     image = swap(copies, "coil")
-    sums = swap(sums, "slab")
     tiles, image_near = call(
         last_kernel,
         (struct((coils, 8, 128)), near_shape),
-        (at, sums, image, rhs, spectrum, sampling, maps, rows_f, columns_f),
+        (at, sums, image, rhs, spectrum, sampling, maps, rows, columns),
         in_smem=(0,),
     )
     image_parts = near_planes(image_near)
     tiles = call(spread_kernel, struct((slabs, 8, 128)), (swap(tiles, "coil"),))
     last = swap(tiles, "slab")
-    middle = jnp.stack([middle_table(w_middle[m]) for m in range(w_middle.shape[0])])
     scratch = [pltpu.VMEM((12, 144, 256), BF16)]
     scratch += [pltpu.VMEM((10 - 2 * m, (16 - 2 * m) * 32, 256), BF16) for m in range(4)]
     return call(
         functools.partial(denoise_kernel, coils, slabs),
         (struct(prior_image.shape), struct(prior_image.shape)),
-        (at, sums, last, *rhs_parts, *image_parts, first_table(w_first), middle, last_table(w_last)),
+        (at, last, *rhs_parts, *image_parts, *weights),
         scratch=scratch,
         in_smem=(0,),
     )

time: 230 us -> 169 us (0.73)
  local copies, waits for them, and re-layouts: 65.9 us -> 5.28 us
  blocking collectives: 0 us -> 53.2 us
  waiting for transfers between devices: 48.7 us -> 23.9 us
  starting transfers between devices: 79.5 us -> 56.4 us
  other arithmetic: 5.25 us -> 0.08 us
    all_to_all x0 -> x2, blocking collectives: none -> 53.2 us  [swap(): return lax.all_to_all(blocks, axis, 0, 0, tiled=True)]
    all_to_all x7 -> x4, waiting for transfers between devices: 48.7 us -> 22.8 us  [swap(): return lax.all_to_all(blocks, axis, 0, 0, tiled=True)]
    all_to_all x7 -> x4, starting transfers between devices: 48.1 us -> 22.6 us  [swap(): return lax.all_to_all(blocks, axis, 0, 0, tiled=True)]
    unnamed x78 -> x28, local copies, waits for them, and re-layouts: 28.7 us -> 5.02 us
    another operation x10 -> x0, local copies, waits for them, and re-layouts: 20.3 us -> none  [the longest x6 17.8 us: body(): jnp.stack([middle_table(w_middle[m]) for m in range(w_middle.shape[0])])]
    reshape x3, local copies, waits for them, and re-layouts: 13.4 us -> 0.22 us  [the longest x2 0.11 us: tables(): first = w_first.reshape(w_first.shape[0], 54)]
    another operation x4 -> x0, other arithmetic: 5.17 us -> none  [the longest x3 3.91 us: banded(): return jnp.stack(bands, axis=1)]
    ppermute x12, starting transfers between devices: 31.3 us -> 33.7 us  [shifted(): return lax.ppermute(part, 'slab', pairs)]
  transfers between devices with their start and end apart: 19 -> 16, of which waited for: 5 -> 4; matrix products, arithmetic and copies ran while one was open for 25% -> 0% of each run, Pallas kernels for 1% -> 2%
where the time goes in v2:
time: 169 us; the launch traced here: 166 us
  starting transfers between devices  56.4 us (33%)
  blocking collectives  53.2 us (31%)
  Pallas kernels  25.9 us (15%)
  waiting for transfers between devices  23.9 us (14%)
  local copies, waits for them, and re-layouts  5.28 us (3%)
    all_to_all x2, blocking collectives, swap(): return lax.all_to_all(blocks, axis, 0, 0, tiled=True)  53.2 us
    ppermute x12, starting transfers between devices, shifted(): return lax.ppermute(part, 'slab', pairs)  33.7 us
    pallas_call x8, Pallas kernels, call(): pl.pallas_call(kernel, out_shape=out_shape, in_specs=specs, out_specs=out...  25.9 us
    all_to_all x4, waiting for transfers between devices, swap(): return lax.all_to_all(blocks, axis, 0, 0, tiled=True)  22.8 us
    all_to_all x4, starting transfers between devices, swap(): return lax.all_to_all(blocks, axis, 0, 0, tiled=True)  22.6 us
    unnamed x28, local copies, waits for them, and re-layouts  5.02 us
  transfers between devices with their start and end apart: 16, of which 4 were waited for; matrix products, arithmetic and copies ran while one was open for 0% of the time, Pallas kernels for 2%

profile of v2, /device:TPU:1, one launch (start us, length us, event | category | flops | bytes accessed | tf_op | source)
XLA Modules:
  0.0 165.6 jit_solution(3019882950907738331)
XLA Ops:
  0.6 1.0 copy-done
  1.7 1.0 copy-done.2
  2.7 0.9 copy-done.4
  3.7 0.9 copy-done.6
  4.6 1.0 copy-done.9
  5.6 1.3 shard_map.104
  6.9 28.7 %all_to_all.30.blocks_ref = f32[16,64,128]{2,1,0:T(8,128)S(1)} all-to-all(f32[16,64,128]{2,1,0:T(8,128)S(1)} %shard_map.104), channel_id=1, replica_groups=mesh['slab'=16,'coil'=16] {'coil'}, dimensions={0} | all-to-all | bytes 1048576 | tf_op jit(solution)/shard_map/all_to_all | solution.py:437
  35.6 0.9 shard_map.105
  36.4 4.9 %all-to-all-start.1 = ((f32[16,64,128]{2,1,0:T(8,128)}), f32[16,64,128]{2,1,0:T(8,128)S(1)}, u32[]{:S(2)}, u32[]{:S(2)}) async-start(f32[16,64,128]{2,1,0:T(8,128)} %get-tuple-element.15), calls=%async_computation.1 | async-start | bytes 1048576 | tf_op jit(solution)/shard_map/all_to_all | solution.py:437
  41.5 17.1 %all-to-all-done.1.blocks_ref.rhs_ref = f32[16,64,128]{2,1,0:T(8,128)S(1)} async-done(((f32[16,64,128]{2,1,0:T(8,128)}), f32[16,64,128]{2,1,0:T(8,128)S(1)}, u32[]{:S(2)}, u32[]{:S(2)}) %all-to-all-start.1) | async-done | bytes 524320 | tf_op jit(solution)/shard_map/all_to_all | solution.py:437
  58.6 3.1 %shard_map.106 = (f32[16,72,128]{2,1,0:T(8,128)S(1)}, f32[2,2,256,128]{3,2,1,0:T(8,128)S(1)}, f32[8,128]{1,0:T(8,128)S(1)}, f32[2,2,32,128]{3,2,1,0:T(8,128)S(1)}) custom-call(s32[2]{0:T(128)S(1)} %pad_add_fusion.at_ref.refs_0_, f32[16,64,128]{2,1,0:T(8,128)S(1)} %all-to-all-done.1.blocks_ref.rhs_ref, s32[2,256,128]{2,1,0:T(8,128)S(1)} %copy-done.5, ...), custom_call_target="tpu_custom_call" | custom-call | tf_op jit(solution)/shard_map/pallas_call | solution.py:26
  61.7 24.5 %all_to_all.31.blocks_ref = f32[16,72,128]{2,1,0:T(8,128)S(1)} all-to-all(f32[16,72,128]{2,1,0:T(8,128)S(1)} %get-tuple-element.16), channel_id=1, replica_groups=mesh['slab'=16,'coil'=16] {'coil'}, dimensions={0} | all-to-all | bytes 1179648 | tf_op jit(solution)/shard_map/all_to_all | solution.py:437
  87.0 3.6 %all-to-all-start.3 = ((f32[16,64,128]{2,1,0:T(8,128)}), f32[16,64,128]{2,1,0:T(8,128)S(1)}, u32[]{:S(2)}, u32[]{:S(2)}) async-start(f32[16,64,128]{2,1,0:T(8,128)} %get-tuple-element.20), calls=%async_computation.3 | async-start | bytes 1048576 | tf_op jit(solution)/shard_map/all_to_all | solution.py:437
  90.6 1.3 collective-permute-start.5
  91.9 1.3 collective-permute-start.4
  93.2 3.9 %collective-permute-start.3 = (f32[2,2,32,128]{3,2,1,0:T(8,128)S(1)}, f32[2,2,32,128]{3,2,1,0:T(8,128)S(1)}, u32[]{:S(2)}, u32[]{:S(2)}) collective-permute-start(f32[2,2,32,128]{3,2,1,0:T(8,128)S(1)} %get-tuple-element.23.refs_5_), channel_id=1, source_target_pairs={{16,0},{32,16},{48,32},{64,48},{80,64},{96,80},{112,96},{128,112},... | collective-permute-start | bytes 196616 | tf_op jit(solution)/shard_map/ppermute | solution.py:445
  97.1 4.2 %collective-permute-start.2 = (f32[2,2,32,128]{3,2,1,0:T(8,128)S(1)}, f32[2,2,32,128]{3,2,1,0:T(8,128)S(1)}, u32[]{:S(2)}, u32[]{:S(2)}) collective-permute-start(f32[2,2,32,128]{3,2,1,0:T(8,128)S(1)} %get-tuple-element.23.refs_5_), channel_id=1, source_target_pairs={{0,16},{16,32},{32,48},{48,64},{64,80},{80,96},{96,112},{112,128},... | collective-permute-start | bytes 196616 | tf_op jit(solution)/shard_map/ppermute | solution.py:445
  101.3 4.9 %collective-permute-start.1 = (f32[2,2,32,128]{3,2,1,0:T(8,128)S(1)}, f32[2,2,32,128]{3,2,1,0:T(8,128)S(1)}, u32[]{:S(2)}, u32[]{:S(2)}) collective-permute-start(f32[2,2,32,128]{3,2,1,0:T(8,128)S(1)} %get-tuple-element.23.refs_5_), channel_id=1, source_target_pairs={{0,32},{16,48},{32,64},{48,80},{64,96},{80,112},{96,128},{112,144}... | collective-permute-start | bytes 196616 | tf_op jit(solution)/shard_map/ppermute | solution.py:445
  106.2 1.2 all-to-all-done.3.blocks_ref
  107.4 2.3 %shard_map.108 = (f32[16,8,128]{2,1,0:T(8,128)}, f32[2,2,32,128]{3,2,1,0:T(8,128)S(1)}) custom-call(s32[2]{0:T(128)S(1)} %pad_add_fusion.at_ref.refs_0_, f32[8,128]{1,0:T(8,128)S(1)} %get-tuple-element.19.sums_ref, f32[16,64,128]{2,1,0:T(8,128)S(1)} %all-to-all-done.3.blocks_ref, f32[16,64,128]{2,1,0:T(8,128)S(1)} %all-to-all-done.1.blocks_ref.rhs_ref, ...), custom_call_target="tpu_custom_call" | custom-call | tf_op jit(solution)/shard_map/pallas_call | solution.py:26
  109.7 8.2 %all-to-all-start.4 = ((f32[16,8,128]{2,1,0:T(8,128)}), f32[16,8,128]{2,1,0:T(8,128)S(1)}, u32[]{:S(2)}, u32[]{:S(2)}) async-start(f32[16,8,128]{2,1,0:T(8,128)} %get-tuple-element.22), calls=%async_computation.4 | async-start | bytes 131072 | tf_op jit(solution)/shard_map/all_to_all | solution.py:437
  118.0 2.8 %collective-permute-start = (f32[1,2,32,128]{3,2,1,0:T(8,128)S(1)}, f32[1,2,32,128]{3,2,1,0:T(8,128)S(1)}, u32[]{:S(2)}, u32[]{:S(2)}) collective-permute-start(f32[1,2,32,128]{3,2,1,0:T(8,128)S(1)} %get-tuple-element.31), channel_id=1, source_target_pairs={{0,48},{16,64},{32,80},{48,96},{64,112},{80,128},{96,144},{112,160... | collective-permute-start | bytes 98312 | tf_op jit(solution)/shard_map/ppermute | solution.py:445
  120.7 1.0 collective-permute-done.refs_2_
  121.7 1.3 collective-permute-start.11
  123.2 4.5 %all-to-all-done.4.tiles_ref = f32[16,8,128]{2,1,0:T(8,128)S(1)} async-done(((f32[16,8,128]{2,1,0:T(8,128)}), f32[16,8,128]{2,1,0:T(8,128)S(1)}, u32[]{:S(2)}, u32[]{:S(2)}) %all-to-all-start.4) | async-done | bytes 65568 | tf_op jit(solution)/shard_map/all_to_all | solution.py:437
  128.3 5.9 %all-to-all-start.5 = ((f32[16,8,128]{2,1,0:T(8,128)}), f32[16,8,128]{2,1,0:T(8,128)S(1)}, u32[]{:S(2)}, u32[]{:S(2)}) async-start(f32[16,8,128]{2,1,0:T(8,128)} %shard_map.109), calls=%async_computation.5 | async-start | bytes 131072 | tf_op jit(solution)/shard_map/all_to_all | solution.py:437
  134.3 1.3 collective-permute-start.10
  135.6 2.0 %collective-permute-start.9 = (f32[2,2,32,128]{3,2,1,0:T(8,128)S(1)}, f32[2,2,32,128]{3,2,1,0:T(8,128)S(1)}, u32[]{:S(2)}, u32[]{:S(2)}) collective-permute-start(f32[2,2,32,128]{3,2,1,0:T(8,128)S(1)} %get-tuple-element.24.refs_12_), channel_id=1, source_target_pairs={{16,0},{32,16},{48,32},{64,48},{80,64},{96,80},{112,96},{128,112},... | collective-permute-start | bytes 196616 | tf_op jit(solution)/shard_map/ppermute | solution.py:445
  137.6 4.2 %collective-permute-start.8 = (f32[2,2,32,128]{3,2,1,0:T(8,128)S(1)}, f32[2,2,32,128]{3,2,1,0:T(8,128)S(1)}, u32[]{:S(2)}, u32[]{:S(2)}) collective-permute-start(f32[2,2,32,128]{3,2,1,0:T(8,128)S(1)} %get-tuple-element.24.refs_12_), channel_id=1, source_target_pairs={{0,16},{16,32},{32,48},{48,64},{64,80},{80,96},{96,112},{112,128},... | collective-permute-start | bytes 196616 | tf_op jit(solution)/shard_map/ppermute | solution.py:445
  141.8 4.4 %collective-permute-start.7 = (f32[2,2,32,128]{3,2,1,0:T(8,128)S(1)}, f32[2,2,32,128]{3,2,1,0:T(8,128)S(1)}, u32[]{:S(2)}, u32[]{:S(2)}) collective-permute-start(f32[2,2,32,128]{3,2,1,0:T(8,128)S(1)} %get-tuple-element.24.refs_12_), channel_id=1, source_target_pairs={{0,32},{16,48},{32,64},{48,80},{64,96},{80,112},{96,128},{112,144}... | collective-permute-start | bytes 196616 | tf_op jit(solution)/shard_map/ppermute | solution.py:445
  146.3 2.2 %collective-permute-start.6 = (f32[1,2,32,128]{3,2,1,0:T(8,128)S(1)}, f32[1,2,32,128]{3,2,1,0:T(8,128)S(1)}, u32[]{:S(2)}, u32[]{:S(2)}) collective-permute-start(f32[1,2,32,128]{3,2,1,0:T(8,128)S(1)} %get-tuple-element.29), channel_id=1, source_target_pairs={{0,48},{16,64},{32,80},{48,96},{64,112},{80,128},{96,144},{112,160... | collective-permute-start | bytes 98312 | tf_op jit(solution)/shard_map/ppermute | solution.py:445
  149.5 16.0 %shard_map.111 = (f32[2,2,16,128]{3,2,1,0:T(8,128)}, f32[2,2,16,128]{3,2,1,0:T(8,128)}) custom-call(s32[2]{0:T(128)S(1)} %pad_add_fusion.at_ref.refs_0_, f32[16,8,128]{2,1,0:T(8,128)S(1)} %all-to-all-done.5.refs_1_, f32[1,2,32,128]{3,2,1,0:T(8,128)S(1)} %collective-permute-done.refs_2_, f32[2,2,32,128]{3,2,1,0:T(8,128)S(1)} %collective-permute-done.1.refs_3_, ...), custom_call_target="tpu_custom_call" | custom-call | tf_op jit(solution)/shard_map/pallas_call | solution.py:26
  (46 shorter events, 2.8 us)
Async XLA Ops:
  0.6 1.0 copy-start
  1.7 1.0 copy-start.2
  2.7 0.9 copy-start.4
  3.7 0.9 copy-start.6
  4.6 1.0 copy-start.9
  6.9 28.7 %copy-start.10 = (f32[2,2,16,128]{3,2,1,0:T(8,128)S(1)}, f32[2,2,16,128]{3,2,1,0:T(8,128)}, u32[]{:S(2)}) copy-start(f32[2,2,16,128]{3,2,1,0:T(8,128)} %prior_ref.1) | copy-start | bytes 98308
  35.6 23.0 %copy-start.5 = (s32[2,256,128]{2,1,0:T(8,128)S(1)}, s32[2,256,128]{2,1,0:T(8,128)}, u32[]{:S(2)}) copy-start(s32[2,256,128]{2,1,0:T(8,128)} %mask_ref.5) | copy-start | bytes 786436
  35.6 23.0 %copy-start.7 = (bf16[128,512]{1,0:T(8,128)(2,1)S(1)}, bf16[128,512]{1,0:T(8,128)(2,1)}, u32[]{:S(2)}) copy-start(bf16[128,512]{1,0:T(8,128)(2,1)} %constant.15.clone.columns_ref) | copy-start | bytes 393220
  36.4 22.1 %copy-start.1 = (f32[1,2,2,256,128]{4,3,2,1,0:T(8,128)S(1)}, f32[1,2,2,256,128]{4,3,2,1,0:T(8,128)}, u32[]{:S(2)}) copy-start(f32[1,2,2,256,128]{4,3,2,1,0:T(8,128)} %param.9) | copy-start | bytes 1572868
  36.4 22.1 %copy-start.3 = (bf16[512,512]{1,0:T(8,128)(2,1)S(1)}, bf16[512,512]{1,0:T(8,128)(2,1)}, u32[]{:S(2)}) copy-start(bf16[512,512]{1,0:T(8,128)(2,1)} %constant.14.clone.rows_ref) | copy-start | bytes 1572868
  36.4 22.1 %all-to-all-start.1 = ((f32[16,64,128]{2,1,0:T(8,128)}), f32[16,64,128]{2,1,0:T(8,128)S(1)}, u32[]{:S(2)}, u32[]{:S(2)}) async-start(f32[16,64,128]{2,1,0:T(8,128)} %get-tuple-element.15), calls=%async_computation.1 | async-start | bytes 1048576 | tf_op jit(solution)/shard_map/all_to_all | solution.py:437
  87.0 20.3 %all-to-all-start.3 = ((f32[16,64,128]{2,1,0:T(8,128)}), f32[16,64,128]{2,1,0:T(8,128)S(1)}, u32[]{:S(2)}, u32[]{:S(2)}) async-start(f32[16,64,128]{2,1,0:T(8,128)} %get-tuple-element.20), calls=%async_computation.3 | async-start | bytes 1048576 | tf_op jit(solution)/shard_map/all_to_all | solution.py:437
  90.6 27.3 %collective-permute-start.5 = (f32[1,2,32,128]{3,2,1,0:T(8,128)S(1)}, f32[1,2,32,128]{3,2,1,0:T(8,128)S(1)}, u32[]{:S(2)}, u32[]{:S(2)}) collective-permute-start(f32[1,2,32,128]{3,2,1,0:T(8,128)S(1)} %get-tuple-element.30), channel_id=1, source_target_pairs={{48,0},{64,16},{80,32},{96,48},{112,64},{128,80},{144,96},{160,112... | collective-permute-start | bytes 98312 | tf_op jit(solution)/shard_map/ppermute | solution.py:445
  91.9 42.4 %collective-permute-start.4 = (f32[2,2,32,128]{3,2,1,0:T(8,128)S(1)}, f32[2,2,32,128]{3,2,1,0:T(8,128)S(1)}, u32[]{:S(2)}, u32[]{:S(2)}) collective-permute-start(f32[2,2,32,128]{3,2,1,0:T(8,128)S(1)} %get-tuple-element.23.refs_5_), channel_id=1, source_target_pairs={{32,0},{48,16},{64,32},{80,48},{96,64},{112,80},{128,96},{144,112}... | collective-permute-start | bytes 196616 | tf_op jit(solution)/shard_map/ppermute | solution.py:445
  93.2 42.4 %collective-permute-start.3 = (f32[2,2,32,128]{3,2,1,0:T(8,128)S(1)}, f32[2,2,32,128]{3,2,1,0:T(8,128)S(1)}, u32[]{:S(2)}, u32[]{:S(2)}) collective-permute-start(f32[2,2,32,128]{3,2,1,0:T(8,128)S(1)} %get-tuple-element.23.refs_5_), channel_id=1, source_target_pairs={{16,0},{32,16},{48,32},{64,48},{80,64},{96,80},{112,96},{128,112},... | collective-permute-start | bytes 196616 | tf_op jit(solution)/shard_map/ppermute | solution.py:445
  97.1 40.5 %collective-permute-start.2 = (f32[2,2,32,128]{3,2,1,0:T(8,128)S(1)}, f32[2,2,32,128]{3,2,1,0:T(8,128)S(1)}, u32[]{:S(2)}, u32[]{:S(2)}) collective-permute-start(f32[2,2,32,128]{3,2,1,0:T(8,128)S(1)} %get-tuple-element.23.refs_5_), channel_id=1, source_target_pairs={{0,16},{16,32},{32,48},{48,64},{64,80},{80,96},{96,112},{112,128},... | collective-permute-start | bytes 196616 | tf_op jit(solution)/shard_map/ppermute | solution.py:445
  101.3 40.5 %collective-permute-start.1 = (f32[2,2,32,128]{3,2,1,0:T(8,128)S(1)}, f32[2,2,32,128]{3,2,1,0:T(8,128)S(1)}, u32[]{:S(2)}, u32[]{:S(2)}) collective-permute-start(f32[2,2,32,128]{3,2,1,0:T(8,128)S(1)} %get-tuple-element.23.refs_5_), channel_id=1, source_target_pairs={{0,32},{16,48},{32,64},{48,80},{64,96},{80,112},{96,128},{112,144}... | collective-permute-start | bytes 196616 | tf_op jit(solution)/shard_map/ppermute | solution.py:445
  107.4 15.7 %copy-start.11 = (bf16[2,32,3,3,3]{1,0,4,3,2:T(2,128)(2,1)S(1)}, bf16[2,32,3,3,3]{1,0,4,3,2:T(2,128)(2,1)}, u32[]{:S(2)}) copy-start(bf16[2,32,3,3,3]{1,0,4,3,2:T(2,128)(2,1)} %param.15) | copy-start | bytes 10372
  109.7 39.0 %copy-start.8 = (bf16[3,32,32,3,3,3]{2,1,5,4,3,0:T(8,128)(2,1)S(1)}, bf16[3,32,32,3,3,3]{2,1,5,4,3,0:T(8,128)(2,1)}, u32[]{:S(2)}) copy-start(bf16[3,32,32,3,3,3]{2,1,5,4,3,0:T(8,128)(2,1)} %param.14) | copy-start | bytes 497668
  109.7 18.0 %all-to-all-start.4 = ((f32[16,8,128]{2,1,0:T(8,128)}), f32[16,8,128]{2,1,0:T(8,128)S(1)}, u32[]{:S(2)}, u32[]{:S(2)}) async-start(f32[16,8,128]{2,1,0:T(8,128)} %get-tuple-element.22), calls=%async_computation.4 | async-start | bytes 131072 | tf_op jit(solution)/shard_map/all_to_all | solution.py:437
  118.0 3.8 %collective-permute-start = (f32[1,2,32,128]{3,2,1,0:T(8,128)S(1)}, f32[1,2,32,128]{3,2,1,0:T(8,128)S(1)}, u32[]{:S(2)}, u32[]{:S(2)}) collective-permute-start(f32[1,2,32,128]{3,2,1,0:T(8,128)S(1)} %get-tuple-element.31), channel_id=1, source_target_pairs={{0,48},{16,64},{32,80},{48,96},{64,112},{80,128},{96,144},{112,160... | collective-permute-start | bytes 98312 | tf_op jit(solution)/shard_map/ppermute | solution.py:445
  121.7 24.5 %collective-permute-start.11 = (f32[1,2,32,128]{3,2,1,0:T(8,128)S(1)}, f32[1,2,32,128]{3,2,1,0:T(8,128)S(1)}, u32[]{:S(2)}, u32[]{:S(2)}) collective-permute-start(f32[1,2,32,128]{3,2,1,0:T(8,128)S(1)} %get-tuple-element.28), channel_id=1, source_target_pairs={{48,0},{64,16},{80,32},{96,48},{112,64},{128,80},{144,96},{160,112... | collective-permute-start | bytes 98312 | tf_op jit(solution)/shard_map/ppermute | solution.py:445
  128.3 21.2 %all-to-all-start.5 = ((f32[16,8,128]{2,1,0:T(8,128)}), f32[16,8,128]{2,1,0:T(8,128)S(1)}, u32[]{:S(2)}, u32[]{:S(2)}) async-start(f32[16,8,128]{2,1,0:T(8,128)} %shard_map.109), calls=%async_computation.5 | async-start | bytes 131072 | tf_op jit(solution)/shard_map/all_to_all | solution.py:437
  134.3 15.2 %collective-permute-start.10 = (f32[2,2,32,128]{3,2,1,0:T(8,128)S(1)}, f32[2,2,32,128]{3,2,1,0:T(8,128)S(1)}, u32[]{:S(2)}, u32[]{:S(2)}) collective-permute-start(f32[2,2,32,128]{3,2,1,0:T(8,128)S(1)} %get-tuple-element.24.refs_12_), channel_id=1, source_target_pairs={{32,0},{48,16},{64,32},{80,48},{96,64},{112,80},{128,96},{144,112}... | collective-permute-start | bytes 196616 | tf_op jit(solution)/shard_map/ppermute | solution.py:445
  135.6 13.9 %collective-permute-start.9 = (f32[2,2,32,128]{3,2,1,0:T(8,128)S(1)}, f32[2,2,32,128]{3,2,1,0:T(8,128)S(1)}, u32[]{:S(2)}, u32[]{:S(2)}) collective-permute-start(f32[2,2,32,128]{3,2,1,0:T(8,128)S(1)} %get-tuple-element.24.refs_12_), channel_id=1, source_target_pairs={{16,0},{32,16},{48,32},{64,48},{80,64},{96,80},{112,96},{128,112},... | collective-permute-start | bytes 196616 | tf_op jit(solution)/shard_map/ppermute | solution.py:445
  137.6 11.9 %collective-permute-start.8 = (f32[2,2,32,128]{3,2,1,0:T(8,128)S(1)}, f32[2,2,32,128]{3,2,1,0:T(8,128)S(1)}, u32[]{:S(2)}, u32[]{:S(2)}) collective-permute-start(f32[2,2,32,128]{3,2,1,0:T(8,128)S(1)} %get-tuple-element.24.refs_12_), channel_id=1, source_target_pairs={{0,16},{16,32},{32,48},{48,64},{64,80},{80,96},{96,112},{112,128},... | collective-permute-start | bytes 196616 | tf_op jit(solution)/shard_map/ppermute | solution.py:445
  141.8 7.7 %collective-permute-start.7 = (f32[2,2,32,128]{3,2,1,0:T(8,128)S(1)}, f32[2,2,32,128]{3,2,1,0:T(8,128)S(1)}, u32[]{:S(2)}, u32[]{:S(2)}) collective-permute-start(f32[2,2,32,128]{3,2,1,0:T(8,128)S(1)} %get-tuple-element.24.refs_12_), channel_id=1, source_target_pairs={{0,32},{16,48},{32,64},{48,80},{64,96},{80,112},{96,128},{112,144}... | collective-permute-start | bytes 196616 | tf_op jit(solution)/shard_map/ppermute | solution.py:445
  146.3 2.3 %copy-start.12 = (bf16[32,2,3,3,3]{0,1,4,3,2:T(2,128)(2,1)S(1)}, bf16[32,2,3,3,3]{0,1,4,3,2:T(2,128)(2,1)}, u32[]{:S(2)}) copy-start(bf16[32,2,3,3,3]{0,1,4,3,2:T(2,128)(2,1)} %param.13) | copy-start | bytes 10372
  146.3 3.2 %collective-permute-start.6 = (f32[1,2,32,128]{3,2,1,0:T(8,128)S(1)}, f32[1,2,32,128]{3,2,1,0:T(8,128)S(1)}, u32[]{:S(2)}, u32[]{:S(2)}) collective-permute-start(f32[1,2,32,128]{3,2,1,0:T(8,128)S(1)} %get-tuple-element.29), channel_id=1, source_target_pairs={{0,48},{16,64},{32,80},{48,96},{64,112},{80,128},{96,144},{112,160... | collective-permute-start | bytes 98312 | tf_op jit(solution)/shard_map/ppermute | solution.py:445

commit v3 on v2

--- a/solution.py
+++ b/solution.py
@@ -12,16 +12,23 @@
 LAMBDA = 0.5
 HALO = 5
 SIDE = 8
-GROUP = 3
+GROUP = 2
 F32 = jnp.float32
 BF16 = jnp.bfloat16
-VMEM_BYTES = 48 * 1024 * 1024
-
-
-def call(kernel, out_shape, args, scratch=(), in_smem=()):
+VMEM_BYTES = 20 * 1024 * 1024
+
+
+def call(kernel, out_shape, args, scratch=(), in_smem=(), after=()):
     specs = [
         pl.BlockSpec(memory_space=pltpu.SMEM if i in in_smem else pltpu.VMEM) for i in range(len(args))
     ]
+    specs += [pl.BlockSpec(memory_space=pl.ANY)] * len(after)
+    if after:
+        inner_kernel, count = kernel, len(args)
+
+        def kernel(*refs):
+            inner_kernel(*refs[:count], *refs[count + len(after) :])
+
     outs = jax.tree.map(lambda _: pl.BlockSpec(memory_space=pltpu.VMEM), out_shape)
     return pl.pallas_call(
         kernel,
@@ -30,7 +37,7 @@
         out_specs=outs,
         scratch_shapes=list(scratch),
         compiler_params=pltpu.CompilerParams(vmem_limit_bytes=VMEM_BYTES),
-    )(*args)
+    )(*args, *after)
 
 
 def struct(shape, dtype=F32):
@@ -173,10 +180,34 @@
             near_ref[p, a, 24:32, :] = jnp.where(at < count - 1, after, 0.0)
 
 
-def adjoint_kernel(kspace_ref, mask_ref, rows_ref, columns_ref, maps_ref, out_ref):
+def adjoint_kernel(
+    mask_hbm, kspace_hbm, rows_hbm, columns_hbm, maps_hbm, out_ref, mask_ref, kspace_ref, rows_ref, columns_ref, maps_ref, sems
+):
+    sources = (mask_hbm, kspace_hbm, rows_hbm, columns_hbm, maps_hbm)
+    targets = (mask_ref, kspace_ref, rows_ref, columns_ref, maps_ref)
+    copies = [pltpu.make_async_copy(src, dst, sems.at[i]) for i, (src, dst) in enumerate(zip(sources, targets))]
+    for copy in copies:
+        copy.start()
+    for copy in copies[:3]:
+        copy.wait()
     field = masked([[kspace_ref[a, p] for p in range(2)] for a in range(2)], mask_ref)
-    field = dft_columns(dft_rows(field, rows_ref, 1.0), columns_ref, 1.0)
+    field = dft_rows(field, rows_ref, 1.0)
+    copies[3].wait()
+    field = dft_columns(field, columns_ref, 1.0)
+    copies[4].wait()
     store_image(out_ref, coil_term(maps_ref, field))
+
+
+def adjoint(mask, kspace, rows, columns, maps, coils):
+    args = (mask, kspace, rows, columns, maps)
+    return pl.pallas_call(
+        adjoint_kernel,
+        out_shape=struct((coils, 64, 128)),
+        in_specs=[pl.BlockSpec(memory_space=pl.ANY)] * len(args),
+        out_specs=pl.BlockSpec(memory_space=pltpu.VMEM),
+        scratch_shapes=[pltpu.VMEM(arg.shape, arg.dtype) for arg in args] + [pltpu.SemaphoreType.DMA((len(args),))],
+        compiler_params=pltpu.CompilerParams(vmem_limit_bytes=60 * 1024 * 1024),
+    )(*args)
 
 
 def rows_kernel(blocks_ref, prior_ref, rows_ref, copies_ref):
@@ -331,46 +362,47 @@
         extra = 4 - depth
         first = 2 * slab_at - extra
 
-        @pl.when(coil_at == 0)
+        last_plane = 2 * slab_at + 1 + extra
+        edge = (coil_at == 0) | (coil_at == coil_count - 1) | (first < 0) | (last_plane >= 2 * slab_count)
+
+        @pl.when(edge)
         def _():
-            out_ref[:, 0 : extra * 32, 0:128] = jnp.zeros((planes, extra * 32, 128), BF16)
-
-        @pl.when(coil_at == coil_count - 1)
-        def _():
-            out_ref[:, cells - extra * 32 : cells, 128:256] = jnp.zeros((planes, extra * 32, 128), BF16)
-
-        for p in list(range(extra)) + list(range(planes - extra, planes)):
-
-            @pl.when((first + p < 0) | (first + p >= 2 * slab_count))
+            blank = jnp.zeros((planes, extra * 32, 128), BF16)
+
+            @pl.when(coil_at == 0)
             def _():
-                out_ref[p] = jnp.zeros(out_ref.shape[1:], BF16)
+                out_ref[:, 0 : extra * 32, 0:128] = blank
+
+            @pl.when(coil_at == coil_count - 1)
+            def _():
+                out_ref[:, cells - extra * 32 : cells, 128:256] = blank
+
+            for p in list(range(extra)) + list(range(planes - extra, planes)):
+
+                @pl.when((first + p < 0) | (first + p >= 2 * slab_count))
+                def _():
+                    out_ref[p] = jnp.zeros(out_ref.shape[1:], BF16)
 
     first_out = hidden_refs[0]
 
-    def first_plane(p, carry):
+    for p in range(first_out.shape[0]):
         taps = jnp.concatenate([features_ref[p + u] for u in range(3)], axis=0)
         values = jnp.dot(w_first_ref[:, :432], taps, preferred_element_type=F32)
         first_out[p] = jnp.maximum(values, 0.0).astype(BF16)
-        return carry
-
-    lax.fori_loop(0, first_out.shape[0], first_plane, 0)
     outside(first_out, 0)
 
     for m in range(len(hidden_refs) - 1):
         in_ref, out_ref = hidden_refs[m], hidden_refs[m + 1]
         starts = starts_of(out_ref.shape[1] // 32)
 
-        def middle_plane(p, carry, m=m, in_ref=in_ref, out_ref=out_ref, starts=starts):
+        cells = GROUP * 32
+        for p in range(out_ref.shape[0]):
             for start in starts:
                 rows = slice(start * 32, (start + GROUP + 2) * 32)
                 taps = jnp.concatenate([in_ref[p + u, rows] for u in range(3)], axis=0)
                 sums = jnp.dot(w_middle_ref[m, :, : (GROUP + 2) * 96], taps, preferred_element_type=F32)
-                cells = GROUP * 32
                 values = shifted_sum([sums[t * cells : (t + 1) * cells] for t in range(3)])
-                out_ref[p, start * 32 : (start + GROUP) * 32] = jnp.maximum(values, 0.0).astype(BF16)
-            return carry
-
-        lax.fori_loop(0, out_ref.shape[0], middle_plane, 0)
+                out_ref[p, start * 32 : start * 32 + cells] = jnp.maximum(values, 0.0).astype(BF16)
         outside(out_ref, m + 1)
 
     in_ref = hidden_refs[-1]
@@ -457,9 +489,12 @@
     rows, columns = left_table(len_y), right_table(len_z)
     weights = tables(w_first, w_middle, w_last)
 
-    term = call(adjoint_kernel, struct((coils, 64, 128)), (kspace[0], sampling, rows, columns, maps))
+    term = adjoint(sampling, kspace[0], rows, columns, maps, coils)
     rhs_rows, copies = call(
-        rows_kernel, (struct((64, 128)), struct((coils, 64, 128))), (swap(term, "coil"), prior_image)
+        rows_kernel,
+        (struct((64, 128)), struct((coils, 64, 128))),
+        (swap(term, "coil"), prior_image),
+        after=(),
     )
     rhs = swap(copies, "coil")
     near_shape = struct((2, 2, 32, 128))
@@ -474,6 +509,7 @@
         image_kernel,
         (struct((coils, 64, 128)), struct((8, 128))),
         (swap(term, "coil"), rhs_rows, norms),
+        after=rhs_parts,
     )
     image = swap(copies, "coil")
     tiles, image_near = call(
@@ -483,7 +519,7 @@
         in_smem=(0,),
     )
     image_parts = near_planes(image_near)
-    tiles = call(spread_kernel, struct((slabs, 8, 128)), (swap(tiles, "coil"),))
+    tiles = call(spread_kernel, struct((slabs, 8, 128)), (swap(tiles, "coil"),), after=image_parts[:4])
     last = swap(tiles, "slab")
     scratch = [pltpu.VMEM((12, 144, 256), BF16)]
     scratch += [pltpu.VMEM((10 - 2 * m, (16 - 2 * m) * 32, 256), BF16) for m in range(4)]

time: 169 us -> 160 us (0.947); the launches traced: 166 us -> 159 us
  starting transfers between devices: 56.4 us -> 47.5 us
  waiting for transfers between devices: 23.9 us -> 29.9 us
  local copies, waits for them, and re-layouts: 5.28 us -> 0.99 us
  blocking collectives: 53.2 us -> 56.8 us
  Pallas kernels: 25.9 us -> 22.5 us
    pallas_call x8 -> x7, Pallas kernels: 25.9 us -> 18.9 us  [call(): pl.pallas_call(kernel, out_shape=out_shape, in_specs=specs, out_specs=out...]
    ppermute x12, waiting for transfers between devices: 1.05 us -> 6.34 us  [shifted(): return lax.ppermute(part, 'slab', pairs)]
    ppermute x12, starting transfers between devices: 33.7 us -> 28.9 us  [shifted(): return lax.ppermute(part, 'slab', pairs)]
    unnamed x28 -> x18, local copies, waits for them, and re-layouts: 5.02 us -> 0.73 us
    all_to_all x4, starting transfers between devices: 22.6 us -> 18.6 us  [swap(): return lax.all_to_all(blocks, axis, 0, 0, tiled=True)]
    all_to_all x2, blocking collectives: 53.2 us -> 56.8 us  [swap(): return lax.all_to_all(blocks, axis, 0, 0, tiled=True)]
    pallas_call x0 -> x1, Pallas kernels: none -> 3.56 us  [adjoint(): pl.pallas_call(adjoint_kernel, out_shape=struct((coils, 64, 128)), in_spe...]
  transfers between devices with their start and end apart: 16 -> 16, of which waited for: 4 -> 4; matrix products, arithmetic and copies ran while one was open for 0% -> 0% of each run, Pallas kernels for 2% -> 1%
where the time goes in v3:
time: 160 us; the launch traced here: 159 us
  blocking collectives  56.8 us (36%)
  starting transfers between devices  47.5 us (30%)
  waiting for transfers between devices  29.9 us (19%)
  Pallas kernels  22.5 us (14%)
    all_to_all x2, blocking collectives, swap(): return lax.all_to_all(blocks, axis, 0, 0, tiled=True)  56.8 us
    ppermute x12, starting transfers between devices, shifted(): return lax.ppermute(part, 'slab', pairs)  28.9 us
    all_to_all x4, waiting for transfers between devices, swap(): return lax.all_to_all(blocks, axis, 0, 0, tiled=True)  23.5 us
    pallas_call x7, Pallas kernels, call(): pl.pallas_call(kernel, out_shape=out_shape, in_specs=specs, out_specs=out...  18.9 us
    all_to_all x4, starting transfers between devices, swap(): return lax.all_to_all(blocks, axis, 0, 0, tiled=True)  18.6 us
    ppermute x12, waiting for transfers between devices, shifted(): return lax.ppermute(part, 'slab', pairs)  6.34 us
    pallas_call x1, Pallas kernels, adjoint(): pl.pallas_call(adjoint_kernel, out_shape=struct((coils, 64, 128)), in_spe...  3.56 us
  transfers between devices with their start and end apart: 16, of which 4 were waited for; matrix products, arithmetic and copies ran while one was open for 0% of the time, Pallas kernels for 1%

profile of v3, /device:TPU:1, one launch (start us, length us, event | category | flops | bytes accessed | tf_op | source)
XLA Modules:
  0.0 158.7 jit_solution(17153267247008262341)
XLA Ops:
  0.6 3.6 %shard_map.104 = f32[16,64,128]{2,1,0:T(8,128)} custom-call(s32[2,256,128]{2,1,0:T(8,128)} %mask_ref.3, f32[2,2,256,128]{3,2,1,0:T(8,128)} %bitcast.12, bf16[512,512]{1,0:T(8,128)(2,1)} %constant.14.clone.rows_hbm.rows_ref, bf16[128,512]{1,0:T(8,128)(2,1)} %constant.15.clone.columns_hbm.columns_ref, f32[2,2,256,128]{3,2,1,0:T(8,128)} %bitcast.8), custom_call_target="tpu_custom_call" | custom-call | tf_op jit(solution)/shard_map/pallas_call | solution.py:203
  4.2 28.9 %all_to_all.30.blocks_ref = f32[16,64,128]{2,1,0:T(8,128)S(1)} all-to-all(f32[16,64,128]{2,1,0:T(8,128)} %shard_map.104), channel_id=1, replica_groups=mesh['slab'=16,'coil'=16] {'coil'}, dimensions={0} | all-to-all | bytes 1048576 | tf_op jit(solution)/shard_map/all_to_all | solution.py:469
  33.1 0.9 shard_map.105
  34.0 4.9 %all-to-all-start.1 = ((f32[16,64,128]{2,1,0:T(8,128)}), f32[16,64,128]{2,1,0:T(8,128)S(1)}, u32[]{:S(2)}, u32[]{:S(2)}) async-start(f32[16,64,128]{2,1,0:T(8,128)} %get-tuple-element.15), calls=%async_computation.1 | async-start | bytes 1048576 | tf_op jit(solution)/shard_map/all_to_all | solution.py:469
  39.0 17.1 %all-to-all-done.1.blocks_ref.rhs_ref = f32[16,64,128]{2,1,0:T(8,128)S(1)} async-done(((f32[16,64,128]{2,1,0:T(8,128)}), f32[16,64,128]{2,1,0:T(8,128)S(1)}, u32[]{:S(2)}, u32[]{:S(2)}) %all-to-all-start.1) | async-done | bytes 524320 | tf_op jit(solution)/shard_map/all_to_all | solution.py:469
  56.1 3.9 %shard_map.106 = (f32[16,72,128]{2,1,0:T(8,128)}, f32[2,2,256,128]{3,2,1,0:T(8,128)S(1)}, f32[8,128]{1,0:T(8,128)S(1)}, f32[2,2,32,128]{3,2,1,0:T(8,128)S(1)}) custom-call(s32[2]{0:T(128)S(1)} %pad_add_fusion.at_ref.refs_0_, f32[16,64,128]{2,1,0:T(8,128)S(1)} %all-to-all-done.1.blocks_ref.rhs_ref, s32[2,256,128]{2,1,0:T(8,128)S(1)} %copy-done.2, ...), custom_call_target="tpu_custom_call" | custom-call | tf_op jit(solution)/shard_map/pallas_call | solution.py:33
  60.0 4.6 %all-to-all-start.2 = ((f32[16,72,128]{2,1,0:T(8,128)}), f32[16,72,128]{2,1,0:T(8,128)S(1)}, u32[]{:S(2)}, u32[]{:S(2)}) async-start(f32[16,72,128]{2,1,0:T(8,128)} %get-tuple-element.16), calls=%async_computation.2 | async-start | bytes 1179648 | tf_op jit(solution)/shard_map/all_to_all | solution.py:469
  64.7 4.4 %collective-permute-start = (f32[1,2,32,128]{3,2,1,0:T(8,128)S(1)}, f32[1,2,32,128]{3,2,1,0:T(8,128)S(1)}, u32[]{:S(2)}, u32[]{:S(2)}) collective-permute-start(f32[1,2,32,128]{3,2,1,0:T(8,128)S(1)} %get-tuple-element.31), channel_id=1, source_target_pairs={{0,48},{16,64},{32,80},{48,96},{64,112},{80,128},{96,144},{112,160... | collective-permute-start | bytes 98312 | tf_op jit(solution)/shard_map/ppermute | solution.py:477
  69.1 2.3 %collective-permute-start.1 = (f32[2,2,32,128]{3,2,1,0:T(8,128)S(1)}, f32[2,2,32,128]{3,2,1,0:T(8,128)S(1)}, u32[]{:S(2)}, u32[]{:S(2)}) collective-permute-start(f32[2,2,32,128]{3,2,1,0:T(8,128)S(1)} %get-tuple-element.19.refs_6_.refs_5_), channel_id=1, source_target_pairs={{0,32},{16,48},{32,64},{48,80},{64,96},{80,112},{96,128},{112,144}... | collective-permute-start | bytes 196616 | tf_op jit(solution)/shard_map/ppermute | solution.py:477
  71.4 3.0 %collective-permute-start.2 = (f32[2,2,32,128]{3,2,1,0:T(8,128)S(1)}, f32[2,2,32,128]{3,2,1,0:T(8,128)S(1)}, u32[]{:S(2)}, u32[]{:S(2)}) collective-permute-start(f32[2,2,32,128]{3,2,1,0:T(8,128)S(1)} %get-tuple-element.19.refs_6_.refs_5_), channel_id=1, source_target_pairs={{0,16},{16,32},{32,48},{48,64},{64,80},{80,96},{96,112},{112,128},... | collective-permute-start | bytes 196616 | tf_op jit(solution)/shard_map/ppermute | solution.py:477
  74.4 1.9 %collective-permute-start.3 = (f32[2,2,32,128]{3,2,1,0:T(8,128)S(1)}, f32[2,2,32,128]{3,2,1,0:T(8,128)S(1)}, u32[]{:S(2)}, u32[]{:S(2)}) collective-permute-start(f32[2,2,32,128]{3,2,1,0:T(8,128)S(1)} %get-tuple-element.19.refs_6_.refs_5_), channel_id=1, source_target_pairs={{16,0},{32,16},{48,32},{64,48},{80,64},{96,80},{112,96},{128,112},... | collective-permute-start | bytes 196616 | tf_op jit(solution)/shard_map/ppermute | solution.py:477
  76.3 1.3 collective-permute-start.4
  77.7 1.3 collective-permute-start.5
  79.0 6.3 %collective-permute-done.5.refs_9_.refs_8_ = f32[1,2,32,128]{3,2,1,0:T(8,128)S(1)} collective-permute-done((f32[1,2,32,128]{3,2,1,0:T(8,128)S(1)}, f32[1,2,32,128]{3,2,1,0:T(8,128)S(1)}, u32[]{:S(2)}, u32[]{:S(2)}) %collective-permute-start.5) | collective-permute-done | bytes 32800 | tf_op jit(solution)/shard_map/ppermute | solution.py:477
  85.4 27.9 %all_to_all.31.blocks_ref = f32[16,64,128]{2,1,0:T(8,128)S(1)} all-to-all(f32[16,64,128]{2,1,0:T(8,128)S(1)} %get-tuple-element.21), channel_id=1, replica_groups=mesh['slab'=16,'coil'=16] {'coil'}, dimensions={0} | all-to-all | bytes 1048576 | tf_op jit(solution)/shard_map/all_to_all | solution.py:469
  113.2 2.4 %shard_map.108 = (f32[16,8,128]{2,1,0:T(8,128)}, f32[2,2,32,128]{3,2,1,0:T(8,128)S(1)}) custom-call(s32[2]{0:T(128)S(1)} %pad_add_fusion.at_ref.refs_0_, f32[8,128]{1,0:T(8,128)S(1)} %get-tuple-element.20.sums_ref, f32[16,64,128]{2,1,0:T(8,128)S(1)} %all_to_all.31.blocks_ref, f32[16,64,128]{2,1,0:T(8,128)S(1)} %all-to-all-done.1.blocks_ref.rhs_ref, ...), custom_call_target="tpu_custom_call" | custom-call | tf_op jit(solution)/shard_map/pallas_call | solution.py:33
  115.7 1.4 collective-permute-start.7
  117.1 6.3 %collective-permute-start.8 = (f32[2,2,32,128]{3,2,1,0:T(8,128)S(1)}, f32[2,2,32,128]{3,2,1,0:T(8,128)S(1)}, u32[]{:S(2)}, u32[]{:S(2)}) collective-permute-start(f32[2,2,32,128]{3,2,1,0:T(8,128)S(1)} %get-tuple-element.24.refs_4_.refs_12_), channel_id=1, source_target_pairs={{0,16},{16,32},{32,48},{48,64},{64,80},{80,96},{96,112},{112,128},... | collective-permute-start | bytes 196616 | tf_op jit(solution)/shard_map/ppermute | solution.py:477
  123.4 3.5 %all-to-all-start.4 = ((f32[16,8,128]{2,1,0:T(8,128)}), f32[16,8,128]{2,1,0:T(8,128)S(1)}, u32[]{:S(2)}, u32[]{:S(2)}) async-start(f32[16,8,128]{2,1,0:T(8,128)} %get-tuple-element.23), calls=%async_computation.4 | async-start | bytes 131072 | tf_op jit(solution)/shard_map/all_to_all | solution.py:469
  126.9 1.3 collective-permute-start.6
  128.2 0.1 reshape.11
  128.4 3.1 %collective-permute-start.9 = (f32[2,2,32,128]{3,2,1,0:T(8,128)S(1)}, f32[2,2,32,128]{3,2,1,0:T(8,128)S(1)}, u32[]{:S(2)}, u32[]{:S(2)}) collective-permute-start(f32[2,2,32,128]{3,2,1,0:T(8,128)S(1)} %get-tuple-element.24.refs_4_.refs_12_), channel_id=1, source_target_pairs={{16,0},{32,16},{48,32},{64,48},{80,64},{96,80},{112,96},{128,112},... | collective-permute-start | bytes 196616 | tf_op jit(solution)/shard_map/ppermute | solution.py:477
  131.5 1.3 collective-permute-start.10
  132.8 1.3 collective-permute-start.11
  134.1 2.2 %all-to-all-done.4.refs_0_ = f32[16,8,128]{2,1,0:T(8,128)S(1)} async-done(((f32[16,8,128]{2,1,0:T(8,128)}), f32[16,8,128]{2,1,0:T(8,128)S(1)}, u32[]{:S(2)}, u32[]{:S(2)}) %all-to-all-start.4) | async-done | bytes 65568 | tf_op jit(solution)/shard_map/all_to_all | solution.py:469
  136.3 0.6 shard_map.109
  136.9 5.6 %all-to-all-start.5 = ((f32[16,8,128]{2,1,0:T(8,128)}), f32[16,8,128]{2,1,0:T(8,128)S(1)}, u32[]{:S(2)}, u32[]{:S(2)}) async-start(f32[16,8,128]{2,1,0:T(8,128)} %shard_map.109), calls=%async_computation.5 | async-start | bytes 131072 | tf_op jit(solution)/shard_map/all_to_all | solution.py:469
  142.6 0.7 copy-done.7
  143.3 0.1 copy.15.first_ref
  143.4 0.8 shard_map.110
  144.2 4.2 %all-to-all-done.5.refs_1_ = f32[16,8,128]{2,1,0:T(8,128)S(1)} async-done(((f32[16,8,128]{2,1,0:T(8,128)}), f32[16,8,128]{2,1,0:T(8,128)S(1)}, u32[]{:S(2)}, u32[]{:S(2)}) %all-to-all-start.5) | async-done | bytes 65568 | tf_op jit(solution)/shard_map/all_to_all | solution.py:469
  148.4 10.3 %shard_map.111 = (f32[2,2,16,128]{3,2,1,0:T(8,128)}, f32[2,2,16,128]{3,2,1,0:T(8,128)}) custom-call(s32[2]{0:T(128)S(1)} %pad_add_fusion.at_ref.refs_0_, f32[16,8,128]{2,1,0:T(8,128)S(1)} %all-to-all-done.5.refs_1_, f32[1,2,32,128]{3,2,1,0:T(8,128)S(1)} %collective-permute-done.refs_3_.refs_2_, f32[2,2,32,128]{3,2,1,0:T(8,128)S(1)} %collective-permute-done.1.refs_4_.refs_3_, ...), custom_call_target="tpu_custom_call" | custom-call | tf_op jit(solution)/shard_map/pallas_call | solution.py:33
  (36 shorter events, 0.3 us)
Async XLA Ops:
  4.2 28.9 %copy-start.5 = (f32[2,2,16,128]{3,2,1,0:T(8,128)S(1)}, f32[2,2,16,128]{3,2,1,0:T(8,128)}, u32[]{:S(2)}) copy-start(f32[2,2,16,128]{3,2,1,0:T(8,128)} %prior_ref.1) | copy-start | bytes 98308
  33.1 23.0 %copy-start.2 = (s32[2,256,128]{2,1,0:T(8,128)S(1)}, s32[2,256,128]{2,1,0:T(8,128)}, u32[]{:S(2)}) copy-start(s32[2,256,128]{2,1,0:T(8,128)} %mask_ref.3) | copy-start | bytes 786436
  33.1 23.0 %copy-start.3 = (bf16[128,512]{1,0:T(8,128)(2,1)S(1)}, bf16[128,512]{1,0:T(8,128)(2,1)}, u32[]{:S(2)}) copy-start(bf16[128,512]{1,0:T(8,128)(2,1)} %constant.15.clone.columns_hbm.columns_ref) | copy-start | bytes 393220
  34.0 22.1 %copy-start = (f32[1,2,2,256,128]{4,3,2,1,0:T(8,128)S(1)}, f32[1,2,2,256,128]{4,3,2,1,0:T(8,128)}, u32[]{:S(2)}) copy-start(f32[1,2,2,256,128]{4,3,2,1,0:T(8,128)} %param.9) | copy-start | bytes 1572868
  34.0 22.1 %copy-start.1 = (bf16[512,512]{1,0:T(8,128)(2,1)S(1)}, bf16[512,512]{1,0:T(8,128)(2,1)}, u32[]{:S(2)}) copy-start(bf16[512,512]{1,0:T(8,128)(2,1)} %constant.14.clone.rows_hbm.rows_ref) | copy-start | bytes 1572868
  34.0 22.1 %all-to-all-start.1 = ((f32[16,64,128]{2,1,0:T(8,128)}), f32[16,64,128]{2,1,0:T(8,128)S(1)}, u32[]{:S(2)}, u32[]{:S(2)}) async-start(f32[16,64,128]{2,1,0:T(8,128)} %get-tuple-element.15), calls=%async_computation.1 | async-start | bytes 1048576 | tf_op jit(solution)/shard_map/all_to_all | solution.py:469
  60.0 25.2 %all-to-all-start.2 = ((f32[16,72,128]{2,1,0:T(8,128)}), f32[16,72,128]{2,1,0:T(8,128)S(1)}, u32[]{:S(2)}, u32[]{:S(2)}) async-start(f32[16,72,128]{2,1,0:T(8,128)} %get-tuple-element.16), calls=%async_computation.2 | async-start | bytes 1179648 | tf_op jit(solution)/shard_map/all_to_all | solution.py:469
  64.7 13.0 %collective-permute-start = (f32[1,2,32,128]{3,2,1,0:T(8,128)S(1)}, f32[1,2,32,128]{3,2,1,0:T(8,128)S(1)}, u32[]{:S(2)}, u32[]{:S(2)}) collective-permute-start(f32[1,2,32,128]{3,2,1,0:T(8,128)S(1)} %get-tuple-element.31), channel_id=1, source_target_pairs={{0,48},{16,64},{32,80},{48,96},{64,112},{80,128},{96,144},{112,160... | collective-permute-start | bytes 98312 | tf_op jit(solution)/shard_map/ppermute | solution.py:477
  69.1 16.2 %collective-permute-start.1 = (f32[2,2,32,128]{3,2,1,0:T(8,128)S(1)}, f32[2,2,32,128]{3,2,1,0:T(8,128)S(1)}, u32[]{:S(2)}, u32[]{:S(2)}) collective-permute-start(f32[2,2,32,128]{3,2,1,0:T(8,128)S(1)} %get-tuple-element.19.refs_6_.refs_5_), channel_id=1, source_target_pairs={{0,32},{16,48},{32,64},{48,80},{64,96},{80,112},{96,128},{112,144}... | collective-permute-start | bytes 196616 | tf_op jit(solution)/shard_map/ppermute | solution.py:477
  71.4 13.8 %collective-permute-start.2 = (f32[2,2,32,128]{3,2,1,0:T(8,128)S(1)}, f32[2,2,32,128]{3,2,1,0:T(8,128)S(1)}, u32[]{:S(2)}, u32[]{:S(2)}) collective-permute-start(f32[2,2,32,128]{3,2,1,0:T(8,128)S(1)} %get-tuple-element.19.refs_6_.refs_5_), channel_id=1, source_target_pairs={{0,16},{16,32},{32,48},{48,64},{64,80},{80,96},{96,112},{112,128},... | collective-permute-start | bytes 196616 | tf_op jit(solution)/shard_map/ppermute | solution.py:477
  74.4 10.9 %collective-permute-start.3 = (f32[2,2,32,128]{3,2,1,0:T(8,128)S(1)}, f32[2,2,32,128]{3,2,1,0:T(8,128)S(1)}, u32[]{:S(2)}, u32[]{:S(2)}) collective-permute-start(f32[2,2,32,128]{3,2,1,0:T(8,128)S(1)} %get-tuple-element.19.refs_6_.refs_5_), channel_id=1, source_target_pairs={{16,0},{32,16},{48,32},{64,48},{80,64},{96,80},{112,96},{128,112},... | collective-permute-start | bytes 196616 | tf_op jit(solution)/shard_map/ppermute | solution.py:477
  76.3 8.9 %collective-permute-start.4 = (f32[2,2,32,128]{3,2,1,0:T(8,128)S(1)}, f32[2,2,32,128]{3,2,1,0:T(8,128)S(1)}, u32[]{:S(2)}, u32[]{:S(2)}) collective-permute-start(f32[2,2,32,128]{3,2,1,0:T(8,128)S(1)} %get-tuple-element.19.refs_6_.refs_5_), channel_id=1, source_target_pairs={{32,0},{48,16},{64,32},{80,48},{96,64},{112,80},{128,96},{144,112}... | collective-permute-start | bytes 196616 | tf_op jit(solution)/shard_map/ppermute | solution.py:477
  77.7 7.6 %collective-permute-start.5 = (f32[1,2,32,128]{3,2,1,0:T(8,128)S(1)}, f32[1,2,32,128]{3,2,1,0:T(8,128)S(1)}, u32[]{:S(2)}, u32[]{:S(2)}) collective-permute-start(f32[1,2,32,128]{3,2,1,0:T(8,128)S(1)} %get-tuple-element.30), channel_id=1, source_target_pairs={{48,0},{64,16},{80,32},{96,48},{112,64},{128,80},{144,96},{160,112... | collective-permute-start | bytes 98312 | tf_op jit(solution)/shard_map/ppermute | solution.py:477
  113.2 14.9 %copy-start.6 = (bf16[2,32,3,3,3]{1,0,4,3,2:T(2,128)(2,1)S(1)}, bf16[2,32,3,3,3]{1,0,4,3,2:T(2,128)(2,1)}, u32[]{:S(2)}) copy-start(bf16[2,32,3,3,3]{1,0,4,3,2:T(2,128)(2,1)} %param.15) | copy-start | bytes 10372
  115.7 27.7 %copy-start.4 = (bf16[3,32,32,3,3,3]{2,1,5,4,3,0:T(8,128)(2,1)S(1)}, bf16[3,32,32,3,3,3]{2,1,5,4,3,0:T(8,128)(2,1)}, u32[]{:S(2)}) copy-start(bf16[3,32,32,3,3,3]{2,1,5,4,3,0:T(8,128)(2,1)} %param.14) | copy-start | bytes 497668
  115.7 18.4 %collective-permute-start.7 = (f32[2,2,32,128]{3,2,1,0:T(8,128)S(1)}, f32[2,2,32,128]{3,2,1,0:T(8,128)S(1)}, u32[]{:S(2)}, u32[]{:S(2)}) collective-permute-start(f32[2,2,32,128]{3,2,1,0:T(8,128)S(1)} %get-tuple-element.24.refs_4_.refs_12_), channel_id=1, source_target_pairs={{0,32},{16,48},{32,64},{48,80},{64,96},{80,112},{96,128},{112,144}... | collective-permute-start | bytes 196616 | tf_op jit(solution)/shard_map/ppermute | solution.py:477
  117.1 17.0 %collective-permute-start.8 = (f32[2,2,32,128]{3,2,1,0:T(8,128)S(1)}, f32[2,2,32,128]{3,2,1,0:T(8,128)S(1)}, u32[]{:S(2)}, u32[]{:S(2)}) collective-permute-start(f32[2,2,32,128]{3,2,1,0:T(8,128)S(1)} %get-tuple-element.24.refs_4_.refs_12_), channel_id=1, source_target_pairs={{0,16},{16,32},{32,48},{48,64},{64,80},{80,96},{96,112},{112,128},... | collective-permute-start | bytes 196616 | tf_op jit(solution)/shard_map/ppermute | solution.py:477
  123.4 12.9 %all-to-all-start.4 = ((f32[16,8,128]{2,1,0:T(8,128)}), f32[16,8,128]{2,1,0:T(8,128)S(1)}, u32[]{:S(2)}, u32[]{:S(2)}) async-start(f32[16,8,128]{2,1,0:T(8,128)} %get-tuple-element.23), calls=%async_computation.4 | async-start | bytes 131072 | tf_op jit(solution)/shard_map/all_to_all | solution.py:469
  126.9 5.9 %collective-permute-start.6 = (f32[1,2,32,128]{3,2,1,0:T(8,128)S(1)}, f32[1,2,32,128]{3,2,1,0:T(8,128)S(1)}, u32[]{:S(2)}, u32[]{:S(2)}) collective-permute-start(f32[1,2,32,128]{3,2,1,0:T(8,128)S(1)} %get-tuple-element.29), channel_id=1, source_target_pairs={{0,48},{16,64},{32,80},{48,96},{64,112},{80,128},{96,144},{112,160... | collective-permute-start | bytes 98312 | tf_op jit(solution)/shard_map/ppermute | solution.py:477
  128.4 15.8 %collective-permute-start.9 = (f32[2,2,32,128]{3,2,1,0:T(8,128)S(1)}, f32[2,2,32,128]{3,2,1,0:T(8,128)S(1)}, u32[]{:S(2)}, u32[]{:S(2)}) collective-permute-start(f32[2,2,32,128]{3,2,1,0:T(8,128)S(1)} %get-tuple-element.24.refs_4_.refs_12_), channel_id=1, source_target_pairs={{16,0},{32,16},{48,32},{64,48},{80,64},{96,80},{112,96},{128,112},... | collective-permute-start | bytes 196616 | tf_op jit(solution)/shard_map/ppermute | solution.py:477
  131.5 12.7 %collective-permute-start.10 = (f32[2,2,32,128]{3,2,1,0:T(8,128)S(1)}, f32[2,2,32,128]{3,2,1,0:T(8,128)S(1)}, u32[]{:S(2)}, u32[]{:S(2)}) collective-permute-start(f32[2,2,32,128]{3,2,1,0:T(8,128)S(1)} %get-tuple-element.24.refs_4_.refs_12_), channel_id=1, source_target_pairs={{32,0},{48,16},{64,32},{80,48},{96,64},{112,80},{128,96},{144,112}... | collective-permute-start | bytes 196616 | tf_op jit(solution)/shard_map/ppermute | solution.py:477
  132.8 11.4 %collective-permute-start.11 = (f32[1,2,32,128]{3,2,1,0:T(8,128)S(1)}, f32[1,2,32,128]{3,2,1,0:T(8,128)S(1)}, u32[]{:S(2)}, u32[]{:S(2)}) collective-permute-start(f32[1,2,32,128]{3,2,1,0:T(8,128)S(1)} %get-tuple-element.28), channel_id=1, source_target_pairs={{48,0},{64,16},{80,32},{96,48},{112,64},{128,80},{144,96},{160,112... | collective-permute-start | bytes 98312 | tf_op jit(solution)/shard_map/ppermute | solution.py:477
  136.9 11.5 %all-to-all-start.5 = ((f32[16,8,128]{2,1,0:T(8,128)}), f32[16,8,128]{2,1,0:T(8,128)S(1)}, u32[]{:S(2)}, u32[]{:S(2)}) async-start(f32[16,8,128]{2,1,0:T(8,128)} %shard_map.109), calls=%async_computation.5 | async-start | bytes 131072 | tf_op jit(solution)/shard_map/all_to_all | solution.py:469
  142.5 0.7 copy-start.7

commit v4 on v3

--- a/solution.py
+++ b/solution.py
@@ -13,6 +13,7 @@
 HALO = 5
 SIDE = 8
 GROUP = 2
+AHEAD = 3
 F32 = jnp.float32
 BF16 = jnp.bfloat16
 VMEM_BYTES = 20 * 1024 * 1024
@@ -122,7 +123,7 @@
 
     def one(a, p):
         start = (2 * a + p) * rows
-        return blocks_ref[:, start : start + rows, :].reshape(count * rows, columns)
+        return blocks_ref[:, start : start + rows, :].astype(F32).reshape(count * rows, columns)
 
     return [[one(a, p) for p in range(2)] for a in range(2)]
 
@@ -238,14 +239,6 @@
         out_ref[k, 64:72, :] = energies
 
 
-def image_kernel(blocks_ref, rhs_rows_ref, norms_ref, copies_ref, sums_ref):
-    total = jnp.sum(blocks_ref[...], axis=0)
-    rows = total[:64] + LAMBDA * rhs_rows_ref[...]
-    for k in range(blocks_ref.shape[0]):
-        copies_ref[k] = rows
-    sums_ref[...] = tile_of([norms_ref[0:1, :], total[64:65]])
-
-
 def lane_sum(values):
     return jnp.sum(values, axis=-1, keepdims=True)
 
@@ -255,22 +248,27 @@
     return jnp.where(curved > 0.0, norm / jnp.where(curved > 0.0, curved, 1.0), 1.0)
 
 
-def last_kernel(
-    at_ref, sums_ref, blocks_ref, rhs_ref, spectrum_ref, mask_ref, maps_ref, rows_ref, columns_ref, out_ref, near_ref
-):
-    store_near(near_ref, blocks_ref, at_ref[0])
-    norm, energy = sums_ref[0:1, :], sums_ref[1:2, :]
-    step = slab_step(lane_sum(norm), lane_sum(energy))
-    image = load_image(blocks_ref)
-    rhs = load_image(rhs_ref)
-    field = dft_columns(coil_field(maps_ref, image), columns_ref, -1.0)
+def image_kernel(blocks_ref, rhs_rows_ref, norms_ref, copies_ref, rows_ref, sums_ref):
+    total = jnp.sum(blocks_ref[...], axis=0)
+    rhs = rhs_rows_ref[...]
+    image = total[:64] + LAMBDA * rhs
+    norm, energy = norms_ref[0:1, :], total[64:65]
+    residual = rhs - slab_step(lane_sum(norm), lane_sum(energy)) * image
+    for a in range(2):
+        for p in range(2):
+            rows_ref[p, a] = image[(2 * a + p) * 16 : (2 * a + p + 1) * 16]
+    rounded = residual.astype(BF16)
+    for k in range(blocks_ref.shape[0]):
+        copies_ref[k] = rounded
+    share = 1.0 / blocks_ref.shape[0]
+    sums_ref[...] = tile_of([row_sum(residual * residual), row_sum(residual * rhs), share * norm, share * energy])
+
+
+def last_kernel(sums_ref, blocks_ref, spectrum_ref, mask_ref, maps_ref, rows_ref, columns_ref, out_ref):
+    field = dft_columns(coil_field(maps_ref, load_image(blocks_ref)), columns_ref, -1.0)
     spectrum = masked(dft_rows(field, rows_ref, -1.0), mask_ref)
     before = [[spectrum_ref[a, p] for p in range(2)] for a in range(2)]
-    residual = [[rhs[a][p] - step * image[a][p] for p in range(2)] for a in range(2)]
-    spectrum = [[before[a][p] - step * spectrum[a][p] for p in range(2)] for a in range(2)]
-    share = 1.0 / out_ref.shape[0]
-    local = [inner(residual, residual), inner(residual, rhs), norm, energy]
-    tile = tile_of([inner(spectrum, spectrum), inner(spectrum, before)] + [share * value for value in local])
+    tile = tile_of([inner(spectrum, spectrum), inner(spectrum, before)] + [sums_ref[i : i + 1, :] for i in range(4)])
     for k in range(out_ref.shape[0]):
         out_ref[k] = tile
 
@@ -469,6 +467,13 @@
     return lax.all_to_all(blocks, axis, 0, 0, tiled=True)
 
 
+def near_rows(rows):
+    count = lax.axis_size("coil")
+    before = lax.ppermute(rows[:, :, SIDE:], "coil", [(i, i + 1) for i in range(count - 1)])
+    after = lax.ppermute(rows[:, :, :SIDE], "coil", [(i + 1, i) for i in range(count - 1)])
+    return jnp.concatenate([before, rows, after], axis=2)
+
+
 def near_planes(near):
     count = lax.axis_size("slab")
 
@@ -505,21 +510,20 @@
         in_smem=(0,),
     )
     rhs_parts = near_planes(rhs_near)
-    copies, sums = call(
+    copies, image_rows, sums = call(
         image_kernel,
-        (struct((coils, 64, 128)), struct((8, 128))),
+        (struct((coils, 64, 128), BF16), struct((2, 2, 16, 128)), struct((8, 128))),
         (swap(term, "coil"), rhs_rows, norms),
         after=rhs_parts,
     )
-    image = swap(copies, "coil")
-    tiles, image_near = call(
+    image_parts = near_planes(near_rows(image_rows))
+    tiles = call(
         last_kernel,
-        (struct((coils, 8, 128)), near_shape),
-        (at, sums, image, rhs, spectrum, sampling, maps, rows, columns),
-        in_smem=(0,),
-    )
-    image_parts = near_planes(image_near)
-    tiles = call(spread_kernel, struct((slabs, 8, 128)), (swap(tiles, "coil"),), after=image_parts[:4])
+        struct((coils, 8, 128)),
+        (sums, swap(copies, "coil"), spectrum, sampling, maps, rows, columns),
+        after=image_parts[:AHEAD],
+    )
+    tiles = call(spread_kernel, struct((slabs, 8, 128)), (swap(tiles, "coil"),), after=image_parts[AHEAD:])
     last = swap(tiles, "slab")
     scratch = [pltpu.VMEM((12, 144, 256), BF16)]
     scratch += [pltpu.VMEM((10 - 2 * m, (16 - 2 * m) * 32, 256), BF16) for m in range(4)]

time: 160 us -> 163 us (1.019)
  starting transfers between devices: 47.5 us -> 75.5 us
  blocking collectives: 56.8 us -> 28.9 us
  waiting for transfers between devices: 29.9 us -> 33.6 us
    all_to_all x2 -> x1, blocking collectives: 56.8 us -> 28.9 us  [swap(): return lax.all_to_all(blocks, axis, 0, 0, tiled=True)]
    all_to_all x4 -> x5, starting transfers between devices: 18.6 us -> 33.2 us  [swap(): return lax.all_to_all(blocks, axis, 0, 0, tiled=True)]
    ppermute x12, starting transfers between devices: 28.9 us -> 36.1 us  [shifted(): return lax.ppermute(part, 'slab', pairs)]
    ppermute x0 -> x2, starting transfers between devices: none -> 6.21 us  [the longest x1 4.92 us: near_rows(): lax.ppermute(rows[:, :, SIDE:], 'coil', [(i, i + 1) for i in range(count...]
    ppermute x0 -> x2, waiting for transfers between devices: none -> 4.66 us  [the longest x1 4.65 us: near_rows(): lax.ppermute(rows[:, :, :SIDE], 'coil', [(i + 1, i) for i in range(count...]
    all_to_all x4 -> x5, waiting for transfers between devices: 23.5 us -> 22.2 us  [swap(): return lax.all_to_all(blocks, axis, 0, 0, tiled=True)]
  transfers between devices with their start and end apart: 16 -> 19, of which waited for: 4 -> 6; matrix products, arithmetic and copies ran while one was open for 0% -> 0% of each run, Pallas kernels for 1% -> 0%
where the time goes in v4:
time: 163 us; the launch traced here: 162 us
  starting transfers between devices  75.5 us (46%)
  waiting for transfers between devices  33.6 us (21%)
  blocking collectives  28.9 us (18%)
  Pallas kernels  22.5 us (14%)
    ppermute x12, starting transfers between devices, shifted(): return lax.ppermute(part, 'slab', pairs)  36.1 us
    all_to_all x5, starting transfers between devices, swap(): return lax.all_to_all(blocks, axis, 0, 0, tiled=True)  33.2 us
    all_to_all x1, blocking collectives, swap(): return lax.all_to_all(blocks, axis, 0, 0, tiled=True)  28.9 us
    all_to_all x5, waiting for transfers between devices, swap(): return lax.all_to_all(blocks, axis, 0, 0, tiled=True)  22.2 us
    pallas_call x7, Pallas kernels, call(): pl.pallas_call(kernel, out_shape=out_shape, in_specs=specs, out_specs=out...  18.9 us
    ppermute x12, waiting for transfers between devices, shifted(): return lax.ppermute(part, 'slab', pairs)  6.78 us
    ppermute x1, starting transfers between devices, near_rows(): lax.ppermute(rows[:, :, SIDE:], 'coil', [(i, i + 1) for i in range(count...  4.92 us
    ppermute x1, waiting for transfers between devices, near_rows(): lax.ppermute(rows[:, :, :SIDE], 'coil', [(i + 1, i) for i in range(count...  4.65 us
  transfers between devices with their start and end apart: 19, of which 6 were waited for; matrix products, arithmetic and copies ran while one was open for 0% of the time, Pallas kernels for 0%

profile of v4, /device:TPU:1, one launch (start us, length us, event | category | flops | bytes accessed | tf_op | source)
XLA Modules:
  0.0 161.9 jit_solution(7992317176027601282)
XLA Ops:
  0.6 3.6 %shard_map.104 = f32[16,64,128]{2,1,0:T(8,128)} custom-call(s32[2,256,128]{2,1,0:T(8,128)} %refs_3_.1, f32[2,2,256,128]{3,2,1,0:T(8,128)} %bitcast.12, bf16[512,512]{1,0:T(8,128)(2,1)} %constant.14.clone.rows_hbm.rows_ref.refs_5_, bf16[128,512]{1,0:T(8,128)(2,1)} %constant.15.clone.columns_hbm.columns_ref.refs_6_, f32[2,2,256,128]{3,2,1,0:T(8,128)} %bitcast.8), custom_call_target="tpu_custom_call" | custom-call | tf_op jit(solution)/shard_map/pallas_call | solution.py:204
  4.2 28.9 %all_to_all.30.blocks_ref = f32[16,64,128]{2,1,0:T(8,128)S(1)} all-to-all(f32[16,64,128]{2,1,0:T(8,128)} %shard_map.104), channel_id=1, replica_groups=mesh['slab'=16,'coil'=16] {'coil'}, dimensions={0} | all-to-all | bytes 1048576 | tf_op jit(solution)/shard_map/all_to_all | solution.py:467
  33.1 0.9 shard_map.105
  34.0 4.9 %all-to-all-start.1 = ((f32[16,64,128]{2,1,0:T(8,128)}), f32[16,64,128]{2,1,0:T(8,128)S(1)}, u32[]{:S(2)}, u32[]{:S(2)}) async-start(f32[16,64,128]{2,1,0:T(8,128)} %get-tuple-element.14), calls=%async_computation.1 | async-start | bytes 1048576 | tf_op jit(solution)/shard_map/all_to_all | solution.py:467
  39.0 17.1 %all-to-all-done.1.blocks_ref = f32[16,64,128]{2,1,0:T(8,128)S(1)} async-done(((f32[16,64,128]{2,1,0:T(8,128)}), f32[16,64,128]{2,1,0:T(8,128)S(1)}, u32[]{:S(2)}, u32[]{:S(2)}) %all-to-all-start.1) | async-done | bytes 524320 | tf_op jit(solution)/shard_map/all_to_all | solution.py:467
  56.1 3.9 %shard_map.106 = (f32[16,72,128]{2,1,0:T(8,128)}, f32[2,2,256,128]{3,2,1,0:T(8,128)S(1)}, f32[8,128]{1,0:T(8,128)S(1)}, f32[2,2,32,128]{3,2,1,0:T(8,128)S(1)}) custom-call(s32[2]{0:T(128)S(1)} %pad_add_fusion.at_ref.refs_0_, f32[16,64,128]{2,1,0:T(8,128)S(1)} %all-to-all-done.1.blocks_ref, s32[2,256,128]{2,1,0:T(8,128)S(1)} %copy-done.2, ...), custom_call_target="tpu_custom_call" | custom-call | tf_op jit(solution)/shard_map/pallas_call | solution.py:34
  60.0 4.6 %all-to-all-start.2 = ((f32[16,72,128]{2,1,0:T(8,128)}), f32[16,72,128]{2,1,0:T(8,128)S(1)}, u32[]{:S(2)}, u32[]{:S(2)}) async-start(f32[16,72,128]{2,1,0:T(8,128)} %get-tuple-element.15), calls=%async_computation.2 | async-start | bytes 1179648 | tf_op jit(solution)/shard_map/all_to_all | solution.py:467
  64.7 1.3 collective-permute-start.5
  66.0 1.3 collective-permute-start.4
  67.3 3.3 %collective-permute-start.3 = (f32[2,2,32,128]{3,2,1,0:T(8,128)S(1)}, f32[2,2,32,128]{3,2,1,0:T(8,128)S(1)}, u32[]{:S(2)}, u32[]{:S(2)}) collective-permute-start(f32[2,2,32,128]{3,2,1,0:T(8,128)S(1)} %get-tuple-element.18.refs_6_.refs_5_), channel_id=1, source_target_pairs={{16,0},{32,16},{48,32},{64,48},{80,64},{96,80},{112,96},{128,112},... | collective-permute-start | bytes 196616 | tf_op jit(solution)/shard_map/ppermute | solution.py:482
  70.6 4.2 %collective-permute-start.2 = (f32[2,2,32,128]{3,2,1,0:T(8,128)S(1)}, f32[2,2,32,128]{3,2,1,0:T(8,128)S(1)}, u32[]{:S(2)}, u32[]{:S(2)}) collective-permute-start(f32[2,2,32,128]{3,2,1,0:T(8,128)S(1)} %get-tuple-element.18.refs_6_.refs_5_), channel_id=1, source_target_pairs={{0,16},{16,32},{32,48},{48,64},{64,80},{80,96},{96,112},{112,128},... | collective-permute-start | bytes 196616 | tf_op jit(solution)/shard_map/ppermute | solution.py:482
  74.8 4.9 %collective-permute-start.1 = (f32[2,2,32,128]{3,2,1,0:T(8,128)S(1)}, f32[2,2,32,128]{3,2,1,0:T(8,128)S(1)}, u32[]{:S(2)}, u32[]{:S(2)}) collective-permute-start(f32[2,2,32,128]{3,2,1,0:T(8,128)S(1)} %get-tuple-element.18.refs_6_.refs_5_), channel_id=1, source_target_pairs={{0,32},{16,48},{32,64},{48,80},{64,96},{80,112},{96,128},{112,144}... | collective-permute-start | bytes 196616 | tf_op jit(solution)/shard_map/ppermute | solution.py:482
  79.7 2.5 %collective-permute-start = (f32[1,2,32,128]{3,2,1,0:T(8,128)S(1)}, f32[1,2,32,128]{3,2,1,0:T(8,128)S(1)}, u32[]{:S(2)}, u32[]{:S(2)}) collective-permute-start(f32[1,2,32,128]{3,2,1,0:T(8,128)S(1)} %get-tuple-element.29), channel_id=1, source_target_pairs={{0,48},{16,64},{32,80},{48,96},{64,112},{80,128},{96,144},{112,160... | collective-permute-start | bytes 98312 | tf_op jit(solution)/shard_map/ppermute | solution.py:482
  82.2 1.0 collective-permute-done.refs_3_.refs_2_
  83.2 0.8 shard_map.107
  84.0 4.9 %collective-permute-start.6 = (f32[2,2,8,128]{3,2,1,0:T(8,128)S(1)}, f32[2,2,8,128]{3,2,1,0:T(8,128)S(1)}, u32[]{:S(2)}, u32[]{:S(2)}) collective-permute-start(f32[2,2,8,128]{3,2,1,0:T(8,128)S(1)} %get-tuple-element.31), channel_id=1, source_target_pairs={{0,1},{1,2},{2,3},{3,4},{4,5},{5,6},{6,7},{7,8},{8,9},{9,10},{10,1... | collective-permute-start | bytes 49160 | tf_op jit(solution)/shard_map/ppermute | solution.py:472
  89.0 6.5 %all-to-all-start.3 = ((bf16[16,64,128]{2,1,0:T(8,128)(2,1)}), bf16[16,64,128]{2,1,0:T(8,128)(2,1)S(1)}, u32[]{:S(2)}, u32[]{:S(2)}) async-start(bf16[16,64,128]{2,1,0:T(8,128)(2,1)} %get-tuple-element.20), calls=%async_computation.3 | async-start | bytes 524288 | tf_op jit(solution)/shard_map/all_to_all | solution.py:467
  95.5 1.3 collective-permute-start.7
  96.8 4.7 %collective-permute-done.7 = f32[2,2,8,128]{3,2,1,0:T(8,128)S(1)} collective-permute-done((f32[2,2,8,128]{3,2,1,0:T(8,128)S(1)}, f32[2,2,8,128]{3,2,1,0:T(8,128)S(1)}, u32[]{:S(2)}, u32[]{:S(2)}) %collective-permute-start.7) | collective-permute-done | bytes 16416 | tf_op jit(solution)/shard_map/ppermute | solution.py:473
  101.5 6.7 %collective-permute-start.10 = (f32[2,2,32,128]{3,2,1,0:T(8,128)S(1)}, f32[2,2,32,128]{3,2,1,0:T(8,128)S(1)}, u32[]{:S(2)}, u32[]{:S(2)}) collective-permute-start(f32[2,2,32,128]{3,2,1,0:T(8,128)S(1)} %constant_dynamic-update-slice_fusion.refs_1_.refs_12_), channel_id=1, source_target_pairs={{0,16},{16,32},{32,48},{48,64},{64,80},{80,96},{96,112},{112,128},... | collective-permute-start | bytes 196616 | tf_op jit(solution)/shard_map/ppermute | solution.py:482
  108.2 2.9 %collective-permute-start.9 = (f32[2,2,32,128]{3,2,1,0:T(8,128)S(1)}, f32[2,2,32,128]{3,2,1,0:T(8,128)S(1)}, u32[]{:S(2)}, u32[]{:S(2)}) collective-permute-start(f32[2,2,32,128]{3,2,1,0:T(8,128)S(1)} %constant_dynamic-update-slice_fusion.refs_1_.refs_12_), channel_id=1, source_target_pairs={{0,32},{16,48},{32,64},{48,80},{64,96},{80,112},{96,128},{112,144}... | collective-permute-start | bytes 196616 | tf_op jit(solution)/shard_map/ppermute | solution.py:482
  111.2 2.4 %collective-permute-start.8 = (f32[1,2,32,128]{3,2,1,0:T(8,128)S(1)}, f32[1,2,32,128]{3,2,1,0:T(8,128)S(1)}, u32[]{:S(2)}, u32[]{:S(2)}) collective-permute-start(f32[1,2,32,128]{3,2,1,0:T(8,128)S(1)} %get-tuple-element.27), channel_id=1, source_target_pairs={{0,48},{16,64},{32,80},{48,96},{64,112},{80,128},{96,144},{112,160... | collective-permute-start | bytes 98312 | tf_op jit(solution)/shard_map/ppermute | solution.py:482
  113.6 1.0 collective-permute-done.8.refs_7_.refs_9_
  114.6 1.7 %shard_map.108 = f32[16,8,128]{2,1,0:T(8,128)} custom-call(f32[8,128]{1,0:T(8,128)S(1)} %get-tuple-element.19.refs_0_, bf16[16,64,128]{2,1,0:T(8,128)(2,1)S(1)} %all-to-all-done.3.refs_1_, f32[2,2,256,128]{3,2,1,0:T(8,128)S(1)} %get-tuple-element.21.refs_2_, s32[2,256,128]{2,1,0:T(8,128)S(1)} %copy-done.2, f32[2,2,256,128]{3,2,1,0:T(8,128)S(1)} %bitcast.10, ...), custom_call_target="tpu_custom_call" | custom-call | tf_op jit(solution)/shard_map/pallas_call | solution.py:34
  116.3 10.9 %all-to-all-start.4 = ((f32[16,8,128]{2,1,0:T(8,128)}), f32[16,8,128]{2,1,0:T(8,128)S(1)}, u32[]{:S(2)}, u32[]{:S(2)}) async-start(f32[16,8,128]{2,1,0:T(8,128)} %shard_map.108), calls=%async_computation.4 | async-start | bytes 131072 | tf_op jit(solution)/shard_map/all_to_all | solution.py:467
  127.2 1.3 collective-permute-start.12
  128.5 4.0 %collective-permute-start.11 = (f32[2,2,32,128]{3,2,1,0:T(8,128)S(1)}, f32[2,2,32,128]{3,2,1,0:T(8,128)S(1)}, u32[]{:S(2)}, u32[]{:S(2)}) collective-permute-start(f32[2,2,32,128]{3,2,1,0:T(8,128)S(1)} %constant_dynamic-update-slice_fusion.refs_1_.refs_12_), channel_id=1, source_target_pairs={{16,0},{32,16},{48,32},{64,48},{80,64},{96,80},{112,96},{128,112},... | collective-permute-start | bytes 196616 | tf_op jit(solution)/shard_map/ppermute | solution.py:482
  132.5 1.3 collective-permute-start.13
  134.1 4.8 %collective-permute-done.13.refs_4_.refs_15_ = f32[1,2,32,128]{3,2,1,0:T(8,128)S(1)} collective-permute-done((f32[1,2,32,128]{3,2,1,0:T(8,128)S(1)}, f32[1,2,32,128]{3,2,1,0:T(8,128)S(1)}, u32[]{:S(2)}, u32[]{:S(2)}) %collective-permute-start.13) | collective-permute-done | bytes 32800 | tf_op jit(solution)/shard_map/ppermute | solution.py:482
  139.5 6.2 %all-to-all-start.5 = ((f32[16,8,128]{2,1,0:T(8,128)}), f32[16,8,128]{2,1,0:T(8,128)S(1)}, u32[]{:S(2)}, u32[]{:S(2)}) async-start(f32[16,8,128]{2,1,0:T(8,128)} %shard_map.109), calls=%async_computation.5 | async-start | bytes 131072 | tf_op jit(solution)/shard_map/all_to_all | solution.py:467
  146.5 5.1 %all-to-all-done.5.refs_1_ = f32[16,8,128]{2,1,0:T(8,128)S(1)} async-done(((f32[16,8,128]{2,1,0:T(8,128)}), f32[16,8,128]{2,1,0:T(8,128)S(1)}, u32[]{:S(2)}, u32[]{:S(2)}) %all-to-all-start.5) | async-done | bytes 65568 | tf_op jit(solution)/shard_map/all_to_all | solution.py:467
  151.6 10.3 %shard_map.111 = (f32[2,2,16,128]{3,2,1,0:T(8,128)}, f32[2,2,16,128]{3,2,1,0:T(8,128)}) custom-call(s32[2]{0:T(128)S(1)} %pad_add_fusion.at_ref.refs_0_, f32[16,8,128]{2,1,0:T(8,128)S(1)} %all-to-all-done.5.refs_1_, f32[1,2,32,128]{3,2,1,0:T(8,128)S(1)} %collective-permute-done.refs_3_.refs_2_, f32[2,2,32,128]{3,2,1,0:T(8,128)S(1)} %collective-permute-done.1.refs_4_.refs_3_, ...), custom_call_target="tpu_custom_call" | custom-call | tf_op jit(solution)/shard_map/pallas_call | solution.py:34
  (45 shorter events, 1.9 us)
Async XLA Ops:
  4.2 28.9 %copy-start.5 = (f32[2,2,16,128]{3,2,1,0:T(8,128)S(1)}, f32[2,2,16,128]{3,2,1,0:T(8,128)}, u32[]{:S(2)}) copy-start(f32[2,2,16,128]{3,2,1,0:T(8,128)} %prior_ref.1) | copy-start | bytes 98308
  33.1 23.0 %copy-start.2 = (s32[2,256,128]{2,1,0:T(8,128)S(1)}, s32[2,256,128]{2,1,0:T(8,128)}, u32[]{:S(2)}) copy-start(s32[2,256,128]{2,1,0:T(8,128)} %refs_3_.1) | copy-start | bytes 786436
  33.1 23.0 %copy-start.3 = (bf16[128,512]{1,0:T(8,128)(2,1)S(1)}, bf16[128,512]{1,0:T(8,128)(2,1)}, u32[]{:S(2)}) copy-start(bf16[128,512]{1,0:T(8,128)(2,1)} %constant.15.clone.columns_hbm.columns_ref.refs_6_) | copy-start | bytes 393220
  34.0 22.1 %copy-start = (f32[1,2,2,256,128]{4,3,2,1,0:T(8,128)S(1)}, f32[1,2,2,256,128]{4,3,2,1,0:T(8,128)}, u32[]{:S(2)}) copy-start(f32[1,2,2,256,128]{4,3,2,1,0:T(8,128)} %param.9) | copy-start | bytes 1572868
  34.0 22.1 %copy-start.1 = (bf16[512,512]{1,0:T(8,128)(2,1)S(1)}, bf16[512,512]{1,0:T(8,128)(2,1)}, u32[]{:S(2)}) copy-start(bf16[512,512]{1,0:T(8,128)(2,1)} %constant.14.clone.rows_hbm.rows_ref.refs_5_) | copy-start | bytes 1572868
  34.0 22.1 %all-to-all-start.1 = ((f32[16,64,128]{2,1,0:T(8,128)}), f32[16,64,128]{2,1,0:T(8,128)S(1)}, u32[]{:S(2)}, u32[]{:S(2)}) async-start(f32[16,64,128]{2,1,0:T(8,128)} %get-tuple-element.14), calls=%async_computation.1 | async-start | bytes 1048576 | tf_op jit(solution)/shard_map/all_to_all | solution.py:467
  60.0 23.2 %all-to-all-start.2 = ((f32[16,72,128]{2,1,0:T(8,128)}), f32[16,72,128]{2,1,0:T(8,128)S(1)}, u32[]{:S(2)}, u32[]{:S(2)}) async-start(f32[16,72,128]{2,1,0:T(8,128)} %get-tuple-element.15), calls=%async_computation.2 | async-start | bytes 1179648 | tf_op jit(solution)/shard_map/all_to_all | solution.py:467
  64.7 15.0 %collective-permute-start.5 = (f32[1,2,32,128]{3,2,1,0:T(8,128)S(1)}, f32[1,2,32,128]{3,2,1,0:T(8,128)S(1)}, u32[]{:S(2)}, u32[]{:S(2)}) collective-permute-start(f32[1,2,32,128]{3,2,1,0:T(8,128)S(1)} %get-tuple-element.28), channel_id=1, source_target_pairs={{48,0},{64,16},{80,32},{96,48},{112,64},{128,80},{144,96},{160,112... | collective-permute-start | bytes 98312 | tf_op jit(solution)/shard_map/ppermute | solution.py:482
  66.0 17.2 %collective-permute-start.4 = (f32[2,2,32,128]{3,2,1,0:T(8,128)S(1)}, f32[2,2,32,128]{3,2,1,0:T(8,128)S(1)}, u32[]{:S(2)}, u32[]{:S(2)}) collective-permute-start(f32[2,2,32,128]{3,2,1,0:T(8,128)S(1)} %get-tuple-element.18.refs_6_.refs_5_), channel_id=1, source_target_pairs={{32,0},{48,16},{64,32},{80,48},{96,64},{112,80},{128,96},{144,112}... | collective-permute-start | bytes 196616 | tf_op jit(solution)/shard_map/ppermute | solution.py:482
  67.3 15.9 %collective-permute-start.3 = (f32[2,2,32,128]{3,2,1,0:T(8,128)S(1)}, f32[2,2,32,128]{3,2,1,0:T(8,128)S(1)}, u32[]{:S(2)}, u32[]{:S(2)}) collective-permute-start(f32[2,2,32,128]{3,2,1,0:T(8,128)S(1)} %get-tuple-element.18.refs_6_.refs_5_), channel_id=1, source_target_pairs={{16,0},{32,16},{48,32},{64,48},{80,64},{96,80},{112,96},{128,112},... | collective-permute-start | bytes 196616 | tf_op jit(solution)/shard_map/ppermute | solution.py:482
  70.6 12.6 %collective-permute-start.2 = (f32[2,2,32,128]{3,2,1,0:T(8,128)S(1)}, f32[2,2,32,128]{3,2,1,0:T(8,128)S(1)}, u32[]{:S(2)}, u32[]{:S(2)}) collective-permute-start(f32[2,2,32,128]{3,2,1,0:T(8,128)S(1)} %get-tuple-element.18.refs_6_.refs_5_), channel_id=1, source_target_pairs={{0,16},{16,32},{32,48},{48,64},{64,80},{80,96},{96,112},{112,128},... | collective-permute-start | bytes 196616 | tf_op jit(solution)/shard_map/ppermute | solution.py:482
  74.8 8.4 %collective-permute-start.1 = (f32[2,2,32,128]{3,2,1,0:T(8,128)S(1)}, f32[2,2,32,128]{3,2,1,0:T(8,128)S(1)}, u32[]{:S(2)}, u32[]{:S(2)}) collective-permute-start(f32[2,2,32,128]{3,2,1,0:T(8,128)S(1)} %get-tuple-element.18.refs_6_.refs_5_), channel_id=1, source_target_pairs={{0,32},{16,48},{32,64},{48,80},{64,96},{80,112},{96,128},{112,144}... | collective-permute-start | bytes 196616 | tf_op jit(solution)/shard_map/ppermute | solution.py:482
  79.7 3.5 %collective-permute-start = (f32[1,2,32,128]{3,2,1,0:T(8,128)S(1)}, f32[1,2,32,128]{3,2,1,0:T(8,128)S(1)}, u32[]{:S(2)}, u32[]{:S(2)}) collective-permute-start(f32[1,2,32,128]{3,2,1,0:T(8,128)S(1)} %get-tuple-element.29), channel_id=1, source_target_pairs={{0,48},{16,64},{32,80},{48,96},{64,112},{80,128},{96,144},{112,160... | collective-permute-start | bytes 98312 | tf_op jit(solution)/shard_map/ppermute | solution.py:482
  84.0 12.8 %collective-permute-start.6 = (f32[2,2,8,128]{3,2,1,0:T(8,128)S(1)}, f32[2,2,8,128]{3,2,1,0:T(8,128)S(1)}, u32[]{:S(2)}, u32[]{:S(2)}) collective-permute-start(f32[2,2,8,128]{3,2,1,0:T(8,128)S(1)} %get-tuple-element.31), channel_id=1, source_target_pairs={{0,1},{1,2},{2,3},{3,4},{4,5},{5,6},{6,7},{7,8},{8,9},{9,10},{10,1... | collective-permute-start | bytes 49160 | tf_op jit(solution)/shard_map/ppermute | solution.py:472
  89.0 25.6 %all-to-all-start.3 = ((bf16[16,64,128]{2,1,0:T(8,128)(2,1)}), bf16[16,64,128]{2,1,0:T(8,128)(2,1)S(1)}, u32[]{:S(2)}, u32[]{:S(2)}) async-start(bf16[16,64,128]{2,1,0:T(8,128)(2,1)} %get-tuple-element.20), calls=%async_computation.3 | async-start | bytes 524288 | tf_op jit(solution)/shard_map/all_to_all | solution.py:467
  95.5 6.0 %collective-permute-start.7 = (f32[2,2,8,128]{3,2,1,0:T(8,128)S(1)}, f32[2,2,8,128]{3,2,1,0:T(8,128)S(1)}, u32[]{:S(2)}, u32[]{:S(2)}) collective-permute-start(f32[2,2,8,128]{3,2,1,0:T(8,128)S(1)} %get-tuple-element.30), channel_id=1, source_target_pairs={{1,0},{2,1},{3,2},{4,3},{5,4},{6,5},{7,6},{8,7},{9,8},{10,9},{11,1... | collective-permute-start | bytes 49160 | tf_op jit(solution)/shard_map/ppermute | solution.py:473
  101.5 13.1 %collective-permute-start.10 = (f32[2,2,32,128]{3,2,1,0:T(8,128)S(1)}, f32[2,2,32,128]{3,2,1,0:T(8,128)S(1)}, u32[]{:S(2)}, u32[]{:S(2)}) collective-permute-start(f32[2,2,32,128]{3,2,1,0:T(8,128)S(1)} %constant_dynamic-update-slice_fusion.refs_1_.refs_12_), channel_id=1, source_target_pairs={{0,16},{16,32},{32,48},{48,64},{64,80},{80,96},{96,112},{112,128},... | collective-permute-start | bytes 196616 | tf_op jit(solution)/shard_map/ppermute | solution.py:482
  108.2 6.4 %collective-permute-start.9 = (f32[2,2,32,128]{3,2,1,0:T(8,128)S(1)}, f32[2,2,32,128]{3,2,1,0:T(8,128)S(1)}, u32[]{:S(2)}, u32[]{:S(2)}) collective-permute-start(f32[2,2,32,128]{3,2,1,0:T(8,128)S(1)} %constant_dynamic-update-slice_fusion.refs_1_.refs_12_), channel_id=1, source_target_pairs={{0,32},{16,48},{32,64},{48,80},{64,96},{80,112},{96,128},{112,144}... | collective-permute-start | bytes 196616 | tf_op jit(solution)/shard_map/ppermute | solution.py:482
  111.2 3.4 %collective-permute-start.8 = (f32[1,2,32,128]{3,2,1,0:T(8,128)S(1)}, f32[1,2,32,128]{3,2,1,0:T(8,128)S(1)}, u32[]{:S(2)}, u32[]{:S(2)}) collective-permute-start(f32[1,2,32,128]{3,2,1,0:T(8,128)S(1)} %get-tuple-element.27), channel_id=1, source_target_pairs={{0,48},{16,64},{32,80},{48,96},{64,112},{80,128},{96,144},{112,160... | collective-permute-start | bytes 98312 | tf_op jit(solution)/shard_map/ppermute | solution.py:482
  114.6 19.3 %copy-start.6 = (bf16[32,2,3,3,3]{0,1,4,3,2:T(2,128)(2,1)S(1)}, bf16[32,2,3,3,3]{0,1,4,3,2:T(2,128)(2,1)}, u32[]{:S(2)}) copy-start(bf16[32,2,3,3,3]{0,1,4,3,2:T(2,128)(2,1)} %param.13) | copy-start | bytes 10372
  114.6 19.4 %copy-start.7 = (bf16[2,32,3,3,3]{1,0,4,3,2:T(2,128)(2,1)S(1)}, bf16[2,32,3,3,3]{1,0,4,3,2:T(2,128)(2,1)}, u32[]{:S(2)}) copy-start(bf16[2,32,3,3,3]{1,0,4,3,2:T(2,128)(2,1)} %param.15) | copy-start | bytes 10372
  116.3 29.5 %copy-start.4 = (bf16[3,32,32,3,3,3]{2,1,5,4,3,0:T(8,128)(2,1)S(1)}, bf16[3,32,32,3,3,3]{2,1,5,4,3,0:T(8,128)(2,1)}, u32[]{:S(2)}) copy-start(bf16[3,32,32,3,3,3]{2,1,5,4,3,0:T(8,128)(2,1)} %param.14) | copy-start | bytes 497668
  116.3 22.6 %all-to-all-start.4 = ((f32[16,8,128]{2,1,0:T(8,128)}), f32[16,8,128]{2,1,0:T(8,128)S(1)}, u32[]{:S(2)}, u32[]{:S(2)}) async-start(f32[16,8,128]{2,1,0:T(8,128)} %shard_map.108), calls=%async_computation.4 | async-start | bytes 131072 | tf_op jit(solution)/shard_map/all_to_all | solution.py:467
  127.2 11.7 %collective-permute-start.12 = (f32[2,2,32,128]{3,2,1,0:T(8,128)S(1)}, f32[2,2,32,128]{3,2,1,0:T(8,128)S(1)}, u32[]{:S(2)}, u32[]{:S(2)}) collective-permute-start(f32[2,2,32,128]{3,2,1,0:T(8,128)S(1)} %constant_dynamic-update-slice_fusion.refs_1_.refs_12_), channel_id=1, source_target_pairs={{32,0},{48,16},{64,32},{80,48},{96,64},{112,80},{128,96},{144,112}... | collective-permute-start | bytes 196616 | tf_op jit(solution)/shard_map/ppermute | solution.py:482
  128.5 10.4 %collective-permute-start.11 = (f32[2,2,32,128]{3,2,1,0:T(8,128)S(1)}, f32[2,2,32,128]{3,2,1,0:T(8,128)S(1)}, u32[]{:S(2)}, u32[]{:S(2)}) collective-permute-start(f32[2,2,32,128]{3,2,1,0:T(8,128)S(1)} %constant_dynamic-update-slice_fusion.refs_1_.refs_12_), channel_id=1, source_target_pairs={{16,0},{32,16},{48,32},{64,48},{80,64},{96,80},{112,96},{128,112},... | collective-permute-start | bytes 196616 | tf_op jit(solution)/shard_map/ppermute | solution.py:482
  132.5 6.3 %collective-permute-start.13 = (f32[1,2,32,128]{3,2,1,0:T(8,128)S(1)}, f32[1,2,32,128]{3,2,1,0:T(8,128)S(1)}, u32[]{:S(2)}, u32[]{:S(2)}) collective-permute-start(f32[1,2,32,128]{3,2,1,0:T(8,128)S(1)} %get-tuple-element.26), channel_id=1, source_target_pairs={{48,0},{64,16},{80,32},{96,48},{112,64},{128,80},{144,96},{160,112... | collective-permute-start | bytes 98312 | tf_op jit(solution)/shard_map/ppermute | solution.py:482
  139.5 12.1 %all-to-all-start.5 = ((f32[16,8,128]{2,1,0:T(8,128)}), f32[16,8,128]{2,1,0:T(8,128)S(1)}, u32[]{:S(2)}, u32[]{:S(2)}) async-start(f32[16,8,128]{2,1,0:T(8,128)} %shard_map.109), calls=%async_computation.5 | async-start | bytes 131072 | tf_op jit(solution)/shard_map/all_to_all | solution.py:467

commit v5 on v4

--- a/solution.py
+++ b/solution.py
@@ -13,7 +13,6 @@
 HALO = 5
 SIDE = 8
 GROUP = 2
-AHEAD = 3
 F32 = jnp.float32
 BF16 = jnp.bfloat16
 VMEM_BYTES = 20 * 1024 * 1024
@@ -123,7 +122,7 @@
 
     def one(a, p):
         start = (2 * a + p) * rows
-        return blocks_ref[:, start : start + rows, :].astype(F32).reshape(count * rows, columns)
+        return blocks_ref[:, start : start + rows, :].reshape(count * rows, columns)
 
     return [[one(a, p) for p in range(2)] for a in range(2)]
 
@@ -248,33 +247,36 @@
     return jnp.where(curved > 0.0, norm / jnp.where(curved > 0.0, curved, 1.0), 1.0)
 
 
-def image_kernel(blocks_ref, rhs_rows_ref, norms_ref, copies_ref, rows_ref, sums_ref):
+def image_kernel(blocks_ref, rhs_rows_ref, norms_ref, copies_ref, sums_ref):
     total = jnp.sum(blocks_ref[...], axis=0)
     rhs = rhs_rows_ref[...]
     image = total[:64] + LAMBDA * rhs
+    for k in range(blocks_ref.shape[0]):
+        copies_ref[k] = image
     norm, energy = norms_ref[0:1, :], total[64:65]
     residual = rhs - slab_step(lane_sum(norm), lane_sum(energy)) * image
-    for a in range(2):
-        for p in range(2):
-            rows_ref[p, a] = image[(2 * a + p) * 16 : (2 * a + p + 1) * 16]
-    rounded = residual.astype(BF16)
-    for k in range(blocks_ref.shape[0]):
-        copies_ref[k] = rounded
     share = 1.0 / blocks_ref.shape[0]
     sums_ref[...] = tile_of([row_sum(residual * residual), row_sum(residual * rhs), share * norm, share * energy])
 
 
 def last_kernel(sums_ref, blocks_ref, spectrum_ref, mask_ref, maps_ref, rows_ref, columns_ref, out_ref):
+    step = slab_step(lane_sum(sums_ref[2:3, :]), lane_sum(sums_ref[3:4, :]))
     field = dft_columns(coil_field(maps_ref, load_image(blocks_ref)), columns_ref, -1.0)
     spectrum = masked(dft_rows(field, rows_ref, -1.0), mask_ref)
     before = [[spectrum_ref[a, p] for p in range(2)] for a in range(2)]
+    spectrum = [[before[a][p] - step * spectrum[a][p] for p in range(2)] for a in range(2)]
     tile = tile_of([inner(spectrum, spectrum), inner(spectrum, before)] + [sums_ref[i : i + 1, :] for i in range(4)])
     for k in range(out_ref.shape[0]):
-        out_ref[k] = tile
+        out_ref[k, 0:8] = tile
+        out_ref[k, 8:] = jnp.zeros((out_ref.shape[1] - 8, 128), F32)
+
+
+def near_kernel(at_ref, blocks_ref, near_ref):
+    store_near(near_ref, blocks_ref, at_ref[0])
 
 
 def spread_kernel(tiles_ref, out_ref):
-    total = jnp.sum(tiles_ref[...], axis=0)
+    total = jnp.sum(tiles_ref[:, 0:8, :], axis=0)
     for k in range(out_ref.shape[0]):
         out_ref[k] = total
 
@@ -322,11 +324,11 @@
 
 def denoise_kernel(coil_count, slab_count, *refs):
     at_ref, last_ref = refs[:2]
-    rhs_refs = refs[2:9]
-    image_refs = refs[9:16]
-    w_first_ref, w_middle_ref, w_last_ref, solution_ref, refined_ref = refs[16:21]
-    features_ref = refs[21]
-    hidden_refs = refs[22:]
+    rhs_refs = refs[2:7]
+    image_refs = refs[7:12]
+    w_first_ref, w_middle_ref, w_last_ref, solution_ref, refined_ref = refs[12:17]
+    features_ref = refs[17]
+    hidden_refs = refs[18:]
     coil_at = at_ref[0]
     slab_at = at_ref[1]
 
@@ -421,7 +423,7 @@
                 refined_ref[a, p, 8 * h : 8 * h + 8] = solution_ref[a, p, 8 * h : 8 * h + 8] + piece
 
 
-def tables_kernel(first_ref, middle_ref, last_ref, w_first_ref, w_middle_ref, w_last_ref):
+def tables_kernel(first_ref, middle_ref, w_first_ref, w_middle_ref):
     def spots(size, target, count=512):
         column = lax.broadcasted_iota(jnp.int32, (size, count), 1)
         return jnp.where(column == target(lax.broadcasted_iota(jnp.int32, (size, count), 0)), 1.0, 0.0).astype(BF16)
@@ -445,6 +447,9 @@
             for t in range(3):
                 start = (t * GROUP + r) * 32
                 w_middle_ref[m, start : start + 32] = band[32 * t : 32 * t + 32]
+
+
+def last_table_kernel(last_ref, w_last_ref):
     bands = []
     for r in range(8):
         bands.append(pltpu.roll(last_ref[...], 32 * r, 1) if r else last_ref[...])
@@ -456,22 +461,16 @@
     middle = jnp.transpose(w_middle, (0, 3, 4, 5, 1, 2))
     last = jnp.pad(jnp.transpose(w_last, (4, 0, 2, 3, 1)), ((0, 0), (0, 0), (0, 0), (0, 7), (0, 0)))
     last = jnp.pad(last.reshape(6, 960), ((0, 2), (0, 64))).astype(F32)
-    return call(
+    pair = call(
         tables_kernel,
-        (struct((512, 512), BF16), struct((3, 96 * GROUP, 512), BF16), struct((64, 1024), BF16)),
-        (first, middle, last),
-    )
+        (struct((512, 512), BF16), struct((3, 96 * GROUP, 512), BF16)),
+        (first, middle),
+    )
+    return (*pair, call(last_table_kernel, struct((64, 1024), BF16), (last,))), (first, last)
 
 
 def swap(blocks, axis):
     return lax.all_to_all(blocks, axis, 0, 0, tiled=True)
-
-
-def near_rows(rows):
-    count = lax.axis_size("coil")
-    before = lax.ppermute(rows[:, :, SIDE:], "coil", [(i, i + 1) for i in range(count - 1)])
-    after = lax.ppermute(rows[:, :, :SIDE], "coil", [(i + 1, i) for i in range(count - 1)])
-    return jnp.concatenate([before, rows, after], axis=2)
 
 
 def near_planes(near):
@@ -481,9 +480,10 @@
         pairs = [(i, i + step) for i in range(count) if 0 <= i + step < count]
         return lax.ppermute(part, "slab", pairs)
 
-    below = [shifted(near[1:], 3), shifted(near, 2), shifted(near, 1)]
-    above = [shifted(near, -1), shifted(near, -2), shifted(near[:1], -3)]
-    return below + [near] + above
+    below, above = shifted(near, 1), shifted(near, -1)
+    below_far = shifted(jnp.concatenate([below[1:], near]), 2)
+    above_far = shifted(jnp.concatenate([near, above[:1]]), -2)
+    return [below_far, below, near, above, above_far]
 
 
 def body(sensitivity, kspace, sampling, prior_image, w_first, w_middle, w_last):
@@ -492,14 +492,14 @@
     coils, slabs = lax.axis_size("coil"), lax.axis_size("slab")
     at = jnp.stack([lax.axis_index("coil"), lax.axis_index("slab")]).astype(jnp.int32)
     rows, columns = left_table(len_y), right_table(len_z)
-    weights = tables(w_first, w_middle, w_last)
+    weights, prepared = tables(w_first, w_middle, w_last)
 
     term = adjoint(sampling, kspace[0], rows, columns, maps, coils)
     rhs_rows, copies = call(
         rows_kernel,
         (struct((64, 128)), struct((coils, 64, 128))),
         (swap(term, "coil"), prior_image),
-        after=(),
+        after=prepared,
     )
     rhs = swap(copies, "coil")
     near_shape = struct((2, 2, 32, 128))
@@ -510,20 +510,21 @@
         in_smem=(0,),
     )
     rhs_parts = near_planes(rhs_near)
-    copies, image_rows, sums = call(
+    copies, sums = call(
         image_kernel,
-        (struct((coils, 64, 128), BF16), struct((2, 2, 16, 128)), struct((8, 128))),
+        (struct((coils, 64, 128)), struct((8, 128))),
         (swap(term, "coil"), rhs_rows, norms),
         after=rhs_parts,
     )
-    image_parts = near_planes(near_rows(image_rows))
+    image = swap(copies, "coil")
     tiles = call(
         last_kernel,
-        struct((coils, 8, 128)),
-        (sums, swap(copies, "coil"), spectrum, sampling, maps, rows, columns),
-        after=image_parts[:AHEAD],
-    )
-    tiles = call(spread_kernel, struct((slabs, 8, 128)), (swap(tiles, "coil"),), after=image_parts[AHEAD:])
+        struct((coils, 16, 128)),
+        (sums, image, spectrum, sampling, maps, rows, columns),
+        after=weights[2:],
+    )
+    image_parts = near_planes(call(near_kernel, near_shape, (at, image), in_smem=(0,), after=(tiles,)))
+    tiles = call(spread_kernel, struct((slabs, 8, 128)), (swap(tiles, "coil"),), after=(image_parts[1], image_parts[3]))
     last = swap(tiles, "slab")
     scratch = [pltpu.VMEM((12, 144, 256), BF16)]
     scratch += [pltpu.VMEM((10 - 2 * m, (16 - 2 * m) * 32, 256), BF16) for m in range(4)]

time: 163 us -> 156 us (0.957)
  blocking collectives: 28.9 us -> 0 us
  waiting for transfers between devices: 33.6 us -> 59.5 us
  starting transfers between devices: 75.5 us -> 67.5 us
  local copies, waits for them, and re-layouts: 0.32 us -> 3.67 us
    all_to_all x5 -> x6, waiting for transfers between devices: 22.2 us -> 53.1 us  [swap(): return lax.all_to_all(blocks, axis, 0, 0, tiled=True)]
    all_to_all x1 -> x0, blocking collectives: 28.9 us -> none  [swap(): return lax.all_to_all(blocks, axis, 0, 0, tiled=True)]
    ppermute x12 -> x8, starting transfers between devices: 36.1 us -> 25 us  [shifted(): return lax.ppermute(part, 'slab', pairs)]
    all_to_all x5 -> x6, starting transfers between devices: 33.2 us -> 42.4 us  [swap(): return lax.all_to_all(blocks, axis, 0, 0, tiled=True)]
    ppermute x2 -> x0, starting transfers between devices: 6.21 us -> none  [the longest x1 4.92 us: near_rows(): lax.ppermute(rows[:, :, SIDE:], 'coil', [(i, i + 1) for i in range(count...]
    ppermute x2 -> x0, waiting for transfers between devices: 4.66 us -> none  [the longest x1 4.65 us: near_rows(): lax.ppermute(rows[:, :, :SIDE], 'coil', [(i + 1, i) for i in range(count...]
    unnamed x20 -> x26, local copies, waits for them, and re-layouts: 0.06 us -> 1.92 us
    pallas_call x7 -> x9, Pallas kernels: 18.9 us -> 19.6 us  [call(): pl.pallas_call(kernel, out_shape=out_shape, in_specs=specs, out_specs=out...]
  transfers between devices with their start and end apart: 19 -> 14, of which waited for: 6 -> 11; matrix products, arithmetic and copies ran while one was open for 0% -> 0% of each run, Pallas kernels for 0% -> 1%
where the time goes in v5:
time: 156 us; the launch traced here: 155 us
  starting transfers between devices  67.5 us (43%)
  waiting for transfers between devices  59.5 us (38%)
  Pallas kernels  23.1 us (15%)
  local copies, waits for them, and re-layouts  3.67 us (2%)
    all_to_all x6, waiting for transfers between devices, swap(): return lax.all_to_all(blocks, axis, 0, 0, tiled=True)  53.1 us
    all_to_all x6, starting transfers between devices, swap(): return lax.all_to_all(blocks, axis, 0, 0, tiled=True)  42.4 us
    ppermute x8, starting transfers between devices, shifted(): return lax.ppermute(part, 'slab', pairs)  25 us
    pallas_call x9, Pallas kernels, call(): pl.pallas_call(kernel, out_shape=out_shape, in_specs=specs, out_specs=out...  19.6 us
    ppermute x8, waiting for transfers between devices, shifted(): return lax.ppermute(part, 'slab', pairs)  6.42 us
    pallas_call x1, Pallas kernels, adjoint(): pl.pallas_call(adjoint_kernel, out_shape=struct((coils, 64, 128)), in_spe...  3.54 us
  transfers between devices with their start and end apart: 14, of which 11 were waited for; matrix products, arithmetic and copies ran while one was open for 0% of the time, Pallas kernels for 1%

profile of v5, /device:TPU:1, one launch (start us, length us, event | category | flops | bytes accessed | tf_op | source)
XLA Modules:
  0.0 154.8 jit_solution(8742729052896702144)
XLA Ops:
  0.6 3.5 %shard_map.104 = f32[16,64,128]{2,1,0:T(8,128)} custom-call(s32[2,256,128]{2,1,0:T(8,128)} %refs_3_.1, f32[2,2,256,128]{3,2,1,0:T(8,128)} %bitcast.12, bf16[512,512]{1,0:T(8,128)(2,1)} %constant.14.clone.rows_hbm.rows_ref.refs_5_, bf16[128,512]{1,0:T(8,128)(2,1)} %constant.15.clone.columns_hbm.columns_ref.refs_6_, f32[2,2,256,128]{3,2,1,0:T(8,128)} %bitcast.8), custom_call_target="tpu_custom_call" | custom-call | tf_op jit(solution)/shard_map/pallas_call | solution.py:203
  4.2 11.8 %all-to-all-start = ((f32[16,64,128]{2,1,0:T(8,128)}), f32[16,64,128]{2,1,0:T(8,128)S(1)}, u32[]{:S(2)}, u32[]{:S(2)}) async-start(f32[16,64,128]{2,1,0:T(8,128)} %shard_map.104), calls=%async_computation | async-start | bytes 1048576 | tf_op jit(solution)/shard_map/all_to_all | solution.py:473
  16.9 16.2 %all-to-all-done.refs_0_ = f32[16,64,128]{2,1,0:T(8,128)S(1)} async-done(((f32[16,64,128]{2,1,0:T(8,128)}), f32[16,64,128]{2,1,0:T(8,128)S(1)}, u32[]{:S(2)}, u32[]{:S(2)}) %all-to-all-start) | async-done | bytes 524320 | tf_op jit(solution)/shard_map/all_to_all | solution.py:473
  33.1 0.9 shard_map.105
  34.0 4.9 %all-to-all-start.1 = ((f32[16,64,128]{2,1,0:T(8,128)}), f32[16,64,128]{2,1,0:T(8,128)S(1)}, u32[]{:S(2)}, u32[]{:S(2)}) async-start(f32[16,64,128]{2,1,0:T(8,128)} %get-tuple-element.12), calls=%async_computation.1 | async-start | bytes 1048576 | tf_op jit(solution)/shard_map/all_to_all | solution.py:473
  39.0 17.1 %all-to-all-done.1.blocks_ref = f32[16,64,128]{2,1,0:T(8,128)S(1)} async-done(((f32[16,64,128]{2,1,0:T(8,128)}), f32[16,64,128]{2,1,0:T(8,128)S(1)}, u32[]{:S(2)}, u32[]{:S(2)}) %all-to-all-start.1) | async-done | bytes 524320 | tf_op jit(solution)/shard_map/all_to_all | solution.py:473
  56.1 3.9 %shard_map.106 = (f32[16,72,128]{2,1,0:T(8,128)}, f32[2,2,256,128]{3,2,1,0:T(8,128)S(1)}, f32[8,128]{1,0:T(8,128)S(1)}, f32[2,2,32,128]{3,2,1,0:T(8,128)S(1)}) custom-call(s32[2]{0:T(128)S(1)} %pad_add_fusion.at_ref.refs_0_, f32[16,64,128]{2,1,0:T(8,128)S(1)} %all-to-all-done.1.blocks_ref, s32[2,256,128]{2,1,0:T(8,128)S(1)} %copy-done.2, ...), custom_call_target="tpu_custom_call" | custom-call | tf_op jit(solution)/shard_map/pallas_call | solution.py:33
  60.0 4.6 %all-to-all-start.2 = ((f32[16,72,128]{2,1,0:T(8,128)}), f32[16,72,128]{2,1,0:T(8,128)S(1)}, u32[]{:S(2)}, u32[]{:S(2)}) async-start(f32[16,72,128]{2,1,0:T(8,128)} %get-tuple-element.13), calls=%async_computation.2 | async-start | bytes 1179648 | tf_op jit(solution)/shard_map/all_to_all | solution.py:473
  64.6 3.3 %collective-permute-start.2 = (f32[2,2,32,128]{3,2,1,0:T(8,128)S(1)}, f32[2,2,32,128]{3,2,1,0:T(8,128)S(1)}, u32[]{:S(2)}, u32[]{:S(2)}) collective-permute-start(f32[2,2,32,128]{3,2,1,0:T(8,128)S(1)} %get-tuple-element.16.refs_5_.refs_4_), channel_id=1, source_target_pairs={{16,0},{32,16},{48,32},{64,48},{80,64},{96,80},{112,96},{128,112},... | collective-permute-start | bytes 196616 | tf_op jit(solution)/shard_map/ppermute | solution.py:481
  68.0 2.3 %collective-permute-start = (f32[2,2,32,128]{3,2,1,0:T(8,128)S(1)}, f32[2,2,32,128]{3,2,1,0:T(8,128)S(1)}, u32[]{:S(2)}, u32[]{:S(2)}) collective-permute-start(f32[2,2,32,128]{3,2,1,0:T(8,128)S(1)} %get-tuple-element.16.refs_5_.refs_4_), channel_id=1, source_target_pairs={{0,16},{16,32},{32,48},{48,64},{64,80},{80,96},{96,112},{112,128},... | collective-permute-start | bytes 196616 | tf_op jit(solution)/shard_map/ppermute | solution.py:481
  70.5 0.6 copy-done.5
  71.1 0.6 collective-permute-done.refs_4_.refs_3_
  71.8 0.8 slice-done
  72.6 3.6 %collective-permute-start.1 = (f32[3,2,32,128]{3,2,1,0:T(8,128)S(1)}, f32[3,2,32,128]{3,2,1,0:T(8,128)S(1)}, u32[]{:S(2)}, u32[]{:S(2)}) collective-permute-start(f32[3,2,32,128]{3,2,1,0:T(8,128)S(1)} %get-tuple-element.25), channel_id=1, source_target_pairs={{0,32},{16,48},{32,64},{48,80},{64,96},{80,112},{96,128},{112,144}... | collective-permute-start | bytes 294920 | tf_op jit(solution)/shard_map/ppermute | solution.py:481
  76.2 1.3 collective-permute-start.3
  77.5 4.6 %collective-permute-done.1.refs_3_.refs_2_ = f32[3,2,32,128]{3,2,1,0:T(8,128)S(1)} collective-permute-done((f32[3,2,32,128]{3,2,1,0:T(8,128)S(1)}, f32[3,2,32,128]{3,2,1,0:T(8,128)S(1)}, u32[]{:S(2)}, u32[]{:S(2)}) %collective-permute-start.1) | collective-permute-done | bytes 98336 | tf_op jit(solution)/shard_map/ppermute | solution.py:481
  82.2 0.7 all-to-all-done.2.refs_0_
  83.0 0.9 shard_map.107
  83.8 7.9 %all-to-all-start.3 = ((f32[16,64,128]{2,1,0:T(8,128)}), f32[16,64,128]{2,1,0:T(8,128)S(1)}, u32[]{:S(2)}, u32[]{:S(2)}) async-start(f32[16,64,128]{2,1,0:T(8,128)} %get-tuple-element.18), calls=%async_computation.3 | async-start | bytes 1048576 | tf_op jit(solution)/shard_map/all_to_all | solution.py:473
  91.9 14.0 %all-to-all-done.3.refs_1_ = f32[16,64,128]{2,1,0:T(8,128)S(1)} async-done(((f32[16,64,128]{2,1,0:T(8,128)}), f32[16,64,128]{2,1,0:T(8,128)S(1)}, u32[]{:S(2)}, u32[]{:S(2)}) %all-to-all-start.3) | async-done | bytes 524320 | tf_op jit(solution)/shard_map/all_to_all | solution.py:473
  105.8 1.7 %shard_map.109.refs_2_ = f32[16,16,128]{2,1,0:T(8,128)} custom-call(f32[8,128]{1,0:T(8,128)S(1)} %get-tuple-element.17.refs_0_, f32[16,64,128]{2,1,0:T(8,128)S(1)} %all-to-all-done.3.refs_1_, f32[2,2,256,128]{3,2,1,0:T(8,128)S(1)} %get-tuple-element.19.refs_2_, s32[2,256,128]{2,1,0:T(8,128)S(1)} %copy-done.2, f32[2,2,256,128]{3,2,1,0:T(8,128)S(1)} %bitcast.10, ...), custom_call_target="tpu_custom_call" | custom-call | tf_op jit(solution)/shard_map/pallas_call | solution.py:33
  107.5 5.0 %all-to-all-start.4 = ((f32[16,16,128]{2,1,0:T(8,128)}), f32[16,16,128]{2,1,0:T(8,128)S(1)}, u32[]{:S(2)}, u32[]{:S(2)}) async-start(f32[16,16,128]{2,1,0:T(8,128)} %shard_map.109.refs_2_), calls=%async_computation.4 | async-start | bytes 262144 | tf_op jit(solution)/shard_map/all_to_all | solution.py:473
  113.1 6.1 %collective-permute-start.5 = (f32[2,2,32,128]{3,2,1,0:T(8,128)S(1)}, f32[2,2,32,128]{3,2,1,0:T(8,128)S(1)}, u32[]{:S(2)}, u32[]{:S(2)}) collective-permute-start(f32[2,2,32,128]{3,2,1,0:T(8,128)S(1)} %shard_map.110.refs_9_), channel_id=1, source_target_pairs={{16,0},{32,16},{48,32},{64,48},{80,64},{96,80},{112,96},{128,112},... | collective-permute-start | bytes 196616 | tf_op jit(solution)/shard_map/ppermute | solution.py:481
  119.2 3.5 %collective-permute-start.4 = (f32[2,2,32,128]{3,2,1,0:T(8,128)S(1)}, f32[2,2,32,128]{3,2,1,0:T(8,128)S(1)}, u32[]{:S(2)}, u32[]{:S(2)}) collective-permute-start(f32[2,2,32,128]{3,2,1,0:T(8,128)S(1)} %shard_map.110.refs_9_), channel_id=1, source_target_pairs={{0,16},{16,32},{32,48},{48,64},{64,80},{80,96},{96,112},{112,128},... | collective-permute-start | bytes 196616 | tf_op jit(solution)/shard_map/ppermute | solution.py:481
  124.1 0.8 slice-done.1
  124.8 3.7 %collective-permute-start.6 = (f32[3,2,32,128]{3,2,1,0:T(8,128)S(1)}, f32[3,2,32,128]{3,2,1,0:T(8,128)S(1)}, u32[]{:S(2)}, u32[]{:S(2)}) collective-permute-start(f32[3,2,32,128]{3,2,1,0:T(8,128)S(1)} %get-tuple-element.23), channel_id=1, source_target_pairs={{0,32},{16,48},{32,64},{48,80},{64,96},{80,112},{96,128},{112,144}... | collective-permute-start | bytes 294920 | tf_op jit(solution)/shard_map/ppermute | solution.py:481
  128.5 1.3 collective-permute-start.7
  129.8 0.6 shard_map.111
  130.5 8.2 %all-to-all-start.5 = ((f32[16,8,128]{2,1,0:T(8,128)}), f32[16,8,128]{2,1,0:T(8,128)S(1)}, u32[]{:S(2)}, u32[]{:S(2)}) async-start(f32[16,8,128]{2,1,0:T(8,128)} %shard_map.111), calls=%async_computation.5 | async-start | bytes 131072 | tf_op jit(solution)/shard_map/all_to_all | solution.py:473
  138.7 0.8 shard_map.112
  139.5 5.1 %all-to-all-done.5.refs_1_ = f32[16,8,128]{2,1,0:T(8,128)S(1)} async-done(((f32[16,8,128]{2,1,0:T(8,128)}), f32[16,8,128]{2,1,0:T(8,128)S(1)}, u32[]{:S(2)}, u32[]{:S(2)}) %all-to-all-start.5) | async-done | bytes 65568 | tf_op jit(solution)/shard_map/all_to_all | solution.py:473
  144.5 10.2 %shard_map.113 = (f32[2,2,16,128]{3,2,1,0:T(8,128)}, f32[2,2,16,128]{3,2,1,0:T(8,128)}) custom-call(s32[2]{0:T(128)S(1)} %pad_add_fusion.at_ref.refs_0_, f32[16,8,128]{2,1,0:T(8,128)S(1)} %all-to-all-done.5.refs_1_, f32[3,2,32,128]{3,2,1,0:T(8,128)S(1)} %collective-permute-done.1.refs_3_.refs_2_, f32[2,2,32,128]{3,2,1,0:T(8,128)S(1)} %collective-permute-done.refs_4_.refs_3_, ...), custom_call_target="tpu_custom_call" | custom-call | tf_op jit(solution)/shard_map/pallas_call | solution.py:33
  (46 shorter events, 3.5 us)
Async XLA Ops:
  4.2 11.8 %copy-start.10 = (bf16[32,2,3,3,3]{0,1,4,3,2:T(2,128)(2,1)S(1)}, bf16[32,2,3,3,3]{0,1,4,3,2:T(2,128)(2,1)}, u32[]{:S(2)}) copy-start(bf16[32,2,3,3,3]{0,1,4,3,2:T(2,128)(2,1)} %param.13) | copy-start | bytes 10372
  4.2 28.9 %all-to-all-start = ((f32[16,64,128]{2,1,0:T(8,128)}), f32[16,64,128]{2,1,0:T(8,128)S(1)}, u32[]{:S(2)}, u32[]{:S(2)}) async-start(f32[16,64,128]{2,1,0:T(8,128)} %shard_map.104), calls=%async_computation | async-start | bytes 1048576 | tf_op jit(solution)/shard_map/all_to_all | solution.py:473
  16.0 0.7 copy-start.11
  16.9 16.2 %copy-start.9 = (f32[2,2,16,128]{3,2,1,0:T(8,128)S(1)}, f32[2,2,16,128]{3,2,1,0:T(8,128)}, u32[]{:S(2)}) copy-start(f32[2,2,16,128]{3,2,1,0:T(8,128)} %refs_1_.1) | copy-start | bytes 98308
  33.1 23.0 %copy-start.2 = (s32[2,256,128]{2,1,0:T(8,128)S(1)}, s32[2,256,128]{2,1,0:T(8,128)}, u32[]{:S(2)}) copy-start(s32[2,256,128]{2,1,0:T(8,128)} %refs_3_.1) | copy-start | bytes 786436
  33.1 23.0 %copy-start.3 = (bf16[128,512]{1,0:T(8,128)(2,1)S(1)}, bf16[128,512]{1,0:T(8,128)(2,1)}, u32[]{:S(2)}) copy-start(bf16[128,512]{1,0:T(8,128)(2,1)} %constant.15.clone.columns_hbm.columns_ref.refs_6_) | copy-start | bytes 393220
  34.0 22.1 %copy-start = (f32[1,2,2,256,128]{4,3,2,1,0:T(8,128)S(1)}, f32[1,2,2,256,128]{4,3,2,1,0:T(8,128)}, u32[]{:S(2)}) copy-start(f32[1,2,2,256,128]{4,3,2,1,0:T(8,128)} %param.9) | copy-start | bytes 1572868
  34.0 22.1 %copy-start.1 = (bf16[512,512]{1,0:T(8,128)(2,1)S(1)}, bf16[512,512]{1,0:T(8,128)(2,1)}, u32[]{:S(2)}) copy-start(bf16[512,512]{1,0:T(8,128)(2,1)} %constant.14.clone.rows_hbm.rows_ref.refs_5_) | copy-start | bytes 1572868
  34.0 22.1 %all-to-all-start.1 = ((f32[16,64,128]{2,1,0:T(8,128)}), f32[16,64,128]{2,1,0:T(8,128)S(1)}, u32[]{:S(2)}, u32[]{:S(2)}) async-start(f32[16,64,128]{2,1,0:T(8,128)} %get-tuple-element.12), calls=%async_computation.1 | async-start | bytes 1048576 | tf_op jit(solution)/shard_map/all_to_all | solution.py:473
  60.0 23.0 %all-to-all-start.2 = ((f32[16,72,128]{2,1,0:T(8,128)}), f32[16,72,128]{2,1,0:T(8,128)S(1)}, u32[]{:S(2)}, u32[]{:S(2)}) async-start(f32[16,72,128]{2,1,0:T(8,128)} %get-tuple-element.13), calls=%async_computation.2 | async-start | bytes 1179648 | tf_op jit(solution)/shard_map/all_to_all | solution.py:473
  64.6 5.9 %collective-permute-start.2 = (f32[2,2,32,128]{3,2,1,0:T(8,128)S(1)}, f32[2,2,32,128]{3,2,1,0:T(8,128)S(1)}, u32[]{:S(2)}, u32[]{:S(2)}) collective-permute-start(f32[2,2,32,128]{3,2,1,0:T(8,128)S(1)} %get-tuple-element.16.refs_5_.refs_4_), channel_id=1, source_target_pairs={{16,0},{32,16},{48,32},{64,48},{80,64},{96,80},{112,96},{128,112},... | collective-permute-start | bytes 196616 | tf_op jit(solution)/shard_map/ppermute | solution.py:481
  68.0 3.8 %collective-permute-start = (f32[2,2,32,128]{3,2,1,0:T(8,128)S(1)}, f32[2,2,32,128]{3,2,1,0:T(8,128)S(1)}, u32[]{:S(2)}, u32[]{:S(2)}) collective-permute-start(f32[2,2,32,128]{3,2,1,0:T(8,128)S(1)} %get-tuple-element.16.refs_5_.refs_4_), channel_id=1, source_target_pairs={{0,16},{16,32},{32,48},{48,64},{64,80},{80,96},{96,112},{112,128},... | collective-permute-start | bytes 196616 | tf_op jit(solution)/shard_map/ppermute | solution.py:481
  70.5 0.6 copy-start.5
  71.8 0.8 slice-start
  72.6 10.4 %copy-start.6 = (f32[2,2,32,128]{3,2,1,0:T(8,128)S(1)}, f32[2,2,32,128]{3,2,1,0:T(8,128)}, u32[]{:S(2)}) copy-start(f32[2,2,32,128]{3,2,1,0:T(8,128)} %copy-done.5) | copy-start | bytes 196612
  72.6 9.5 %collective-permute-start.1 = (f32[3,2,32,128]{3,2,1,0:T(8,128)S(1)}, f32[3,2,32,128]{3,2,1,0:T(8,128)S(1)}, u32[]{:S(2)}, u32[]{:S(2)}) collective-permute-start(f32[3,2,32,128]{3,2,1,0:T(8,128)S(1)} %get-tuple-element.25), channel_id=1, source_target_pairs={{0,32},{16,48},{32,64},{48,80},{64,96},{80,112},{96,128},{112,144}... | collective-permute-start | bytes 294920 | tf_op jit(solution)/shard_map/ppermute | solution.py:481
  76.2 6.1 %collective-permute-start.3 = (f32[3,2,32,128]{3,2,1,0:T(8,128)S(1)}, f32[3,2,32,128]{3,2,1,0:T(8,128)S(1)}, u32[]{:S(2)}, u32[]{:S(2)}) collective-permute-start(f32[3,2,32,128]{3,2,1,0:T(8,128)S(1)} %get-tuple-element.24), channel_id=1, source_target_pairs={{32,0},{48,16},{64,32},{80,48},{96,64},{112,80},{128,96},{144,112}... | collective-permute-start | bytes 294920 | tf_op jit(solution)/shard_map/ppermute | solution.py:481
  83.8 22.0 %all-to-all-start.3 = ((f32[16,64,128]{2,1,0:T(8,128)}), f32[16,64,128]{2,1,0:T(8,128)S(1)}, u32[]{:S(2)}, u32[]{:S(2)}) async-start(f32[16,64,128]{2,1,0:T(8,128)} %get-tuple-element.18), calls=%async_computation.3 | async-start | bytes 1048576 | tf_op jit(solution)/shard_map/all_to_all | solution.py:473
  107.5 22.3 %all-to-all-start.4 = ((f32[16,16,128]{2,1,0:T(8,128)}), f32[16,16,128]{2,1,0:T(8,128)S(1)}, u32[]{:S(2)}, u32[]{:S(2)}) async-start(f32[16,16,128]{2,1,0:T(8,128)} %shard_map.109.refs_2_), calls=%async_computation.4 | async-start | bytes 262144 | tf_op jit(solution)/shard_map/all_to_all | solution.py:473
  112.5 26.2 %copy-start.4 = (bf16[3,32,32,3,3,3]{2,1,5,4,3,0:T(8,128)(2,1)S(1)}, bf16[3,32,32,3,3,3]{2,1,5,4,3,0:T(8,128)(2,1)}, u32[]{:S(2)}) copy-start(bf16[3,32,32,3,3,3]{2,1,5,4,3,0:T(8,128)(2,1)} %param.14) | copy-start | bytes 497668
  113.1 10.1 %collective-permute-start.5 = (f32[2,2,32,128]{3,2,1,0:T(8,128)S(1)}, f32[2,2,32,128]{3,2,1,0:T(8,128)S(1)}, u32[]{:S(2)}, u32[]{:S(2)}) collective-permute-start(f32[2,2,32,128]{3,2,1,0:T(8,128)S(1)} %shard_map.110.refs_9_), channel_id=1, source_target_pairs={{16,0},{32,16},{48,32},{64,48},{80,64},{96,80},{112,96},{128,112},... | collective-permute-start | bytes 196616 | tf_op jit(solution)/shard_map/ppermute | solution.py:481
  119.2 4.9 %collective-permute-start.4 = (f32[2,2,32,128]{3,2,1,0:T(8,128)S(1)}, f32[2,2,32,128]{3,2,1,0:T(8,128)S(1)}, u32[]{:S(2)}, u32[]{:S(2)}) collective-permute-start(f32[2,2,32,128]{3,2,1,0:T(8,128)S(1)} %shard_map.110.refs_9_), channel_id=1, source_target_pairs={{0,16},{16,32},{32,48},{48,64},{64,80},{80,96},{96,112},{112,128},... | collective-permute-start | bytes 196616 | tf_op jit(solution)/shard_map/ppermute | solution.py:481
  123.2 0.6 copy-start.7
  124.0 0.8 slice-start.1
  124.8 5.0 %copy-start.8 = (f32[2,2,32,128]{3,2,1,0:T(8,128)S(1)}, f32[2,2,32,128]{3,2,1,0:T(8,128)}, u32[]{:S(2)}) copy-start(f32[2,2,32,128]{3,2,1,0:T(8,128)} %copy-done.7) | copy-start | bytes 196612
  124.8 14.6 %collective-permute-start.6 = (f32[3,2,32,128]{3,2,1,0:T(8,128)S(1)}, f32[3,2,32,128]{3,2,1,0:T(8,128)S(1)}, u32[]{:S(2)}, u32[]{:S(2)}) collective-permute-start(f32[3,2,32,128]{3,2,1,0:T(8,128)S(1)} %get-tuple-element.23), channel_id=1, source_target_pairs={{0,32},{16,48},{32,64},{48,80},{64,96},{80,112},{96,128},{112,144}... | collective-permute-start | bytes 294920 | tf_op jit(solution)/shard_map/ppermute | solution.py:481
  128.5 11.0 %collective-permute-start.7 = (f32[3,2,32,128]{3,2,1,0:T(8,128)S(1)}, f32[3,2,32,128]{3,2,1,0:T(8,128)S(1)}, u32[]{:S(2)}, u32[]{:S(2)}) collective-permute-start(f32[3,2,32,128]{3,2,1,0:T(8,128)S(1)} %get-tuple-element.22), channel_id=1, source_target_pairs={{32,0},{48,16},{64,32},{80,48},{96,64},{112,80},{128,96},{144,112}... | collective-permute-start | bytes 294920 | tf_op jit(solution)/shard_map/ppermute | solution.py:481
  130.5 14.1 %all-to-all-start.5 = ((f32[16,8,128]{2,1,0:T(8,128)}), f32[16,8,128]{2,1,0:T(8,128)S(1)}, u32[]{:S(2)}, u32[]{:S(2)}) async-start(f32[16,8,128]{2,1,0:T(8,128)} %shard_map.111), calls=%async_computation.5 | async-start | bytes 131072 | tf_op jit(solution)/shard_map/all_to_all | solution.py:473

commit v6 on v5

--- a/solution.py
+++ b/solution.py
@@ -122,7 +122,7 @@
 
     def one(a, p):
         start = (2 * a + p) * rows
-        return blocks_ref[:, start : start + rows, :].reshape(count * rows, columns)
+        return blocks_ref[:, start : start + rows, :].astype(F32).reshape(count * rows, columns)
 
     return [[one(a, p) for p in range(2)] for a in range(2)]
 
@@ -247,6 +247,15 @@
     return jnp.where(curved > 0.0, norm / jnp.where(curved > 0.0, curved, 1.0), 1.0)
 
 
+def lane_sum(values):
+    return jnp.sum(values, axis=-1, keepdims=True)
+
+
+def slab_step(norm, energy):
+    curved = energy + LAMBDA * norm
+    return jnp.where(curved > 0.0, norm / jnp.where(curved > 0.0, curved, 1.0), 1.0)
+
+
 def image_kernel(blocks_ref, rhs_rows_ref, norms_ref, copies_ref, sums_ref):
     total = jnp.sum(blocks_ref[...], axis=0)
     rhs = rhs_rows_ref[...]
@@ -259,20 +268,46 @@
     sums_ref[...] = tile_of([row_sum(residual * residual), row_sum(residual * rhs), share * norm, share * energy])
 
 
+def image_kernel(blocks_ref, rhs_rows_ref, norms_ref, copies_ref, rows_ref, head_ref, tail_ref, sums_ref):
+    total = jnp.sum(blocks_ref[...], axis=0)
+    rhs = rhs_rows_ref[...]
+    image = total[:64] + LAMBDA * rhs
+    norm, energy = norms_ref[0:1, :], total[64:65]
+    residual = rhs - slab_step(lane_sum(norm), lane_sum(energy)) * image
+    rounded = residual.astype(BF16)
+    for k in range(blocks_ref.shape[0]):
+        copies_ref[k] = rounded
+    for a in range(2):
+        for p in range(2):
+            rows = image[(2 * a + p) * 16 : (2 * a + p + 1) * 16]
+            rows_ref[p, a] = rows
+            head_ref[p, a] = rows[:SIDE]
+            tail_ref[p, a] = rows[SIDE:]
+    share = 1.0 / blocks_ref.shape[0]
+    sums_ref[...] = tile_of([row_sum(residual * residual), row_sum(residual * rhs), share * norm, share * energy])
+
+
 def last_kernel(sums_ref, blocks_ref, spectrum_ref, mask_ref, maps_ref, rows_ref, columns_ref, out_ref):
-    step = slab_step(lane_sum(sums_ref[2:3, :]), lane_sum(sums_ref[3:4, :]))
     field = dft_columns(coil_field(maps_ref, load_image(blocks_ref)), columns_ref, -1.0)
     spectrum = masked(dft_rows(field, rows_ref, -1.0), mask_ref)
     before = [[spectrum_ref[a, p] for p in range(2)] for a in range(2)]
-    spectrum = [[before[a][p] - step * spectrum[a][p] for p in range(2)] for a in range(2)]
     tile = tile_of([inner(spectrum, spectrum), inner(spectrum, before)] + [sums_ref[i : i + 1, :] for i in range(4)])
     for k in range(out_ref.shape[0]):
         out_ref[k, 0:8] = tile
         out_ref[k, 8:] = jnp.zeros((out_ref.shape[1] - 8, 128), F32)
 
 
-def near_kernel(at_ref, blocks_ref, near_ref):
-    store_near(near_ref, blocks_ref, at_ref[0])
+def join_kernel(before_ref, rows_ref, after_ref, near_ref):
+    near_ref[:, :, 0:8, :] = before_ref[...]
+    near_ref[:, :, 8:24, :] = rows_ref[...]
+    near_ref[:, :, 24:32, :] = after_ref[...]
+
+
+def pack_kernel(below_ref, near_ref, above_ref, low_ref, high_ref):
+    low_ref[0] = below_ref[1]
+    low_ref[1:3] = near_ref[...]
+    high_ref[0:2] = near_ref[...]
+    high_ref[2] = above_ref[0]
 
 
 def spread_kernel(tiles_ref, out_ref):
@@ -473,17 +508,18 @@
     return lax.all_to_all(blocks, axis, 0, 0, tiled=True)
 
 
-def near_planes(near):
-    count = lax.axis_size("slab")
-
-    def shifted(part, step):
-        pairs = [(i, i + step) for i in range(count) if 0 <= i + step < count]
-        return lax.ppermute(part, "slab", pairs)
-
-    below, above = shifted(near, 1), shifted(near, -1)
-    below_far = shifted(jnp.concatenate([below[1:], near]), 2)
-    above_far = shifted(jnp.concatenate([near, above[:1]]), -2)
-    return [below_far, below, near, above, above_far]
+def shifted(part, axis, step):
+    count = lax.axis_size(axis)
+    return lax.ppermute(part, axis, [(i, i + step) for i in range(count) if 0 <= i + step < count])
+
+
+def nearest(near):
+    return shifted(near, "slab", 1), near, shifted(near, "slab", -1)
+
+
+def near_planes(parts, after=()):
+    low, high = call(pack_kernel, (struct((3, 2, 32, 128)),) * 2, parts, after=after)
+    return [shifted(low, "slab", 2), *parts, shifted(high, "slab", -2)]
 
 
 def body(sensitivity, kspace, sampling, prior_image, w_first, w_middle, w_last):
@@ -509,22 +545,25 @@
         (at, rhs, sampling, maps, rows, columns),
         in_smem=(0,),
     )
+    rhs_near = nearest(rhs_near)
+    edge_shape = struct((2, 2, SIDE, 128))
+    copies, image_rows, head, tail, sums = call(
+        image_kernel,
+        (struct((coils, 64, 128), BF16), struct((2, 2, 16, 128)), edge_shape, edge_shape, struct((8, 128))),
+        (swap(term, "coil"), rhs_rows, norms),
+        after=rhs_near,
+    )
+    before, after = shifted(tail, "coil", 1), shifted(head, "coil", -1)
     rhs_parts = near_planes(rhs_near)
-    copies, sums = call(
-        image_kernel,
-        (struct((coils, 64, 128)), struct((8, 128))),
-        (swap(term, "coil"), rhs_rows, norms),
-        after=rhs_parts,
-    )
-    image = swap(copies, "coil")
     tiles = call(
         last_kernel,
         struct((coils, 16, 128)),
-        (sums, image, spectrum, sampling, maps, rows, columns),
-        after=weights[2:],
-    )
-    image_parts = near_planes(call(near_kernel, near_shape, (at, image), in_smem=(0,), after=(tiles,)))
-    tiles = call(spread_kernel, struct((slabs, 8, 128)), (swap(tiles, "coil"),), after=(image_parts[1], image_parts[3]))
+        (sums, swap(copies, "coil"), spectrum, sampling, maps, rows, columns),
+        after=(before, after, rhs_parts[0], rhs_parts[-1]),
+    )
+    image_near = nearest(call(join_kernel, near_shape, (before, image_rows, after), after=(tiles,)))
+    tiles = call(spread_kernel, struct((slabs, 8, 128)), (swap(tiles, "coil"),), after=image_near)
+    image_parts = near_planes(image_near)
     last = swap(tiles, "slab")
     scratch = [pltpu.VMEM((12, 144, 256), BF16)]
     scratch += [pltpu.VMEM((10 - 2 * m, (16 - 2 * m) * 32, 256), BF16) for m in range(4)]

time: 156 us -> 157 us (level)
  starting transfers between devices: 67.5 us -> 74.5 us
  local copies, waits for them, and re-layouts: 3.67 us -> 0.9 us
  waiting for transfers between devices: 59.5 us -> 57.3 us
    ppermute x8 -> x10, starting transfers between devices: 25 us -> 31.8 us  [shifted(): lax.ppermute(part, axis, [(i, i + step) for i in range(count) if 0 <= i +...]
    all_to_all x6, waiting for transfers between devices: 53.1 us -> 49.4 us  [swap(): return lax.all_to_all(blocks, axis, 0, 0, tiled=True)]
    ppermute x8 -> x10, waiting for transfers between devices: 6.42 us -> 7.85 us  [shifted(): lax.ppermute(part, axis, [(i, i + step) for i in range(count) if 0 <= i +...]
    pallas_call x9 -> x11, Pallas kernels: 19.6 us -> 19 us  [call(): pl.pallas_call(kernel, out_shape=out_shape, in_specs=specs, out_specs=out...]
  transfers between devices with their start and end apart: 14 -> 16, of which waited for: 11 -> 9; matrix products, arithmetic and copies ran while one was open for 0% -> 0% of each run, Pallas kernels for 1% -> 1%
where the time goes in v6:
time: 157 us; the launch traced here: 156 us
  starting transfers between devices  74.5 us (47%)
  waiting for transfers between devices  57.3 us (36%)
  Pallas kernels  22.6 us (14%)
    all_to_all x6, waiting for transfers between devices, swap(): return lax.all_to_all(blocks, axis, 0, 0, tiled=True)  49.4 us
    all_to_all x6, starting transfers between devices, swap(): return lax.all_to_all(blocks, axis, 0, 0, tiled=True)  42.6 us
    ppermute x10, starting transfers between devices, shifted(): lax.ppermute(part, axis, [(i, i + step) for i in range(count) if 0 <= i +...  31.8 us
    pallas_call x11, Pallas kernels, call(): pl.pallas_call(kernel, out_shape=out_shape, in_specs=specs, out_specs=out...  19 us
    ppermute x10, waiting for transfers between devices, shifted(): lax.ppermute(part, axis, [(i, i + step) for i in range(count) if 0 <= i +...  7.85 us
    pallas_call x1, Pallas kernels, adjoint(): pl.pallas_call(adjoint_kernel, out_shape=struct((coils, 64, 128)), in_spe...  3.55 us
  transfers between devices with their start and end apart: 16, of which 9 were waited for; matrix products, arithmetic and copies ran while one was open for 0% of the time, Pallas kernels for 1%

profile of v6, /device:TPU:1, one launch (start us, length us, event | category | flops | bytes accessed | tf_op | source)
XLA Modules:
  0.0 156.3 jit_solution(4152681905820653127)
XLA Ops:
  0.6 3.5 %shard_map.104 = f32[16,64,128]{2,1,0:T(8,128)} custom-call(s32[2,256,128]{2,1,0:T(8,128)} %refs_3_.1, f32[2,2,256,128]{3,2,1,0:T(8,128)} %bitcast.12, bf16[512,512]{1,0:T(8,128)(2,1)} %constant.14.clone.rows_hbm.rows_ref.refs_5_, bf16[128,512]{1,0:T(8,128)(2,1)} %constant.15.clone.columns_hbm.columns_ref.refs_6_, f32[2,2,256,128]{3,2,1,0:T(8,128)} %bitcast.8), custom_call_target="tpu_custom_call" | custom-call | tf_op jit(solution)/shard_map/pallas_call | solution.py:203
  4.2 11.8 %all-to-all-start = ((f32[16,64,128]{2,1,0:T(8,128)}), f32[16,64,128]{2,1,0:T(8,128)S(1)}, u32[]{:S(2)}, u32[]{:S(2)}) async-start(f32[16,64,128]{2,1,0:T(8,128)} %shard_map.104), calls=%async_computation | async-start | bytes 1048576 | tf_op jit(solution)/shard_map/all_to_all | solution.py:508
  16.1 0.6 copy-done.7
  16.9 16.2 %all-to-all-done.refs_0_ = f32[16,64,128]{2,1,0:T(8,128)S(1)} async-done(((f32[16,64,128]{2,1,0:T(8,128)}), f32[16,64,128]{2,1,0:T(8,128)S(1)}, u32[]{:S(2)}, u32[]{:S(2)}) %all-to-all-start) | async-done | bytes 524320 | tf_op jit(solution)/shard_map/all_to_all | solution.py:508
  33.1 0.9 shard_map.105
  34.0 4.9 %all-to-all-start.1 = ((f32[16,64,128]{2,1,0:T(8,128)}), f32[16,64,128]{2,1,0:T(8,128)S(1)}, u32[]{:S(2)}, u32[]{:S(2)}) async-start(f32[16,64,128]{2,1,0:T(8,128)} %get-tuple-element.19), calls=%async_computation.1 | async-start | bytes 1048576 | tf_op jit(solution)/shard_map/all_to_all | solution.py:508
  39.0 17.1 %all-to-all-done.1.blocks_ref = f32[16,64,128]{2,1,0:T(8,128)S(1)} async-done(((f32[16,64,128]{2,1,0:T(8,128)}), f32[16,64,128]{2,1,0:T(8,128)S(1)}, u32[]{:S(2)}, u32[]{:S(2)}) %all-to-all-start.1) | async-done | bytes 524320 | tf_op jit(solution)/shard_map/all_to_all | solution.py:508
  56.1 3.9 %shard_map.106 = (f32[16,72,128]{2,1,0:T(8,128)}, f32[2,2,256,128]{3,2,1,0:T(8,128)S(1)}, f32[8,128]{1,0:T(8,128)S(1)}, f32[2,2,32,128]{3,2,1,0:T(8,128)S(1)}) custom-call(s32[2]{0:T(128)S(1)} %pad_add_fusion.at_ref.refs_0_, f32[16,64,128]{2,1,0:T(8,128)S(1)} %all-to-all-done.1.blocks_ref, s32[2,256,128]{2,1,0:T(8,128)S(1)} %copy-done.2, ...), custom_call_target="tpu_custom_call" | custom-call | tf_op jit(solution)/shard_map/pallas_call | solution.py:33
  60.0 4.6 %all-to-all-start.2 = ((f32[16,72,128]{2,1,0:T(8,128)}), f32[16,72,128]{2,1,0:T(8,128)S(1)}, u32[]{:S(2)}, u32[]{:S(2)}) async-start(f32[16,72,128]{2,1,0:T(8,128)} %get-tuple-element.20), calls=%async_computation.2 | async-start | bytes 1179648 | tf_op jit(solution)/shard_map/all_to_all | solution.py:508
  64.7 3.3 %collective-permute-start.1 = (f32[2,2,32,128]{3,2,1,0:T(8,128)S(1)}, f32[2,2,32,128]{3,2,1,0:T(8,128)S(1)}, u32[]{:S(2)}, u32[]{:S(2)}) collective-permute-start(f32[2,2,32,128]{3,2,1,0:T(8,128)S(1)} %get-tuple-element.23.refs_4_.near_ref), channel_id=1, source_target_pairs={{16,0},{32,16},{48,32},{64,48},{80,64},{96,80},{112,96},{128,112},... | collective-permute-start | bytes 196616 | tf_op jit(solution)/shard_map/ppermute | solution.py:513
  68.0 2.3 %collective-permute-start = (f32[2,2,32,128]{3,2,1,0:T(8,128)S(1)}, f32[2,2,32,128]{3,2,1,0:T(8,128)S(1)}, u32[]{:S(2)}, u32[]{:S(2)}) collective-permute-start(f32[2,2,32,128]{3,2,1,0:T(8,128)S(1)} %get-tuple-element.23.refs_4_.near_ref), channel_id=1, source_target_pairs={{0,16},{16,32},{32,48},{48,64},{64,80},{80,96},{96,112},{112,128},... | collective-permute-start | bytes 196616 | tf_op jit(solution)/shard_map/ppermute | solution.py:513
  70.5 1.3 collective-permute-done.refs_3_.below_ref
  71.8 11.2 %all-to-all-done.2.refs_0_ = f32[16,72,128]{2,1,0:T(8,128)S(1)} async-done(((f32[16,72,128]{2,1,0:T(8,128)}), f32[16,72,128]{2,1,0:T(8,128)S(1)}, u32[]{:S(2)}, u32[]{:S(2)}) %all-to-all-start.2) | async-done | bytes 589856 | tf_op jit(solution)/shard_map/all_to_all | solution.py:508
  83.0 0.8 shard_map.107
  83.8 4.4 %all-to-all-start.3 = ((bf16[16,64,128]{2,1,0:T(8,128)(2,1)}), bf16[16,64,128]{2,1,0:T(8,128)(2,1)S(1)}, u32[]{:S(2)}, u32[]{:S(2)}) async-start(bf16[16,64,128]{2,1,0:T(8,128)(2,1)} %get-tuple-element.25), calls=%async_computation.3 | async-start | bytes 524288 | tf_op jit(solution)/shard_map/all_to_all | solution.py:508
  88.2 2.3 %collective-permute-start.4 = (f32[3,2,32,128]{3,2,1,0:T(8,128)S(1)}, f32[3,2,32,128]{3,2,1,0:T(8,128)S(1)}, u32[]{:S(2)}, u32[]{:S(2)}) collective-permute-start(f32[3,2,32,128]{3,2,1,0:T(8,128)S(1)} %get-tuple-element.29), channel_id=1, source_target_pairs={{0,32},{16,48},{32,64},{48,80},{64,96},{80,112},{96,128},{112,144}... | collective-permute-start | bytes 294920 | tf_op jit(solution)/shard_map/ppermute | solution.py:513
  90.5 1.3 collective-permute-start.5
  91.8 5.4 %collective-permute-start.2 = (f32[2,2,8,128]{3,2,1,0:T(8,128)S(1)}, f32[2,2,8,128]{3,2,1,0:T(8,128)S(1)}, u32[]{:S(2)}, u32[]{:S(2)}) collective-permute-start(f32[2,2,8,128]{3,2,1,0:T(8,128)S(1)} %get-tuple-element.27), channel_id=1, source_target_pairs={{0,1},{1,2},{2,3},{3,4},{4,5},{5,6},{6,7},{7,8},{8,9},{9,10},{10,1... | collective-permute-start | bytes 49160 | tf_op jit(solution)/shard_map/ppermute | solution.py:513
  97.2 1.3 collective-permute-start.3
  98.5 4.7 %collective-permute-done.3.refs_8_.refs_2_ = f32[2,2,8,128]{3,2,1,0:T(8,128)S(1)} collective-permute-done((f32[2,2,8,128]{3,2,1,0:T(8,128)S(1)}, f32[2,2,8,128]{3,2,1,0:T(8,128)S(1)}, u32[]{:S(2)}, u32[]{:S(2)}) %collective-permute-start.3) | collective-permute-done | bytes 16416 | tf_op jit(solution)/shard_map/ppermute | solution.py:513
  103.3 1.7 %shard_map.109.refs_3_ = f32[16,16,128]{2,1,0:T(8,128)} custom-call(f32[8,128]{1,0:T(8,128)S(1)} %get-tuple-element.24.refs_0_, bf16[16,64,128]{2,1,0:T(8,128)(2,1)S(1)} %all-to-all-done.3.refs_1_, f32[2,2,256,128]{3,2,1,0:T(8,128)S(1)} %get-tuple-element.26.refs_2_, s32[2,256,128]{2,1,0:T(8,128)S(1)} %copy-done.2, f32[2,2,256,128]{3,2,1,0:T(8,128)S(1)} %bitcast.10, ...), custom_call_target="tpu_custom_call" | custom-call | tf_op jit(solution)/shard_map/pallas_call | solution.py:33
  105.0 8.0 %all-to-all-start.4 = ((f32[16,16,128]{2,1,0:T(8,128)}), f32[16,16,128]{2,1,0:T(8,128)S(1)}, u32[]{:S(2)}, u32[]{:S(2)}) async-start(f32[16,16,128]{2,1,0:T(8,128)} %shard_map.109.refs_3_), calls=%async_computation.4 | async-start | bytes 262144 | tf_op jit(solution)/shard_map/all_to_all | solution.py:508
  113.0 6.0 %collective-permute-start.7 = (f32[2,2,32,128]{3,2,1,0:T(8,128)S(1)}, f32[2,2,32,128]{3,2,1,0:T(8,128)S(1)}, u32[]{:S(2)}, u32[]{:S(2)}) collective-permute-start(f32[2,2,32,128]{3,2,1,0:T(8,128)S(1)} %shard_map.110.refs_2_.near_ref.refs_9_), channel_id=1, source_target_pairs={{16,0},{32,16},{48,32},{64,48},{80,64},{96,80},{112,96},{128,112},... | collective-permute-start | bytes 196616 | tf_op jit(solution)/shard_map/ppermute | solution.py:513
  119.0 4.4 %collective-permute-start.6 = (f32[2,2,32,128]{3,2,1,0:T(8,128)S(1)}, f32[2,2,32,128]{3,2,1,0:T(8,128)S(1)}, u32[]{:S(2)}, u32[]{:S(2)}) collective-permute-start(f32[2,2,32,128]{3,2,1,0:T(8,128)S(1)} %shard_map.110.refs_2_.near_ref.refs_9_), channel_id=1, source_target_pairs={{0,16},{16,32},{32,48},{48,64},{64,80},{80,96},{96,112},{112,128},... | collective-permute-start | bytes 196616 | tf_op jit(solution)/shard_map/ppermute | solution.py:513
  123.9 1.0 collective-permute-done.6.refs_1_.below_ref.refs_8_
  124.9 4.3 %collective-permute-start.8 = (f32[3,2,32,128]{3,2,1,0:T(8,128)S(1)}, f32[3,2,32,128]{3,2,1,0:T(8,128)S(1)}, u32[]{:S(2)}, u32[]{:S(2)}) collective-permute-start(f32[3,2,32,128]{3,2,1,0:T(8,128)S(1)} %get-tuple-element.32), channel_id=1, source_target_pairs={{0,32},{16,48},{32,64},{48,80},{64,96},{80,112},{96,128},{112,144}... | collective-permute-start | bytes 294920 | tf_op jit(solution)/shard_map/ppermute | solution.py:513
  129.3 1.3 collective-permute-start.9
  130.6 0.6 shard_map.111
  131.2 8.9 %all-to-all-start.5 = ((f32[16,8,128]{2,1,0:T(8,128)}), f32[16,8,128]{2,1,0:T(8,128)S(1)}, u32[]{:S(2)}, u32[]{:S(2)}) async-start(f32[16,8,128]{2,1,0:T(8,128)} %shard_map.111), calls=%async_computation.5 | async-start | bytes 131072 | tf_op jit(solution)/shard_map/all_to_all | solution.py:508
  140.3 0.8 shard_map.113
  141.0 5.0 %all-to-all-done.5.refs_1_ = f32[16,8,128]{2,1,0:T(8,128)S(1)} async-done(((f32[16,8,128]{2,1,0:T(8,128)}), f32[16,8,128]{2,1,0:T(8,128)S(1)}, u32[]{:S(2)}, u32[]{:S(2)}) %all-to-all-start.5) | async-done | bytes 65568 | tf_op jit(solution)/shard_map/all_to_all | solution.py:508
  146.0 10.3 %shard_map.115 = (f32[2,2,16,128]{3,2,1,0:T(8,128)}, f32[2,2,16,128]{3,2,1,0:T(8,128)}) custom-call(s32[2]{0:T(128)S(1)} %pad_add_fusion.at_ref.refs_0_, f32[16,8,128]{2,1,0:T(8,128)S(1)} %all-to-all-done.5.refs_1_, f32[3,2,32,128]{3,2,1,0:T(8,128)S(1)} %collective-permute-done.4.refs_9_.refs_2_, ...), custom_call_target="tpu_custom_call" | custom-call | tf_op jit(solution)/shard_map/pallas_call | solution.py:33
  (36 shorter events, 1.3 us)
Async XLA Ops:
  4.2 11.8 %copy-start.6 = (bf16[32,2,3,3,3]{0,1,4,3,2:T(2,128)(2,1)S(1)}, bf16[32,2,3,3,3]{0,1,4,3,2:T(2,128)(2,1)}, u32[]{:S(2)}) copy-start(bf16[32,2,3,3,3]{0,1,4,3,2:T(2,128)(2,1)} %param.13) | copy-start | bytes 10372
  4.2 28.9 %all-to-all-start = ((f32[16,64,128]{2,1,0:T(8,128)}), f32[16,64,128]{2,1,0:T(8,128)S(1)}, u32[]{:S(2)}, u32[]{:S(2)}) async-start(f32[16,64,128]{2,1,0:T(8,128)} %shard_map.104), calls=%async_computation | async-start | bytes 1048576 | tf_op jit(solution)/shard_map/all_to_all | solution.py:508
  16.0 0.7 copy-start.7
  16.9 16.2 %copy-start.5 = (f32[2,2,16,128]{3,2,1,0:T(8,128)S(1)}, f32[2,2,16,128]{3,2,1,0:T(8,128)}, u32[]{:S(2)}) copy-start(f32[2,2,16,128]{3,2,1,0:T(8,128)} %refs_1_.1) | copy-start | bytes 98308
  33.1 23.0 %copy-start.2 = (s32[2,256,128]{2,1,0:T(8,128)S(1)}, s32[2,256,128]{2,1,0:T(8,128)}, u32[]{:S(2)}) copy-start(s32[2,256,128]{2,1,0:T(8,128)} %refs_3_.1) | copy-start | bytes 786436
  33.1 23.0 %copy-start.3 = (bf16[128,512]{1,0:T(8,128)(2,1)S(1)}, bf16[128,512]{1,0:T(8,128)(2,1)}, u32[]{:S(2)}) copy-start(bf16[128,512]{1,0:T(8,128)(2,1)} %constant.15.clone.columns_hbm.columns_ref.refs_6_) | copy-start | bytes 393220
  34.0 22.1 %copy-start = (f32[1,2,2,256,128]{4,3,2,1,0:T(8,128)S(1)}, f32[1,2,2,256,128]{4,3,2,1,0:T(8,128)}, u32[]{:S(2)}) copy-start(f32[1,2,2,256,128]{4,3,2,1,0:T(8,128)} %param.9) | copy-start | bytes 1572868
  34.0 22.1 %copy-start.1 = (bf16[512,512]{1,0:T(8,128)(2,1)S(1)}, bf16[512,512]{1,0:T(8,128)(2,1)}, u32[]{:S(2)}) copy-start(bf16[512,512]{1,0:T(8,128)(2,1)} %constant.14.clone.rows_hbm.rows_ref.refs_5_) | copy-start | bytes 1572868
  34.0 22.1 %all-to-all-start.1 = ((f32[16,64,128]{2,1,0:T(8,128)}), f32[16,64,128]{2,1,0:T(8,128)S(1)}, u32[]{:S(2)}, u32[]{:S(2)}) async-start(f32[16,64,128]{2,1,0:T(8,128)} %get-tuple-element.19), calls=%async_computation.1 | async-start | bytes 1048576 | tf_op jit(solution)/shard_map/all_to_all | solution.py:508
  60.0 23.0 %all-to-all-start.2 = ((f32[16,72,128]{2,1,0:T(8,128)}), f32[16,72,128]{2,1,0:T(8,128)S(1)}, u32[]{:S(2)}, u32[]{:S(2)}) async-start(f32[16,72,128]{2,1,0:T(8,128)} %get-tuple-element.20), calls=%async_computation.2 | async-start | bytes 1179648 | tf_op jit(solution)/shard_map/all_to_all | solution.py:508
  64.7 5.9 %collective-permute-start.1 = (f32[2,2,32,128]{3,2,1,0:T(8,128)S(1)}, f32[2,2,32,128]{3,2,1,0:T(8,128)S(1)}, u32[]{:S(2)}, u32[]{:S(2)}) collective-permute-start(f32[2,2,32,128]{3,2,1,0:T(8,128)S(1)} %get-tuple-element.23.refs_4_.near_ref), channel_id=1, source_target_pairs={{16,0},{32,16},{48,32},{64,48},{80,64},{96,80},{112,96},{128,112},... | collective-permute-start | bytes 196616 | tf_op jit(solution)/shard_map/ppermute | solution.py:513
  68.0 3.8 %collective-permute-start = (f32[2,2,32,128]{3,2,1,0:T(8,128)S(1)}, f32[2,2,32,128]{3,2,1,0:T(8,128)S(1)}, u32[]{:S(2)}, u32[]{:S(2)}) collective-permute-start(f32[2,2,32,128]{3,2,1,0:T(8,128)S(1)} %get-tuple-element.23.refs_4_.near_ref), channel_id=1, source_target_pairs={{0,16},{16,32},{32,48},{48,64},{64,80},{80,96},{96,112},{112,128},... | collective-permute-start | bytes 196616 | tf_op jit(solution)/shard_map/ppermute | solution.py:513
  83.8 19.5 %all-to-all-start.3 = ((bf16[16,64,128]{2,1,0:T(8,128)(2,1)}), bf16[16,64,128]{2,1,0:T(8,128)(2,1)S(1)}, u32[]{:S(2)}, u32[]{:S(2)}) async-start(bf16[16,64,128]{2,1,0:T(8,128)(2,1)} %get-tuple-element.25), calls=%async_computation.3 | async-start | bytes 524288 | tf_op jit(solution)/shard_map/all_to_all | solution.py:508
  88.2 10.3 %collective-permute-start.4 = (f32[3,2,32,128]{3,2,1,0:T(8,128)S(1)}, f32[3,2,32,128]{3,2,1,0:T(8,128)S(1)}, u32[]{:S(2)}, u32[]{:S(2)}) collective-permute-start(f32[3,2,32,128]{3,2,1,0:T(8,128)S(1)} %get-tuple-element.29), channel_id=1, source_target_pairs={{0,32},{16,48},{32,64},{48,80},{64,96},{80,112},{96,128},{112,144}... | collective-permute-start | bytes 294920 | tf_op jit(solution)/shard_map/ppermute | solution.py:513
  90.5 8.0 %collective-permute-start.5 = (f32[3,2,32,128]{3,2,1,0:T(8,128)S(1)}, f32[3,2,32,128]{3,2,1,0:T(8,128)S(1)}, u32[]{:S(2)}, u32[]{:S(2)}) collective-permute-start(f32[3,2,32,128]{3,2,1,0:T(8,128)S(1)} %get-tuple-element.30), channel_id=1, source_target_pairs={{32,0},{48,16},{64,32},{80,48},{96,64},{112,80},{128,96},{144,112}... | collective-permute-start | bytes 294920 | tf_op jit(solution)/shard_map/ppermute | solution.py:513
  91.8 6.7 %collective-permute-start.2 = (f32[2,2,8,128]{3,2,1,0:T(8,128)S(1)}, f32[2,2,8,128]{3,2,1,0:T(8,128)S(1)}, u32[]{:S(2)}, u32[]{:S(2)}) collective-permute-start(f32[2,2,8,128]{3,2,1,0:T(8,128)S(1)} %get-tuple-element.27), channel_id=1, source_target_pairs={{0,1},{1,2},{2,3},{3,4},{4,5},{5,6},{6,7},{7,8},{8,9},{9,10},{10,1... | collective-permute-start | bytes 49160 | tf_op jit(solution)/shard_map/ppermute | solution.py:513
  97.2 6.1 %collective-permute-start.3 = (f32[2,2,8,128]{3,2,1,0:T(8,128)S(1)}, f32[2,2,8,128]{3,2,1,0:T(8,128)S(1)}, u32[]{:S(2)}, u32[]{:S(2)}) collective-permute-start(f32[2,2,8,128]{3,2,1,0:T(8,128)S(1)} %get-tuple-element.28), channel_id=1, source_target_pairs={{1,0},{2,1},{3,2},{4,3},{5,4},{6,5},{7,6},{8,7},{9,8},{10,9},{11,1... | collective-permute-start | bytes 49160 | tf_op jit(solution)/shard_map/ppermute | solution.py:513
  105.0 35.3 %copy-start.4 = (bf16[3,32,32,3,3,3]{2,1,5,4,3,0:T(8,128)(2,1)S(1)}, bf16[3,32,32,3,3,3]{2,1,5,4,3,0:T(8,128)(2,1)}, u32[]{:S(2)}) copy-start(bf16[3,32,32,3,3,3]{2,1,5,4,3,0:T(8,128)(2,1)} %param.14) | copy-start | bytes 497668
  105.0 25.6 %all-to-all-start.4 = ((f32[16,16,128]{2,1,0:T(8,128)}), f32[16,16,128]{2,1,0:T(8,128)S(1)}, u32[]{:S(2)}, u32[]{:S(2)}) async-start(f32[16,16,128]{2,1,0:T(8,128)} %shard_map.109.refs_3_), calls=%async_computation.4 | async-start | bytes 262144 | tf_op jit(solution)/shard_map/all_to_all | solution.py:508
  113.0 10.9 %collective-permute-start.7 = (f32[2,2,32,128]{3,2,1,0:T(8,128)S(1)}, f32[2,2,32,128]{3,2,1,0:T(8,128)S(1)}, u32[]{:S(2)}, u32[]{:S(2)}) collective-permute-start(f32[2,2,32,128]{3,2,1,0:T(8,128)S(1)} %shard_map.110.refs_2_.near_ref.refs_9_), channel_id=1, source_target_pairs={{16,0},{32,16},{48,32},{64,48},{80,64},{96,80},{112,96},{128,112},... | collective-permute-start | bytes 196616 | tf_op jit(solution)/shard_map/ppermute | solution.py:513
  119.0 6.0 %collective-permute-start.6 = (f32[2,2,32,128]{3,2,1,0:T(8,128)S(1)}, f32[2,2,32,128]{3,2,1,0:T(8,128)S(1)}, u32[]{:S(2)}, u32[]{:S(2)}) collective-permute-start(f32[2,2,32,128]{3,2,1,0:T(8,128)S(1)} %shard_map.110.refs_2_.near_ref.refs_9_), channel_id=1, source_target_pairs={{0,16},{16,32},{32,48},{48,64},{64,80},{80,96},{96,112},{112,128},... | collective-permute-start | bytes 196616 | tf_op jit(solution)/shard_map/ppermute | solution.py:513
  124.9 16.1 %collective-permute-start.8 = (f32[3,2,32,128]{3,2,1,0:T(8,128)S(1)}, f32[3,2,32,128]{3,2,1,0:T(8,128)S(1)}, u32[]{:S(2)}, u32[]{:S(2)}) collective-permute-start(f32[3,2,32,128]{3,2,1,0:T(8,128)S(1)} %get-tuple-element.32), channel_id=1, source_target_pairs={{0,32},{16,48},{32,64},{48,80},{64,96},{80,112},{96,128},{112,144}... | collective-permute-start | bytes 294920 | tf_op jit(solution)/shard_map/ppermute | solution.py:513
  129.3 11.8 %collective-permute-start.9 = (f32[3,2,32,128]{3,2,1,0:T(8,128)S(1)}, f32[3,2,32,128]{3,2,1,0:T(8,128)S(1)}, u32[]{:S(2)}, u32[]{:S(2)}) collective-permute-start(f32[3,2,32,128]{3,2,1,0:T(8,128)S(1)} %get-tuple-element.33), channel_id=1, source_target_pairs={{32,0},{48,16},{64,32},{80,48},{96,64},{112,80},{128,96},{144,112}... | collective-permute-start | bytes 294920 | tf_op jit(solution)/shard_map/ppermute | solution.py:513
  131.2 14.8 %all-to-all-start.5 = ((f32[16,8,128]{2,1,0:T(8,128)}), f32[16,8,128]{2,1,0:T(8,128)S(1)}, u32[]{:S(2)}, u32[]{:S(2)}) async-start(f32[16,8,128]{2,1,0:T(8,128)} %shard_map.111), calls=%async_computation.5 | async-start | bytes 131072 | tf_op jit(solution)/shard_map/all_to_all | solution.py:508

commit v7 on v5

--- a/solution.py
+++ b/solution.py
@@ -11,6 +11,7 @@
 
 LAMBDA = 0.5
 HALO = 5
+STEPS = 32000.0
 SIDE = 8
 GROUP = 2
 F32 = jnp.float32
@@ -116,24 +117,65 @@
     return [[values[p * rows : (p + 1) * rows, a * columns : (a + 1) * columns] for p in range(2)] for a in range(2)]
 
 
+def to_float(values):
+    return values.astype(jnp.int32).astype(F32)
+
+
+def to_short(values):
+    return jnp.floor(values + 0.5).astype(jnp.int32).astype(jnp.int16)
+
+
+def exponent_of(largest):
+    return jnp.ceil(jnp.log2(jnp.maximum(largest, 1e-30)))
+
+
+def scales_of(blocks_ref):
+    return jnp.exp2(to_float(blocks_ref[:, 64:80, :])[:, 0:1, :]) * (1.0 / STEPS)
+
+
 def load_image(blocks_ref):
     count, _, columns = blocks_ref.shape
-    rows = 16
+    scales = scales_of(blocks_ref)
 
     def one(a, p):
-        start = (2 * a + p) * rows
-        return blocks_ref[:, start : start + rows, :].reshape(count * rows, columns)
+        start = (2 * a + p) * 16
+        return (to_float(blocks_ref[:, start : start + 16, :]) * scales).reshape(count * 16, columns)
 
     return [[one(a, p) for p in range(2)] for a in range(2)]
 
 
-def store_image(blocks_ref, image):
+def store_image(blocks_ref, image, extra):
     count, _, columns = blocks_ref.shape
-    rows = 16
-    for a in range(2):
-        for p in range(2):
-            start = (2 * a + p) * rows
-            blocks_ref[:, start : start + rows, :] = image[a][p].reshape(count, rows, columns)
+    blocks = [image[a][p].reshape(count, 16, columns) for a in range(2) for p in range(2)]
+    largest = jnp.maximum(
+        jnp.maximum(jnp.abs(blocks[0]), jnp.abs(blocks[1])), jnp.maximum(jnp.abs(blocks[2]), jnp.abs(blocks[3]))
+    )
+    largest = jnp.max(jnp.max(largest, axis=1, keepdims=True), axis=2, keepdims=True)
+    exponents = exponent_of(largest)
+    factors = jnp.exp2(-exponents) * STEPS
+    for i in range(4):
+        blocks_ref[:, 16 * i : 16 * i + 16, :] = to_short(blocks[i] * factors)
+    row = lax.broadcasted_iota(jnp.int32, (count, 16, columns), 1)
+    last = jnp.where(row == 0, exponents, extra)
+    blocks_ref[:, 64:80, :] = to_short(last)
+
+
+def store_copies(blocks_ref, rows):
+    exponent = exponent_of(jnp.max(jnp.max(jnp.abs(rows), axis=0, keepdims=True), axis=1, keepdims=True))
+    shorts = to_short(rows * (jnp.exp2(-exponent) * STEPS))
+    tail = to_short(jnp.broadcast_to(exponent, (16, 128)))
+    for k in range(blocks_ref.shape[0]):
+        blocks_ref[k, 0:64, :] = shorts
+        blocks_ref[k, 64:80, :] = tail
+    return to_float(shorts) * (jnp.exp2(exponent) * (1.0 / STEPS))
+
+
+def sum_blocks(blocks_ref):
+    scales = scales_of(blocks_ref)
+    total = to_float(blocks_ref[0, 0:64, :]) * scales[0]
+    for k in range(1, blocks_ref.shape[0]):
+        total = total + to_float(blocks_ref[k, 0:64, :]) * scales[k]
+    return total
 
 
 def coil_field(maps_ref, image):
@@ -170,12 +212,17 @@
 
 def store_near(near_ref, blocks_ref, at):
     count = blocks_ref.shape[0]
+
+    def one(at, start):
+        scale = jnp.exp2(to_float(blocks_ref[at, 64:80, :])[0:1]) * (1.0 / STEPS)
+        return to_float(blocks_ref[at, start : start + 16, :]) * scale
+
     for a in range(2):
         for p in range(2):
             start = (2 * a + p) * 16
-            near_ref[p, a, 8:24, :] = blocks_ref[at, start : start + 16, :]
-            before = blocks_ref[jnp.maximum(at - 1, 0), start + 8 : start + 16, :]
-            after = blocks_ref[jnp.minimum(at + 1, count - 1), start : start + 8, :]
+            near_ref[p, a, 8:24, :] = one(at, start)
+            before = one(jnp.maximum(at - 1, 0), start)[8:16]
+            after = one(jnp.minimum(at + 1, count - 1), start)[0:8]
             near_ref[p, a, 0:8, :] = jnp.where(at > 0, before, 0.0)
             near_ref[p, a, 24:32, :] = jnp.where(at < count - 1, after, 0.0)
 
@@ -195,14 +242,14 @@
     copies[3].wait()
     field = dft_columns(field, columns_ref, 1.0)
     copies[4].wait()
-    store_image(out_ref, coil_term(maps_ref, field))
+    store_image(out_ref, coil_term(maps_ref, field), 0.0)
 
 
 def adjoint(mask, kspace, rows, columns, maps, coils):
     args = (mask, kspace, rows, columns, maps)
     return pl.pallas_call(
         adjoint_kernel,
-        out_shape=struct((coils, 64, 128)),
+        out_shape=struct((coils, 80, 128), jnp.int16),
         in_specs=[pl.BlockSpec(memory_space=pl.ANY)] * len(args),
         out_specs=pl.BlockSpec(memory_space=pltpu.VMEM),
         scratch_shapes=[pltpu.VMEM(arg.shape, arg.dtype) for arg in args] + [pltpu.SemaphoreType.DMA((len(args),))],
@@ -211,13 +258,8 @@
 
 
 def rows_kernel(blocks_ref, prior_ref, rows_ref, copies_ref):
-    count = blocks_ref.shape[0]
-    total = jnp.sum(blocks_ref[...], axis=0)
     prior = jnp.concatenate([prior_ref[a, p] for a in range(2) for p in range(2)], axis=0)
-    total = total + LAMBDA * prior
-    rows_ref[...] = total
-    for k in range(count):
-        copies_ref[k] = total
+    rows_ref[...] = store_copies(copies_ref, sum_blocks(blocks_ref) + LAMBDA * prior)
 
 
 def normal_kernel(
@@ -231,11 +273,26 @@
         for p in range(2):
             spectrum_ref[a, p] = spectrum[a][p]
     field = dft_columns(dft_rows(spectrum, rows_ref, 1.0), columns_ref, 1.0)
-    store_image(out_ref, coil_term(maps_ref, field))
-    tile_ref[...] = tile_of([inner(image, image)])
-    energies = tile_of([inner(spectrum, spectrum)])
-    for k in range(blocks_ref.shape[0]):
-        out_ref[k, 64:72, :] = energies
+    energy = inner(spectrum, spectrum)
+    tile_ref[...] = tile_of([inner(image, image), energy])
+    coarse = lane_sum(energy)
+    level = exponent_of(coarse)
+    row = lax.broadcasted_iota(jnp.int32, (1, 16, 128), 1)
+    extra = jnp.where(row == 1, level, jnp.exp2(-level) * STEPS * coarse)
+    store_image(out_ref, coil_term(maps_ref, field), extra)
+
+
+def image_kernel(blocks_ref, rhs_rows_ref, tile_ref, copies_ref, sums_ref):
+    rhs = rhs_rows_ref[...]
+    image = store_copies(copies_ref, sum_blocks(blocks_ref) + LAMBDA * rhs)
+    extra = to_float(blocks_ref[:, 64:80, :])
+    coarse = jnp.sum(jnp.exp2(extra[:, 1:2, :]) * extra[:, 2:3, :], axis=0) * (1.0 / STEPS)
+    norm, energy = tile_ref[0:1, :], tile_ref[1:2, :]
+    step = slab_step(lane_sum(norm), coarse)
+    residual = rhs - step * image
+    share = 1.0 / blocks_ref.shape[0]
+    rows = [row_sum(residual * residual), row_sum(residual * rhs), share * norm, energy, share * step]
+    sums_ref[...] = tile_of(rows)
 
 
 def lane_sum(values):
@@ -247,25 +304,13 @@
     return jnp.where(curved > 0.0, norm / jnp.where(curved > 0.0, curved, 1.0), 1.0)
 
 
-def image_kernel(blocks_ref, rhs_rows_ref, norms_ref, copies_ref, sums_ref):
-    total = jnp.sum(blocks_ref[...], axis=0)
-    rhs = rhs_rows_ref[...]
-    image = total[:64] + LAMBDA * rhs
-    for k in range(blocks_ref.shape[0]):
-        copies_ref[k] = image
-    norm, energy = norms_ref[0:1, :], total[64:65]
-    residual = rhs - slab_step(lane_sum(norm), lane_sum(energy)) * image
-    share = 1.0 / blocks_ref.shape[0]
-    sums_ref[...] = tile_of([row_sum(residual * residual), row_sum(residual * rhs), share * norm, share * energy])
-
-
 def last_kernel(sums_ref, blocks_ref, spectrum_ref, mask_ref, maps_ref, rows_ref, columns_ref, out_ref):
-    step = slab_step(lane_sum(sums_ref[2:3, :]), lane_sum(sums_ref[3:4, :]))
+    step = sums_ref[4:5, :] * float(blocks_ref.shape[0])
     field = dft_columns(coil_field(maps_ref, load_image(blocks_ref)), columns_ref, -1.0)
     spectrum = masked(dft_rows(field, rows_ref, -1.0), mask_ref)
     before = [[spectrum_ref[a, p] for p in range(2)] for a in range(2)]
     spectrum = [[before[a][p] - step * spectrum[a][p] for p in range(2)] for a in range(2)]
-    tile = tile_of([inner(spectrum, spectrum), inner(spectrum, before)] + [sums_ref[i : i + 1, :] for i in range(4)])
+    tile = tile_of([inner(spectrum, spectrum), inner(spectrum, before)] + [sums_ref[i : i + 1, :] for i in range(5)])
     for k in range(out_ref.shape[0]):
         out_ref[k, 0:8] = tile
         out_ref[k, 8:] = jnp.zeros((out_ref.shape[1] - 8, 128), F32)
@@ -273,6 +318,13 @@
 
 def near_kernel(at_ref, blocks_ref, near_ref):
     store_near(near_ref, blocks_ref, at_ref[0])
+
+
+def pack_kernel(below_ref, near_ref, above_ref, low_ref, high_ref):
+    low_ref[0] = below_ref[1]
+    low_ref[1:3] = near_ref[...]
+    high_ref[0:2] = near_ref[...]
+    high_ref[2] = above_ref[0]
 
 
 def spread_kernel(tiles_ref, out_ref):
@@ -285,13 +337,14 @@
     curve, curve_cross, norm, cross, norm_first, energy_first = [
         lane_sum(tiles_ref[:, i, :]) for i in range(6)
     ]
+    step_here = tiles_ref[:, 6, 0:1]
 
     def over_slabs(values):
         return jnp.sum(values, axis=0, keepdims=True)
 
     all_norm, all_energy = over_slabs(norm_first), over_slabs(energy_first)
     step_first = all_norm / (all_energy + LAMBDA * all_norm)
-    here = step_first / slab_step(norm_first, energy_first)
+    here = step_first / step_here
     rest = 1.0 - here
     curve = over_slabs(here * here * curve + rest * (2.0 * here * curve_cross + rest * energy_first))
     curve_cross = over_slabs(here * curve_cross + rest * energy_first)
@@ -473,17 +526,15 @@
     return lax.all_to_all(blocks, axis, 0, 0, tiled=True)
 
 
+def shifted(part, axis, step):
+    count = lax.axis_size(axis)
+    return lax.ppermute(part, axis, [(i, i + step) for i in range(count) if 0 <= i + step < count])
+
+
 def near_planes(near):
-    count = lax.axis_size("slab")
-
-    def shifted(part, step):
-        pairs = [(i, i + step) for i in range(count) if 0 <= i + step < count]
-        return lax.ppermute(part, "slab", pairs)
-
-    below, above = shifted(near, 1), shifted(near, -1)
-    below_far = shifted(jnp.concatenate([below[1:], near]), 2)
-    above_far = shifted(jnp.concatenate([near, above[:1]]), -2)
-    return [below_far, below, near, above, above_far]
+    below, above = shifted(near, "slab", 1), shifted(near, "slab", -1)
+    low, high = call(pack_kernel, (struct((3, 2, 32, 128)),) * 2, (below, near, above))
+    return [shifted(low, "slab", 2), below, near, above, shifted(high, "slab", -2)]
 
 
 def body(sensitivity, kspace, sampling, prior_image, w_first, w_middle, w_last):
@@ -497,7 +548,7 @@
     term = adjoint(sampling, kspace[0], rows, columns, maps, coils)
     rhs_rows, copies = call(
         rows_kernel,
-        (struct((64, 128)), struct((coils, 64, 128))),
+        (struct((64, 128)), struct((coils, 80, 128), jnp.int16)),
         (swap(term, "coil"), prior_image),
         after=prepared,
     )
@@ -505,14 +556,19 @@
     near_shape = struct((2, 2, 32, 128))
     term, spectrum, norms, rhs_near = call(
         normal_kernel,
-        (struct((coils, 72, 128)), struct((2, 2, len_y, len_z)), struct((8, 128)), near_shape),
+        (
+            struct((coils, 80, 128), jnp.int16),
+            struct((2, 2, len_y, len_z)),
+            struct((8, 128)),
+            near_shape,
+        ),
         (at, rhs, sampling, maps, rows, columns),
         in_smem=(0,),
     )
     rhs_parts = near_planes(rhs_near)
     copies, sums = call(
         image_kernel,
-        (struct((coils, 64, 128)), struct((8, 128))),
+        (struct((coils, 80, 128), jnp.int16), struct((8, 128))),
         (swap(term, "coil"), rhs_rows, norms),
         after=rhs_parts,
     )

time: 156 us -> 143 us (0.917)
  waiting for transfers between devices: 59.5 us -> 48.8 us
  local copies, waits for them, and re-layouts: 3.67 us -> 0.86 us
    all_to_all x6, waiting for transfers between devices: 53.1 us -> 41.6 us  [swap(): return lax.all_to_all(blocks, axis, 0, 0, tiled=True)]
    pallas_call x9 -> x11, Pallas kernels: 19.6 us -> 20 us  [call(): pl.pallas_call(kernel, out_shape=out_shape, in_specs=specs, out_specs=out...]
  transfers between devices with their start and end apart: 14 -> 14, of which waited for: 11 -> 10; matrix products, arithmetic and copies ran while one was open for 0% -> 0% of each run, Pallas kernels for 1% -> 1%
where the time goes in v7:
time: 143 us; the launch traced here: 142 us
  starting transfers between devices  67.5 us (47%)
  waiting for transfers between devices  48.8 us (34%)
  Pallas kernels  23.7 us (17%)
    all_to_all x6, waiting for transfers between devices, swap(): return lax.all_to_all(blocks, axis, 0, 0, tiled=True)  41.6 us
    all_to_all x6, starting transfers between devices, swap(): return lax.all_to_all(blocks, axis, 0, 0, tiled=True)  41.1 us
    ppermute x8, starting transfers between devices, shifted(): lax.ppermute(part, axis, [(i, i + step) for i in range(count) if 0 <= i +...  26.4 us
    pallas_call x11, Pallas kernels, call(): pl.pallas_call(kernel, out_shape=out_shape, in_specs=specs, out_specs=out...  20 us
    ppermute x8, waiting for transfers between devices, shifted(): lax.ppermute(part, axis, [(i, i + step) for i in range(count) if 0 <= i +...  7.22 us
    pallas_call x1, Pallas kernels, adjoint(): pl.pallas_call(adjoint_kernel, out_shape=struct((coils, 80, 128), jnp.int...  3.66 us
  transfers between devices with their start and end apart: 14, of which 10 were waited for; matrix products, arithmetic and copies ran while one was open for 0% of the time, Pallas kernels for 1%

profile of v7, /device:TPU:1, one launch (start us, length us, event | category | flops | bytes accessed | tf_op | source)
XLA Modules:
  0.0 141.9 jit_solution(14021089372492305675)
XLA Ops:
  0.6 3.7 %shard_map.104 = s16[16,80,128]{2,1,0:T(8,128)(2,1)} custom-call(s32[2,256,128]{2,1,0:T(8,128)} %refs_3_.1, f32[2,2,256,128]{3,2,1,0:T(8,128)} %bitcast.12, bf16[512,512]{1,0:T(8,128)(2,1)} %constant.14.clone.rows_hbm.rows_ref.refs_5_, bf16[128,512]{1,0:T(8,128)(2,1)} %constant.15.clone.columns_hbm.columns_ref.refs_6_, f32[2,2,256,128]{3,2,1,0:T(8,128)} %bitcast.8), custom_call_target="tpu_custom_call" | custom-call | tf_op jit(solution)/shard_map/pallas_call | solution.py:250
  4.3 11.9 %all-to-all-start = ((s16[16,80,128]{2,1,0:T(8,128)(2,1)}), s16[16,80,128]{2,1,0:T(8,128)(2,1)S(1)}, u32[]{:S(2)}, u32[]{:S(2)}) async-start(s16[16,80,128]{2,1,0:T(8,128)(2,1)} %shard_map.104), calls=%async_computation | async-start | bytes 655360 | tf_op jit(solution)/shard_map/all_to_all | solution.py:526
  16.4 0.6 copy-done.7
  17.1 12.5 %all-to-all-done.refs_0_ = s16[16,80,128]{2,1,0:T(8,128)(2,1)S(1)} async-done(((s16[16,80,128]{2,1,0:T(8,128)(2,1)}), s16[16,80,128]{2,1,0:T(8,128)(2,1)S(1)}, u32[]{:S(2)}, u32[]{:S(2)}) %all-to-all-start) | async-done | bytes 327712 | tf_op jit(solution)/shard_map/all_to_all | solution.py:526
  29.6 0.9 shard_map.105
  30.6 3.9 %all-to-all-start.1 = ((s16[16,80,128]{2,1,0:T(8,128)(2,1)}), s16[16,80,128]{2,1,0:T(8,128)(2,1)S(1)}, u32[]{:S(2)}, u32[]{:S(2)}) async-start(s16[16,80,128]{2,1,0:T(8,128)(2,1)} %get-tuple-element.16), calls=%async_computation.1 | async-start | bytes 655360 | tf_op jit(solution)/shard_map/all_to_all | solution.py:526
  34.6 12.2 %all-to-all-done.1.blocks_ref = s16[16,80,128]{2,1,0:T(8,128)(2,1)S(1)} async-done(((s16[16,80,128]{2,1,0:T(8,128)(2,1)}), s16[16,80,128]{2,1,0:T(8,128)(2,1)S(1)}, u32[]{:S(2)}, u32[]{:S(2)}) %all-to-all-start.1) | async-done | bytes 327712 | tf_op jit(solution)/shard_map/all_to_all | solution.py:526
  46.9 4.0 %shard_map.106 = (s16[16,80,128]{2,1,0:T(8,128)(2,1)}, f32[2,2,256,128]{3,2,1,0:T(8,128)S(1)}, f32[8,128]{1,0:T(8,128)S(1)}, f32[2,2,32,128]{3,2,1,0:T(8,128)S(1)}) custom-call(s32[2]{0:T(128)S(1)} %pad_add_fusion.at_ref.refs_0_, s16[16,80,128]{2,1,0:T(8,128)(2,1)S(1)} %all-to-all-done.1.blocks_ref, s32[2,256,128]{2,1,0:T(8,128)S(1)} %copy-done.2, ...), custom_call_target="tpu_custom_call" | custom-call | tf_op jit(solution)/shard_map/pallas_call | solution.py:34
  50.8 3.9 %all-to-all-start.2 = ((s16[16,80,128]{2,1,0:T(8,128)(2,1)}), s16[16,80,128]{2,1,0:T(8,128)(2,1)S(1)}, u32[]{:S(2)}, u32[]{:S(2)}) async-start(s16[16,80,128]{2,1,0:T(8,128)(2,1)} %get-tuple-element.17), calls=%async_computation.2 | async-start | bytes 655360 | tf_op jit(solution)/shard_map/all_to_all | solution.py:526
  54.7 5.1 %collective-permute-start.1 = (f32[2,2,32,128]{3,2,1,0:T(8,128)S(1)}, f32[2,2,32,128]{3,2,1,0:T(8,128)S(1)}, u32[]{:S(2)}, u32[]{:S(2)}) collective-permute-start(f32[2,2,32,128]{3,2,1,0:T(8,128)S(1)} %get-tuple-element.20.near_ref.refs_5_.refs_4_), channel_id=1, source_target_pairs={{16,0},{32,16},{48,32},{64,48},{80,64},{96,80},{112,96},{128,112},... | collective-permute-start | bytes 196616 | tf_op jit(solution)/shard_map/ppermute | solution.py:531
  59.9 2.2 %collective-permute-start = (f32[2,2,32,128]{3,2,1,0:T(8,128)S(1)}, f32[2,2,32,128]{3,2,1,0:T(8,128)S(1)}, u32[]{:S(2)}, u32[]{:S(2)}) collective-permute-start(f32[2,2,32,128]{3,2,1,0:T(8,128)S(1)} %get-tuple-element.20.near_ref.refs_5_.refs_4_), channel_id=1, source_target_pairs={{0,16},{16,32},{32,48},{48,64},{64,80},{80,96},{96,112},{112,128},... | collective-permute-start | bytes 196616 | tf_op jit(solution)/shard_map/ppermute | solution.py:531
  62.5 1.5 %collective-permute-done.below_ref.refs_4_.refs_3_ = f32[2,2,32,128]{3,2,1,0:T(8,128)S(1)} collective-permute-done((f32[2,2,32,128]{3,2,1,0:T(8,128)S(1)}, f32[2,2,32,128]{3,2,1,0:T(8,128)S(1)}, u32[]{:S(2)}, u32[]{:S(2)}) %collective-permute-start) | collective-permute-done | bytes 65568 | tf_op jit(solution)/shard_map/ppermute | solution.py:531
  64.0 3.4 %collective-permute-start.2 = (f32[3,2,32,128]{3,2,1,0:T(8,128)S(1)}, f32[3,2,32,128]{3,2,1,0:T(8,128)S(1)}, u32[]{:S(2)}, u32[]{:S(2)}) collective-permute-start(f32[3,2,32,128]{3,2,1,0:T(8,128)S(1)} %get-tuple-element.21), channel_id=1, source_target_pairs={{0,32},{16,48},{32,64},{48,80},{64,96},{80,112},{96,128},{112,144}... | collective-permute-start | bytes 294920 | tf_op jit(solution)/shard_map/ppermute | solution.py:531
  67.3 1.3 collective-permute-start.3
  68.9 3.7 %collective-permute-done.3.refs_7_.refs_6_ = f32[3,2,32,128]{3,2,1,0:T(8,128)S(1)} collective-permute-done((f32[3,2,32,128]{3,2,1,0:T(8,128)S(1)}, f32[3,2,32,128]{3,2,1,0:T(8,128)S(1)}, u32[]{:S(2)}, u32[]{:S(2)}) %collective-permute-start.3) | collective-permute-done | bytes 98336 | tf_op jit(solution)/shard_map/ppermute | solution.py:531
  72.7 0.9 shard_map.108
  73.6 9.3 %all-to-all-start.3 = ((s16[16,80,128]{2,1,0:T(8,128)(2,1)}), s16[16,80,128]{2,1,0:T(8,128)(2,1)S(1)}, u32[]{:S(2)}, u32[]{:S(2)}) async-start(s16[16,80,128]{2,1,0:T(8,128)(2,1)} %get-tuple-element.24), calls=%async_computation.3 | async-start | bytes 655360 | tf_op jit(solution)/shard_map/all_to_all | solution.py:526
  83.0 11.8 %all-to-all-done.3.refs_1_ = s16[16,80,128]{2,1,0:T(8,128)(2,1)S(1)} async-done(((s16[16,80,128]{2,1,0:T(8,128)(2,1)}), s16[16,80,128]{2,1,0:T(8,128)(2,1)S(1)}, u32[]{:S(2)}, u32[]{:S(2)}) %all-to-all-start.3) | async-done | bytes 327712 | tf_op jit(solution)/shard_map/all_to_all | solution.py:526
  94.8 1.7 %shard_map.110.refs_2_ = f32[16,16,128]{2,1,0:T(8,128)} custom-call(f32[8,128]{1,0:T(8,128)S(1)} %get-tuple-element.23.refs_0_, s16[16,80,128]{2,1,0:T(8,128)(2,1)S(1)} %all-to-all-done.3.refs_1_, f32[2,2,256,128]{3,2,1,0:T(8,128)S(1)} %get-tuple-element.25.refs_2_, s32[2,256,128]{2,1,0:T(8,128)S(1)} %copy-done.2, f32[2,2,256,128]{3,2,1,0:T(8,128)S(1)} %bitcast.10, ...), custom_call_target="tpu_custom_call" | custom-call | tf_op jit(solution)/shard_map/pallas_call | solution.py:34
  96.5 3.6 %all-to-all-start.4 = ((f32[16,16,128]{2,1,0:T(8,128)}), f32[16,16,128]{2,1,0:T(8,128)S(1)}, u32[]{:S(2)}, u32[]{:S(2)}) async-start(f32[16,16,128]{2,1,0:T(8,128)} %shard_map.110.refs_2_), calls=%async_computation.4 | async-start | bytes 262144 | tf_op jit(solution)/shard_map/all_to_all | solution.py:526
  100.2 0.6 shard_map.111.near_ref.refs_9_
  100.7 6.3 %collective-permute-start.5 = (f32[2,2,32,128]{3,2,1,0:T(8,128)S(1)}, f32[2,2,32,128]{3,2,1,0:T(8,128)S(1)}, u32[]{:S(2)}, u32[]{:S(2)}) collective-permute-start(f32[2,2,32,128]{3,2,1,0:T(8,128)S(1)} %shard_map.111.near_ref.refs_9_), channel_id=1, source_target_pairs={{16,0},{32,16},{48,32},{64,48},{80,64},{96,80},{112,96},{128,112},... | collective-permute-start | bytes 196616 | tf_op jit(solution)/shard_map/ppermute | solution.py:531
  107.0 3.8 %collective-permute-start.4 = (f32[2,2,32,128]{3,2,1,0:T(8,128)S(1)}, f32[2,2,32,128]{3,2,1,0:T(8,128)S(1)}, u32[]{:S(2)}, u32[]{:S(2)}) collective-permute-start(f32[2,2,32,128]{3,2,1,0:T(8,128)S(1)} %shard_map.111.near_ref.refs_9_), channel_id=1, source_target_pairs={{0,16},{16,32},{32,48},{48,64},{64,80},{80,96},{96,112},{112,128},... | collective-permute-start | bytes 196616 | tf_op jit(solution)/shard_map/ppermute | solution.py:531
  110.8 0.5 collective-permute-done.5.refs_2_.above_ref.refs_10_
  111.3 0.8 collective-permute-done.4.refs_1_.below_ref.refs_8_
  112.1 3.0 %collective-permute-start.6 = (f32[3,2,32,128]{3,2,1,0:T(8,128)S(1)}, f32[3,2,32,128]{3,2,1,0:T(8,128)S(1)}, u32[]{:S(2)}, u32[]{:S(2)}) collective-permute-start(f32[3,2,32,128]{3,2,1,0:T(8,128)S(1)} %get-tuple-element.26), channel_id=1, source_target_pairs={{0,32},{16,48},{32,64},{48,80},{64,96},{80,112},{96,128},{112,144}... | collective-permute-start | bytes 294920 | tf_op jit(solution)/shard_map/ppermute | solution.py:531
  115.2 1.3 collective-permute-start.7
  116.5 0.6 shard_map.112
  117.1 8.5 %all-to-all-start.5 = ((f32[16,8,128]{2,1,0:T(8,128)}), f32[16,8,128]{2,1,0:T(8,128)S(1)}, u32[]{:S(2)}, u32[]{:S(2)}) async-start(f32[16,8,128]{2,1,0:T(8,128)} %shard_map.112), calls=%async_computation.5 | async-start | bytes 131072 | tf_op jit(solution)/shard_map/all_to_all | solution.py:526
  125.7 0.8 shard_map.114
  126.4 5.1 %all-to-all-done.5.refs_1_ = f32[16,8,128]{2,1,0:T(8,128)S(1)} async-done(((f32[16,8,128]{2,1,0:T(8,128)}), f32[16,8,128]{2,1,0:T(8,128)S(1)}, u32[]{:S(2)}, u32[]{:S(2)}) %all-to-all-start.5) | async-done | bytes 65568 | tf_op jit(solution)/shard_map/all_to_all | solution.py:526
  131.5 10.4 %shard_map.115 = (f32[2,2,16,128]{3,2,1,0:T(8,128)}, f32[2,2,16,128]{3,2,1,0:T(8,128)}) custom-call(s32[2]{0:T(128)S(1)} %pad_add_fusion.at_ref.refs_0_, f32[16,8,128]{2,1,0:T(8,128)S(1)} %all-to-all-done.5.refs_1_, f32[3,2,32,128]{3,2,1,0:T(8,128)S(1)} %collective-permute-done.2.refs_3_.refs_2_, ...), custom_call_target="tpu_custom_call" | custom-call | tf_op jit(solution)/shard_map/pallas_call | solution.py:34
  (32 shorter events, 1.2 us)
Async XLA Ops:
  4.3 11.9 %copy-start.6 = (bf16[32,2,3,3,3]{0,1,4,3,2:T(2,128)(2,1)S(1)}, bf16[32,2,3,3,3]{0,1,4,3,2:T(2,128)(2,1)}, u32[]{:S(2)}) copy-start(bf16[32,2,3,3,3]{0,1,4,3,2:T(2,128)(2,1)} %param.13) | copy-start | bytes 10372
  4.3 42.5 %copy-start.3 = (bf16[128,512]{1,0:T(8,128)(2,1)S(1)}, bf16[128,512]{1,0:T(8,128)(2,1)}, u32[]{:S(2)}) copy-start(bf16[128,512]{1,0:T(8,128)(2,1)} %constant.15.clone.columns_hbm.columns_ref.refs_6_) | copy-start | bytes 393220
  4.3 25.3 %all-to-all-start = ((s16[16,80,128]{2,1,0:T(8,128)(2,1)}), s16[16,80,128]{2,1,0:T(8,128)(2,1)S(1)}, u32[]{:S(2)}, u32[]{:S(2)}) async-start(s16[16,80,128]{2,1,0:T(8,128)(2,1)} %shard_map.104), calls=%async_computation | async-start | bytes 655360 | tf_op jit(solution)/shard_map/all_to_all | solution.py:526
  16.2 0.7 copy-start.7
  16.3 13.4 %copy-start.5 = (f32[2,2,16,128]{3,2,1,0:T(8,128)S(1)}, f32[2,2,16,128]{3,2,1,0:T(8,128)}, u32[]{:S(2)}) copy-start(f32[2,2,16,128]{3,2,1,0:T(8,128)} %refs_1_.1) | copy-start | bytes 98308
  16.3 30.5 %copy-start.2 = (s32[2,256,128]{2,1,0:T(8,128)S(1)}, s32[2,256,128]{2,1,0:T(8,128)}, u32[]{:S(2)}) copy-start(s32[2,256,128]{2,1,0:T(8,128)} %refs_3_.1) | copy-start | bytes 786436
  17.1 29.7 %copy-start = (f32[1,2,2,256,128]{4,3,2,1,0:T(8,128)S(1)}, f32[1,2,2,256,128]{4,3,2,1,0:T(8,128)}, u32[]{:S(2)}) copy-start(f32[1,2,2,256,128]{4,3,2,1,0:T(8,128)} %param.9) | copy-start | bytes 1572868
  17.1 29.7 %copy-start.1 = (bf16[512,512]{1,0:T(8,128)(2,1)S(1)}, bf16[512,512]{1,0:T(8,128)(2,1)}, u32[]{:S(2)}) copy-start(bf16[512,512]{1,0:T(8,128)(2,1)} %constant.14.clone.rows_hbm.rows_ref.refs_5_) | copy-start | bytes 1572868
  30.6 16.2 %all-to-all-start.1 = ((s16[16,80,128]{2,1,0:T(8,128)(2,1)}), s16[16,80,128]{2,1,0:T(8,128)(2,1)S(1)}, u32[]{:S(2)}, u32[]{:S(2)}) async-start(s16[16,80,128]{2,1,0:T(8,128)(2,1)} %get-tuple-element.16), calls=%async_computation.1 | async-start | bytes 655360 | tf_op jit(solution)/shard_map/all_to_all | solution.py:526
  50.8 21.8 %all-to-all-start.2 = ((s16[16,80,128]{2,1,0:T(8,128)(2,1)}), s16[16,80,128]{2,1,0:T(8,128)(2,1)S(1)}, u32[]{:S(2)}, u32[]{:S(2)}) async-start(s16[16,80,128]{2,1,0:T(8,128)(2,1)} %get-tuple-element.17), calls=%async_computation.2 | async-start | bytes 655360 | tf_op jit(solution)/shard_map/all_to_all | solution.py:526
  54.7 7.7 %collective-permute-start.1 = (f32[2,2,32,128]{3,2,1,0:T(8,128)S(1)}, f32[2,2,32,128]{3,2,1,0:T(8,128)S(1)}, u32[]{:S(2)}, u32[]{:S(2)}) collective-permute-start(f32[2,2,32,128]{3,2,1,0:T(8,128)S(1)} %get-tuple-element.20.near_ref.refs_5_.refs_4_), channel_id=1, source_target_pairs={{16,0},{32,16},{48,32},{64,48},{80,64},{96,80},{112,96},{128,112},... | collective-permute-start | bytes 196616 | tf_op jit(solution)/shard_map/ppermute | solution.py:531
  59.9 4.1 %collective-permute-start = (f32[2,2,32,128]{3,2,1,0:T(8,128)S(1)}, f32[2,2,32,128]{3,2,1,0:T(8,128)S(1)}, u32[]{:S(2)}, u32[]{:S(2)}) collective-permute-start(f32[2,2,32,128]{3,2,1,0:T(8,128)S(1)} %get-tuple-element.20.near_ref.refs_5_.refs_4_), channel_id=1, source_target_pairs={{0,16},{16,32},{32,48},{48,64},{64,80},{80,96},{96,112},{112,128},... | collective-permute-start | bytes 196616 | tf_op jit(solution)/shard_map/ppermute | solution.py:531
  64.0 5.0 %collective-permute-start.2 = (f32[3,2,32,128]{3,2,1,0:T(8,128)S(1)}, f32[3,2,32,128]{3,2,1,0:T(8,128)S(1)}, u32[]{:S(2)}, u32[]{:S(2)}) collective-permute-start(f32[3,2,32,128]{3,2,1,0:T(8,128)S(1)} %get-tuple-element.21), channel_id=1, source_target_pairs={{0,32},{16,48},{32,64},{48,80},{64,96},{80,112},{96,128},{112,144}... | collective-permute-start | bytes 294920 | tf_op jit(solution)/shard_map/ppermute | solution.py:531
  67.3 5.4 %collective-permute-start.3 = (f32[3,2,32,128]{3,2,1,0:T(8,128)S(1)}, f32[3,2,32,128]{3,2,1,0:T(8,128)S(1)}, u32[]{:S(2)}, u32[]{:S(2)}) collective-permute-start(f32[3,2,32,128]{3,2,1,0:T(8,128)S(1)} %get-tuple-element.22), channel_id=1, source_target_pairs={{32,0},{48,16},{64,32},{80,48},{96,64},{112,80},{128,96},{144,112}... | collective-permute-start | bytes 294920 | tf_op jit(solution)/shard_map/ppermute | solution.py:531
  73.6 21.2 %all-to-all-start.3 = ((s16[16,80,128]{2,1,0:T(8,128)(2,1)}), s16[16,80,128]{2,1,0:T(8,128)(2,1)S(1)}, u32[]{:S(2)}, u32[]{:S(2)}) async-start(s16[16,80,128]{2,1,0:T(8,128)(2,1)} %get-tuple-element.24), calls=%async_computation.3 | async-start | bytes 655360 | tf_op jit(solution)/shard_map/all_to_all | solution.py:526
  96.5 29.1 %copy-start.4 = (bf16[3,32,32,3,3,3]{2,1,5,4,3,0:T(8,128)(2,1)S(1)}, bf16[3,32,32,3,3,3]{2,1,5,4,3,0:T(8,128)(2,1)}, u32[]{:S(2)}) copy-start(bf16[3,32,32,3,3,3]{2,1,5,4,3,0:T(8,128)(2,1)} %param.14) | copy-start | bytes 497668
  96.5 20.0 %all-to-all-start.4 = ((f32[16,16,128]{2,1,0:T(8,128)}), f32[16,16,128]{2,1,0:T(8,128)S(1)}, u32[]{:S(2)}, u32[]{:S(2)}) async-start(f32[16,16,128]{2,1,0:T(8,128)} %shard_map.110.refs_2_), calls=%async_computation.4 | async-start | bytes 262144 | tf_op jit(solution)/shard_map/all_to_all | solution.py:526
  100.7 10.5 %collective-permute-start.5 = (f32[2,2,32,128]{3,2,1,0:T(8,128)S(1)}, f32[2,2,32,128]{3,2,1,0:T(8,128)S(1)}, u32[]{:S(2)}, u32[]{:S(2)}) collective-permute-start(f32[2,2,32,128]{3,2,1,0:T(8,128)S(1)} %shard_map.111.near_ref.refs_9_), channel_id=1, source_target_pairs={{16,0},{32,16},{48,32},{64,48},{80,64},{96,80},{112,96},{128,112},... | collective-permute-start | bytes 196616 | tf_op jit(solution)/shard_map/ppermute | solution.py:531
  107.0 5.1 %collective-permute-start.4 = (f32[2,2,32,128]{3,2,1,0:T(8,128)S(1)}, f32[2,2,32,128]{3,2,1,0:T(8,128)S(1)}, u32[]{:S(2)}, u32[]{:S(2)}) collective-permute-start(f32[2,2,32,128]{3,2,1,0:T(8,128)S(1)} %shard_map.111.near_ref.refs_9_), channel_id=1, source_target_pairs={{0,16},{16,32},{32,48},{48,64},{64,80},{80,96},{96,112},{112,128},... | collective-permute-start | bytes 196616 | tf_op jit(solution)/shard_map/ppermute | solution.py:531
  112.1 14.3 %collective-permute-start.6 = (f32[3,2,32,128]{3,2,1,0:T(8,128)S(1)}, f32[3,2,32,128]{3,2,1,0:T(8,128)S(1)}, u32[]{:S(2)}, u32[]{:S(2)}) collective-permute-start(f32[3,2,32,128]{3,2,1,0:T(8,128)S(1)} %get-tuple-element.26), channel_id=1, source_target_pairs={{0,32},{16,48},{32,64},{48,80},{64,96},{80,112},{96,128},{112,144}... | collective-permute-start | bytes 294920 | tf_op jit(solution)/shard_map/ppermute | solution.py:531
  115.2 11.3 %collective-permute-start.7 = (f32[3,2,32,128]{3,2,1,0:T(8,128)S(1)}, f32[3,2,32,128]{3,2,1,0:T(8,128)S(1)}, u32[]{:S(2)}, u32[]{:S(2)}) collective-permute-start(f32[3,2,32,128]{3,2,1,0:T(8,128)S(1)} %get-tuple-element.27), channel_id=1, source_target_pairs={{32,0},{48,16},{64,32},{80,48},{96,64},{112,80},{128,96},{144,112}... | collective-permute-start | bytes 294920 | tf_op jit(solution)/shard_map/ppermute | solution.py:531
  117.1 14.4 %all-to-all-start.5 = ((f32[16,8,128]{2,1,0:T(8,128)}), f32[16,8,128]{2,1,0:T(8,128)S(1)}, u32[]{:S(2)}, u32[]{:S(2)}) async-start(f32[16,8,128]{2,1,0:T(8,128)} %shard_map.112), calls=%async_computation.5 | async-start | bytes 131072 | tf_op jit(solution)/shard_map/all_to_all | solution.py:526

commit v8 on v7

--- a/solution.py
+++ b/solution.py
@@ -12,6 +12,7 @@
 LAMBDA = 0.5
 HALO = 5
 STEPS = 32000.0
+FINE = 256.0
 SIDE = 8
 GROUP = 2
 F32 = jnp.float32
@@ -126,11 +127,11 @@
 
 
 def exponent_of(largest):
-    return jnp.ceil(jnp.log2(jnp.maximum(largest, 1e-30)))
+    return jnp.ceil(jnp.log2(jnp.maximum(largest, 1e-30)) * FINE) * (1.0 / FINE)
 
 
 def scales_of(blocks_ref):
-    return jnp.exp2(to_float(blocks_ref[:, 64:80, :])[:, 0:1, :]) * (1.0 / STEPS)
+    return jnp.exp2(to_float(blocks_ref[:, 64:80, :])[:, 0:1, :] * (1.0 / FINE)) * (1.0 / STEPS)
 
 
 def load_image(blocks_ref):
@@ -156,14 +157,14 @@
     for i in range(4):
         blocks_ref[:, 16 * i : 16 * i + 16, :] = to_short(blocks[i] * factors)
     row = lax.broadcasted_iota(jnp.int32, (count, 16, columns), 1)
-    last = jnp.where(row == 0, exponents, extra)
+    last = jnp.where(row == 0, exponents * FINE, extra)
     blocks_ref[:, 64:80, :] = to_short(last)
 
 
 def store_copies(blocks_ref, rows):
     exponent = exponent_of(jnp.max(jnp.max(jnp.abs(rows), axis=0, keepdims=True), axis=1, keepdims=True))
     shorts = to_short(rows * (jnp.exp2(-exponent) * STEPS))
-    tail = to_short(jnp.broadcast_to(exponent, (16, 128)))
+    tail = to_short(jnp.broadcast_to(exponent * FINE, (16, 128)))
     for k in range(blocks_ref.shape[0]):
         blocks_ref[k, 0:64, :] = shorts
         blocks_ref[k, 64:80, :] = tail
@@ -214,7 +215,7 @@
     count = blocks_ref.shape[0]
 
     def one(at, start):
-        scale = jnp.exp2(to_float(blocks_ref[at, 64:80, :])[0:1]) * (1.0 / STEPS)
+        scale = jnp.exp2(to_float(blocks_ref[at, 64:80, :])[0:1] * (1.0 / FINE)) * (1.0 / STEPS)
         return to_float(blocks_ref[at, start : start + 16, :]) * scale
 
     for a in range(2):
@@ -278,7 +279,7 @@
     coarse = lane_sum(energy)
     level = exponent_of(coarse)
     row = lax.broadcasted_iota(jnp.int32, (1, 16, 128), 1)
-    extra = jnp.where(row == 1, level, jnp.exp2(-level) * STEPS * coarse)
+    extra = jnp.where(row == 1, level * FINE, jnp.exp2(-level) * STEPS * coarse)
     store_image(out_ref, coil_term(maps_ref, field), extra)
 
 
@@ -286,7 +287,7 @@
     rhs = rhs_rows_ref[...]
     image = store_copies(copies_ref, sum_blocks(blocks_ref) + LAMBDA * rhs)
     extra = to_float(blocks_ref[:, 64:80, :])
-    coarse = jnp.sum(jnp.exp2(extra[:, 1:2, :]) * extra[:, 2:3, :], axis=0) * (1.0 / STEPS)
+    coarse = jnp.sum(jnp.exp2(extra[:, 1:2, :] * (1.0 / FINE)) * extra[:, 2:3, :], axis=0) * (1.0 / STEPS)
     norm, energy = tile_ref[0:1, :], tile_ref[1:2, :]
     step = slab_step(lane_sum(norm), coarse)
     residual = rhs - step * image
@@ -570,14 +571,14 @@
         image_kernel,
         (struct((coils, 80, 128), jnp.int16), struct((8, 128))),
         (swap(term, "coil"), rhs_rows, norms),
-        after=rhs_parts,
+        after=(rhs_parts[1], rhs_parts[3]),
     )
     image = swap(copies, "coil")
     tiles = call(
         last_kernel,
         struct((coils, 16, 128)),
         (sums, image, spectrum, sampling, maps, rows, columns),
-        after=weights[2:],
+        after=(*weights[2:], rhs_parts[0], rhs_parts[4]),
     )
     image_parts = near_planes(call(near_kernel, near_shape, (at, image), in_smem=(0,), after=(tiles,)))
     tiles = call(spread_kernel, struct((slabs, 8, 128)), (swap(tiles, "coil"),), after=(image_parts[1], image_parts[3]))

time: 143 us -> 136 us (0.951)
  waiting for transfers between devices: 48.8 us -> 44.7 us
  starting transfers between devices: 67.5 us -> 64.7 us
    all_to_all x6, waiting for transfers between devices: 41.6 us -> 36.7 us  [swap(): return lax.all_to_all(blocks, axis, 0, 0, tiled=True)]
    ppermute x8, starting transfers between devices: 26.4 us -> 23.7 us  [shifted(): lax.ppermute(part, axis, [(i, i + step) for i in range(count) if 0 <= i +...]
  transfers between devices with their start and end apart: 14 -> 14, of which waited for: 10 -> 11; matrix products, arithmetic and copies ran while one was open for 0% -> 0% of each run, Pallas kernels for 1% -> 2%
where the time goes in v8:
time: 136 us; the launch traced here: 135 us
  starting transfers between devices  64.7 us (48%)
  waiting for transfers between devices  44.7 us (33%)
  Pallas kernels  23.7 us (17%)
    all_to_all x6, starting transfers between devices, swap(): return lax.all_to_all(blocks, axis, 0, 0, tiled=True)  41 us
    all_to_all x6, waiting for transfers between devices, swap(): return lax.all_to_all(blocks, axis, 0, 0, tiled=True)  36.7 us
    ppermute x8, starting transfers between devices, shifted(): lax.ppermute(part, axis, [(i, i + step) for i in range(count) if 0 <= i +...  23.7 us
    pallas_call x11, Pallas kernels, call(): pl.pallas_call(kernel, out_shape=out_shape, in_specs=specs, out_specs=out...  20.1 us
    ppermute x8, waiting for transfers between devices, shifted(): lax.ppermute(part, axis, [(i, i + step) for i in range(count) if 0 <= i +...  8.03 us
    pallas_call x1, Pallas kernels, adjoint(): pl.pallas_call(adjoint_kernel, out_shape=struct((coils, 80, 128), jnp.int...  3.67 us
  transfers between devices with their start and end apart: 14, of which 11 were waited for; matrix products, arithmetic and copies ran while one was open for 0% of the time, Pallas kernels for 2%

profile of v8, /device:TPU:1, one launch (start us, length us, event | category | flops | bytes accessed | tf_op | source)
XLA Modules:
  0.0 135.0 jit_solution(17886877057284361667)
XLA Ops:
  0.6 3.7 %shard_map.104 = s16[16,80,128]{2,1,0:T(8,128)(2,1)} custom-call(s32[2,256,128]{2,1,0:T(8,128)} %refs_3_.1, f32[2,2,256,128]{3,2,1,0:T(8,128)} %bitcast.12, bf16[512,512]{1,0:T(8,128)(2,1)} %constant.14.clone.rows_hbm.rows_ref.refs_5_, bf16[128,512]{1,0:T(8,128)(2,1)} %constant.15.clone.columns_hbm.columns_ref.refs_6_, f32[2,2,256,128]{3,2,1,0:T(8,128)} %bitcast.8), custom_call_target="tpu_custom_call" | custom-call | tf_op jit(solution)/shard_map/pallas_call | solution.py:251
  4.3 11.9 %all-to-all-start = ((s16[16,80,128]{2,1,0:T(8,128)(2,1)}), s16[16,80,128]{2,1,0:T(8,128)(2,1)S(1)}, u32[]{:S(2)}, u32[]{:S(2)}) async-start(s16[16,80,128]{2,1,0:T(8,128)(2,1)} %shard_map.104), calls=%async_computation | async-start | bytes 655360 | tf_op jit(solution)/shard_map/all_to_all | solution.py:527
  16.4 0.6 copy-done.7
  17.2 12.5 %all-to-all-done.refs_0_ = s16[16,80,128]{2,1,0:T(8,128)(2,1)S(1)} async-done(((s16[16,80,128]{2,1,0:T(8,128)(2,1)}), s16[16,80,128]{2,1,0:T(8,128)(2,1)S(1)}, u32[]{:S(2)}, u32[]{:S(2)}) %all-to-all-start) | async-done | bytes 327712 | tf_op jit(solution)/shard_map/all_to_all | solution.py:527
  29.7 1.0 shard_map.105
  30.6 3.9 %all-to-all-start.1 = ((s16[16,80,128]{2,1,0:T(8,128)(2,1)}), s16[16,80,128]{2,1,0:T(8,128)(2,1)S(1)}, u32[]{:S(2)}, u32[]{:S(2)}) async-start(s16[16,80,128]{2,1,0:T(8,128)(2,1)} %get-tuple-element.16), calls=%async_computation.1 | async-start | bytes 655360 | tf_op jit(solution)/shard_map/all_to_all | solution.py:527
  34.6 12.2 %all-to-all-done.1.blocks_ref = s16[16,80,128]{2,1,0:T(8,128)(2,1)S(1)} async-done(((s16[16,80,128]{2,1,0:T(8,128)(2,1)}), s16[16,80,128]{2,1,0:T(8,128)(2,1)S(1)}, u32[]{:S(2)}, u32[]{:S(2)}) %all-to-all-start.1) | async-done | bytes 327712 | tf_op jit(solution)/shard_map/all_to_all | solution.py:527
  46.9 4.0 %shard_map.106 = (s16[16,80,128]{2,1,0:T(8,128)(2,1)}, f32[2,2,256,128]{3,2,1,0:T(8,128)S(1)}, f32[8,128]{1,0:T(8,128)S(1)}, f32[2,2,32,128]{3,2,1,0:T(8,128)S(1)}) custom-call(s32[2]{0:T(128)S(1)} %pad_add_fusion.at_ref.refs_0_, s16[16,80,128]{2,1,0:T(8,128)(2,1)S(1)} %all-to-all-done.1.blocks_ref, s32[2,256,128]{2,1,0:T(8,128)S(1)} %copy-done.2, ...), custom_call_target="tpu_custom_call" | custom-call | tf_op jit(solution)/shard_map/pallas_call | solution.py:35
  50.9 3.9 %all-to-all-start.2 = ((s16[16,80,128]{2,1,0:T(8,128)(2,1)}), s16[16,80,128]{2,1,0:T(8,128)(2,1)S(1)}, u32[]{:S(2)}, u32[]{:S(2)}) async-start(s16[16,80,128]{2,1,0:T(8,128)(2,1)} %get-tuple-element.17), calls=%async_computation.2 | async-start | bytes 655360 | tf_op jit(solution)/shard_map/all_to_all | solution.py:527
  54.8 5.1 %collective-permute-start.1 = (f32[2,2,32,128]{3,2,1,0:T(8,128)S(1)}, f32[2,2,32,128]{3,2,1,0:T(8,128)S(1)}, u32[]{:S(2)}, u32[]{:S(2)}) collective-permute-start(f32[2,2,32,128]{3,2,1,0:T(8,128)S(1)} %get-tuple-element.20.near_ref.refs_4_), channel_id=1, source_target_pairs={{16,0},{32,16},{48,32},{64,48},{80,64},{96,80},{112,96},{128,112},... | collective-permute-start | bytes 196616 | tf_op jit(solution)/shard_map/ppermute | solution.py:532
  59.9 2.2 %collective-permute-start = (f32[2,2,32,128]{3,2,1,0:T(8,128)S(1)}, f32[2,2,32,128]{3,2,1,0:T(8,128)S(1)}, u32[]{:S(2)}, u32[]{:S(2)}) collective-permute-start(f32[2,2,32,128]{3,2,1,0:T(8,128)S(1)} %get-tuple-element.20.near_ref.refs_4_), channel_id=1, source_target_pairs={{0,16},{16,32},{32,48},{48,64},{64,80},{80,96},{96,112},{112,128},... | collective-permute-start | bytes 196616 | tf_op jit(solution)/shard_map/ppermute | solution.py:532
  62.5 1.5 %collective-permute-done.refs_3_.below_ref = f32[2,2,32,128]{3,2,1,0:T(8,128)S(1)} collective-permute-done((f32[2,2,32,128]{3,2,1,0:T(8,128)S(1)}, f32[2,2,32,128]{3,2,1,0:T(8,128)S(1)}, u32[]{:S(2)}, u32[]{:S(2)}) %collective-permute-start) | collective-permute-done | bytes 65568 | tf_op jit(solution)/shard_map/ppermute | solution.py:532
  64.0 2.6 %all-to-all-done.2.refs_0_ = s16[16,80,128]{2,1,0:T(8,128)(2,1)S(1)} async-done(((s16[16,80,128]{2,1,0:T(8,128)(2,1)}), s16[16,80,128]{2,1,0:T(8,128)(2,1)S(1)}, u32[]{:S(2)}, u32[]{:S(2)}) %all-to-all-start.2) | async-done | bytes 327712 | tf_op jit(solution)/shard_map/all_to_all | solution.py:527
  66.5 0.9 shard_map.107
  67.5 6.8 %all-to-all-start.3 = ((s16[16,80,128]{2,1,0:T(8,128)(2,1)}), s16[16,80,128]{2,1,0:T(8,128)(2,1)S(1)}, u32[]{:S(2)}, u32[]{:S(2)}) async-start(s16[16,80,128]{2,1,0:T(8,128)(2,1)} %get-tuple-element.22), calls=%async_computation.3 | async-start | bytes 655360 | tf_op jit(solution)/shard_map/all_to_all | solution.py:527
  74.3 2.6 %collective-permute-start.2 = (f32[3,2,32,128]{3,2,1,0:T(8,128)S(1)}, f32[3,2,32,128]{3,2,1,0:T(8,128)S(1)}, u32[]{:S(2)}, u32[]{:S(2)}) collective-permute-start(f32[3,2,32,128]{3,2,1,0:T(8,128)S(1)} %get-tuple-element.24), channel_id=1, source_target_pairs={{0,32},{16,48},{32,64},{48,80},{64,96},{80,112},{96,128},{112,144}... | collective-permute-start | bytes 294920 | tf_op jit(solution)/shard_map/ppermute | solution.py:532
  77.0 1.3 collective-permute-start.3
  78.9 4.4 %collective-permute-done.3.refs_9_.refs_6_ = f32[3,2,32,128]{3,2,1,0:T(8,128)S(1)} collective-permute-done((f32[3,2,32,128]{3,2,1,0:T(8,128)S(1)}, f32[3,2,32,128]{3,2,1,0:T(8,128)S(1)}, u32[]{:S(2)}, u32[]{:S(2)}) %collective-permute-start.3) | collective-permute-done | bytes 98336 | tf_op jit(solution)/shard_map/ppermute | solution.py:532
  83.2 4.3 %all-to-all-done.3.refs_1_ = s16[16,80,128]{2,1,0:T(8,128)(2,1)S(1)} async-done(((s16[16,80,128]{2,1,0:T(8,128)(2,1)}), s16[16,80,128]{2,1,0:T(8,128)(2,1)S(1)}, u32[]{:S(2)}, u32[]{:S(2)}) %all-to-all-start.3) | async-done | bytes 327712 | tf_op jit(solution)/shard_map/all_to_all | solution.py:527
  87.5 1.7 %shard_map.110.refs_2_ = f32[16,16,128]{2,1,0:T(8,128)} custom-call(f32[8,128]{1,0:T(8,128)S(1)} %get-tuple-element.21.refs_0_, s16[16,80,128]{2,1,0:T(8,128)(2,1)S(1)} %all-to-all-done.3.refs_1_, f32[2,2,256,128]{3,2,1,0:T(8,128)S(1)} %get-tuple-element.23.refs_2_, s32[2,256,128]{2,1,0:T(8,128)S(1)} %copy-done.2, f32[2,2,256,128]{3,2,1,0:T(8,128)S(1)} %bitcast.10, ...), custom_call_target="tpu_custom_call" | custom-call | tf_op jit(solution)/shard_map/pallas_call | solution.py:35
  89.2 5.9 %all-to-all-start.4 = ((f32[16,16,128]{2,1,0:T(8,128)}), f32[16,16,128]{2,1,0:T(8,128)S(1)}, u32[]{:S(2)}, u32[]{:S(2)}) async-start(f32[16,16,128]{2,1,0:T(8,128)} %shard_map.110.refs_2_), calls=%async_computation.4 | async-start | bytes 262144 | tf_op jit(solution)/shard_map/all_to_all | solution.py:527
  95.1 0.6 shard_map.111.near_ref.refs_9_
  95.7 4.5 %collective-permute-start.5 = (f32[2,2,32,128]{3,2,1,0:T(8,128)S(1)}, f32[2,2,32,128]{3,2,1,0:T(8,128)S(1)}, u32[]{:S(2)}, u32[]{:S(2)}) collective-permute-start(f32[2,2,32,128]{3,2,1,0:T(8,128)S(1)} %shard_map.111.near_ref.refs_9_), channel_id=1, source_target_pairs={{16,0},{32,16},{48,32},{64,48},{80,64},{96,80},{112,96},{128,112},... | collective-permute-start | bytes 196616 | tf_op jit(solution)/shard_map/ppermute | solution.py:532
  100.3 3.8 %collective-permute-start.4 = (f32[2,2,32,128]{3,2,1,0:T(8,128)S(1)}, f32[2,2,32,128]{3,2,1,0:T(8,128)S(1)}, u32[]{:S(2)}, u32[]{:S(2)}) collective-permute-start(f32[2,2,32,128]{3,2,1,0:T(8,128)S(1)} %shard_map.111.near_ref.refs_9_), channel_id=1, source_target_pairs={{0,16},{16,32},{32,48},{48,64},{64,80},{80,96},{96,112},{112,128},... | collective-permute-start | bytes 196616 | tf_op jit(solution)/shard_map/ppermute | solution.py:532
  104.6 0.8 collective-permute-done.4.refs_1_.below_ref.refs_8_
  105.4 2.8 %collective-permute-start.6 = (f32[3,2,32,128]{3,2,1,0:T(8,128)S(1)}, f32[3,2,32,128]{3,2,1,0:T(8,128)S(1)}, u32[]{:S(2)}, u32[]{:S(2)}) collective-permute-start(f32[3,2,32,128]{3,2,1,0:T(8,128)S(1)} %get-tuple-element.26), channel_id=1, source_target_pairs={{0,32},{16,48},{32,64},{48,80},{64,96},{80,112},{96,128},{112,144}... | collective-permute-start | bytes 294920 | tf_op jit(solution)/shard_map/ppermute | solution.py:532
  108.2 1.3 collective-permute-start.7
  109.5 0.6 shard_map.112
  110.2 8.6 %all-to-all-start.5 = ((f32[16,8,128]{2,1,0:T(8,128)}), f32[16,8,128]{2,1,0:T(8,128)S(1)}, u32[]{:S(2)}, u32[]{:S(2)}) async-start(f32[16,8,128]{2,1,0:T(8,128)} %shard_map.112), calls=%async_computation.5 | async-start | bytes 131072 | tf_op jit(solution)/shard_map/all_to_all | solution.py:527
  118.8 0.8 shard_map.114
  119.6 5.1 %all-to-all-done.5.refs_1_ = f32[16,8,128]{2,1,0:T(8,128)S(1)} async-done(((f32[16,8,128]{2,1,0:T(8,128)}), f32[16,8,128]{2,1,0:T(8,128)S(1)}, u32[]{:S(2)}, u32[]{:S(2)}) %all-to-all-start.5) | async-done | bytes 65568 | tf_op jit(solution)/shard_map/all_to_all | solution.py:527
  124.7 10.4 %shard_map.115 = (f32[2,2,16,128]{3,2,1,0:T(8,128)}, f32[2,2,16,128]{3,2,1,0:T(8,128)}) custom-call(s32[2]{0:T(128)S(1)} %pad_add_fusion.at_ref.refs_0_, f32[16,8,128]{2,1,0:T(8,128)S(1)} %all-to-all-done.5.refs_1_, f32[3,2,32,128]{3,2,1,0:T(8,128)S(1)} %collective-permute-done.2.refs_8_.refs_2_, ...), custom_call_target="tpu_custom_call" | custom-call | tf_op jit(solution)/shard_map/pallas_call | solution.py:35
  (32 shorter events, 1.9 us)
Async XLA Ops:
  4.3 11.9 %copy-start.6 = (bf16[32,2,3,3,3]{0,1,4,3,2:T(2,128)(2,1)S(1)}, bf16[32,2,3,3,3]{0,1,4,3,2:T(2,128)(2,1)}, u32[]{:S(2)}) copy-start(bf16[32,2,3,3,3]{0,1,4,3,2:T(2,128)(2,1)} %param.13) | copy-start | bytes 10372
  4.3 42.5 %copy-start.3 = (bf16[128,512]{1,0:T(8,128)(2,1)S(1)}, bf16[128,512]{1,0:T(8,128)(2,1)}, u32[]{:S(2)}) copy-start(bf16[128,512]{1,0:T(8,128)(2,1)} %constant.15.clone.columns_hbm.columns_ref.refs_6_) | copy-start | bytes 393220
  4.3 25.3 %all-to-all-start = ((s16[16,80,128]{2,1,0:T(8,128)(2,1)}), s16[16,80,128]{2,1,0:T(8,128)(2,1)S(1)}, u32[]{:S(2)}, u32[]{:S(2)}) async-start(s16[16,80,128]{2,1,0:T(8,128)(2,1)} %shard_map.104), calls=%async_computation | async-start | bytes 655360 | tf_op jit(solution)/shard_map/all_to_all | solution.py:527
  16.3 0.7 copy-start.7
  16.3 13.4 %copy-start.5 = (f32[2,2,16,128]{3,2,1,0:T(8,128)S(1)}, f32[2,2,16,128]{3,2,1,0:T(8,128)}, u32[]{:S(2)}) copy-start(f32[2,2,16,128]{3,2,1,0:T(8,128)} %refs_1_.1) | copy-start | bytes 98308
  16.3 30.6 %copy-start.2 = (s32[2,256,128]{2,1,0:T(8,128)S(1)}, s32[2,256,128]{2,1,0:T(8,128)}, u32[]{:S(2)}) copy-start(s32[2,256,128]{2,1,0:T(8,128)} %refs_3_.1) | copy-start | bytes 786436
  17.1 29.7 %copy-start = (f32[1,2,2,256,128]{4,3,2,1,0:T(8,128)S(1)}, f32[1,2,2,256,128]{4,3,2,1,0:T(8,128)}, u32[]{:S(2)}) copy-start(f32[1,2,2,256,128]{4,3,2,1,0:T(8,128)} %param.9) | copy-start | bytes 1572868
  17.1 29.7 %copy-start.1 = (bf16[512,512]{1,0:T(8,128)(2,1)S(1)}, bf16[512,512]{1,0:T(8,128)(2,1)}, u32[]{:S(2)}) copy-start(bf16[512,512]{1,0:T(8,128)(2,1)} %constant.14.clone.rows_hbm.rows_ref.refs_5_) | copy-start | bytes 1572868
  30.6 16.2 %all-to-all-start.1 = ((s16[16,80,128]{2,1,0:T(8,128)(2,1)}), s16[16,80,128]{2,1,0:T(8,128)(2,1)S(1)}, u32[]{:S(2)}, u32[]{:S(2)}) async-start(s16[16,80,128]{2,1,0:T(8,128)(2,1)} %get-tuple-element.16), calls=%async_computation.1 | async-start | bytes 655360 | tf_op jit(solution)/shard_map/all_to_all | solution.py:527
  50.9 15.7 %all-to-all-start.2 = ((s16[16,80,128]{2,1,0:T(8,128)(2,1)}), s16[16,80,128]{2,1,0:T(8,128)(2,1)S(1)}, u32[]{:S(2)}, u32[]{:S(2)}) async-start(s16[16,80,128]{2,1,0:T(8,128)(2,1)} %get-tuple-element.17), calls=%async_computation.2 | async-start | bytes 655360 | tf_op jit(solution)/shard_map/all_to_all | solution.py:527
  54.8 7.7 %collective-permute-start.1 = (f32[2,2,32,128]{3,2,1,0:T(8,128)S(1)}, f32[2,2,32,128]{3,2,1,0:T(8,128)S(1)}, u32[]{:S(2)}, u32[]{:S(2)}) collective-permute-start(f32[2,2,32,128]{3,2,1,0:T(8,128)S(1)} %get-tuple-element.20.near_ref.refs_4_), channel_id=1, source_target_pairs={{16,0},{32,16},{48,32},{64,48},{80,64},{96,80},{112,96},{128,112},... | collective-permute-start | bytes 196616 | tf_op jit(solution)/shard_map/ppermute | solution.py:532
  59.9 4.1 %collective-permute-start = (f32[2,2,32,128]{3,2,1,0:T(8,128)S(1)}, f32[2,2,32,128]{3,2,1,0:T(8,128)S(1)}, u32[]{:S(2)}, u32[]{:S(2)}) collective-permute-start(f32[2,2,32,128]{3,2,1,0:T(8,128)S(1)} %get-tuple-element.20.near_ref.refs_4_), channel_id=1, source_target_pairs={{0,16},{16,32},{32,48},{48,64},{64,80},{80,96},{96,112},{112,128},... | collective-permute-start | bytes 196616 | tf_op jit(solution)/shard_map/ppermute | solution.py:532
  67.5 20.0 %all-to-all-start.3 = ((s16[16,80,128]{2,1,0:T(8,128)(2,1)}), s16[16,80,128]{2,1,0:T(8,128)(2,1)S(1)}, u32[]{:S(2)}, u32[]{:S(2)}) async-start(s16[16,80,128]{2,1,0:T(8,128)(2,1)} %get-tuple-element.22), calls=%async_computation.3 | async-start | bytes 655360 | tf_op jit(solution)/shard_map/all_to_all | solution.py:527
  74.3 4.5 %collective-permute-start.2 = (f32[3,2,32,128]{3,2,1,0:T(8,128)S(1)}, f32[3,2,32,128]{3,2,1,0:T(8,128)S(1)}, u32[]{:S(2)}, u32[]{:S(2)}) collective-permute-start(f32[3,2,32,128]{3,2,1,0:T(8,128)S(1)} %get-tuple-element.24), channel_id=1, source_target_pairs={{0,32},{16,48},{32,64},{48,80},{64,96},{80,112},{96,128},{112,144}... | collective-permute-start | bytes 294920 | tf_op jit(solution)/shard_map/ppermute | solution.py:532
  77.0 6.3 %collective-permute-start.3 = (f32[3,2,32,128]{3,2,1,0:T(8,128)S(1)}, f32[3,2,32,128]{3,2,1,0:T(8,128)S(1)}, u32[]{:S(2)}, u32[]{:S(2)}) collective-permute-start(f32[3,2,32,128]{3,2,1,0:T(8,128)S(1)} %get-tuple-element.25), channel_id=1, source_target_pairs={{32,0},{48,16},{64,32},{80,48},{96,64},{112,80},{128,96},{144,112}... | collective-permute-start | bytes 294920 | tf_op jit(solution)/shard_map/ppermute | solution.py:532
  89.2 29.6 %copy-start.4 = (bf16[3,32,32,3,3,3]{2,1,5,4,3,0:T(8,128)(2,1)S(1)}, bf16[3,32,32,3,3,3]{2,1,5,4,3,0:T(8,128)(2,1)}, u32[]{:S(2)}) copy-start(bf16[3,32,32,3,3,3]{2,1,5,4,3,0:T(8,128)(2,1)} %param.14) | copy-start | bytes 497668
  89.2 20.3 %all-to-all-start.4 = ((f32[16,16,128]{2,1,0:T(8,128)}), f32[16,16,128]{2,1,0:T(8,128)S(1)}, u32[]{:S(2)}, u32[]{:S(2)}) async-start(f32[16,16,128]{2,1,0:T(8,128)} %shard_map.110.refs_2_), calls=%async_computation.4 | async-start | bytes 262144 | tf_op jit(solution)/shard_map/all_to_all | solution.py:527
  95.7 8.9 %collective-permute-start.5 = (f32[2,2,32,128]{3,2,1,0:T(8,128)S(1)}, f32[2,2,32,128]{3,2,1,0:T(8,128)S(1)}, u32[]{:S(2)}, u32[]{:S(2)}) collective-permute-start(f32[2,2,32,128]{3,2,1,0:T(8,128)S(1)} %shard_map.111.near_ref.refs_9_), channel_id=1, source_target_pairs={{16,0},{32,16},{48,32},{64,48},{80,64},{96,80},{112,96},{128,112},... | collective-permute-start | bytes 196616 | tf_op jit(solution)/shard_map/ppermute | solution.py:532
  100.3 5.2 %collective-permute-start.4 = (f32[2,2,32,128]{3,2,1,0:T(8,128)S(1)}, f32[2,2,32,128]{3,2,1,0:T(8,128)S(1)}, u32[]{:S(2)}, u32[]{:S(2)}) collective-permute-start(f32[2,2,32,128]{3,2,1,0:T(8,128)S(1)} %shard_map.111.near_ref.refs_9_), channel_id=1, source_target_pairs={{0,16},{16,32},{32,48},{48,64},{64,80},{80,96},{96,112},{112,128},... | collective-permute-start | bytes 196616 | tf_op jit(solution)/shard_map/ppermute | solution.py:532
  105.4 14.2 %collective-permute-start.6 = (f32[3,2,32,128]{3,2,1,0:T(8,128)S(1)}, f32[3,2,32,128]{3,2,1,0:T(8,128)S(1)}, u32[]{:S(2)}, u32[]{:S(2)}) collective-permute-start(f32[3,2,32,128]{3,2,1,0:T(8,128)S(1)} %get-tuple-element.26), channel_id=1, source_target_pairs={{0,32},{16,48},{32,64},{48,80},{64,96},{80,112},{96,128},{112,144}... | collective-permute-start | bytes 294920 | tf_op jit(solution)/shard_map/ppermute | solution.py:532
  108.2 11.4 %collective-permute-start.7 = (f32[3,2,32,128]{3,2,1,0:T(8,128)S(1)}, f32[3,2,32,128]{3,2,1,0:T(8,128)S(1)}, u32[]{:S(2)}, u32[]{:S(2)}) collective-permute-start(f32[3,2,32,128]{3,2,1,0:T(8,128)S(1)} %get-tuple-element.27), channel_id=1, source_target_pairs={{32,0},{48,16},{64,32},{80,48},{96,64},{112,80},{128,96},{144,112}... | collective-permute-start | bytes 294920 | tf_op jit(solution)/shard_map/ppermute | solution.py:532
  110.2 14.5 %all-to-all-start.5 = ((f32[16,8,128]{2,1,0:T(8,128)}), f32[16,8,128]{2,1,0:T(8,128)S(1)}, u32[]{:S(2)}, u32[]{:S(2)}) async-start(f32[16,8,128]{2,1,0:T(8,128)} %shard_map.112), calls=%async_computation.5 | async-start | bytes 131072 | tf_op jit(solution)/shard_map/all_to_all | solution.py:527

commit v9 on v8

--- a/solution.py
+++ b/solution.py
@@ -234,10 +234,12 @@
     sources = (mask_hbm, kspace_hbm, rows_hbm, columns_hbm, maps_hbm)
     targets = (mask_ref, kspace_ref, rows_ref, columns_ref, maps_ref)
     copies = [pltpu.make_async_copy(src, dst, sems.at[i]) for i, (src, dst) in enumerate(zip(sources, targets))]
-    for copy in copies:
+    for copy in copies[:4]:
         copy.start()
-    for copy in copies[:3]:
+    for copy in copies[:2]:
         copy.wait()
+    copies[4].start()
+    copies[2].wait()
     field = masked([[kspace_ref[a, p] for p in range(2)] for a in range(2)], mask_ref)
     field = dft_rows(field, rows_ref, 1.0)
     copies[3].wait()
@@ -314,7 +316,6 @@
     tile = tile_of([inner(spectrum, spectrum), inner(spectrum, before)] + [sums_ref[i : i + 1, :] for i in range(5)])
     for k in range(out_ref.shape[0]):
         out_ref[k, 0:8] = tile
-        out_ref[k, 8:] = jnp.zeros((out_ref.shape[1] - 8, 128), F32)
 
 
 def near_kernel(at_ref, blocks_ref, near_ref):
@@ -574,13 +575,14 @@
         after=(rhs_parts[1], rhs_parts[3]),
     )
     image = swap(copies, "coil")
+    image_near = call(near_kernel, near_shape, (at, image), in_smem=(0,))
     tiles = call(
         last_kernel,
-        struct((coils, 16, 128)),
+        struct((coils, 8, 128)),
         (sums, image, spectrum, sampling, maps, rows, columns),
-        after=(*weights[2:], rhs_parts[0], rhs_parts[4]),
-    )
-    image_parts = near_planes(call(near_kernel, near_shape, (at, image), in_smem=(0,), after=(tiles,)))
+        after=(*weights[2:], rhs_parts[0], rhs_parts[4], image_near),
+    )
+    image_parts = near_planes(image_near)
     tiles = call(spread_kernel, struct((slabs, 8, 128)), (swap(tiles, "coil"),), after=(image_parts[1], image_parts[3]))
     last = swap(tiles, "slab")
     scratch = [pltpu.VMEM((12, 144, 256), BF16)]

time: 136 us -> 135 us (level)
    all_to_all x6, waiting for transfers between devices: 36.7 us -> 41.5 us  [swap(): return lax.all_to_all(blocks, axis, 0, 0, tiled=True)]
    ppermute x8, waiting for transfers between devices: 8.03 us -> 3.17 us  [shifted(): lax.ppermute(part, axis, [(i, i + step) for i in range(count) if 0 <= i +...]
  transfers between devices with their start and end apart: 14 -> 14, of which waited for: 11 -> 9; matrix products, arithmetic and copies ran while one was open for 0% -> 0% of each run, Pallas kernels for 2% -> 2%
where the time goes in v9:
time: 135 us; the launch traced here: 134 us
  starting transfers between devices  64.2 us (48%)
  waiting for transfers between devices  44.7 us (33%)
  Pallas kernels  23.7 us (18%)
    all_to_all x6, waiting for transfers between devices, swap(): return lax.all_to_all(blocks, axis, 0, 0, tiled=True)  41.5 us
    all_to_all x6, starting transfers between devices, swap(): return lax.all_to_all(blocks, axis, 0, 0, tiled=True)  40.5 us
    ppermute x8, starting transfers between devices, shifted(): lax.ppermute(part, axis, [(i, i + step) for i in range(count) if 0 <= i +...  23.7 us
    pallas_call x11, Pallas kernels, call(): pl.pallas_call(kernel, out_shape=out_shape, in_specs=specs, out_specs=out...  20 us
    pallas_call x1, Pallas kernels, adjoint(): pl.pallas_call(adjoint_kernel, out_shape=struct((coils, 80, 128), jnp.int...  3.67 us
    ppermute x8, waiting for transfers between devices, shifted(): lax.ppermute(part, axis, [(i, i + step) for i in range(count) if 0 <= i +...  3.17 us
  transfers between devices with their start and end apart: 14, of which 9 were waited for; matrix products, arithmetic and copies ran while one was open for 0% of the time, Pallas kernels for 2%

profile of v9, /device:TPU:1, one launch (start us, length us, event | category | flops | bytes accessed | tf_op | source)
XLA Modules:
  0.0 134.5 jit_solution(17558535117787568564)
XLA Ops:
  0.6 3.7 %shard_map.104 = s16[16,80,128]{2,1,0:T(8,128)(2,1)} custom-call(s32[2,256,128]{2,1,0:T(8,128)} %refs_3_.1, f32[2,2,256,128]{3,2,1,0:T(8,128)} %bitcast.12, bf16[512,512]{1,0:T(8,128)(2,1)} %constant.14.clone.rows_hbm.rows_ref.refs_5_, bf16[128,512]{1,0:T(8,128)(2,1)} %constant.15.clone.columns_hbm.columns_ref.refs_6_, f32[2,2,256,128]{3,2,1,0:T(8,128)} %bitcast.8), custom_call_target="tpu_custom_call" | custom-call | tf_op jit(solution)/shard_map/pallas_call | solution.py:253
  4.3 11.9 %all-to-all-start = ((s16[16,80,128]{2,1,0:T(8,128)(2,1)}), s16[16,80,128]{2,1,0:T(8,128)(2,1)S(1)}, u32[]{:S(2)}, u32[]{:S(2)}) async-start(s16[16,80,128]{2,1,0:T(8,128)(2,1)} %shard_map.104), calls=%async_computation | async-start | bytes 655360 | tf_op jit(solution)/shard_map/all_to_all | solution.py:528
  16.4 0.6 copy-done.7
  17.2 12.5 %all-to-all-done.refs_0_ = s16[16,80,128]{2,1,0:T(8,128)(2,1)S(1)} async-done(((s16[16,80,128]{2,1,0:T(8,128)(2,1)}), s16[16,80,128]{2,1,0:T(8,128)(2,1)S(1)}, u32[]{:S(2)}, u32[]{:S(2)}) %all-to-all-start) | async-done | bytes 327712 | tf_op jit(solution)/shard_map/all_to_all | solution.py:528
  29.7 1.0 shard_map.105
  30.6 3.9 %all-to-all-start.1 = ((s16[16,80,128]{2,1,0:T(8,128)(2,1)}), s16[16,80,128]{2,1,0:T(8,128)(2,1)S(1)}, u32[]{:S(2)}, u32[]{:S(2)}) async-start(s16[16,80,128]{2,1,0:T(8,128)(2,1)} %get-tuple-element.16), calls=%async_computation.1 | async-start | bytes 655360 | tf_op jit(solution)/shard_map/all_to_all | solution.py:528
  34.6 12.2 %all-to-all-done.1.blocks_ref = s16[16,80,128]{2,1,0:T(8,128)(2,1)S(1)} async-done(((s16[16,80,128]{2,1,0:T(8,128)(2,1)}), s16[16,80,128]{2,1,0:T(8,128)(2,1)S(1)}, u32[]{:S(2)}, u32[]{:S(2)}) %all-to-all-start.1) | async-done | bytes 327712 | tf_op jit(solution)/shard_map/all_to_all | solution.py:528
  46.9 4.0 %shard_map.106 = (s16[16,80,128]{2,1,0:T(8,128)(2,1)}, f32[2,2,256,128]{3,2,1,0:T(8,128)S(1)}, f32[8,128]{1,0:T(8,128)S(1)}, f32[2,2,32,128]{3,2,1,0:T(8,128)S(1)}) custom-call(s32[2]{0:T(128)S(1)} %pad_add_fusion.at_ref.refs_0_, s16[16,80,128]{2,1,0:T(8,128)(2,1)S(1)} %all-to-all-done.1.blocks_ref, s32[2,256,128]{2,1,0:T(8,128)S(1)} %copy-done.2, ...), custom_call_target="tpu_custom_call" | custom-call | tf_op jit(solution)/shard_map/pallas_call | solution.py:35
  50.9 3.9 %all-to-all-start.2 = ((s16[16,80,128]{2,1,0:T(8,128)(2,1)}), s16[16,80,128]{2,1,0:T(8,128)(2,1)S(1)}, u32[]{:S(2)}, u32[]{:S(2)}) async-start(s16[16,80,128]{2,1,0:T(8,128)(2,1)} %get-tuple-element.17), calls=%async_computation.2 | async-start | bytes 655360 | tf_op jit(solution)/shard_map/all_to_all | solution.py:528
  54.8 5.1 %collective-permute-start.1 = (f32[2,2,32,128]{3,2,1,0:T(8,128)S(1)}, f32[2,2,32,128]{3,2,1,0:T(8,128)S(1)}, u32[]{:S(2)}, u32[]{:S(2)}) collective-permute-start(f32[2,2,32,128]{3,2,1,0:T(8,128)S(1)} %get-tuple-element.20.near_ref.refs_4_), channel_id=1, source_target_pairs={{16,0},{32,16},{48,32},{64,48},{80,64},{96,80},{112,96},{128,112},... | collective-permute-start | bytes 196616 | tf_op jit(solution)/shard_map/ppermute | solution.py:533
  59.9 2.2 %collective-permute-start = (f32[2,2,32,128]{3,2,1,0:T(8,128)S(1)}, f32[2,2,32,128]{3,2,1,0:T(8,128)S(1)}, u32[]{:S(2)}, u32[]{:S(2)}) collective-permute-start(f32[2,2,32,128]{3,2,1,0:T(8,128)S(1)} %get-tuple-element.20.near_ref.refs_4_), channel_id=1, source_target_pairs={{0,16},{16,32},{32,48},{48,64},{64,80},{80,96},{96,112},{112,128},... | collective-permute-start | bytes 196616 | tf_op jit(solution)/shard_map/ppermute | solution.py:533
  62.1 0.4 collective-permute-done.1.refs_4_.above_ref.refs_5_
  62.5 1.5 %collective-permute-done.refs_3_.below_ref = f32[2,2,32,128]{3,2,1,0:T(8,128)S(1)} collective-permute-done((f32[2,2,32,128]{3,2,1,0:T(8,128)S(1)}, f32[2,2,32,128]{3,2,1,0:T(8,128)S(1)}, u32[]{:S(2)}, u32[]{:S(2)}) %collective-permute-start) | collective-permute-done | bytes 65568 | tf_op jit(solution)/shard_map/ppermute | solution.py:533
  64.0 2.6 %all-to-all-done.2.refs_0_ = s16[16,80,128]{2,1,0:T(8,128)(2,1)S(1)} async-done(((s16[16,80,128]{2,1,0:T(8,128)(2,1)}), s16[16,80,128]{2,1,0:T(8,128)(2,1)S(1)}, u32[]{:S(2)}, u32[]{:S(2)}) %all-to-all-start.2) | async-done | bytes 327712 | tf_op jit(solution)/shard_map/all_to_all | solution.py:528
  66.5 0.9 shard_map.107
  67.5 6.8 %all-to-all-start.3 = ((s16[16,80,128]{2,1,0:T(8,128)(2,1)}), s16[16,80,128]{2,1,0:T(8,128)(2,1)S(1)}, u32[]{:S(2)}, u32[]{:S(2)}) async-start(s16[16,80,128]{2,1,0:T(8,128)(2,1)} %get-tuple-element.22), calls=%async_computation.3 | async-start | bytes 655360 | tf_op jit(solution)/shard_map/all_to_all | solution.py:528
  74.3 2.6 %collective-permute-start.2 = (f32[3,2,32,128]{3,2,1,0:T(8,128)S(1)}, f32[3,2,32,128]{3,2,1,0:T(8,128)S(1)}, u32[]{:S(2)}, u32[]{:S(2)}) collective-permute-start(f32[3,2,32,128]{3,2,1,0:T(8,128)S(1)} %get-tuple-element.24), channel_id=1, source_target_pairs={{0,32},{16,48},{32,64},{48,80},{64,96},{80,112},{96,128},{112,144}... | collective-permute-start | bytes 294920 | tf_op jit(solution)/shard_map/ppermute | solution.py:533
  77.0 1.3 collective-permute-start.3
  78.4 9.1 %all-to-all-done.3.blocks_ref.refs_1_ = s16[16,80,128]{2,1,0:T(8,128)(2,1)S(1)} async-done(((s16[16,80,128]{2,1,0:T(8,128)(2,1)}), s16[16,80,128]{2,1,0:T(8,128)(2,1)S(1)}, u32[]{:S(2)}, u32[]{:S(2)}) %all-to-all-start.3) | async-done | bytes 327712 | tf_op jit(solution)/shard_map/all_to_all | solution.py:528
  87.5 0.6 shard_map.110.refs_10_.near_ref.refs_9_
  88.1 1.7 %shard_map.111 = f32[16,8,128]{2,1,0:T(8,128)} custom-call(f32[8,128]{1,0:T(8,128)S(1)} %get-tuple-element.21.refs_0_, s16[16,80,128]{2,1,0:T(8,128)(2,1)S(1)} %all-to-all-done.3.blocks_ref.refs_1_, f32[2,2,256,128]{3,2,1,0:T(8,128)S(1)} %get-tuple-element.23.refs_2_, s32[2,256,128]{2,1,0:T(8,128)S(1)} %copy-done.2, f32[2,2,256,128]{3,2,1,0:T(8,128)S(1)} %bitcast.10, ...), custom_call_target="tpu_custom_call" | custom-call | tf_op jit(solution)/shard_map/pallas_call | solution.py:35
  89.8 5.3 %all-to-all-start.4 = ((f32[16,8,128]{2,1,0:T(8,128)}), f32[16,8,128]{2,1,0:T(8,128)S(1)}, u32[]{:S(2)}, u32[]{:S(2)}) async-start(f32[16,8,128]{2,1,0:T(8,128)} %shard_map.111), calls=%async_computation.4 | async-start | bytes 131072 | tf_op jit(solution)/shard_map/all_to_all | solution.py:528
  95.1 4.5 %collective-permute-start.5 = (f32[2,2,32,128]{3,2,1,0:T(8,128)S(1)}, f32[2,2,32,128]{3,2,1,0:T(8,128)S(1)}, u32[]{:S(2)}, u32[]{:S(2)}) collective-permute-start(f32[2,2,32,128]{3,2,1,0:T(8,128)S(1)} %shard_map.110.refs_10_.near_ref.refs_9_), channel_id=1, source_target_pairs={{16,0},{32,16},{48,32},{64,48},{80,64},{96,80},{112,96},{128,112},... | collective-permute-start | bytes 196616 | tf_op jit(solution)/shard_map/ppermute | solution.py:533
  99.7 3.8 %collective-permute-start.4 = (f32[2,2,32,128]{3,2,1,0:T(8,128)S(1)}, f32[2,2,32,128]{3,2,1,0:T(8,128)S(1)}, u32[]{:S(2)}, u32[]{:S(2)}) collective-permute-start(f32[2,2,32,128]{3,2,1,0:T(8,128)S(1)} %shard_map.110.refs_10_.near_ref.refs_9_), channel_id=1, source_target_pairs={{0,16},{16,32},{32,48},{48,64},{64,80},{80,96},{96,112},{112,128},... | collective-permute-start | bytes 196616 | tf_op jit(solution)/shard_map/ppermute | solution.py:533
  103.8 1.0 collective-permute-done.4.refs_1_.below_ref.refs_8_
  104.8 2.8 %collective-permute-start.6 = (f32[3,2,32,128]{3,2,1,0:T(8,128)S(1)}, f32[3,2,32,128]{3,2,1,0:T(8,128)S(1)}, u32[]{:S(2)}, u32[]{:S(2)}) collective-permute-start(f32[3,2,32,128]{3,2,1,0:T(8,128)S(1)} %get-tuple-element.26), channel_id=1, source_target_pairs={{0,32},{16,48},{32,64},{48,80},{64,96},{80,112},{96,128},{112,144}... | collective-permute-start | bytes 294920 | tf_op jit(solution)/shard_map/ppermute | solution.py:533
  107.6 1.3 collective-permute-start.7
  108.9 0.6 shard_map.112
  109.6 8.7 %all-to-all-start.5 = ((f32[16,8,128]{2,1,0:T(8,128)}), f32[16,8,128]{2,1,0:T(8,128)S(1)}, u32[]{:S(2)}, u32[]{:S(2)}) async-start(f32[16,8,128]{2,1,0:T(8,128)} %shard_map.112), calls=%async_computation.5 | async-start | bytes 131072 | tf_op jit(solution)/shard_map/all_to_all | solution.py:528
  118.2 0.8 shard_map.114
  119.0 5.1 %all-to-all-done.5.refs_1_ = f32[16,8,128]{2,1,0:T(8,128)S(1)} async-done(((f32[16,8,128]{2,1,0:T(8,128)}), f32[16,8,128]{2,1,0:T(8,128)S(1)}, u32[]{:S(2)}, u32[]{:S(2)}) %all-to-all-start.5) | async-done | bytes 65568 | tf_op jit(solution)/shard_map/all_to_all | solution.py:528
  124.1 10.4 %shard_map.115 = (f32[2,2,16,128]{3,2,1,0:T(8,128)}, f32[2,2,16,128]{3,2,1,0:T(8,128)}) custom-call(s32[2]{0:T(128)S(1)} %pad_add_fusion.at_ref.refs_0_, f32[16,8,128]{2,1,0:T(8,128)S(1)} %all-to-all-done.5.refs_1_, f32[3,2,32,128]{3,2,1,0:T(8,128)S(1)} %collective-permute-done.2.refs_8_.refs_2_, ...), custom_call_target="tpu_custom_call" | custom-call | tf_op jit(solution)/shard_map/pallas_call | solution.py:35
  (32 shorter events, 0.8 us)
Async XLA Ops:
  4.3 11.9 %copy-start.6 = (bf16[32,2,3,3,3]{0,1,4,3,2:T(2,128)(2,1)S(1)}, bf16[32,2,3,3,3]{0,1,4,3,2:T(2,128)(2,1)}, u32[]{:S(2)}) copy-start(bf16[32,2,3,3,3]{0,1,4,3,2:T(2,128)(2,1)} %param.13) | copy-start | bytes 10372
  4.3 42.5 %copy-start.3 = (bf16[128,512]{1,0:T(8,128)(2,1)S(1)}, bf16[128,512]{1,0:T(8,128)(2,1)}, u32[]{:S(2)}) copy-start(bf16[128,512]{1,0:T(8,128)(2,1)} %constant.15.clone.columns_hbm.columns_ref.refs_6_) | copy-start | bytes 393220
  4.3 25.3 %all-to-all-start = ((s16[16,80,128]{2,1,0:T(8,128)(2,1)}), s16[16,80,128]{2,1,0:T(8,128)(2,1)S(1)}, u32[]{:S(2)}, u32[]{:S(2)}) async-start(s16[16,80,128]{2,1,0:T(8,128)(2,1)} %shard_map.104), calls=%async_computation | async-start | bytes 655360 | tf_op jit(solution)/shard_map/all_to_all | solution.py:528
  16.3 0.7 copy-start.7
  16.3 13.4 %copy-start.5 = (f32[2,2,16,128]{3,2,1,0:T(8,128)S(1)}, f32[2,2,16,128]{3,2,1,0:T(8,128)}, u32[]{:S(2)}) copy-start(f32[2,2,16,128]{3,2,1,0:T(8,128)} %refs_1_.1) | copy-start | bytes 98308
  16.3 30.6 %copy-start.2 = (s32[2,256,128]{2,1,0:T(8,128)S(1)}, s32[2,256,128]{2,1,0:T(8,128)}, u32[]{:S(2)}) copy-start(s32[2,256,128]{2,1,0:T(8,128)} %refs_3_.1) | copy-start | bytes 786436
  17.1 29.7 %copy-start = (f32[1,2,2,256,128]{4,3,2,1,0:T(8,128)S(1)}, f32[1,2,2,256,128]{4,3,2,1,0:T(8,128)}, u32[]{:S(2)}) copy-start(f32[1,2,2,256,128]{4,3,2,1,0:T(8,128)} %param.9) | copy-start | bytes 1572868
  17.1 29.7 %copy-start.1 = (bf16[512,512]{1,0:T(8,128)(2,1)S(1)}, bf16[512,512]{1,0:T(8,128)(2,1)}, u32[]{:S(2)}) copy-start(bf16[512,512]{1,0:T(8,128)(2,1)} %constant.14.clone.rows_hbm.rows_ref.refs_5_) | copy-start | bytes 1572868
  30.6 16.2 %all-to-all-start.1 = ((s16[16,80,128]{2,1,0:T(8,128)(2,1)}), s16[16,80,128]{2,1,0:T(8,128)(2,1)S(1)}, u32[]{:S(2)}, u32[]{:S(2)}) async-start(s16[16,80,128]{2,1,0:T(8,128)(2,1)} %get-tuple-element.16), calls=%async_computation.1 | async-start | bytes 655360 | tf_op jit(solution)/shard_map/all_to_all | solution.py:528
  50.9 15.7 %all-to-all-start.2 = ((s16[16,80,128]{2,1,0:T(8,128)(2,1)}), s16[16,80,128]{2,1,0:T(8,128)(2,1)S(1)}, u32[]{:S(2)}, u32[]{:S(2)}) async-start(s16[16,80,128]{2,1,0:T(8,128)(2,1)} %get-tuple-element.17), calls=%async_computation.2 | async-start | bytes 655360 | tf_op jit(solution)/shard_map/all_to_all | solution.py:528
  54.8 7.7 %collective-permute-start.1 = (f32[2,2,32,128]{3,2,1,0:T(8,128)S(1)}, f32[2,2,32,128]{3,2,1,0:T(8,128)S(1)}, u32[]{:S(2)}, u32[]{:S(2)}) collective-permute-start(f32[2,2,32,128]{3,2,1,0:T(8,128)S(1)} %get-tuple-element.20.near_ref.refs_4_), channel_id=1, source_target_pairs={{16,0},{32,16},{48,32},{64,48},{80,64},{96,80},{112,96},{128,112},... | collective-permute-start | bytes 196616 | tf_op jit(solution)/shard_map/ppermute | solution.py:533
  59.9 4.1 %collective-permute-start = (f32[2,2,32,128]{3,2,1,0:T(8,128)S(1)}, f32[2,2,32,128]{3,2,1,0:T(8,128)S(1)}, u32[]{:S(2)}, u32[]{:S(2)}) collective-permute-start(f32[2,2,32,128]{3,2,1,0:T(8,128)S(1)} %get-tuple-element.20.near_ref.refs_4_), channel_id=1, source_target_pairs={{0,16},{16,32},{32,48},{48,64},{64,80},{80,96},{96,112},{112,128},... | collective-permute-start | bytes 196616 | tf_op jit(solution)/shard_map/ppermute | solution.py:533
  67.5 20.0 %all-to-all-start.3 = ((s16[16,80,128]{2,1,0:T(8,128)(2,1)}), s16[16,80,128]{2,1,0:T(8,128)(2,1)S(1)}, u32[]{:S(2)}, u32[]{:S(2)}) async-start(s16[16,80,128]{2,1,0:T(8,128)(2,1)} %get-tuple-element.22), calls=%async_computation.3 | async-start | bytes 655360 | tf_op jit(solution)/shard_map/all_to_all | solution.py:528
  74.3 13.7 %collective-permute-start.2 = (f32[3,2,32,128]{3,2,1,0:T(8,128)S(1)}, f32[3,2,32,128]{3,2,1,0:T(8,128)S(1)}, u32[]{:S(2)}, u32[]{:S(2)}) collective-permute-start(f32[3,2,32,128]{3,2,1,0:T(8,128)S(1)} %get-tuple-element.24), channel_id=1, source_target_pairs={{0,32},{16,48},{32,64},{48,80},{64,96},{80,112},{96,128},{112,144}... | collective-permute-start | bytes 294920 | tf_op jit(solution)/shard_map/ppermute | solution.py:533
  77.0 11.1 %collective-permute-start.3 = (f32[3,2,32,128]{3,2,1,0:T(8,128)S(1)}, f32[3,2,32,128]{3,2,1,0:T(8,128)S(1)}, u32[]{:S(2)}, u32[]{:S(2)}) collective-permute-start(f32[3,2,32,128]{3,2,1,0:T(8,128)S(1)} %get-tuple-element.25), channel_id=1, source_target_pairs={{32,0},{48,16},{64,32},{80,48},{96,64},{112,80},{128,96},{144,112}... | collective-permute-start | bytes 294920 | tf_op jit(solution)/shard_map/ppermute | solution.py:533
  89.8 28.4 %copy-start.4 = (bf16[3,32,32,3,3,3]{2,1,5,4,3,0:T(8,128)(2,1)S(1)}, bf16[3,32,32,3,3,3]{2,1,5,4,3,0:T(8,128)(2,1)}, u32[]{:S(2)}) copy-start(bf16[3,32,32,3,3,3]{2,1,5,4,3,0:T(8,128)(2,1)} %param.14) | copy-start | bytes 497668
  89.8 19.1 %all-to-all-start.4 = ((f32[16,8,128]{2,1,0:T(8,128)}), f32[16,8,128]{2,1,0:T(8,128)S(1)}, u32[]{:S(2)}, u32[]{:S(2)}) async-start(f32[16,8,128]{2,1,0:T(8,128)} %shard_map.111), calls=%async_computation.4 | async-start | bytes 131072 | tf_op jit(solution)/shard_map/all_to_all | solution.py:528
  95.1 8.7 %collective-permute-start.5 = (f32[2,2,32,128]{3,2,1,0:T(8,128)S(1)}, f32[2,2,32,128]{3,2,1,0:T(8,128)S(1)}, u32[]{:S(2)}, u32[]{:S(2)}) collective-permute-start(f32[2,2,32,128]{3,2,1,0:T(8,128)S(1)} %shard_map.110.refs_10_.near_ref.refs_9_), channel_id=1, source_target_pairs={{16,0},{32,16},{48,32},{64,48},{80,64},{96,80},{112,96},{128,112},... | collective-permute-start | bytes 196616 | tf_op jit(solution)/shard_map/ppermute | solution.py:533
  99.7 5.1 %collective-permute-start.4 = (f32[2,2,32,128]{3,2,1,0:T(8,128)S(1)}, f32[2,2,32,128]{3,2,1,0:T(8,128)S(1)}, u32[]{:S(2)}, u32[]{:S(2)}) collective-permute-start(f32[2,2,32,128]{3,2,1,0:T(8,128)S(1)} %shard_map.110.refs_10_.near_ref.refs_9_), channel_id=1, source_target_pairs={{0,16},{16,32},{32,48},{48,64},{64,80},{80,96},{96,112},{112,128},... | collective-permute-start | bytes 196616 | tf_op jit(solution)/shard_map/ppermute | solution.py:533
  104.8 14.2 %collective-permute-start.6 = (f32[3,2,32,128]{3,2,1,0:T(8,128)S(1)}, f32[3,2,32,128]{3,2,1,0:T(8,128)S(1)}, u32[]{:S(2)}, u32[]{:S(2)}) collective-permute-start(f32[3,2,32,128]{3,2,1,0:T(8,128)S(1)} %get-tuple-element.26), channel_id=1, source_target_pairs={{0,32},{16,48},{32,64},{48,80},{64,96},{80,112},{96,128},{112,144}... | collective-permute-start | bytes 294920 | tf_op jit(solution)/shard_map/ppermute | solution.py:533
  107.6 11.4 %collective-permute-start.7 = (f32[3,2,32,128]{3,2,1,0:T(8,128)S(1)}, f32[3,2,32,128]{3,2,1,0:T(8,128)S(1)}, u32[]{:S(2)}, u32[]{:S(2)}) collective-permute-start(f32[3,2,32,128]{3,2,1,0:T(8,128)S(1)} %get-tuple-element.27), channel_id=1, source_target_pairs={{32,0},{48,16},{64,32},{80,48},{96,64},{112,80},{128,96},{144,112}... | collective-permute-start | bytes 294920 | tf_op jit(solution)/shard_map/ppermute | solution.py:533
  109.6 14.5 %all-to-all-start.5 = ((f32[16,8,128]{2,1,0:T(8,128)}), f32[16,8,128]{2,1,0:T(8,128)S(1)}, u32[]{:S(2)}, u32[]{:S(2)}) async-start(f32[16,8,128]{2,1,0:T(8,128)} %shard_map.112), calls=%async_computation.5 | async-start | bytes 131072 | tf_op jit(solution)/shard_map/all_to_all | solution.py:528

commit v10 on v9

--- a/solution.py
+++ b/solution.py
@@ -583,7 +583,7 @@
         after=(*weights[2:], rhs_parts[0], rhs_parts[4], image_near),
     )
     image_parts = near_planes(image_near)
-    tiles = call(spread_kernel, struct((slabs, 8, 128)), (swap(tiles, "coil"),), after=(image_parts[1], image_parts[3]))
+    tiles = call(spread_kernel, struct((slabs, 8, 128)), (swap(tiles, "coil"),), after=(image_parts[0], image_parts[4]))
     last = swap(tiles, "slab")
     scratch = [pltpu.VMEM((12, 144, 256), BF16)]
     scratch += [pltpu.VMEM((10 - 2 * m, (16 - 2 * m) * 32, 256), BF16) for m in range(4)]

time: 135 us -> 134 us (level)
  starting transfers between devices: 64.2 us -> 59.1 us
  waiting for transfers between devices: 44.7 us -> 48.6 us
    all_to_all x6, starting transfers between devices: 40.5 us -> 35.6 us  [swap(): return lax.all_to_all(blocks, axis, 0, 0, tiled=True)]
    all_to_all x6, waiting for transfers between devices: 41.5 us -> 45.8 us  [swap(): return lax.all_to_all(blocks, axis, 0, 0, tiled=True)]
where the time goes in v10:
time: 134 us; the launch traced here: 133 us
  starting transfers between devices  59.1 us (44%)
  waiting for transfers between devices  48.6 us (36%)
  Pallas kernels  23.7 us (18%)
    all_to_all x6, waiting for transfers between devices, swap(): return lax.all_to_all(blocks, axis, 0, 0, tiled=True)  45.8 us
    all_to_all x6, starting transfers between devices, swap(): return lax.all_to_all(blocks, axis, 0, 0, tiled=True)  35.6 us
    ppermute x8, starting transfers between devices, shifted(): lax.ppermute(part, axis, [(i, i + step) for i in range(count) if 0 <= i +...  23.5 us
    pallas_call x11, Pallas kernels, call(): pl.pallas_call(kernel, out_shape=out_shape, in_specs=specs, out_specs=out...  20 us
    pallas_call x1, Pallas kernels, adjoint(): pl.pallas_call(adjoint_kernel, out_shape=struct((coils, 80, 128), jnp.int...  3.67 us
    ppermute x8, waiting for transfers between devices, shifted(): lax.ppermute(part, axis, [(i, i + step) for i in range(count) if 0 <= i +...  2.71 us
  transfers between devices with their start and end apart: 14, of which 9 were waited for; matrix products, arithmetic and copies ran while one was open for 0% of the time, Pallas kernels for 2%

profile of v10, /device:TPU:1, one launch (start us, length us, event | category | flops | bytes accessed | tf_op | source)
XLA Modules:
  0.0 133.2 jit_solution(14344076289880697159)
XLA Ops:
  0.6 3.7 %shard_map.104 = s16[16,80,128]{2,1,0:T(8,128)(2,1)} custom-call(s32[2,256,128]{2,1,0:T(8,128)} %refs_3_.1, f32[2,2,256,128]{3,2,1,0:T(8,128)} %bitcast.12, bf16[512,512]{1,0:T(8,128)(2,1)} %constant.14.clone.rows_hbm.rows_ref.refs_5_, bf16[128,512]{1,0:T(8,128)(2,1)} %constant.15.clone.columns_hbm.columns_ref.refs_6_, f32[2,2,256,128]{3,2,1,0:T(8,128)} %bitcast.8), custom_call_target="tpu_custom_call" | custom-call | tf_op jit(solution)/shard_map/pallas_call | solution.py:253
  4.3 11.9 %all-to-all-start = ((s16[16,80,128]{2,1,0:T(8,128)(2,1)}), s16[16,80,128]{2,1,0:T(8,128)(2,1)S(1)}, u32[]{:S(2)}, u32[]{:S(2)}) async-start(s16[16,80,128]{2,1,0:T(8,128)(2,1)} %shard_map.104), calls=%async_computation | async-start | bytes 655360 | tf_op jit(solution)/shard_map/all_to_all | solution.py:528
  16.4 0.6 copy-done.7
  17.2 12.5 %all-to-all-done.refs_0_ = s16[16,80,128]{2,1,0:T(8,128)(2,1)S(1)} async-done(((s16[16,80,128]{2,1,0:T(8,128)(2,1)}), s16[16,80,128]{2,1,0:T(8,128)(2,1)S(1)}, u32[]{:S(2)}, u32[]{:S(2)}) %all-to-all-start) | async-done | bytes 327712 | tf_op jit(solution)/shard_map/all_to_all | solution.py:528
  29.7 1.0 shard_map.105
  30.6 3.9 %all-to-all-start.1 = ((s16[16,80,128]{2,1,0:T(8,128)(2,1)}), s16[16,80,128]{2,1,0:T(8,128)(2,1)S(1)}, u32[]{:S(2)}, u32[]{:S(2)}) async-start(s16[16,80,128]{2,1,0:T(8,128)(2,1)} %get-tuple-element.16), calls=%async_computation.1 | async-start | bytes 655360 | tf_op jit(solution)/shard_map/all_to_all | solution.py:528
  34.6 12.2 %all-to-all-done.1.blocks_ref = s16[16,80,128]{2,1,0:T(8,128)(2,1)S(1)} async-done(((s16[16,80,128]{2,1,0:T(8,128)(2,1)}), s16[16,80,128]{2,1,0:T(8,128)(2,1)S(1)}, u32[]{:S(2)}, u32[]{:S(2)}) %all-to-all-start.1) | async-done | bytes 327712 | tf_op jit(solution)/shard_map/all_to_all | solution.py:528
  46.9 4.0 %shard_map.106 = (s16[16,80,128]{2,1,0:T(8,128)(2,1)}, f32[2,2,256,128]{3,2,1,0:T(8,128)S(1)}, f32[8,128]{1,0:T(8,128)S(1)}, f32[2,2,32,128]{3,2,1,0:T(8,128)S(1)}) custom-call(s32[2]{0:T(128)S(1)} %pad_add_fusion.at_ref.refs_0_, s16[16,80,128]{2,1,0:T(8,128)(2,1)S(1)} %all-to-all-done.1.blocks_ref, s32[2,256,128]{2,1,0:T(8,128)S(1)} %copy-done.2, ...), custom_call_target="tpu_custom_call" | custom-call | tf_op jit(solution)/shard_map/pallas_call | solution.py:35
  50.9 3.9 %all-to-all-start.2 = ((s16[16,80,128]{2,1,0:T(8,128)(2,1)}), s16[16,80,128]{2,1,0:T(8,128)(2,1)S(1)}, u32[]{:S(2)}, u32[]{:S(2)}) async-start(s16[16,80,128]{2,1,0:T(8,128)(2,1)} %get-tuple-element.17), calls=%async_computation.2 | async-start | bytes 655360 | tf_op jit(solution)/shard_map/all_to_all | solution.py:528
  54.8 5.1 %collective-permute-start.1 = (f32[2,2,32,128]{3,2,1,0:T(8,128)S(1)}, f32[2,2,32,128]{3,2,1,0:T(8,128)S(1)}, u32[]{:S(2)}, u32[]{:S(2)}) collective-permute-start(f32[2,2,32,128]{3,2,1,0:T(8,128)S(1)} %get-tuple-element.20.near_ref.refs_4_), channel_id=1, source_target_pairs={{16,0},{32,16},{48,32},{64,48},{80,64},{96,80},{112,96},{128,112},... | collective-permute-start | bytes 196616 | tf_op jit(solution)/shard_map/ppermute | solution.py:533
  59.9 2.2 %collective-permute-start = (f32[2,2,32,128]{3,2,1,0:T(8,128)S(1)}, f32[2,2,32,128]{3,2,1,0:T(8,128)S(1)}, u32[]{:S(2)}, u32[]{:S(2)}) collective-permute-start(f32[2,2,32,128]{3,2,1,0:T(8,128)S(1)} %get-tuple-element.20.near_ref.refs_4_), channel_id=1, source_target_pairs={{0,16},{16,32},{32,48},{48,64},{64,80},{80,96},{96,112},{112,128},... | collective-permute-start | bytes 196616 | tf_op jit(solution)/shard_map/ppermute | solution.py:533
  62.5 1.5 %collective-permute-done.refs_3_.below_ref = f32[2,2,32,128]{3,2,1,0:T(8,128)S(1)} collective-permute-done((f32[2,2,32,128]{3,2,1,0:T(8,128)S(1)}, f32[2,2,32,128]{3,2,1,0:T(8,128)S(1)}, u32[]{:S(2)}, u32[]{:S(2)}) %collective-permute-start) | collective-permute-done | bytes 65568 | tf_op jit(solution)/shard_map/ppermute | solution.py:533
  64.0 2.6 %all-to-all-done.2.refs_0_ = s16[16,80,128]{2,1,0:T(8,128)(2,1)S(1)} async-done(((s16[16,80,128]{2,1,0:T(8,128)(2,1)}), s16[16,80,128]{2,1,0:T(8,128)(2,1)S(1)}, u32[]{:S(2)}, u32[]{:S(2)}) %all-to-all-start.2) | async-done | bytes 327712 | tf_op jit(solution)/shard_map/all_to_all | solution.py:528
  66.5 0.9 shard_map.107
  67.5 6.8 %all-to-all-start.3 = ((s16[16,80,128]{2,1,0:T(8,128)(2,1)}), s16[16,80,128]{2,1,0:T(8,128)(2,1)S(1)}, u32[]{:S(2)}, u32[]{:S(2)}) async-start(s16[16,80,128]{2,1,0:T(8,128)(2,1)} %get-tuple-element.22), calls=%async_computation.3 | async-start | bytes 655360 | tf_op jit(solution)/shard_map/all_to_all | solution.py:528
  74.3 2.6 %collective-permute-start.2 = (f32[3,2,32,128]{3,2,1,0:T(8,128)S(1)}, f32[3,2,32,128]{3,2,1,0:T(8,128)S(1)}, u32[]{:S(2)}, u32[]{:S(2)}) collective-permute-start(f32[3,2,32,128]{3,2,1,0:T(8,128)S(1)} %get-tuple-element.24), channel_id=1, source_target_pairs={{0,32},{16,48},{32,64},{48,80},{64,96},{80,112},{96,128},{112,144}... | collective-permute-start | bytes 294920 | tf_op jit(solution)/shard_map/ppermute | solution.py:533
  77.0 1.3 collective-permute-start.3
  78.3 9.2 %all-to-all-done.3.blocks_ref.refs_1_ = s16[16,80,128]{2,1,0:T(8,128)(2,1)S(1)} async-done(((s16[16,80,128]{2,1,0:T(8,128)(2,1)}), s16[16,80,128]{2,1,0:T(8,128)(2,1)S(1)}, u32[]{:S(2)}, u32[]{:S(2)}) %all-to-all-start.3) | async-done | bytes 327712 | tf_op jit(solution)/shard_map/all_to_all | solution.py:528
  87.5 0.6 shard_map.110.refs_10_.near_ref.refs_9_
  88.1 4.6 %collective-permute-start.5 = (f32[2,2,32,128]{3,2,1,0:T(8,128)S(1)}, f32[2,2,32,128]{3,2,1,0:T(8,128)S(1)}, u32[]{:S(2)}, u32[]{:S(2)}) collective-permute-start(f32[2,2,32,128]{3,2,1,0:T(8,128)S(1)} %shard_map.110.refs_10_.near_ref.refs_9_), channel_id=1, source_target_pairs={{16,0},{32,16},{48,32},{64,48},{80,64},{96,80},{112,96},{128,112},... | collective-permute-start | bytes 196616 | tf_op jit(solution)/shard_map/ppermute | solution.py:533
  92.7 2.4 %collective-permute-start.4 = (f32[2,2,32,128]{3,2,1,0:T(8,128)S(1)}, f32[2,2,32,128]{3,2,1,0:T(8,128)S(1)}, u32[]{:S(2)}, u32[]{:S(2)}) collective-permute-start(f32[2,2,32,128]{3,2,1,0:T(8,128)S(1)} %shard_map.110.refs_10_.near_ref.refs_9_), channel_id=1, source_target_pairs={{0,16},{16,32},{32,48},{48,64},{64,80},{80,96},{96,112},{112,128},... | collective-permute-start | bytes 196616 | tf_op jit(solution)/shard_map/ppermute | solution.py:533
  95.2 1.7 %shard_map.111 = f32[16,8,128]{2,1,0:T(8,128)} custom-call(f32[8,128]{1,0:T(8,128)S(1)} %get-tuple-element.21.refs_0_, s16[16,80,128]{2,1,0:T(8,128)(2,1)S(1)} %all-to-all-done.3.blocks_ref.refs_1_, f32[2,2,256,128]{3,2,1,0:T(8,128)S(1)} %get-tuple-element.23.refs_2_, s32[2,256,128]{2,1,0:T(8,128)S(1)} %copy-done.2, f32[2,2,256,128]{3,2,1,0:T(8,128)S(1)} %bitcast.10, ...), custom_call_target="tpu_custom_call" | custom-call | tf_op jit(solution)/shard_map/pallas_call | solution.py:35
  96.9 3.6 %all-to-all-start.4 = ((f32[16,8,128]{2,1,0:T(8,128)}), f32[16,8,128]{2,1,0:T(8,128)S(1)}, u32[]{:S(2)}, u32[]{:S(2)}) async-start(f32[16,8,128]{2,1,0:T(8,128)} %shard_map.111), calls=%async_computation.4 | async-start | bytes 131072 | tf_op jit(solution)/shard_map/all_to_all | solution.py:528
  100.6 3.9 %collective-permute-start.6 = (f32[3,2,32,128]{3,2,1,0:T(8,128)S(1)}, f32[3,2,32,128]{3,2,1,0:T(8,128)S(1)}, u32[]{:S(2)}, u32[]{:S(2)}) collective-permute-start(f32[3,2,32,128]{3,2,1,0:T(8,128)S(1)} %get-tuple-element.26), channel_id=1, source_target_pairs={{0,32},{16,48},{32,64},{48,80},{64,96},{80,112},{96,128},{112,144}... | collective-permute-start | bytes 294920 | tf_op jit(solution)/shard_map/ppermute | solution.py:533
  104.5 1.3 collective-permute-start.7
  105.8 4.2 %all-to-all-done.4.refs_0_ = f32[16,8,128]{2,1,0:T(8,128)S(1)} async-done(((f32[16,8,128]{2,1,0:T(8,128)}), f32[16,8,128]{2,1,0:T(8,128)S(1)}, u32[]{:S(2)}, u32[]{:S(2)}) %all-to-all-start.4) | async-done | bytes 65568 | tf_op jit(solution)/shard_map/all_to_all | solution.py:528
  110.0 0.9 collective-permute-done.7.refs_2_.refs_11_
  110.9 0.6 shard_map.113
  111.5 5.5 %all-to-all-start.5 = ((f32[16,8,128]{2,1,0:T(8,128)}), f32[16,8,128]{2,1,0:T(8,128)S(1)}, u32[]{:S(2)}, u32[]{:S(2)}) async-start(f32[16,8,128]{2,1,0:T(8,128)} %shard_map.113), calls=%async_computation.5 | async-start | bytes 131072 | tf_op jit(solution)/shard_map/all_to_all | solution.py:528
  117.0 0.8 shard_map.114
  117.8 5.1 %all-to-all-done.5.refs_1_ = f32[16,8,128]{2,1,0:T(8,128)S(1)} async-done(((f32[16,8,128]{2,1,0:T(8,128)}), f32[16,8,128]{2,1,0:T(8,128)S(1)}, u32[]{:S(2)}, u32[]{:S(2)}) %all-to-all-start.5) | async-done | bytes 65568 | tf_op jit(solution)/shard_map/all_to_all | solution.py:528
  122.8 10.4 %shard_map.115 = (f32[2,2,16,128]{3,2,1,0:T(8,128)}, f32[2,2,16,128]{3,2,1,0:T(8,128)}) custom-call(s32[2]{0:T(128)S(1)} %pad_add_fusion.at_ref.refs_0_, f32[16,8,128]{2,1,0:T(8,128)S(1)} %all-to-all-done.5.refs_1_, f32[3,2,32,128]{3,2,1,0:T(8,128)S(1)} %collective-permute-done.2.refs_8_.refs_2_, ...), custom_call_target="tpu_custom_call" | custom-call | tf_op jit(solution)/shard_map/pallas_call | solution.py:35
  (32 shorter events, 0.9 us)
Async XLA Ops:
  4.3 11.9 %copy-start.6 = (bf16[32,2,3,3,3]{0,1,4,3,2:T(2,128)(2,1)S(1)}, bf16[32,2,3,3,3]{0,1,4,3,2:T(2,128)(2,1)}, u32[]{:S(2)}) copy-start(bf16[32,2,3,3,3]{0,1,4,3,2:T(2,128)(2,1)} %param.13) | copy-start | bytes 10372
  4.3 42.5 %copy-start.3 = (bf16[128,512]{1,0:T(8,128)(2,1)S(1)}, bf16[128,512]{1,0:T(8,128)(2,1)}, u32[]{:S(2)}) copy-start(bf16[128,512]{1,0:T(8,128)(2,1)} %constant.15.clone.columns_hbm.columns_ref.refs_6_) | copy-start | bytes 393220
  4.3 25.3 %all-to-all-start = ((s16[16,80,128]{2,1,0:T(8,128)(2,1)}), s16[16,80,128]{2,1,0:T(8,128)(2,1)S(1)}, u32[]{:S(2)}, u32[]{:S(2)}) async-start(s16[16,80,128]{2,1,0:T(8,128)(2,1)} %shard_map.104), calls=%async_computation | async-start | bytes 655360 | tf_op jit(solution)/shard_map/all_to_all | solution.py:528
  16.3 0.7 copy-start.7
  16.3 13.4 %copy-start.5 = (f32[2,2,16,128]{3,2,1,0:T(8,128)S(1)}, f32[2,2,16,128]{3,2,1,0:T(8,128)}, u32[]{:S(2)}) copy-start(f32[2,2,16,128]{3,2,1,0:T(8,128)} %refs_1_.1) | copy-start | bytes 98308
  16.3 30.6 %copy-start.2 = (s32[2,256,128]{2,1,0:T(8,128)S(1)}, s32[2,256,128]{2,1,0:T(8,128)}, u32[]{:S(2)}) copy-start(s32[2,256,128]{2,1,0:T(8,128)} %refs_3_.1) | copy-start | bytes 786436
  17.1 29.7 %copy-start = (f32[1,2,2,256,128]{4,3,2,1,0:T(8,128)S(1)}, f32[1,2,2,256,128]{4,3,2,1,0:T(8,128)}, u32[]{:S(2)}) copy-start(f32[1,2,2,256,128]{4,3,2,1,0:T(8,128)} %param.9) | copy-start | bytes 1572868
  17.1 29.7 %copy-start.1 = (bf16[512,512]{1,0:T(8,128)(2,1)S(1)}, bf16[512,512]{1,0:T(8,128)(2,1)}, u32[]{:S(2)}) copy-start(bf16[512,512]{1,0:T(8,128)(2,1)} %constant.14.clone.rows_hbm.rows_ref.refs_5_) | copy-start | bytes 1572868
  30.6 16.2 %all-to-all-start.1 = ((s16[16,80,128]{2,1,0:T(8,128)(2,1)}), s16[16,80,128]{2,1,0:T(8,128)(2,1)S(1)}, u32[]{:S(2)}, u32[]{:S(2)}) async-start(s16[16,80,128]{2,1,0:T(8,128)(2,1)} %get-tuple-element.16), calls=%async_computation.1 | async-start | bytes 655360 | tf_op jit(solution)/shard_map/all_to_all | solution.py:528
  50.9 15.7 %all-to-all-start.2 = ((s16[16,80,128]{2,1,0:T(8,128)(2,1)}), s16[16,80,128]{2,1,0:T(8,128)(2,1)S(1)}, u32[]{:S(2)}, u32[]{:S(2)}) async-start(s16[16,80,128]{2,1,0:T(8,128)(2,1)} %get-tuple-element.17), calls=%async_computation.2 | async-start | bytes 655360 | tf_op jit(solution)/shard_map/all_to_all | solution.py:528
  54.8 7.7 %collective-permute-start.1 = (f32[2,2,32,128]{3,2,1,0:T(8,128)S(1)}, f32[2,2,32,128]{3,2,1,0:T(8,128)S(1)}, u32[]{:S(2)}, u32[]{:S(2)}) collective-permute-start(f32[2,2,32,128]{3,2,1,0:T(8,128)S(1)} %get-tuple-element.20.near_ref.refs_4_), channel_id=1, source_target_pairs={{16,0},{32,16},{48,32},{64,48},{80,64},{96,80},{112,96},{128,112},... | collective-permute-start | bytes 196616 | tf_op jit(solution)/shard_map/ppermute | solution.py:533
  59.9 4.1 %collective-permute-start = (f32[2,2,32,128]{3,2,1,0:T(8,128)S(1)}, f32[2,2,32,128]{3,2,1,0:T(8,128)S(1)}, u32[]{:S(2)}, u32[]{:S(2)}) collective-permute-start(f32[2,2,32,128]{3,2,1,0:T(8,128)S(1)} %get-tuple-element.20.near_ref.refs_4_), channel_id=1, source_target_pairs={{0,16},{16,32},{32,48},{48,64},{64,80},{80,96},{96,112},{112,128},... | collective-permute-start | bytes 196616 | tf_op jit(solution)/shard_map/ppermute | solution.py:533
  67.5 20.0 %all-to-all-start.3 = ((s16[16,80,128]{2,1,0:T(8,128)(2,1)}), s16[16,80,128]{2,1,0:T(8,128)(2,1)S(1)}, u32[]{:S(2)}, u32[]{:S(2)}) async-start(s16[16,80,128]{2,1,0:T(8,128)(2,1)} %get-tuple-element.22), calls=%async_computation.3 | async-start | bytes 655360 | tf_op jit(solution)/shard_map/all_to_all | solution.py:528
  74.3 20.9 %collective-permute-start.2 = (f32[3,2,32,128]{3,2,1,0:T(8,128)S(1)}, f32[3,2,32,128]{3,2,1,0:T(8,128)S(1)}, u32[]{:S(2)}, u32[]{:S(2)}) collective-permute-start(f32[3,2,32,128]{3,2,1,0:T(8,128)S(1)} %get-tuple-element.24), channel_id=1, source_target_pairs={{0,32},{16,48},{32,64},{48,80},{64,96},{80,112},{96,128},{112,144}... | collective-permute-start | bytes 294920 | tf_op jit(solution)/shard_map/ppermute | solution.py:533
  77.0 18.3 %collective-permute-start.3 = (f32[3,2,32,128]{3,2,1,0:T(8,128)S(1)}, f32[3,2,32,128]{3,2,1,0:T(8,128)S(1)}, u32[]{:S(2)}, u32[]{:S(2)}) collective-permute-start(f32[3,2,32,128]{3,2,1,0:T(8,128)S(1)} %get-tuple-element.25), channel_id=1, source_target_pairs={{32,0},{48,16},{64,32},{80,48},{96,64},{112,80},{128,96},{144,112}... | collective-permute-start | bytes 294920 | tf_op jit(solution)/shard_map/ppermute | solution.py:533
  88.1 12.5 %collective-permute-start.5 = (f32[2,2,32,128]{3,2,1,0:T(8,128)S(1)}, f32[2,2,32,128]{3,2,1,0:T(8,128)S(1)}, u32[]{:S(2)}, u32[]{:S(2)}) collective-permute-start(f32[2,2,32,128]{3,2,1,0:T(8,128)S(1)} %shard_map.110.refs_10_.near_ref.refs_9_), channel_id=1, source_target_pairs={{16,0},{32,16},{48,32},{64,48},{80,64},{96,80},{112,96},{128,112},... | collective-permute-start | bytes 196616 | tf_op jit(solution)/shard_map/ppermute | solution.py:533
  92.7 7.8 %collective-permute-start.4 = (f32[2,2,32,128]{3,2,1,0:T(8,128)S(1)}, f32[2,2,32,128]{3,2,1,0:T(8,128)S(1)}, u32[]{:S(2)}, u32[]{:S(2)}) collective-permute-start(f32[2,2,32,128]{3,2,1,0:T(8,128)S(1)} %shard_map.110.refs_10_.near_ref.refs_9_), channel_id=1, source_target_pairs={{0,16},{16,32},{32,48},{48,64},{64,80},{80,96},{96,112},{112,128},... | collective-permute-start | bytes 196616 | tf_op jit(solution)/shard_map/ppermute | solution.py:533
  96.9 20.0 %copy-start.4 = (bf16[3,32,32,3,3,3]{2,1,5,4,3,0:T(8,128)(2,1)S(1)}, bf16[3,32,32,3,3,3]{2,1,5,4,3,0:T(8,128)(2,1)}, u32[]{:S(2)}) copy-start(bf16[3,32,32,3,3,3]{2,1,5,4,3,0:T(8,128)(2,1)} %param.14) | copy-start | bytes 497668
  96.9 13.1 %all-to-all-start.4 = ((f32[16,8,128]{2,1,0:T(8,128)}), f32[16,8,128]{2,1,0:T(8,128)S(1)}, u32[]{:S(2)}, u32[]{:S(2)}) async-start(f32[16,8,128]{2,1,0:T(8,128)} %shard_map.111), calls=%async_computation.4 | async-start | bytes 131072 | tf_op jit(solution)/shard_map/all_to_all | solution.py:528
  100.6 9.4 %collective-permute-start.6 = (f32[3,2,32,128]{3,2,1,0:T(8,128)S(1)}, f32[3,2,32,128]{3,2,1,0:T(8,128)S(1)}, u32[]{:S(2)}, u32[]{:S(2)}) collective-permute-start(f32[3,2,32,128]{3,2,1,0:T(8,128)S(1)} %get-tuple-element.26), channel_id=1, source_target_pairs={{0,32},{16,48},{32,64},{48,80},{64,96},{80,112},{96,128},{112,144}... | collective-permute-start | bytes 294920 | tf_op jit(solution)/shard_map/ppermute | solution.py:533
  104.5 6.4 %collective-permute-start.7 = (f32[3,2,32,128]{3,2,1,0:T(8,128)S(1)}, f32[3,2,32,128]{3,2,1,0:T(8,128)S(1)}, u32[]{:S(2)}, u32[]{:S(2)}) collective-permute-start(f32[3,2,32,128]{3,2,1,0:T(8,128)S(1)} %get-tuple-element.27), channel_id=1, source_target_pairs={{32,0},{48,16},{64,32},{80,48},{96,64},{112,80},{128,96},{144,112}... | collective-permute-start | bytes 294920 | tf_op jit(solution)/shard_map/ppermute | solution.py:533
  111.5 11.3 %all-to-all-start.5 = ((f32[16,8,128]{2,1,0:T(8,128)}), f32[16,8,128]{2,1,0:T(8,128)S(1)}, u32[]{:S(2)}, u32[]{:S(2)}) async-start(f32[16,8,128]{2,1,0:T(8,128)} %shard_map.113), calls=%async_computation.5 | async-start | bytes 131072 | tf_op jit(solution)/shard_map/all_to_all | solution.py:528

commit v11 on v10

--- a/solution.py
+++ b/solution.py
@@ -583,7 +583,7 @@
         after=(*weights[2:], rhs_parts[0], rhs_parts[4], image_near),
     )
     image_parts = near_planes(image_near)
-    tiles = call(spread_kernel, struct((slabs, 8, 128)), (swap(tiles, "coil"),), after=(image_parts[0], image_parts[4]))
+    tiles = call(spread_kernel, struct((slabs, 8, 128)), (swap(tiles, "coil"),), after=image_parts[:1])
     last = swap(tiles, "slab")
     scratch = [pltpu.VMEM((12, 144, 256), BF16)]
     scratch += [pltpu.VMEM((10 - 2 * m, (16 - 2 * m) * 32, 256), BF16) for m in range(4)]

time: 134 us -> 133 us (level)
  transfers between devices with their start and end apart: 14 -> 14, of which waited for: 9 -> 8; matrix products, arithmetic and copies ran while one was open for 0% -> 0% of each run, Pallas kernels for 2% -> 3%
where the time goes in v11:
time: 133 us
  starting transfers between devices  59.3 us (45%)
  waiting for transfers between devices  47.7 us (36%)
  Pallas kernels  23.7 us (18%)
    all_to_all x6, waiting for transfers between devices, swap(): return lax.all_to_all(blocks, axis, 0, 0, tiled=True)  45.8 us
    all_to_all x6, starting transfers between devices, swap(): return lax.all_to_all(blocks, axis, 0, 0, tiled=True)  35.8 us
    ppermute x8, starting transfers between devices, shifted(): lax.ppermute(part, axis, [(i, i + step) for i in range(count) if 0 <= i +...  23.5 us
    pallas_call x11, Pallas kernels, call(): pl.pallas_call(kernel, out_shape=out_shape, in_specs=specs, out_specs=out...  20 us
    pallas_call x1, Pallas kernels, adjoint(): pl.pallas_call(adjoint_kernel, out_shape=struct((coils, 80, 128), jnp.int...  3.67 us
  transfers between devices with their start and end apart: 14, of which 8 were waited for; matrix products, arithmetic and copies ran while one was open for 0% of the time, Pallas kernels for 3%

profile of v11, /device:TPU:1, one launch (start us, length us, event | category | flops | bytes accessed | tf_op | source)
XLA Modules:
  0.0 132.6 jit_solution(2746398420195765779)
XLA Ops:
  0.6 3.7 %shard_map.104 = s16[16,80,128]{2,1,0:T(8,128)(2,1)} custom-call(s32[2,256,128]{2,1,0:T(8,128)} %refs_3_.1, f32[2,2,256,128]{3,2,1,0:T(8,128)} %bitcast.12, bf16[512,512]{1,0:T(8,128)(2,1)} %constant.14.clone.rows_hbm.rows_ref.refs_5_, bf16[128,512]{1,0:T(8,128)(2,1)} %constant.15.clone.columns_hbm.columns_ref.refs_6_, f32[2,2,256,128]{3,2,1,0:T(8,128)} %bitcast.8), custom_call_target="tpu_custom_call" | custom-call | tf_op jit(solution)/shard_map/pallas_call | solution.py:253
  4.3 11.9 %all-to-all-start = ((s16[16,80,128]{2,1,0:T(8,128)(2,1)}), s16[16,80,128]{2,1,0:T(8,128)(2,1)S(1)}, u32[]{:S(2)}, u32[]{:S(2)}) async-start(s16[16,80,128]{2,1,0:T(8,128)(2,1)} %shard_map.104), calls=%async_computation | async-start | bytes 655360 | tf_op jit(solution)/shard_map/all_to_all | solution.py:528
  16.4 0.6 copy-done.7
  17.2 12.5 %all-to-all-done.refs_0_ = s16[16,80,128]{2,1,0:T(8,128)(2,1)S(1)} async-done(((s16[16,80,128]{2,1,0:T(8,128)(2,1)}), s16[16,80,128]{2,1,0:T(8,128)(2,1)S(1)}, u32[]{:S(2)}, u32[]{:S(2)}) %all-to-all-start) | async-done | bytes 327712 | tf_op jit(solution)/shard_map/all_to_all | solution.py:528
  29.7 1.0 shard_map.105
  30.6 3.9 %all-to-all-start.1 = ((s16[16,80,128]{2,1,0:T(8,128)(2,1)}), s16[16,80,128]{2,1,0:T(8,128)(2,1)S(1)}, u32[]{:S(2)}, u32[]{:S(2)}) async-start(s16[16,80,128]{2,1,0:T(8,128)(2,1)} %get-tuple-element.16), calls=%async_computation.1 | async-start | bytes 655360 | tf_op jit(solution)/shard_map/all_to_all | solution.py:528
  34.6 12.2 %all-to-all-done.1.blocks_ref = s16[16,80,128]{2,1,0:T(8,128)(2,1)S(1)} async-done(((s16[16,80,128]{2,1,0:T(8,128)(2,1)}), s16[16,80,128]{2,1,0:T(8,128)(2,1)S(1)}, u32[]{:S(2)}, u32[]{:S(2)}) %all-to-all-start.1) | async-done | bytes 327712 | tf_op jit(solution)/shard_map/all_to_all | solution.py:528
  46.9 4.0 %shard_map.106 = (s16[16,80,128]{2,1,0:T(8,128)(2,1)}, f32[2,2,256,128]{3,2,1,0:T(8,128)S(1)}, f32[8,128]{1,0:T(8,128)S(1)}, f32[2,2,32,128]{3,2,1,0:T(8,128)S(1)}) custom-call(s32[2]{0:T(128)S(1)} %pad_add_fusion.at_ref.refs_0_, s16[16,80,128]{2,1,0:T(8,128)(2,1)S(1)} %all-to-all-done.1.blocks_ref, s32[2,256,128]{2,1,0:T(8,128)S(1)} %copy-done.2, ...), custom_call_target="tpu_custom_call" | custom-call | tf_op jit(solution)/shard_map/pallas_call | solution.py:35
  50.9 3.9 %all-to-all-start.2 = ((s16[16,80,128]{2,1,0:T(8,128)(2,1)}), s16[16,80,128]{2,1,0:T(8,128)(2,1)S(1)}, u32[]{:S(2)}, u32[]{:S(2)}) async-start(s16[16,80,128]{2,1,0:T(8,128)(2,1)} %get-tuple-element.17), calls=%async_computation.2 | async-start | bytes 655360 | tf_op jit(solution)/shard_map/all_to_all | solution.py:528
  54.8 5.1 %collective-permute-start.1 = (f32[2,2,32,128]{3,2,1,0:T(8,128)S(1)}, f32[2,2,32,128]{3,2,1,0:T(8,128)S(1)}, u32[]{:S(2)}, u32[]{:S(2)}) collective-permute-start(f32[2,2,32,128]{3,2,1,0:T(8,128)S(1)} %get-tuple-element.20.near_ref.refs_4_), channel_id=1, source_target_pairs={{16,0},{32,16},{48,32},{64,48},{80,64},{96,80},{112,96},{128,112},... | collective-permute-start | bytes 196616 | tf_op jit(solution)/shard_map/ppermute | solution.py:533
  59.9 2.2 %collective-permute-start = (f32[2,2,32,128]{3,2,1,0:T(8,128)S(1)}, f32[2,2,32,128]{3,2,1,0:T(8,128)S(1)}, u32[]{:S(2)}, u32[]{:S(2)}) collective-permute-start(f32[2,2,32,128]{3,2,1,0:T(8,128)S(1)} %get-tuple-element.20.near_ref.refs_4_), channel_id=1, source_target_pairs={{0,16},{16,32},{32,48},{48,64},{64,80},{80,96},{96,112},{112,128},... | collective-permute-start | bytes 196616 | tf_op jit(solution)/shard_map/ppermute | solution.py:533
  62.1 0.4 collective-permute-done.1.refs_4_.above_ref.refs_5_
  62.5 1.5 %collective-permute-done.refs_3_.below_ref = f32[2,2,32,128]{3,2,1,0:T(8,128)S(1)} collective-permute-done((f32[2,2,32,128]{3,2,1,0:T(8,128)S(1)}, f32[2,2,32,128]{3,2,1,0:T(8,128)S(1)}, u32[]{:S(2)}, u32[]{:S(2)}) %collective-permute-start) | collective-permute-done | bytes 65568 | tf_op jit(solution)/shard_map/ppermute | solution.py:533
  64.0 2.6 %all-to-all-done.2.refs_0_ = s16[16,80,128]{2,1,0:T(8,128)(2,1)S(1)} async-done(((s16[16,80,128]{2,1,0:T(8,128)(2,1)}), s16[16,80,128]{2,1,0:T(8,128)(2,1)S(1)}, u32[]{:S(2)}, u32[]{:S(2)}) %all-to-all-start.2) | async-done | bytes 327712 | tf_op jit(solution)/shard_map/all_to_all | solution.py:528
  66.5 0.9 shard_map.107
  67.5 6.8 %all-to-all-start.3 = ((s16[16,80,128]{2,1,0:T(8,128)(2,1)}), s16[16,80,128]{2,1,0:T(8,128)(2,1)S(1)}, u32[]{:S(2)}, u32[]{:S(2)}) async-start(s16[16,80,128]{2,1,0:T(8,128)(2,1)} %get-tuple-element.22), calls=%async_computation.3 | async-start | bytes 655360 | tf_op jit(solution)/shard_map/all_to_all | solution.py:528
  74.3 2.6 %collective-permute-start.2 = (f32[3,2,32,128]{3,2,1,0:T(8,128)S(1)}, f32[3,2,32,128]{3,2,1,0:T(8,128)S(1)}, u32[]{:S(2)}, u32[]{:S(2)}) collective-permute-start(f32[3,2,32,128]{3,2,1,0:T(8,128)S(1)} %get-tuple-element.24), channel_id=1, source_target_pairs={{0,32},{16,48},{32,64},{48,80},{64,96},{80,112},{96,128},{112,144}... | collective-permute-start | bytes 294920 | tf_op jit(solution)/shard_map/ppermute | solution.py:533
  77.0 1.3 collective-permute-start.3
  78.3 9.2 %all-to-all-done.3.blocks_ref.refs_1_ = s16[16,80,128]{2,1,0:T(8,128)(2,1)S(1)} async-done(((s16[16,80,128]{2,1,0:T(8,128)(2,1)}), s16[16,80,128]{2,1,0:T(8,128)(2,1)S(1)}, u32[]{:S(2)}, u32[]{:S(2)}) %all-to-all-start.3) | async-done | bytes 327712 | tf_op jit(solution)/shard_map/all_to_all | solution.py:528
  87.5 0.6 shard_map.110.refs_10_.near_ref.refs_9_
  88.1 4.6 %collective-permute-start.5 = (f32[2,2,32,128]{3,2,1,0:T(8,128)S(1)}, f32[2,2,32,128]{3,2,1,0:T(8,128)S(1)}, u32[]{:S(2)}, u32[]{:S(2)}) collective-permute-start(f32[2,2,32,128]{3,2,1,0:T(8,128)S(1)} %shard_map.110.refs_10_.near_ref.refs_9_), channel_id=1, source_target_pairs={{16,0},{32,16},{48,32},{64,48},{80,64},{96,80},{112,96},{128,112},... | collective-permute-start | bytes 196616 | tf_op jit(solution)/shard_map/ppermute | solution.py:533
  92.7 2.4 %collective-permute-start.4 = (f32[2,2,32,128]{3,2,1,0:T(8,128)S(1)}, f32[2,2,32,128]{3,2,1,0:T(8,128)S(1)}, u32[]{:S(2)}, u32[]{:S(2)}) collective-permute-start(f32[2,2,32,128]{3,2,1,0:T(8,128)S(1)} %shard_map.110.refs_10_.near_ref.refs_9_), channel_id=1, source_target_pairs={{0,16},{16,32},{32,48},{48,64},{64,80},{80,96},{96,112},{112,128},... | collective-permute-start | bytes 196616 | tf_op jit(solution)/shard_map/ppermute | solution.py:533
  95.2 1.7 %shard_map.111 = f32[16,8,128]{2,1,0:T(8,128)} custom-call(f32[8,128]{1,0:T(8,128)S(1)} %get-tuple-element.21.refs_0_, s16[16,80,128]{2,1,0:T(8,128)(2,1)S(1)} %all-to-all-done.3.blocks_ref.refs_1_, f32[2,2,256,128]{3,2,1,0:T(8,128)S(1)} %get-tuple-element.23.refs_2_, s32[2,256,128]{2,1,0:T(8,128)S(1)} %copy-done.2, f32[2,2,256,128]{3,2,1,0:T(8,128)S(1)} %bitcast.10, ...), custom_call_target="tpu_custom_call" | custom-call | tf_op jit(solution)/shard_map/pallas_call | solution.py:35
  96.9 3.6 %all-to-all-start.4 = ((f32[16,8,128]{2,1,0:T(8,128)}), f32[16,8,128]{2,1,0:T(8,128)S(1)}, u32[]{:S(2)}, u32[]{:S(2)}) async-start(f32[16,8,128]{2,1,0:T(8,128)} %shard_map.111), calls=%async_computation.4 | async-start | bytes 131072 | tf_op jit(solution)/shard_map/all_to_all | solution.py:528
  100.6 3.9 %collective-permute-start.6 = (f32[3,2,32,128]{3,2,1,0:T(8,128)S(1)}, f32[3,2,32,128]{3,2,1,0:T(8,128)S(1)}, u32[]{:S(2)}, u32[]{:S(2)}) collective-permute-start(f32[3,2,32,128]{3,2,1,0:T(8,128)S(1)} %get-tuple-element.26), channel_id=1, source_target_pairs={{0,32},{16,48},{32,64},{48,80},{64,96},{80,112},{96,128},{112,144}... | collective-permute-start | bytes 294920 | tf_op jit(solution)/shard_map/ppermute | solution.py:533
  104.5 1.3 collective-permute-start.7
  105.8 4.2 %all-to-all-done.4.refs_0_ = f32[16,8,128]{2,1,0:T(8,128)S(1)} async-done(((f32[16,8,128]{2,1,0:T(8,128)}), f32[16,8,128]{2,1,0:T(8,128)S(1)}, u32[]{:S(2)}, u32[]{:S(2)}) %all-to-all-start.4) | async-done | bytes 65568 | tf_op jit(solution)/shard_map/all_to_all | solution.py:528
  110.0 0.6 shard_map.113
  110.7 5.7 %all-to-all-start.5 = ((f32[16,8,128]{2,1,0:T(8,128)}), f32[16,8,128]{2,1,0:T(8,128)S(1)}, u32[]{:S(2)}, u32[]{:S(2)}) async-start(f32[16,8,128]{2,1,0:T(8,128)} %shard_map.113), calls=%async_computation.5 | async-start | bytes 131072 | tf_op jit(solution)/shard_map/all_to_all | solution.py:528
  116.4 0.8 shard_map.114
  117.2 5.1 %all-to-all-done.5.refs_1_ = f32[16,8,128]{2,1,0:T(8,128)S(1)} async-done(((f32[16,8,128]{2,1,0:T(8,128)}), f32[16,8,128]{2,1,0:T(8,128)S(1)}, u32[]{:S(2)}, u32[]{:S(2)}) %all-to-all-start.5) | async-done | bytes 65568 | tf_op jit(solution)/shard_map/all_to_all | solution.py:528
  122.2 10.4 %shard_map.115 = (f32[2,2,16,128]{3,2,1,0:T(8,128)}, f32[2,2,16,128]{3,2,1,0:T(8,128)}) custom-call(s32[2]{0:T(128)S(1)} %pad_add_fusion.at_ref.refs_0_, f32[16,8,128]{2,1,0:T(8,128)S(1)} %all-to-all-done.5.refs_1_, f32[3,2,32,128]{3,2,1,0:T(8,128)S(1)} %collective-permute-done.2.refs_8_.refs_2_, ...), custom_call_target="tpu_custom_call" | custom-call | tf_op jit(solution)/shard_map/pallas_call | solution.py:35
  (32 shorter events, 0.5 us)
Async XLA Ops:
  4.3 11.9 %copy-start.6 = (bf16[32,2,3,3,3]{0,1,4,3,2:T(2,128)(2,1)S(1)}, bf16[32,2,3,3,3]{0,1,4,3,2:T(2,128)(2,1)}, u32[]{:S(2)}) copy-start(bf16[32,2,3,3,3]{0,1,4,3,2:T(2,128)(2,1)} %param.13) | copy-start | bytes 10372
  4.3 42.5 %copy-start.3 = (bf16[128,512]{1,0:T(8,128)(2,1)S(1)}, bf16[128,512]{1,0:T(8,128)(2,1)}, u32[]{:S(2)}) copy-start(bf16[128,512]{1,0:T(8,128)(2,1)} %constant.15.clone.columns_hbm.columns_ref.refs_6_) | copy-start | bytes 393220
  4.3 25.3 %all-to-all-start = ((s16[16,80,128]{2,1,0:T(8,128)(2,1)}), s16[16,80,128]{2,1,0:T(8,128)(2,1)S(1)}, u32[]{:S(2)}, u32[]{:S(2)}) async-start(s16[16,80,128]{2,1,0:T(8,128)(2,1)} %shard_map.104), calls=%async_computation | async-start | bytes 655360 | tf_op jit(solution)/shard_map/all_to_all | solution.py:528
  16.3 0.7 copy-start.7
  16.3 13.4 %copy-start.5 = (f32[2,2,16,128]{3,2,1,0:T(8,128)S(1)}, f32[2,2,16,128]{3,2,1,0:T(8,128)}, u32[]{:S(2)}) copy-start(f32[2,2,16,128]{3,2,1,0:T(8,128)} %refs_1_.1) | copy-start | bytes 98308
  16.3 30.6 %copy-start.2 = (s32[2,256,128]{2,1,0:T(8,128)S(1)}, s32[2,256,128]{2,1,0:T(8,128)}, u32[]{:S(2)}) copy-start(s32[2,256,128]{2,1,0:T(8,128)} %refs_3_.1) | copy-start | bytes 786436
  17.1 29.7 %copy-start = (f32[1,2,2,256,128]{4,3,2,1,0:T(8,128)S(1)}, f32[1,2,2,256,128]{4,3,2,1,0:T(8,128)}, u32[]{:S(2)}) copy-start(f32[1,2,2,256,128]{4,3,2,1,0:T(8,128)} %param.9) | copy-start | bytes 1572868
  17.1 29.7 %copy-start.1 = (bf16[512,512]{1,0:T(8,128)(2,1)S(1)}, bf16[512,512]{1,0:T(8,128)(2,1)}, u32[]{:S(2)}) copy-start(bf16[512,512]{1,0:T(8,128)(2,1)} %constant.14.clone.rows_hbm.rows_ref.refs_5_) | copy-start | bytes 1572868
  30.6 16.2 %all-to-all-start.1 = ((s16[16,80,128]{2,1,0:T(8,128)(2,1)}), s16[16,80,128]{2,1,0:T(8,128)(2,1)S(1)}, u32[]{:S(2)}, u32[]{:S(2)}) async-start(s16[16,80,128]{2,1,0:T(8,128)(2,1)} %get-tuple-element.16), calls=%async_computation.1 | async-start | bytes 655360 | tf_op jit(solution)/shard_map/all_to_all | solution.py:528
  50.9 15.7 %all-to-all-start.2 = ((s16[16,80,128]{2,1,0:T(8,128)(2,1)}), s16[16,80,128]{2,1,0:T(8,128)(2,1)S(1)}, u32[]{:S(2)}, u32[]{:S(2)}) async-start(s16[16,80,128]{2,1,0:T(8,128)(2,1)} %get-tuple-element.17), calls=%async_computation.2 | async-start | bytes 655360 | tf_op jit(solution)/shard_map/all_to_all | solution.py:528
  54.8 7.7 %collective-permute-start.1 = (f32[2,2,32,128]{3,2,1,0:T(8,128)S(1)}, f32[2,2,32,128]{3,2,1,0:T(8,128)S(1)}, u32[]{:S(2)}, u32[]{:S(2)}) collective-permute-start(f32[2,2,32,128]{3,2,1,0:T(8,128)S(1)} %get-tuple-element.20.near_ref.refs_4_), channel_id=1, source_target_pairs={{16,0},{32,16},{48,32},{64,48},{80,64},{96,80},{112,96},{128,112},... | collective-permute-start | bytes 196616 | tf_op jit(solution)/shard_map/ppermute | solution.py:533
  59.9 4.1 %collective-permute-start = (f32[2,2,32,128]{3,2,1,0:T(8,128)S(1)}, f32[2,2,32,128]{3,2,1,0:T(8,128)S(1)}, u32[]{:S(2)}, u32[]{:S(2)}) collective-permute-start(f32[2,2,32,128]{3,2,1,0:T(8,128)S(1)} %get-tuple-element.20.near_ref.refs_4_), channel_id=1, source_target_pairs={{0,16},{16,32},{32,48},{48,64},{64,80},{80,96},{96,112},{112,128},... | collective-permute-start | bytes 196616 | tf_op jit(solution)/shard_map/ppermute | solution.py:533
  67.5 20.0 %all-to-all-start.3 = ((s16[16,80,128]{2,1,0:T(8,128)(2,1)}), s16[16,80,128]{2,1,0:T(8,128)(2,1)S(1)}, u32[]{:S(2)}, u32[]{:S(2)}) async-start(s16[16,80,128]{2,1,0:T(8,128)(2,1)} %get-tuple-element.22), calls=%async_computation.3 | async-start | bytes 655360 | tf_op jit(solution)/shard_map/all_to_all | solution.py:528
  74.3 20.9 %collective-permute-start.2 = (f32[3,2,32,128]{3,2,1,0:T(8,128)S(1)}, f32[3,2,32,128]{3,2,1,0:T(8,128)S(1)}, u32[]{:S(2)}, u32[]{:S(2)}) collective-permute-start(f32[3,2,32,128]{3,2,1,0:T(8,128)S(1)} %get-tuple-element.24), channel_id=1, source_target_pairs={{0,32},{16,48},{32,64},{48,80},{64,96},{80,112},{96,128},{112,144}... | collective-permute-start | bytes 294920 | tf_op jit(solution)/shard_map/ppermute | solution.py:533
  77.0 18.3 %collective-permute-start.3 = (f32[3,2,32,128]{3,2,1,0:T(8,128)S(1)}, f32[3,2,32,128]{3,2,1,0:T(8,128)S(1)}, u32[]{:S(2)}, u32[]{:S(2)}) collective-permute-start(f32[3,2,32,128]{3,2,1,0:T(8,128)S(1)} %get-tuple-element.25), channel_id=1, source_target_pairs={{32,0},{48,16},{64,32},{80,48},{96,64},{112,80},{128,96},{144,112}... | collective-permute-start | bytes 294920 | tf_op jit(solution)/shard_map/ppermute | solution.py:533
  88.1 12.5 %collective-permute-start.5 = (f32[2,2,32,128]{3,2,1,0:T(8,128)S(1)}, f32[2,2,32,128]{3,2,1,0:T(8,128)S(1)}, u32[]{:S(2)}, u32[]{:S(2)}) collective-permute-start(f32[2,2,32,128]{3,2,1,0:T(8,128)S(1)} %shard_map.110.refs_10_.near_ref.refs_9_), channel_id=1, source_target_pairs={{16,0},{32,16},{48,32},{64,48},{80,64},{96,80},{112,96},{128,112},... | collective-permute-start | bytes 196616 | tf_op jit(solution)/shard_map/ppermute | solution.py:533
  92.7 7.8 %collective-permute-start.4 = (f32[2,2,32,128]{3,2,1,0:T(8,128)S(1)}, f32[2,2,32,128]{3,2,1,0:T(8,128)S(1)}, u32[]{:S(2)}, u32[]{:S(2)}) collective-permute-start(f32[2,2,32,128]{3,2,1,0:T(8,128)S(1)} %shard_map.110.refs_10_.near_ref.refs_9_), channel_id=1, source_target_pairs={{0,16},{16,32},{32,48},{48,64},{64,80},{80,96},{96,112},{112,128},... | collective-permute-start | bytes 196616 | tf_op jit(solution)/shard_map/ppermute | solution.py:533
  96.9 19.4 %copy-start.4 = (bf16[3,32,32,3,3,3]{2,1,5,4,3,0:T(8,128)(2,1)S(1)}, bf16[3,32,32,3,3,3]{2,1,5,4,3,0:T(8,128)(2,1)}, u32[]{:S(2)}) copy-start(bf16[3,32,32,3,3,3]{2,1,5,4,3,0:T(8,128)(2,1)} %param.14) | copy-start | bytes 497668
  96.9 13.1 %all-to-all-start.4 = ((f32[16,8,128]{2,1,0:T(8,128)}), f32[16,8,128]{2,1,0:T(8,128)S(1)}, u32[]{:S(2)}, u32[]{:S(2)}) async-start(f32[16,8,128]{2,1,0:T(8,128)} %shard_map.111), calls=%async_computation.4 | async-start | bytes 131072 | tf_op jit(solution)/shard_map/all_to_all | solution.py:528
  100.6 9.4 %collective-permute-start.6 = (f32[3,2,32,128]{3,2,1,0:T(8,128)S(1)}, f32[3,2,32,128]{3,2,1,0:T(8,128)S(1)}, u32[]{:S(2)}, u32[]{:S(2)}) collective-permute-start(f32[3,2,32,128]{3,2,1,0:T(8,128)S(1)} %get-tuple-element.26), channel_id=1, source_target_pairs={{0,32},{16,48},{32,64},{48,80},{64,96},{80,112},{96,128},{112,144}... | collective-permute-start | bytes 294920 | tf_op jit(solution)/shard_map/ppermute | solution.py:533
  104.5 12.6 %collective-permute-start.7 = (f32[3,2,32,128]{3,2,1,0:T(8,128)S(1)}, f32[3,2,32,128]{3,2,1,0:T(8,128)S(1)}, u32[]{:S(2)}, u32[]{:S(2)}) collective-permute-start(f32[3,2,32,128]{3,2,1,0:T(8,128)S(1)} %get-tuple-element.27), channel_id=1, source_target_pairs={{32,0},{48,16},{64,32},{80,48},{96,64},{112,80},{128,96},{144,112}... | collective-permute-start | bytes 294920 | tf_op jit(solution)/shard_map/ppermute | solution.py:533
  110.7 11.6 %all-to-all-start.5 = ((f32[16,8,128]{2,1,0:T(8,128)}), f32[16,8,128]{2,1,0:T(8,128)S(1)}, u32[]{:S(2)}, u32[]{:S(2)}) async-start(f32[16,8,128]{2,1,0:T(8,128)} %shard_map.113), calls=%async_computation.5 | async-start | bytes 131072 | tf_op jit(solution)/shard_map/all_to_all | solution.py:528
